TPU v7x, 32 devices: a whole 2x2x4 slice. The times are simulated.
32 devices in a mesh: cells: 4 (over y, x), genes: 8 (over z, core).
Axes of the slice: x: 2, y: 2, z: 4, core: 2. Of those that a mesh axis runs over, the one named last changes fastest.
Arguments:
- counts: bfloat16 [32768, 2560], P('cells', 'genes'), may hold values from 0 to 8, as said below
- library: float32 [32768], P('cells'), may hold values from 7 to 10
- noise: float32 [32768, 10], P('cells'), may hold values from -4 to 4
- batch_ids: int32 [32768], P('cells'), may hold values from 0 to 127
- gene_mask: int32 [2560], P('genes'), may hold values 0 or 1
- kl_weight: float32 [1], replicated, may hold values from 0.5 to 1
- enc_w: float32 [2560, 128], P('genes'), may hold values from -0.125 to 0.125
- enc_m: float32 [2560, 128], P('genes'), may hold values from -6.1035156e-05 to 6.1035156e-05
- enc_v: float32 [2560, 128], P('genes'), may hold values from 1.0172526e-11 to 4.0690104e-11
- dec_w: float32 [2, 128, 2560], P(None, None, 'genes'), may hold values from -0.5 to 0.5
- dec_m: float32 [2, 128, 2560], P(None, None, 'genes'), may hold values from -6.1035156e-05 to 6.1035156e-05
- dec_v: float32 [2, 128, 2560], P(None, None, 'genes'), may hold values from 1.0172526e-11 to 4.0690104e-11
- gene_par: float32 [3, 2560], P(None, 'genes'), may hold values from -3 to 3
- gene_m: float32 [3, 2560], P(None, 'genes'), may hold values from -0.00024414062 to 0.00024414062
- gene_v: float32 [3, 2560], P(None, 'genes'), may hold values from 1.6276042e-10 to 6.5104167e-10
- small_w: float32 [266, 128], replicated, may hold values from -3 to 3
- small_m: float32 [266, 128], replicated, may hold values from -3.0517578e-05 to 3.0517578e-05
- small_v: float32 [266, 128], replicated, may hold values from 3.0517578e-12 to 1.2207031e-11
- head_w: float32 [129, 20], replicated, may hold values from -0.5 to 0.5
- head_m: float32 [129, 20], replicated, may hold values from -0.00024414062 to 0.00024414062
- head_v: float32 [129, 20], replicated, may hold values from 1.6276042e-10 to 6.5104167e-10
- norm_par: float32 [4, 128], replicated, may hold values from 0.5 to 1.5
- norm_m: float32 [4, 128], replicated, may hold values from -0.00024414062 to 0.00024414062
- norm_v: float32 [4, 128], replicated, may hold values from 1.6276042e-10 to 6.5104167e-10
Outputs:
- enc_new: float32 [2560, 128], P('genes')
- enc_m_new: float32 [2560, 128], P('genes')
- enc_v_new: float32 [2560, 128], P('genes')
- enc_low: bfloat16 [2560, 128], P('genes')
- dec_new: float32 [2, 128, 2560], P(None, None, 'genes')
- dec_m_new: float32 [2, 128, 2560], P(None, None, 'genes')
- dec_v_new: float32 [2, 128, 2560], P(None, None, 'genes')
- dec_low: bfloat16 [2, 128, 2560], P(None, None, 'genes')
- gene_new: float32 [3, 2560], P(None, 'genes')
- gene_m_new: float32 [3, 2560], P(None, 'genes')
- gene_v_new: float32 [3, 2560], P(None, 'genes')
- small_new: float32 [266, 128], replicated
- small_m_new: float32 [266, 128], replicated
- small_v_new: float32 [266, 128], replicated
- head_new: float32 [129, 20], replicated
- head_m_new: float32 [129, 20], replicated
- head_v_new: float32 [129, 20], replicated
- norm_new: float32 [4, 128], replicated
- norm_m_new: float32 [4, 128], replicated
- norm_v_new: float32 [4, 128], replicated
- grad_norm: float32 [], replicated
- loss: float32 [32768], P(('cells', 'genes'))
Inputs may be any that keep to these rules, and one draw needn't show every extreme that they name: `counts`: whole numbers.
All inputs are finite; a program needn't handle non-finite values. No bound on the sum of `gene_mask` on one device may be relied on, other than what follows from the above.
Results may differ from a plain program's by a relative error of at most 0.0047.
Values may be sent and summed in bfloat16 or wider, within the bound.
No kernel may reach another device: no remote copies, remote signals or barrier semaphores. Data moves between devices by JAX's collectives and lax.ppermute only.
A program may use at most 192 MiB of HBM per device.

v0:
```python
import jax
import jax.numpy as jnp
from jax import lax
from jax.sharding import PartitionSpec as P

norm_epsilon = 0.001
zinb_epsilon = 1e-08
beta_one = 0.9
beta_two = 0.999
step_number = 5.0
decay_rate = 0.01
rate_genes = 0.03
rate_small = 0.2
max_norm = 0.1


def exact_dot(left, right):
    return jnp.dot(left, right, precision=lax.Precision.HIGHEST, preferred_element_type=jnp.float32)


def exact_inner(left, right):
    return lax.dot_general(
        left,
        right,
        (((0,), (0,)), ((), ())),
        precision=lax.Precision.HIGHEST,
        preferred_element_type=jnp.float32,
    )


def exact_back(left, right):
    return lax.dot_general(
        left,
        right,
        (((1,), (1,)), ((), ())),
        precision=lax.Precision.HIGHEST,
        preferred_element_type=jnp.float32,
    )


def plain_inner(left, right):
    return lax.dot_general(
        left, right, (((0,), (0,)), ((), ())), preferred_element_type=jnp.float32
    )


def plain_back(left, right):
    return lax.dot_general(
        left, right, (((1,), (1,)), ((), ())), preferred_element_type=jnp.float32
    )


def zinb_loglik(observed, log_mean, drop_logit, log_disp):
    dispersion = jnp.exp(log_disp)
    mean_rate = jnp.exp(log_mean)
    soft_drop = jax.nn.softplus(-drop_logit)
    log_disp_eps = jnp.log(dispersion + zinb_epsilon)
    log_both = jnp.log(dispersion + mean_rate + zinb_epsilon)
    drop_term = -drop_logit + dispersion * (log_disp_eps - log_both)
    case_zero = jax.nn.softplus(drop_term) - soft_drop
    case_other = (
        -soft_drop
        + drop_term
        + observed * (jnp.log(mean_rate + zinb_epsilon) - log_both)
        + lax.lgamma(observed + dispersion)
        - lax.lgamma(dispersion)
        - lax.lgamma(observed + 1.0)
    )
    return jnp.where(observed < zinb_epsilon, case_zero, case_other)


def wide_sum(values):
    return lax.psum((values[0], values[1]), ("cells", "genes"))


def norm_forward(pre_act, gain_row, shift_row, cell_total):
    stat_sums = wide_sum((jnp.sum(pre_act, 0), jnp.sum(pre_act * pre_act, 0)))
    stat_mean = stat_sums[0] / cell_total
    stat_var = stat_sums[1] / cell_total - stat_mean * stat_mean
    inv_std = lax.rsqrt(stat_var + norm_epsilon)
    centred = (pre_act - stat_mean) * inv_std
    affine = gain_row * centred + shift_row
    return (jax.nn.relu(affine), (centred, inv_std, affine > 0))


def norm_backward(gradient, saved, gain_row, cell_total):
    centred, inv_std, active = saved
    grad_affine = jnp.where(active, gradient, 0.0)
    stat_sums = wide_sum((jnp.sum(grad_affine, 0), jnp.sum(grad_affine * centred, 0)))
    grad_pre = (
        gain_row
        * inv_std
        * (grad_affine - stat_sums[0] / cell_total - centred * stat_sums[1] / cell_total)
    )
    return (grad_pre, stat_sums[1], stat_sums[0])


def adamw(weight, gradient, moment_one, moment_two, step_rate):
    moment_one = beta_one * moment_one + (1.0 - beta_one) * gradient
    moment_two = beta_two * moment_two + (1.0 - beta_two) * gradient * gradient
    fixed_one = moment_one / (1.0 - beta_one**step_number)
    fixed_two = moment_two / (1.0 - beta_two**step_number)
    update = fixed_one / (jnp.sqrt(fixed_two) + 1e-08) + decay_rate * weight
    return (weight - step_rate * update, moment_one, moment_two)


def per_device(
    counts,
    library,
    noise,
    batch_ids,
    gene_mask,
    kl_weight,
    enc_w,
    enc_m,
    enc_v,
    dec_w,
    dec_m,
    dec_v,
    gene_par,
    gene_m,
    gene_v,
    small_w,
    small_m,
    small_v,
    head_w,
    head_m,
    head_v,
    norm_par,
    norm_m,
    norm_v,
):
    rows_all = counts.shape[0]
    local_genes = counts.shape[1]
    cell_total = rows_all * lax.axis_size("cells")
    groups = lax.axis_size("genes")
    hidden = enc_w.shape[1]
    latent = head_w.shape[1] // 2
    batch_kinds = (small_w.shape[0] - latent) // 2
    log_counts = jnp.log1p(counts.astype(jnp.float32)).astype(jnp.bfloat16)
    enc_low = enc_w.astype(jnp.bfloat16)
    dec_cat = jnp.concatenate([dec_w[0], dec_w[1]], axis=1).astype(jnp.bfloat16)
    gene_keep = gene_mask > 0
    share_rows = rows_all // groups
    first_row = lax.axis_index("genes") * share_rows
    cell_rows = log_counts
    enc_part = lax.psum_scatter(
        jnp.dot(cell_rows, enc_low, preferred_element_type=jnp.float32),
        "genes",
        scatter_dimension=0,
        tiled=True,
    )
    own_batch = lax.dynamic_slice_in_dim(batch_ids, first_row, share_rows, 0)
    own_noise = lax.dynamic_slice_in_dim(noise, first_row, share_rows, 0)
    batch_table = (own_batch[:, None] == jnp.arange(batch_kinds, dtype=jnp.int32)[None, :]).astype(
        jnp.float32
    )
    pre_enc = enc_part + exact_dot(batch_table, small_w[:batch_kinds])
    hidden_enc, saved_enc = norm_forward(pre_enc, norm_par[0], norm_par[1], cell_total)
    head_out = exact_dot(hidden_enc, head_w[:hidden]) + head_w[hidden]
    latent_mean = head_out[:, :latent]
    latent_logvar = head_out[:, latent:]
    spread = jnp.exp(latent_logvar)
    latent_var = spread + 0.0001
    latent_std = jnp.sqrt(latent_var)
    latent_draw = latent_mean + latent_std * own_noise
    pre_dec = exact_dot(latent_draw, small_w[2 * batch_kinds :]) + exact_dot(
        batch_table, small_w[batch_kinds : 2 * batch_kinds]
    )
    hidden_dec, saved_dec = norm_forward(pre_dec, norm_par[2], norm_par[3], cell_total)
    hidden_low = hidden_dec.astype(jnp.bfloat16)
    hidden_all = lax.all_gather(hidden_low, "genes", axis=0, tiled=True)
    logits = jnp.dot(hidden_all, dec_cat, preferred_element_type=jnp.float32)
    score = logits[:, :local_genes] + gene_par[0]
    drop_logit = logits[:, local_genes:] + gene_par[1]
    masked = jnp.where(gene_keep, score, -1e30)
    local_top = jnp.max(masked, axis=1)
    top_logit = lax.pmax(local_top.astype(jnp.bfloat16), "genes").astype(local_top.dtype)
    local_mass = jnp.sum(jnp.where(gene_keep, jnp.exp(masked - top_logit[:, None]), 0.0), 1)
    exp_mass = lax.psum(local_mass, "genes")
    log_total = top_logit + jnp.log(exp_mass)
    log_mean = library[:, None] + score - log_total[:, None]
    block_rows = min(2048, rows_all)
    count_blocks = rows_all // block_rows
    disp_row = gene_par[2]

    def block_grad(block_args):
        block_counts, block_mean, block_drop = block_args

        def local_loss(mean_part, drop_part, disp_part):
            terms = zinb_loglik(block_counts.astype(jnp.float32), mean_part, drop_part, disp_part)
            return jnp.sum(jnp.where(gene_keep, terms, 0.0), axis=1)

        block_value, pullback = jax.vjp(local_loss, block_mean, block_drop, disp_row)
        grad_mean, grad_drop, grad_disp = pullback(
            jnp.full((block_counts.shape[0],), -1.0 / cell_total, jnp.float32)
        )
        return (block_value, grad_mean, grad_drop, grad_disp)

    block_values, grad_mean, grad_drop, grad_disp = lax.map(
        block_grad,
        (
            counts.reshape(count_blocks, block_rows, local_genes),
            log_mean.reshape(count_blocks, block_rows, local_genes),
            drop_logit.reshape(count_blocks, block_rows, local_genes),
        ),
    )
    recon_rows = block_values.reshape(rows_all)
    grad_mean = grad_mean.reshape(rows_all, local_genes)
    grad_drop = grad_drop.reshape(rows_all, local_genes)
    softmax_ratio = jnp.where(gene_keep, jnp.exp(score - log_total[:, None]), 0.0)
    back_mass, recon_cells = lax.psum((jnp.sum(grad_mean, 1), recon_rows), "genes")
    grad_score = grad_mean - softmax_ratio * back_mass[:, None]
    grad_cat = jnp.concatenate([grad_score, grad_drop], axis=1).astype(jnp.bfloat16)
    grad_dec = plain_inner(hidden_all, grad_cat)
    grad_gene = jnp.stack([jnp.sum(grad_score, 0), jnp.sum(grad_drop, 0), jnp.sum(grad_disp, 0)])
    cell_rows = grad_cat
    grad_hidden = lax.psum_scatter(
        plain_back(cell_rows, dec_cat), "genes", scatter_dimension=0, tiled=True
    )
    grad_pre_dec, gain_dec, shift_dec = norm_backward(
        grad_hidden, saved_dec, norm_par[2], cell_total
    )
    grad_latent_w = exact_inner(latent_draw, grad_pre_dec)
    grad_cov_dec = exact_inner(batch_table, grad_pre_dec)
    grad_draw = exact_back(grad_pre_dec, small_w[2 * batch_kinds :])
    kl_scale = kl_weight[0] / cell_total
    grad_lmean = grad_draw + kl_scale * latent_mean
    grad_lvar = grad_draw * own_noise * 0.5 * spread / latent_std + kl_scale * 0.5 * (
        spread - spread / latent_var
    )
    grad_head_out = jnp.concatenate([grad_lmean, grad_lvar], axis=1)
    grad_head = jnp.concatenate(
        [exact_inner(hidden_enc, grad_head_out), jnp.sum(grad_head_out, 0)[None, :]], axis=0
    )
    grad_hidden_enc = exact_back(grad_head_out, head_w[:hidden])
    grad_pre_enc, gain_enc, shift_enc = norm_backward(
        grad_hidden_enc, saved_enc, norm_par[0], cell_total
    )
    grad_cov_enc = exact_inner(batch_table, grad_pre_enc)
    grad_small = jnp.concatenate([grad_cov_enc, grad_cov_dec, grad_latent_w], axis=0)
    grad_norm_par = jnp.stack([gain_enc, shift_enc, gain_dec, shift_dec])
    grad_pre_low = grad_pre_enc.astype(jnp.bfloat16)
    diverge_rows = 0.5 * jnp.sum(
        latent_var + latent_mean * latent_mean - 1.0 - jnp.log(latent_var), axis=1
    )
    cell_rows = log_counts
    grad_enc = plain_inner(cell_rows, lax.all_gather(grad_pre_low, "genes", axis=0, tiled=True))
    grad_enc, grad_dec, grad_gene = lax.psum((grad_enc, grad_dec, grad_gene), "cells")
    grad_small, grad_head = lax.psum((grad_small, grad_head), ("cells", "genes"))
    own_recon = lax.dynamic_slice_in_dim(recon_cells, first_row, share_rows, 0)
    cell_loss = kl_weight[0] * diverge_rows - own_recon
    gene_square = (
        jnp.sum(grad_enc * grad_enc) + jnp.sum(grad_dec * grad_dec) + jnp.sum(grad_gene * grad_gene)
    )
    gene_square = lax.psum(gene_square, "genes")
    small_square = (
        jnp.sum(grad_small * grad_small)
        + jnp.sum(grad_head * grad_head)
        + jnp.sum(grad_norm_par * grad_norm_par)
    )
    norm_value = jnp.sqrt(gene_square + small_square)
    factor = jnp.minimum(1.0, max_norm / norm_value)
    grad_dec_split = jnp.stack([grad_dec[:, :local_genes], grad_dec[:, local_genes:]])
    enc_res = adamw(enc_w, grad_enc * factor, enc_m, enc_v, rate_genes)
    dec_res = adamw(dec_w, grad_dec_split * factor, dec_m, dec_v, rate_genes)
    gene_res = adamw(gene_par, grad_gene * factor, gene_m, gene_v, rate_small)
    small_res = adamw(small_w, grad_small * factor, small_m, small_v, rate_small)
    head_res = adamw(head_w, grad_head * factor, head_m, head_v, rate_small)
    norm_res = adamw(norm_par, grad_norm_par * factor, norm_m, norm_v, rate_small)
    return (
        enc_res[0],
        enc_res[1],
        enc_res[2],
        enc_res[0].astype(jnp.bfloat16),
        dec_res[0],
        dec_res[1],
        dec_res[2],
        dec_res[0].astype(jnp.bfloat16),
        gene_res[0],
        gene_res[1],
        gene_res[2],
        small_res[0],
        small_res[1],
        small_res[2],
        head_res[0],
        head_res[1],
        head_res[2],
        norm_res[0],
        norm_res[1],
        norm_res[2],
        norm_value,
        cell_loss,
    )


def solution(mesh):
    placed = (
        P("cells", "genes"),
        P("cells"),
        P("cells", None),
        P("cells"),
        P("genes"),
        P(),
        P("genes", None),
        P("genes", None),
        P("genes", None),
        P(None, None, "genes"),
        P(None, None, "genes"),
        P(None, None, "genes"),
        P(None, "genes"),
        P(None, "genes"),
        P(None, "genes"),
        P(),
        P(),
        P(),
        P(),
        P(),
        P(),
        P(),
        P(),
        P(),
    )
    return jax.shard_map(
        per_device,
        mesh=mesh,
        in_specs=placed,
        out_specs=(
            P("genes", None),
            P("genes", None),
            P("genes", None),
            P("genes", None),
            P(None, None, "genes"),
            P(None, None, "genes"),
            P(None, None, "genes"),
            P(None, None, "genes"),
            P(None, "genes"),
            P(None, "genes"),
            P(None, "genes"),
            P(),
            P(),
            P(),
            P(),
            P(),
            P(),
            P(),
            P(),
            P(),
            P(),
            P(("cells", "genes")),
        ),
        check_vma=False,
    )
```

profile of v0, /device:TPU:0, one launch (start us, length us, event | category | flops | bytes accessed | tf_op | source)
XLA Modules:
  0.0 1099.6 jit_solution(12833105348551881705)
XLA Ops:
  7.2 8.7 fusion.89
  16.9 51.9 %reduce-scatter.3.cloned.1.call-done = f32[1024,128]{1,0:T(8,128)} async-done(((f32[8192,128]{1,0:T(8,128)}), f32[1024,128]{1,0:T(8,128)}) %reduce-scatter.3.cloned.1.call-update) | async-done | bytes 524304 | tf_op jit(solution)/shard_map/reduce_scatter | solution.py:147
  70.3 37.8 %all-reduce.3 = (f32[128]{0:T(128)S(1)}, f32[128]{0:T(128)S(1)}) all-reduce(f32[128]{0:T(128)S(1)} %get-tuple-element.381, f32[128]{0:T(128)S(1)} %get-tuple-element.380), channel_id=1, replica_groups=mesh['cells'=4,'genes'=8] {'cells','genes'}, use_global_device_ids=true, to_apply=%region_2.0 | all-reduce | flops 256 | bytes 2048 | tf_op jit(solution)/shard_map/psum | solution.py:73
  112.4 41.4 %all-reduce.2 = (f32[128]{0:T(128)S(1)}, f32[128]{0:T(128)S(1)}) all-reduce(f32[128]{0:T(128)S(1)} %get-tuple-element.379, f32[128]{0:T(128)S(1)} %get-tuple-element.378), channel_id=1, replica_groups=mesh['cells'=4,'genes'=8] {'cells','genes'}, use_global_device_ids=true, to_apply=%region_6.7 | all-reduce | flops 256 | bytes 2048 | tf_op jit(solution)/shard_map/psum | solution.py:73
  164.2 20.2 %all-gather.3.cloned.1.call-done = bf16[8192,128]{1,0:T(8,128)(2,1)} async-done(((bf16[1024,128]{1,0:T(8,128)(2,1)}), bf16[8192,128]{1,0:T(8,128)(2,1)}) %all-gather.3.cloned.1.call-update) | async-done | bytes 2097168 | tf_op jit(solution)/shard_map/all_gather | solution.py:172
  198.1 27.6 %pmax.7 = bf16[8192]{0:T(1024)(128)(2,1)S(1)} all-reduce(bf16[8192]{0:T(1024)(128)(2,1)S(1)} %select_reduce_fusion.2), channel_id=1, replica_groups=mesh['cells'=4,'genes'=8] {'genes'}, use_global_device_ids=true, to_apply=%region_10.11 | all-reduce | flops 8192 | bytes 32768 | tf_op jit(solution)/shard_map/pmax | solution.py:178
  232.7 26.1 %psum.123 = f32[8192]{0:T(1024)S(1)} all-reduce(f32[8192]{0:T(1024)S(1)} %select_reduce_fusion.1), channel_id=1, replica_groups=mesh['cells'=4,'genes'=8] {'genes'}, use_global_device_ids=true, to_apply=%region_12.13 | all-reduce | flops 8192 | bytes 65536 | tf_op jit(solution)/shard_map/psum | solution.py:180
  258.9 15.5 %add_subtract_fusion = (f32[8192,320]{0,1:T(8,128)}, f32[8192,320]{0,1:T(8,128)}) fusion(f32[8192,640]{0,1:T(8,128)} %copy-done.1, f32[8192]{0:T(1024)S(1)} %log_add_fusion, f32[320]{0:T(512)S(1)} %get-tuple-element.466, f32[8192]{0:T(1024)S(1)} %copy-done.29, f32[320]{0:T(512)S(1)} %get-tuple-element.465), kind=kLoop, calls=%fused_computation.155 | loop fusion | flops 10485760 | bytes 42011136 | tf_op jit(solution)/shard_map/sub | solution.py:182
  274.4 11.9 %copy.74 = f32[8192,320]{1,0:T(8,128)} copy(f32[8192,320]{0,1:T(8,128)} %get-tuple-element.452) | data formatting | bytes 20971520 | tf_op jit(solution)/shard_map/while | solution.py:200
  286.3 11.8 %copy.75 = f32[8192,320]{1,0:T(8,128)} copy(f32[8192,320]{0,1:T(8,128)} %get-tuple-element.451) | data formatting | bytes 20971520 | tf_op jit(solution)/shard_map/while | solution.py:200
  298.1 323.2 %while.21 = (s32[]{:T(128)}, f32[4,2048]{1,0:T(4,128)S(1)}, f32[4,2048,320]{2,1,0:T(8,128)}, f32[4,2048,320]{2,1,0:T(8,128)}, f32[4,320]{1,0:T(4,128)S(1)}, /*in...) while((s32[]{:T(128)}, f32[4,2048]{1,0:T(4,128)S(1)}, ...), condition=%wide.region_20.22_spmd, body=%wide.region_13.21_spmd.sunk | while | flops 162566592 | bytes 51453508 | solution.py:200
  305.3 64.6 %multiply_reduce_fusion.13 = (f32[320]{0:T(512)S(1)}, f32[2048]{0:T(1024)S(1)}, f32[320]{0:T(512)S(1)}, f32[320]{0:T(512)S(1)}, f32[320]{0:T(512)S(1)}) fusion(f32[2048,320]{1,0:T(8,128)S(1)} %get-tuple-element.570, f32[4,2048,320]{2,1,0:T(8,128)} %get-tuple-element.620, s32[]{:T(128)} %get-tuple-element.596, f32[320]{0:T(512)S(1)} %get-tuple-element.569, ...), kind=kLoop, calls=%fused_computation.91.clone.1 | loop fusion | flops 124515072 | bytes 9193796 | tf_op jit(solution)/shard_map/while/body/eval_jaxpr/transpose(jvp())/reduce_sum | solution.py:59
  370.1 8.6 fusion.172
  386.0 64.6 %multiply_reduce_fusion.13 = (f32[320]{0:T(512)S(1)}, f32[2048]{0:T(1024)S(1)}, f32[320]{0:T(512)S(1)}, f32[320]{0:T(512)S(1)}, f32[320]{0:T(512)S(1)}) fusion(f32[2048,320]{1,0:T(8,128)S(1)} %get-tuple-element.570, f32[4,2048,320]{2,1,0:T(8,128)} %get-tuple-element.620, s32[]{:T(128)} %get-tuple-element.596, f32[320]{0:T(512)S(1)} %get-tuple-element.569, ...), kind=kLoop, calls=%fused_computation.91.clone.1 | loop fusion | flops 124515072 | bytes 9193796 | tf_op jit(solution)/shard_map/while/body/eval_jaxpr/transpose(jvp())/reduce_sum | solution.py:59
  450.9 8.7 fusion.172
  466.9 64.6 %multiply_reduce_fusion.13 = (f32[320]{0:T(512)S(1)}, f32[2048]{0:T(1024)S(1)}, f32[320]{0:T(512)S(1)}, f32[320]{0:T(512)S(1)}, f32[320]{0:T(512)S(1)}) fusion(f32[2048,320]{1,0:T(8,128)S(1)} %get-tuple-element.570, f32[4,2048,320]{2,1,0:T(8,128)} %get-tuple-element.620, s32[]{:T(128)} %get-tuple-element.596, f32[320]{0:T(512)S(1)} %get-tuple-element.569, ...), kind=kLoop, calls=%fused_computation.91.clone.1 | loop fusion | flops 124515072 | bytes 9193796 | tf_op jit(solution)/shard_map/while/body/eval_jaxpr/transpose(jvp())/reduce_sum | solution.py:59
  531.7 8.7 fusion.172
  547.7 64.6 %multiply_reduce_fusion.13 = (f32[320]{0:T(512)S(1)}, f32[2048]{0:T(1024)S(1)}, f32[320]{0:T(512)S(1)}, f32[320]{0:T(512)S(1)}, f32[320]{0:T(512)S(1)}) fusion(f32[2048,320]{1,0:T(8,128)S(1)} %get-tuple-element.570, f32[4,2048,320]{2,1,0:T(8,128)} %get-tuple-element.620, s32[]{:T(128)} %get-tuple-element.596, f32[320]{0:T(512)S(1)} %get-tuple-element.569, ...), kind=kLoop, calls=%fused_computation.91.clone.1 | loop fusion | flops 124515072 | bytes 9193796 | tf_op jit(solution)/shard_map/while/body/eval_jaxpr/transpose(jvp())/reduce_sum | solution.py:59
  612.5 8.6 fusion.172
  621.3 11.9 %copy.76 = f32[8192,320]{0,1:T(8,128)} copy(f32[8192,320]{1,0:T(8,128)} %bitcast.145) | data formatting | bytes 20971520 | tf_op jit(solution)/shard_map/reshape | solution.py:209
  638.9 26.2 %psum.124 = f32[8192]{0:T(1024)S(1)} all-reduce(f32[8192]{0:T(1024)S(1)} %bitcast.150), channel_id=1, replica_groups=mesh['cells'=4,'genes'=8] {'genes'}, use_global_device_ids=true, to_apply=%region_22.24 | all-reduce | flops 8192 | bytes 65536 | tf_op jit(solution)/shard_map/psum | solution.py:212
  665.1 12.6 %fusion.159 = (f32[320]{0:T(512)S(1)}, bf16[4,2048,320]{2,1,0:T(8,128)(2,1)}) fusion(f32[4,2048,320]{2,1,0:T(8,128)} %get-tuple-element.298), kind=kLoop, calls=%fused_computation.301 | loop fusion | flops 5242560 | bytes 15729920 | tf_op jit(solution)/shard_map/reduce_sum | solution.py:216
  685.9 9.0 fusion.158
  702.8 47.4 %reduce-scatter.5.cloned.1.call-done = f32[1024,128]{1,0:T(8,128)} async-done(((f32[8192,128]{1,0:T(8,128)}), f32[1024,128]{1,0:T(8,128)}) %reduce-scatter.5.cloned.1.call-update) | async-done | bytes 524304 | tf_op jit(solution)/shard_map/reduce_scatter | solution.py:218
  751.4 37.8 %all-reduce.1 = (f32[128]{0:T(128)S(1)}, f32[128]{0:T(128)S(1)}) all-reduce(f32[128]{0:T(128)S(1)} %get-tuple-element.375, f32[128]{0:T(128)S(1)} %get-tuple-element.374), channel_id=1, replica_groups=mesh['cells'=4,'genes'=8] {'cells','genes'}, use_global_device_ids=true, to_apply=%region_27.29 | all-reduce | flops 256 | bytes 2048 | tf_op jit(solution)/shard_map/psum | solution.py:73
  794.2 41.7 %all-reduce = (f32[128]{0:T(128)S(1)}, f32[128]{0:T(128)S(1)}, f32[129,20]{0,1:T(8,128)S(1)}) all-reduce(f32[128]{0:T(128)S(1)} %get-tuple-element.377, f32[128]{0:T(128)S(1)} %get-tuple-element.376, f32[129,20]{0,1:T(8,128)S(1)} %pad_maximum_fusion.10), channel_id=1, replica_groups=mesh['cells'=4,'genes'=8] {'cells','genes'}, use_global_device_ids=true, to_apply=%region_31.33 | all-reduce | flops 2836 | bytes 22688 | tf_op jit(solution)/shard_map/psum | solution.py:73
  837.2 8.7 fusion.86
  848.5 17.5 %all-gather.5.cloned.1.call-done = bf16[8192,128]{1,0:T(8,128)(2,1)} async-done(((bf16[1024,128]{1,0:T(8,128)(2,1)}), bf16[8192,128]{1,0:T(8,128)(2,1)}) %all-gather.5.cloned.1.call-update) | async-done | bytes 2097168 | tf_op jit(solution)/shard_map/all_gather | solution.py:248
  874.2 10.0 psum.131
  886.1 105.7 %all-reduce.9.cloned.1.call-done = f32[266,128]{1,0:T(8,128)} async-done(((f32[266,128]{1,0:T(8,128)}), f32[266,128]{1,0:T(8,128)}) %all-reduce.9.cloned.1.call-update) | async-done | bytes 136208 | tf_op jit(solution)/shard_map/psum | solution.py:250
  995.3 47.6 %all-reduce.11.cloned.1.call-done = (f32[320,128]{1,0:T(8,128)}, f32[128,640]{1,0:T(8,128)}) async-done(((f32[320,128]{1,0:T(8,128)}, f32[128,640]{1,0:T(8,128)}), (f32[320,128]{1,0:T(8,128)}, f32[128,640]{1,0:T(8,128)})) %all-reduce.11.cloned.1.call-update) | async-done | bytes 491536 | tf_op jit(solution)/shard_map/psum | solution.py:249
  1049.3 29.1 %all-reduce.4 = (f32[]{:T(128)}, f32[8192]{0:T(1024)}) all-reduce(f32[]{:T(128)S(6)} %add.455, f32[8192]{0:T(1024)S(1)} %bitcast.149), channel_id=1, replica_groups=mesh['cells'=4,'genes'=8] {'genes'}, use_global_device_ids=true, to_apply=%region_41.43 | all-reduce | flops 8193 | bytes 65544 | tf_op jit(solution)/shard_map/psum | solution.py:256
  (238 shorter events, 126.2 us)
Async XLA Ops:
  7.2 61.6 %reduce-scatter.3.cloned.1.call-start = ((), (), s32[]{:S(2)}) async-start(), calls=%async_computation.2 | async-start | bytes 4718592 | tf_op jit(solution)/shard_map/reduce_scatter | solution.py:147
  15.9 52.9 %copy-start.12 = (f32[266,128]{1,0:T(8,128)S(1)}, f32[266,128]{1,0:T(8,128)}, u32[]{:S(2)}) copy-start(f32[266,128]{1,0:T(8,128)} %param.42) | copy-start | bytes 408580
  15.9 168.4 %all-gather.3.cloned.1.call-start = ((), (), s32[]{:S(2)}) async-start(), calls=%async_computation.3 | async-start | bytes 2359296 | tf_op jit(solution)/shard_map/all_gather | solution.py:172
  16.7 139.0 %copy-start.23 = (s32[1024]{0:T(1024)}, s32[1024]{0:T(1024)S(1)}, u32[]{:S(2)}) copy-start(s32[1024]{0:T(1024)S(1)} %dynamic_slice.41) | copy-start | bytes 12292
  16.9 138.9 %copy-start.37 = (f32[128]{0:T(128)}, f32[128]{0:T(128)S(1)}, u32[]{:S(2)}) copy-start(f32[128]{0:T(128)S(1)} %get-tuple-element.469) | copy-start | bytes 1540
  16.9 138.9 %copy-start.39 = (f32[128]{0:T(128)}, f32[128]{0:T(128)S(1)}, u32[]{:S(2)}) copy-start(f32[128]{0:T(128)S(1)} %get-tuple-element.472) | copy-start | bytes 1540
  16.9 138.9 %copy-start.52 = (f32[128]{0:T(128)}, f32[128]{0:T(128)S(1)}, u32[]{:S(2)}) copy-start(f32[128]{0:T(128)S(1)} %get-tuple-element.470) | copy-start | bytes 1540
  16.9 138.9 %copy-start.54 = (f32[128]{0:T(128)}, f32[128]{0:T(128)S(1)}, u32[]{:S(2)}) copy-start(f32[128]{0:T(128)S(1)} %get-tuple-element.471) | copy-start | bytes 1540
  112.4 51.7 %copy-start.2 = (f32[1024,128]{1,0:T(8,128)}, f32[1024,128]{1,0:T(8,128)S(1)}, u32[]{:S(2)}) copy-start(f32[1024,128]{1,0:T(8,128)S(1)} %get-tuple-element.478) | copy-start | bytes 1572868
  155.2 594.9 %reduce-scatter.5.cloned.1.call-start = ((), (), s32[]{:S(2)}) async-start(), calls=%async_computation.4 | async-start | bytes 4718592 | tf_op jit(solution)/shard_map/reduce_scatter | solution.py:218
  305.2 64.7 %copy-start = (f32[2048,320]{1,0:T(8,128)}, f32[2048,320]{1,0:T(8,128)S(1)}, u32[]{:S(2)}) copy-start(f32[2048,320]{1,0:T(8,128)S(1)} %get-tuple-element.570) | copy-start | bytes 7864324 | tf_op jit(solution)/shard_map/while
  386.0 64.7 %copy-start = (f32[2048,320]{1,0:T(8,128)}, f32[2048,320]{1,0:T(8,128)S(1)}, u32[]{:S(2)}) copy-start(f32[2048,320]{1,0:T(8,128)S(1)} %get-tuple-element.570) | copy-start | bytes 7864324 | tf_op jit(solution)/shard_map/while
  466.8 64.7 %copy-start = (f32[2048,320]{1,0:T(8,128)}, f32[2048,320]{1,0:T(8,128)S(1)}, u32[]{:S(2)}) copy-start(f32[2048,320]{1,0:T(8,128)S(1)} %get-tuple-element.570) | copy-start | bytes 7864324 | tf_op jit(solution)/shard_map/while
  547.7 64.7 %copy-start = (f32[2048,320]{1,0:T(8,128)}, f32[2048,320]{1,0:T(8,128)S(1)}, u32[]{:S(2)}) copy-start(f32[2048,320]{1,0:T(8,128)S(1)} %get-tuple-element.570) | copy-start | bytes 7864324 | tf_op jit(solution)/shard_map/while
  701.8 87.5 %copy-start.48 = (f32[128]{0:T(128)S(1)}, f32[128]{0:T(128)}, u32[]{:S(2)}) copy-start(f32[128]{0:T(128)} %get-tuple-element.468) | copy-start | bytes 1540
  701.8 88.7 %copy-start.13 = (f32[266,128]{1,0:T(8,128)S(1)}, f32[266,128]{1,0:T(8,128)}, u32[]{:S(2)}) copy-start(f32[266,128]{1,0:T(8,128)} %param.42) | copy-start | bytes 408580
  701.8 88.7 %copy-start.18 = (f32[1024,20]{0,1:T(8,128)S(1)}, f32[1024,20]{0,1:T(8,128)}, u32[]{:S(2)}) copy-start(f32[1024,20]{0,1:T(8,128)} %copy-done.17) | copy-start | bytes 245764
  701.8 90.7 %copy-start.7 = (f32[1024,128]{1,0:T(8,128)S(1)}, f32[1024,128]{1,0:T(8,128)}, u32[]{:S(2)}) copy-start(f32[1024,128]{1,0:T(8,128)} %copy-done.6) | copy-start | bytes 1572868
  701.8 90.7 %copy-start.45 = (f32[128]{0:T(128)S(1)}, f32[128]{0:T(128)}, u32[]{:S(2)}) copy-start(f32[128]{0:T(128)} %copy-done.44) | copy-start | bytes 1540
  701.8 90.7 %copy-start.47 = (f32[128]{0:T(128)S(1)}, f32[128]{0:T(128)}, u32[]{:S(2)}) copy-start(f32[128]{0:T(128)} %copy-done.46) | copy-start | bytes 1540
  701.8 90.7 %copy-start.53 = (f32[128]{0:T(128)S(1)}, f32[128]{0:T(128)}, u32[]{:S(2)}) copy-start(f32[128]{0:T(128)} %copy-done.52) | copy-start | bytes 1540
  701.8 90.7 %copy-start.55 = (f32[128]{0:T(128)S(1)}, f32[128]{0:T(128)}, u32[]{:S(2)}) copy-start(f32[128]{0:T(128)} %copy-done.54) | copy-start | bytes 1540
  701.9 91.2 %copy-start.28 = (f32[129,20]{0,1:T(8,128)S(1)}, f32[129,20]{0,1:T(8,128)}, u32[]{:S(2)}) copy-start(f32[129,20]{0,1:T(8,128)} %param.45) | copy-start | bytes 30964
  701.9 134.1 %copy-start.43 = (f32[128]{0:T(128)S(1)}, f32[128]{0:T(128)}, u32[]{:S(2)}) copy-start(f32[128]{0:T(128)} %get-tuple-element.467) | copy-start | bytes 1540
  701.9 164.2 %all-gather.5.cloned.1.call-start = ((), (), s32[]{:S(2)}) async-start(), calls=%async_computation.5 | async-start | bytes 2359296 | tf_op jit(solution)/shard_map/all_gather | solution.py:248
  789.2 95.6 %copy-start.42 = (f32[128]{0:T(128)}, f32[128]{0:T(128)S(1)}, u32[]{:S(2)}) copy-start(f32[128]{0:T(128)S(1)} %get-tuple-element.411) | copy-start | bytes 1540
  789.2 95.6 %copy-start.50 = (f32[128]{0:T(128)}, f32[128]{0:T(128)S(1)}, u32[]{:S(2)}) copy-start(f32[128]{0:T(128)S(1)} %get-tuple-element.412) | copy-start | bytes 1540
  835.9 48.9 %copy-start.41 = (f32[128]{0:T(128)}, f32[128]{0:T(128)S(1)}, u32[]{:S(2)}) copy-start(f32[128]{0:T(128)S(1)} %get-tuple-element.408) | copy-start | bytes 1540
  836.0 49.5 %copy-start.25 = (f32[129,20]{0,1:T(8,128)}, f32[129,20]{0,1:T(8,128)S(1)}, u32[]{:S(2)}) copy-start(f32[129,20]{0,1:T(8,128)S(1)} %get-tuple-element.410) | copy-start | bytes 30964
  836.9 154.9 %all-reduce.9.cloned.1.call-start = ((), (), s32[]{:S(2)}) async-start(), calls=%async_computation.6 | async-start | bytes 278528 | tf_op jit(solution)/shard_map/psum | solution.py:250
  848.5 194.4 %all-reduce.11.cloned.1.call-start = ((), (), s32[]{:S(2)}) async-start(), calls=%async_computation.7 | async-start | bytes 983040 | tf_op jit(solution)/shard_map/psum | solution.py:249
  884.2 194.9 %copy-start.26 = (f32[3,320]{1,0:T(4,128)}, f32[3,320]{1,0:T(4,128)S(1)}, u32[]{:S(2)}) copy-start(f32[3,320]{1,0:T(4,128)S(1)} %psum.131) | copy-start | bytes 11524
  (33 other events, 637.0 us)
Sparse Core Ops, SparseCore 0:
  16.1 52.6 reduce-scatter.2
  155.3 29.0 all-gather.2
  702.0 48.0 reduce-scatter.4
  837.0 29.0 all-gather.4
  872.0 119.7 all-reduce.8
  995.3 47.5 all-reduce.10
where the time goes:
time: 1110 us; the launch traced here: 1100 us
  other arithmetic  396 us (36%)
  waiting for transfers between devices  290 us (26%)
  blocking collectives  278 us (25%)
  local copies, waits for them, and re-layouts  69.4 us (6%)
  matrix products  42.9 us (4%)
  between operations  22 us (2%)
    reduce_sum x4, other arithmetic, zinb_loglik(): drop_term = -drop_logit + dispersion * (log_disp_eps - log_both)  259 us
    psum x4, blocking collectives, wide_sum(): return lax.psum((values[0], values[1]), ('cells', 'genes'))  159 us
    psum x1, waiting for transfers between devices, per_device(): lax.psum((grad_small, grad_head), ('cells', 'genes'))  106 us
    reduce_scatter x1, waiting for transfers between devices, per_device(): lax.psum_scatter(jnp.dot(cell_rows, enc_low, preferred_element_type=jnp.f...  51.9 us
    psum x1, waiting for transfers between devices, per_device(): lax.psum((grad_enc, grad_dec, grad_gene), 'cells')  47.6 us
    reduce_scatter x1, waiting for transfers between devices, per_device(): lax.psum_scatter(plain_back(cell_rows, dec_cat), 'genes', scatter_dimensi...  47.4 us
    dynamic_update_slice x4, other arithmetic, per_device(): lax.map(block_grad, (counts.reshape(count_blocks, block_rows, local_genes...  34.7 us
    psum x1, blocking collectives, per_device(): gene_square = lax.psum(gene_square, 'genes')  29.1 us
  transfers between devices with their start and end apart: 6, of which 6 were waited for; matrix products, arithmetic and copies ran while one was open for 3% of the time, Pallas kernels for 0%

commit v1 on v0

v1 whole, which is shorter than its diff:
```python
import jax
import jax.numpy as jnp
from jax import lax
from jax.experimental import pallas as pl
from jax.experimental.pallas import tpu as pltpu
from jax.sharding import PartitionSpec as P

norm_epsilon = 0.001
zinb_epsilon = 1e-08
beta_one = 0.9
beta_two = 0.999
step_number = 5.0
decay_rate = 0.01
rate_genes = 0.03
rate_small = 0.2
max_norm = 0.1

F32 = jnp.float32
BF = jnp.bfloat16
HI = lax.Precision.HIGHEST
VMEM_LIMIT = 56 * 1024 * 1024
COUNT_TOP = 8


def nn(left, right, precision=None):
    return lax.dot_general(
        left, right, (((1,), (0,)), ((), ())), precision=precision, preferred_element_type=F32
    )


def nt(left, right, precision=None):
    return lax.dot_general(
        left, right, (((1,), (1,)), ((), ())), precision=precision, preferred_element_type=F32
    )


def params():
    return pltpu.CompilerParams(vmem_limit_bytes=VMEM_LIMIT)


def whole(shape):
    return pl.BlockSpec(shape, lambda *_: (0,) * len(shape))


def call(kernel, grid, ins, outs, scratch=(), scalars=0, flops=0, moved=0):
    return pl.pallas_call(
        kernel,
        out_shape=[jax.ShapeDtypeStruct(shape, dtype) for shape, dtype, _ in outs],
        grid_spec=pltpu.PrefetchScalarGridSpec(
            num_scalar_prefetch=scalars,
            grid=grid,
            in_specs=[spec for _, spec in ins[scalars:]],
            out_specs=[spec for _, _, spec in outs],
            scratch_shapes=list(scratch),
        ),
        compiler_params=params(),
        cost_estimate=pl.CostEstimate(flops=flops, bytes_accessed=moved, transcendentals=0),
    )(*[array for array, _ in ins])


def swap(value, axis, bit):
    count = lax.axis_size(axis)
    return lax.ppermute(value, axis, [(i, i ^ bit) for i in range(count)])


def bit_groups(axis):
    count = lax.axis_size(axis)
    if axis == "genes":
        groups, bit = [[1]], 2
    else:
        groups, bit = [], 1
    while bit < count:
        groups.append([bit, 2 * bit] if 2 * bit < count else [bit])
        bit *= 4
    return groups


def total(value, axis):
    for group in bit_groups(axis):
        if len(group) == 1:
            value = value + swap(value, axis, group[0])
        else:
            low, high = group
            value = (value + swap(value, axis, low)) + (
                swap(value, axis, high) + swap(value, axis, low ^ high)
            )
    return value


def log_total_of(value, axis):
    for group in bit_groups(axis):
        if len(group) == 1:
            parts = [value, swap(value, axis, group[0])]
        else:
            low, high = group
            parts = [value] + [swap(value, axis, k) for k in (low, high, low ^ high)]
        top = parts[0]
        for part in parts[1:]:
            top = jnp.maximum(top, part)
        mass = sum(jnp.exp(part - top) for part in parts)
        value = top + jnp.log(mass)
    return value


def three(value):
    high = value.astype(BF)
    rest = value - high.astype(F32)
    mid = rest.astype(BF)
    low = (rest - mid.astype(F32)).astype(BF)
    return high, mid, low


def one_hot(batch_row, kinds):
    ids = lax.broadcasted_iota(jnp.int32, (kinds, batch_row.shape[1]), 0)
    return jnp.where(ids == batch_row, 1.0, 0.0)


def prep_kernel(enc_b_ref, dec_b_ref, lat_ref, enc_out, dec_out):
    hidden, kinds = enc_b_ref.shape
    for index, piece in enumerate(three(enc_b_ref[...])):
        enc_out[index * hidden : (index + 1) * hidden, :] = piece
    batch_pieces = three(dec_b_ref[...])
    lat = three(lat_ref[...])
    zero = jnp.zeros_like(lat[0])
    tails = ((lat[0], lat[0], lat[0]), (lat[1], lat[1], zero), (lat[2], zero, zero))
    for index in range(3):
        rows = slice(index * hidden, (index + 1) * hidden)
        dec_out[rows, :] = jnp.concatenate((batch_pieces[index],) + tails[index], axis=1)


def exact_rows(stacked, table):
    out = nn(stacked, table)
    hidden = out.shape[0] // 3
    return out[:hidden] + out[hidden : 2 * hidden] + out[2 * hidden :]


def dec_table(z, batch_row, kinds):
    high, mid, low = three(z)
    return jnp.concatenate((one_hot(batch_row, kinds).astype(BF), high, mid, low), axis=0)


def row_sums(value):
    return nt(jnp.ones((8, value.shape[1]), F32), value, HI)


def stat_rows(first, second, at):
    sums, squares = row_sums(first), row_sums(second)
    row = lax.broadcasted_iota(jnp.int32, sums.shape, 0)
    return jnp.where(row == at, sums, jnp.where(row == at + 1, squares, 0.0))


def enc_kernel(me_ref, x_ref, w_ref, keep_ref, send_ref):
    log_counts = jnp.log(1.0 + x_ref[...].astype(F32)).astype(BF)
    part = nn(w_ref[...], log_counts)
    odd = lax.rem(pl.program_id(0), 2)

    @pl.when(odd == 0)
    def _():
        keep_ref[0] = part

    @pl.when(odd == 1)
    def _():
        send_ref[0] = part.astype(BF)


def counts_kernel(rows, x_ref, lg_ref, dg_ref, logc_ref, cell_ref, disp_ref):
    step = pl.program_id(0)
    genes, width = x_ref.shape

    @pl.when(step == 0)
    def _():
        disp_ref[...] = jnp.zeros_like(disp_ref)

    def chunk(g, cell):
        at = pl.ds(pl.multiple_of(g * rows, rows), rows)
        digamma = disp_ref[at, :]
        out = []
        for tile in range(width // 128):
            lanes = slice(tile * 128, (tile + 1) * 128)
            x = x_ref[at, lanes].astype(F32)
            logc_ref[at, lanes] = jnp.log(1.0 + x).astype(BF)
            gam = jnp.zeros_like(x)
            dig = jnp.zeros_like(x)
            for k in range(COUNT_TOP):
                more = x > (k + 0.5)
                gam = jnp.where(more, lg_ref[k, at, :], gam)
                dig = jnp.where(more, dg_ref[k, at, :], dig)
            digamma = digamma + dig
            folded = gam[:8]
            for part in range(1, rows // 8):
                folded = folded + gam[part * 8 : (part + 1) * 8]
            out.append(cell[tile] + folded)
        disp_ref[at, :] = digamma
        return tuple(out)

    zero = tuple(jnp.zeros((8, 128), F32) for _ in range(width // 128))
    cell = lax.fori_loop(0, genes // rows, chunk, zero)
    cell_ref[pl.ds(step, 1), :] = jnp.sum(jnp.concatenate(cell, axis=1), axis=0, keepdims=True)


def own_kernel(me_ref, keep_ref, got_ref, one_ref, two_ref, six_ref, batch_ref, enc_b_ref, pre_ref, stat_ref):
    kinds = enc_b_ref.shape[1]
    gathered = (keep_ref[0] + got_ref[0].astype(F32) + one_ref[0].astype(F32)) + (
        two_ref[0].astype(F32) + six_ref[0].astype(F32)
    )
    table = one_hot(batch_ref[0], kinds).astype(BF)
    pre = gathered + exact_rows(enc_b_ref[...], table)
    pre_ref[...] = pre
    stat_ref[...] = stat_rows(pre, pre * pre, 0)


def norm_columns(stat, first, cells):
    turned = jnp.transpose(stat)
    mean = turned[:, first : first + 1] / cells
    var = turned[:, first + 1 : first + 2] / cells - mean * mean
    return mean, lax.rsqrt(var + norm_epsilon)


def norm_rows(stat, first, cells):
    mean = stat[first : first + 1] / cells
    var = stat[first + 1 : first + 2] / cells - mean * mean
    return mean, lax.rsqrt(var + norm_epsilon)


def latent_kernel(cells, latent, me_ref, pre_ref, stat_ref, norm_ref, head_ref, bias_ref, noise_ref, batch_ref, dec_b_ref, kinds_ref, z_ref, head_out_ref, kl_ref):
    kinds = kinds_ref.shape[1]
    mean, inv = norm_columns(stat_ref[...], 0, cells)
    phat = (pre_ref[...] - mean) * inv
    hidden = jnp.maximum(norm_ref[:, 0:1] * phat + norm_ref[:, 1:2], 0.0)
    out = nn(head_ref[...], hidden, HI) + bias_ref[:, 0:1]
    head_out_ref[...] = out
    lat_mean, lat_logvar = out[:16], out[16:]
    var = jnp.exp(lat_logvar) + 0.0001
    z = lat_mean + jnp.sqrt(var) * noise_ref[...]
    row = lax.broadcasted_iota(jnp.int32, z.shape, 0)
    terms = jnp.where(row < latent, var + lat_mean * lat_mean - 1.0 - jnp.log(var), 0.0)
    kl_ref[...] = 0.5 * jnp.sum(terms, axis=0, keepdims=True)
    pre_dec = exact_rows(dec_b_ref[...], dec_table(z, batch_ref[0], kinds))
    hidden_rows = pre_dec.shape[0]
    z_ref[...] = z
    stat = stat_rows(pre_dec, pre_dec * pre_dec, 0)
    z_ref[latent : latent + 1, 0:hidden_rows] = stat[0:1]
    z_ref[latent + 1 : latent + 2, 0:hidden_rows] = stat[1:2]


def decode_kernel(cells, latent, me_ref, z_ref, batch_ref, stat_ref, norm_ref, dec_b_ref, kinds_ref, w_ref, bias_ref, hid_ref, phat_ref, lse_ref, score_ref):
    kinds = kinds_ref.shape[1]
    step = pl.program_id(0)
    genes = w_ref.shape[0]
    mean, inv = norm_columns(stat_ref[...], latent - 8, cells)
    z = z_ref[0]
    row = lax.broadcasted_iota(jnp.int32, z.shape, 0)
    z = jnp.where(row < latent, z, 0.0)
    pre_dec = exact_rows(dec_b_ref[...], dec_table(z, batch_ref[0], kinds))
    phat = (pre_dec - mean) * inv
    phat_ref[...] = phat
    hidden = jnp.maximum(norm_ref[:, 2:3] * phat + norm_ref[:, 3:4], 0.0).astype(BF)
    hid_ref[...] = hidden
    score_ref[...] = nn(w_ref[...], hidden)
    width = score_ref.shape[1]
    tiles = width // 128

    def top(g, best):
        at = pl.ds(pl.multiple_of(g * 8, 8), 8)
        bias = bias_ref[at, :]
        new = []
        for tile in range(tiles):
            lanes = slice(tile * 128, (tile + 1) * 128)
            value = score_ref[at, lanes] + bias
            score_ref[at, lanes] = value
            new.append(jnp.maximum(best[tile], value))
        return tuple(new)

    best = lax.fori_loop(0, genes // 8, top, tuple(jnp.full((8, 128), -3e38, F32) for _ in range(tiles)))
    high = [jnp.max(part, axis=0, keepdims=True) for part in best]
    wide = [jnp.broadcast_to(part, (8, 128)) for part in high]

    def mass(g, sums):
        at = pl.ds(pl.multiple_of(g * 8, 8), 8)
        return tuple(
            sums[tile] + jnp.exp(score_ref[at, slice(tile * 128, (tile + 1) * 128)] - wide[tile])
            for tile in range(tiles)
        )

    sums = lax.fori_loop(0, genes // 8, mass, tuple(jnp.zeros((8, 128), F32) for _ in range(tiles)))
    lse = [high[tile] + jnp.log(jnp.sum(sums[tile], axis=0, keepdims=True)) for tile in range(tiles)]
    lse_ref[pl.ds(step, 1), :] = jnp.concatenate(lse, axis=1)


def zinb_kernel(rows, span, hid_ref, w_ref, x_ref, keep_ref, par_ref, lib_ref, lse_ref, gam_ref, gm_ref, gd_ref, rt_ref, mass_ref, recon_ref, acc_ref, sc_ref):
    step = pl.program_id(0)
    genes, width = x_ref.shape

    @pl.when(step == 0)
    def _():
        acc_ref[...] = jnp.zeros_like(acc_ref)

    sc_ref[...] = nn(w_ref[...], hid_ref[...])
    tiles = span // 128

    one_row = pl.ds(step, 1)
    lib_row, lse_row, gam_row = lib_ref[one_row, :], lse_ref[one_row, :], gam_ref[one_row, :]
    mass_out, recon_out = [], []
    for first in range(0, width, span):
        lanes = [slice(first + tile * 128, first + (tile + 1) * 128) for tile in range(tiles)]
        shift, ratio_of = [], []
        for tile in range(tiles):
            lib = lib_row[:, lanes[tile]]
            shift.append(jnp.broadcast_to(lib - lse_row[:, lanes[tile]], (rows, 128)))
            ratio_of.append(jnp.broadcast_to(jnp.exp(-lib), (rows, 128)))

        def chunk(g, state):
            at = pl.ds(pl.multiple_of(g * rows, rows), rows)
            at_drop = pl.ds(pl.multiple_of(genes + g * rows, rows), rows)
            bias_s, bias_d, the, th, log_the, part_th = (par_ref[i, at, :] for i in range(6))
            keep = keep_ref[at, :]
            sum_s, sum_d, sum_t = acc_ref[0, at, :], acc_ref[1, at, :], acc_ref[2, at, :]
            new = []
            for tile in range(tiles):
                rec, prod, back = state[tile]
                x = (x_ref[at, lanes[tile]] * keep).astype(F32)
                log_mean = (sc_ref[at, lanes[tile]] + bias_s) + shift[tile]
                drop = sc_ref[at_drop, lanes[tile]] + bias_d
                mu = jnp.exp(log_mean)
                both = mu + the
                r = 1.0 / both
                log_gap = log_the - jnp.log(both)
                log_both = log_the - log_gap
                u = th * log_gap - drop
                eu = jnp.exp(-jnp.abs(u))
                ed = jnp.exp(-jnp.abs(drop))
                is_zero = x < 0.5
                mu_eps = mu + zinb_epsilon
                den = jnp.where(is_zero, 1.0 + eu, mu_eps)
                q = 1.0 / den
                rd = 1.0 / (1.0 + ed)
                w0 = jnp.where(is_zero, jnp.where(u >= 0.0, 1.0, eu) * q, 1.0)
                rec_term = (
                    jnp.where(is_zero, jnp.maximum(u, 0.0), u)
                    + x * (jnp.log(mu_eps) - log_both)
                    + jnp.minimum(drop, 0.0)
                )
                factor = jnp.where(is_zero, den, 1.0) * rd
                y = (x + w0 * th) * r
                g_mean = mu * (x * q - y)
                g_drop = jnp.where(drop >= 0.0, ed, 1.0) * rd - w0
                g_disp = w0 * (log_gap + part_th) - y
                gm_ref[at, lanes[tile]] = g_mean.astype(BF)
                gd_ref[at, lanes[tile]] = g_drop.astype(BF)
                rt_ref[at, lanes[tile]] = (mu * ratio_of[tile]).astype(BF)
                sum_s = sum_s + g_mean
                sum_d = sum_d + g_drop
                sum_t = sum_t + g_disp
                for part in range(rows // 8):
                    sub = slice(part * 8, (part + 1) * 8)
                    rec = rec + rec_term[sub]
                    prod = prod * factor[sub]
                    back = back + g_mean[sub]
                new.append((rec, prod, back))
            acc_ref[0, at, :] = sum_s
            acc_ref[1, at, :] = sum_d
            acc_ref[2, at, :] = sum_t
            return tuple(new)

        zero = jnp.zeros((8, 128), F32)
        state = tuple((zero, zero + 1.0, zero) for _ in range(tiles))
        state = lax.fori_loop(0, genes // rows, chunk, state)
        for tile in range(tiles):
            rec, prod, back = state[tile]
            mass_out.append(jnp.sum(back, axis=0, keepdims=True))
            recon_out.append(jnp.sum(rec + jnp.log(prod), axis=0, keepdims=True))
    mass_ref[one_row, :] = jnp.concatenate(mass_out, axis=1)
    recon_ref[one_row, :] = jnp.concatenate(recon_out, axis=1) + gam_row


def back_kernel(gm_ref, gd_ref, rt_ref, hid_ref, w_ref, a_ref, r_ref, g_ref):
    genes = gm_ref.shape[0]

    @pl.when(pl.program_id(0) == 0)
    def _():
        g_ref[...] = jnp.zeros_like(g_ref)

    gm, gd, rt, hid = gm_ref[...], gd_ref[...], rt_ref[...], hid_ref[...]
    scale_w = w_ref[:, :genes]
    a_ref[...] = nn(scale_w, gm) + nn(w_ref[:, genes:], gd)
    r_ref[...] = nn(scale_w, rt)
    g_ref[:genes, :] += nt(gm, hid)
    g_ref[genes:, :] += nt(gd, hid)


def hidden_grad_kernel(cells, latent, me_ref, a_ref, r_ref, mass_ref, hid_ref, phat_ref, stat_ref, gain_ref, lat_ref, recon_ref, dy_ref, keep_ref, send_ref, sum_ref):
    step = pl.program_id(0)
    steps = pl.num_programs(0)
    place = step ^ me_ref[0]

    @pl.when(step == 0)
    def _():
        sum_ref[...] = jnp.zeros_like(sum_ref)

    back = mass_ref[pl.ds(step, 1), :]
    dy = jnp.where(hid_ref[...] > 0, (a_ref[...] - back * r_ref[...]) * (-1.0 / cells), 0.0)
    dy_ref[...] = dy
    hidden, width = dy.shape
    weighted = dy * phat_ref[...]
    first, second = dy[:, :128], weighted[:, :128]
    for tile in range(1, width // 128):
        lanes = slice(tile * 128, (tile + 1) * 128)
        first = first + dy[:, lanes]
        second = second + weighted[:, lanes]
    sum_ref[0] += first
    sum_ref[1] += second
    _, inv = norm_rows(stat_ref[...], latent - 8, cells)
    lat = lat_ref[...] * (gain_ref[2:3] * inv)
    lat_high, lat_mid, _ = three(lat)
    dy_high, dy_mid, _ = three(dy)
    table = jnp.concatenate((dy_high, dy_mid), axis=0)
    left = jnp.concatenate(
        (
            jnp.concatenate((lat_high, lat_high), axis=1),
            jnp.concatenate((lat_mid, jnp.zeros_like(lat_mid)), axis=1),
        ),
        axis=0,
    )
    both = nn(left, table)
    block = both[:16] + both[16:]
    row = lax.broadcasted_iota(jnp.int32, block.shape, 0)
    block = jnp.where(row == latent, recon_ref[pl.ds(step, 1), :], block)
    slot = lax.div(place, 2)

    @pl.when(lax.rem(place, 2) == 0)
    def _():
        keep_ref[slot] = block

    @pl.when(lax.rem(place, 2) == 1)
    def _():
        send_ref[slot] = block

    @pl.when(step == steps - 1)
    def _():
        one, two = row_sums(sum_ref[0]), row_sums(sum_ref[1])
        for ref in (keep_ref, send_ref):
            for index in range(ref.shape[0]):
                ref[index, latent + 1 : latent + 2, 0:hidden] = one[0:1]
                ref[index, latent + 2 : latent + 3, 0:hidden] = two[0:1]


def dec_grad_kernel(cells, latent, me_ref, rt_ref, hid_ref, mass_ref, dy_ref, z_ref, batch_ref, g_ref, acc_ref, dig_ref, th_ref, dec_ref, oh_ref, mix_ref):
    step = pl.program_id(0)
    steps = pl.num_programs(0)
    genes = rt_ref.shape[0]
    hidden = hid_ref.shape[0]
    kinds = oh_ref.shape[0] - 16

    @pl.when(step == 0)
    def _():
        mix_ref[...] = jnp.zeros_like(mix_ref)
        oh_ref[...] = jnp.zeros_like(oh_ref)

    back = mass_ref[pl.ds(step, 1), :]
    back_high, back_mid, back_low = three(back)
    row = lax.broadcasted_iota(jnp.int32, (16, back.shape[1]), 0)
    extra = jnp.where(row == 0, back_high.astype(F32), jnp.where(row == 1, back_mid.astype(F32), 0.0))
    scaled = (hid_ref[...].astype(F32) * back).astype(BF)
    mix_ref[...] += nt(rt_ref[...], jnp.concatenate((scaled, extra.astype(BF)), axis=0))
    z = z_ref[0]
    z = jnp.where(lax.broadcasted_iota(jnp.int32, z.shape, 0) < latent, z, 0.0)
    z_high, z_mid, _ = three(z)
    left = jnp.concatenate((one_hot(batch_ref[0], kinds).astype(BF), z_high, z_mid), axis=0)
    dy_high, dy_mid, _ = three(dy_ref[...])
    part = nt(left, dy_high) + nt(left, dy_mid)
    oh_ref[:kinds, :] += part[:kinds]
    oh_ref[kinds:, :] += part[kinds : kinds + 16] + part[kinds + 16 :]

    @pl.when(step == steps - 1)
    def _():
        scale = -1.0 / cells
        mix = mix_ref[...]
        dec_ref[:genes, :] = (g_ref[:genes, :] - mix[:, :hidden]) * scale
        dec_ref[genes : 2 * genes, :] = g_ref[genes:, :] * scale
        pick = jnp.where(lax.broadcasted_iota(jnp.int32, (8, 16), 1) < 2, 1.0, 0.0)
        score_row = row_sums(acc_ref[0]) - nt(pick, mix[:, hidden:], HI)
        drop_row = row_sums(acc_ref[1])
        disp_row = row_sums((acc_ref[2] + dig_ref[...]) * th_ref[...])
        line = lax.broadcasted_iota(jnp.int32, score_row.shape, 0)
        gene_rows = scale * jnp.where(
            line == 0, score_row, jnp.where(line == 1, drop_row, jnp.where(line == 2, disp_row, 0.0))
        )
        base = 2 * genes
        for index in range(pl.cdiv(genes, 128)):
            wide = min(128, genes - index * 128)
            piece = gene_rows[:, index * 128 : index * 128 + wide]
            if wide < 128:
                piece = jnp.concatenate((piece, jnp.zeros((8, 128 - wide), F32)), axis=1)
            dec_ref[base + index * 8 : base + (index + 1) * 8, :] = piece


def own_phat(pre, stat, first, cells):
    mean, inv = norm_columns(stat, first, cells)
    return (pre - mean) * inv


def head_grad_kernel(cells, latent, me_ref, d0_ref, d1_ref, d2_ref, d3_ref, d4_ref, sums_ref, phat_ref, stat_dec_ref, gain_ref, lat_ref, head_out_ref, noise_ref, kl_ref, klw_ref, pre_ref, stat_ref, norm_ref, head_ref, dy_ref, gh_ref, loss_ref, stat_out_ref):
    block = (d0_ref[0] + d1_ref[0] + d2_ref[0]) + (d3_ref[0] + d4_ref[0])
    loss_ref[...] = klw_ref[0:1, 0:1] * kl_ref[...] - block[latent : latent + 1]
    row = lax.broadcasted_iota(jnp.int32, block.shape, 0)
    _, inv = norm_rows(stat_dec_ref[...], latent - 8, cells)
    lat = lat_ref[...] * (gain_ref[2:3] * inv)
    at = latent + 1 - 8
    m_one = sums_ref[at : at + 1] * (1.0 / cells)
    m_two = sums_ref[at + 1 : at + 2] * (1.0 / cells)
    fixed = jnp.sum(lat * m_one, axis=1, keepdims=True)
    grad_z = block - fixed - nn(lat * m_two, phat_ref[...], HI)
    grad_z = jnp.where(row < latent, grad_z, 0.0)
    out = head_out_ref[...]
    lat_mean, lat_logvar = out[:16], out[16:]
    spread = jnp.exp(lat_logvar)
    var = spread + 0.0001
    std = jnp.sqrt(var)
    scale = klw_ref[0:1, 0:1] * (1.0 / cells)
    g_mean = grad_z + scale * lat_mean
    g_var = grad_z * noise_ref[...] * 0.5 * spread / std + scale * 0.5 * (spread - spread / var)
    g_var = jnp.where(row < latent, g_var, 0.0)
    g_head = jnp.concatenate((g_mean, g_var), axis=0)
    gh_ref[...] = g_head
    phat = own_phat(pre_ref[...], stat_ref[...], 0, cells)
    affine = norm_ref[:, 0:1] * phat + norm_ref[:, 1:2]
    dy = jnp.where(affine > 0, nn(head_ref[...], g_head, HI), 0.0)
    dy_ref[...] = dy
    stat_out_ref[...] = stat_rows(dy, dy * phat, 0)


def pre_grad_kernel(cells, dy_ref, pre_ref, stat_ref, norm_ref, sums_ref, out_ref, low_ref):
    mean, inv = norm_columns(stat_ref[...], 0, cells)
    phat = (pre_ref[...] - mean) * inv
    turned = jnp.transpose(sums_ref[...])
    grad = (norm_ref[:, 0:1] * inv) * (
        dy_ref[...] - turned[:, 0:1] * (1.0 / cells) - phat * (turned[:, 1:2] * (1.0 / cells))
    )
    out_ref[...] = grad
    low_ref[...] = grad.astype(BF)


def small_grad_kernel(cells, latent, me_ref, grad_ref, gh_ref, pre_ref, stat_ref, norm_ref, batch_ref, phat_ref, z_ref, oh_ref, sums_ref, stat_dec_ref, gain_ref, out_ref):
    kinds = oh_ref.shape[0] - 16
    table = one_hot(batch_ref[0], kinds)
    phat = own_phat(pre_ref[...], stat_ref[...], 0, cells)
    hidden = jnp.maximum(norm_ref[:, 0:1] * phat + norm_ref[:, 1:2], 0.0)
    out_ref[:kinds, :] = nt(table, grad_ref[...], HI)
    z = z_ref[...]
    z = jnp.where(lax.broadcasted_iota(jnp.int32, z.shape, 0) < latent, z, 0.0)
    left = jnp.concatenate((table, z), axis=0)
    _, inv = norm_rows(stat_dec_ref[...], latent - 8, cells)
    at = latent + 1 - 8
    m_one = sums_ref[at : at + 1] * (1.0 / cells)
    m_two = sums_ref[at + 1 : at + 2] * (1.0 / cells)
    held = jnp.sum(left, axis=1, keepdims=True)
    out_ref[kinds : 2 * kinds + 16, :] = (gain_ref[2:3] * inv) * (
        oh_ref[...] - held * m_one - nt(left, phat_ref[...], HI) * m_two
    )
    base = 2 * kinds + 16
    g_head = gh_ref[...]
    out_ref[base : base + 32, :] = nt(g_head, hidden, HI)
    out_ref[base + 32 : base + 64, :] = jnp.broadcast_to(
        jnp.sum(g_head, axis=1, keepdims=True), (32, out_ref.shape[1])
    )


def enc_grad_kernel(logc_ref, grad_ref, out_ref):
    @pl.when(pl.program_id(0) == 0)
    def _():
        out_ref[...] = jnp.zeros_like(out_ref)

    part = jnp.zeros(out_ref.shape, F32)
    share = grad_ref.shape[2]
    for index in range(grad_ref.shape[0]):
        part = part + nt(logc_ref[:, index * share : (index + 1) * share], grad_ref[index])
    out_ref[...] += part


def square_kernel(enc_ref, dec_ref, out_ref):
    enc, dec = enc_ref[...], dec_ref[...]
    whole_sum = jnp.sum(jnp.sum(enc * enc, axis=0, keepdims=True) + jnp.sum(dec * dec, axis=0, keepdims=True), axis=1, keepdims=True)
    out_ref[...] = jnp.broadcast_to(whole_sum, out_ref.shape)


def step_of(weight, gradient, first, second, rate):
    first = beta_one * first + (1.0 - beta_one) * gradient
    second = beta_two * second + (1.0 - beta_two) * gradient * gradient
    fixed_one = first * (1.0 / (1.0 - beta_one**step_number))
    fixed_two = second * (1.0 / (1.0 - beta_two**step_number))
    update = fixed_one / (jnp.sqrt(fixed_two) + 1e-08) + decay_rate * weight
    return weight - rate * update, first, second


def update_kernel(latent, square_ref, enc_g_ref, dec_g_ref, small_g_ref, enc_s_ref, dec_s_ref, *refs):
    ins, outs, scratch = refs[:18], refs[18:-1], refs[-1]
    enc, dec, gene, small, head, norm = (ins[3 * i : 3 * i + 3] for i in range(6))
    genes = enc[0].shape[0]
    hidden = enc[0].shape[1]
    kinds = (small[0].shape[0] - latent) // 2
    base = 2 * kinds + 16
    small_g = small_g_ref[...]
    at = latent + 1 - 8
    norm_g = (enc_s_ref[1:2], enc_s_ref[0:1], dec_s_ref[at + 1 : at + 2], dec_s_ref[at : at + 1])
    shared = small_g[: base + 32]
    tail = small_g[base + 32 : base + 64, 0:1]
    lanes = jnp.sum(shared * shared, axis=0, keepdims=True)
    for part in norm_g:
        lanes = lanes + part * part
    small_square = jnp.sum(lanes, axis=1, keepdims=True) + jnp.sum(tail * tail, axis=0, keepdims=True)
    value = jnp.sqrt(square_ref[0:1, 0:1] + small_square)
    factor = jnp.minimum(1.0, max_norm / value)
    (enc_n, enc_m, enc_v, enc_l, dec_n, dec_m, dec_v, dec_l, gene_n, gene_m, gene_v, small_n, small_m, small_v, head_n, head_m, head_v, norm_n, norm_m, norm_v, norm_out) = outs
    norm_out[...] = jnp.broadcast_to(value, norm_out.shape)
    new, first, second = step_of(enc[0][...], enc_g_ref[...] * factor, enc[1][...], enc[2][...], rate_genes)
    enc_n[...], enc_m[...], enc_v[...], enc_l[...] = new, first, second, new.astype(BF)
    for index in range(2):
        gradient = dec_g_ref[index * genes : (index + 1) * genes, :] * factor
        new, first, second = step_of(dec[0][index], gradient, dec[1][index], dec[2][index], rate_genes)
        dec_n[index], dec_m[index], dec_v[index], dec_l[index] = new, first, second, new.astype(BF)
    for index in range(pl.cdiv(genes, 128)):
        span = slice(index * 128, min(genes, (index + 1) * 128))
        gradient = dec_g_ref[2 * genes + index * 8 : 2 * genes + index * 8 + 3, 0 : span.stop - span.start] * factor
        new, first, second = step_of(gene[0][:, span], gradient, gene[1][:, span], gene[2][:, span], rate_small)
        gene_n[:, span], gene_m[:, span], gene_v[:, span] = new, first, second
    rows = 2 * kinds + latent
    new, first, second = step_of(small[0][...], small_g_ref[0:rows, :] * factor, small[1][...], small[2][...], rate_small)
    small_n[...], small_m[...], small_v[...] = new, first, second
    for half in range(2):
        take = slice(base + 16 * half, base + 16 * half + latent)
        take_bias = slice(base + 32 + 16 * half, base + 32 + 16 * half + latent)
        into = slice(half * latent, (half + 1) * latent)
        scratch[into, 0:hidden] = small_g_ref[take, :]
        scratch[into, hidden : 2 * hidden] = small_g_ref[take_bias, :]
    gradient = scratch[0 : 2 * latent, 0 : hidden + 1] * factor
    new, first, second = step_of(head[0][...], gradient, head[1][...], head[2][...], rate_small)
    head_n[...], head_m[...], head_v[...] = new, first, second
    for index in range(4):
        line = slice(index, index + 1)
        new, first, second = step_of(norm[0][line], norm_g[index] * factor, norm[1][line], norm[2][line], rate_small)
        norm_n[line], norm_m[line], norm_v[line] = new, first, second


def per_device(counts, library, noise, batch_ids, gene_mask, kl_weight, enc_w, enc_m, enc_v, dec_w, dec_m, dec_v, gene_par, gene_m, gene_v, small_w, small_m, small_v, head_w, head_m, head_v, norm_par, norm_m, norm_v):
    rows_all, genes = counts.shape
    cells = float(rows_all * lax.axis_size("cells"))
    groups = lax.axis_size("genes")
    hidden = enc_w.shape[1]
    latent = head_w.shape[1] // 2
    kinds = (small_w.shape[0] - latent) // 2
    share = rows_all // groups
    width = min(1024, rows_all)
    blocks = rows_all // width
    fast = groups == 8 and blocks == 8
    me = lax.axis_index("genes").astype(jnp.int32).reshape(1)
    chunk = 16

    x_t = counts.T
    enc_low = enc_w.T.astype(BF)
    dec_t = dec_w.transpose(0, 2, 1).astype(BF).reshape(2 * genes, hidden)
    dec_n = jnp.concatenate([dec_w[0], dec_w[1]], axis=1).astype(BF)
    keep = gene_mask > 0
    th_row = jnp.exp(gene_par[2])

    def tall(row):
        return jnp.broadcast_to(row[..., None], row.shape + (128,))

    the_row = th_row + zinb_epsilon
    par = tall(
        jnp.stack(
            [
                jnp.where(keep, gene_par[0], -1e30),
                jnp.where(keep, gene_par[1], 1e30),
                the_row,
                th_row,
                jnp.log(the_row),
                th_row / the_row,
            ]
        )
    )
    keep_bf = tall(keep.astype(BF))
    lg_rows, dg_rows = [jnp.zeros_like(th_row)], [jnp.zeros_like(th_row)]
    for k in range(COUNT_TOP):
        lg_rows.append(lg_rows[-1] + jnp.where(keep, jnp.log((th_row + k) / (1.0 + k)), 0.0))
        dg_rows.append(dg_rows[-1] + jnp.where(keep, 1.0 / (th_row + k), 0.0))
    lg_tab = tall(jnp.stack(lg_rows[1:]))
    dg_tab = tall(jnp.stack(dg_rows[1:]))
    enc_b_t = small_w[:kinds].T
    dec_b_t = small_w[kinds : 2 * kinds].T
    lat_row = jnp.pad(small_w[2 * kinds :], ((0, 16 - latent), (0, 0)))
    lat_t = lat_row.T
    norm_t = norm_par.T
    head_t = head_w.T
    pad = ((0, 16 - latent), (0, 0))
    head_all = jnp.concatenate([jnp.pad(head_t[:latent], pad), jnp.pad(head_t[latent:], pad)], axis=0)
    head_rows = head_all[:, :hidden]
    head_bias = jnp.broadcast_to(head_all[:, hidden:], (32, 128))
    head_cols = head_rows.T
    noise_t = jnp.pad(noise.T, pad)
    lib8 = library.reshape(blocks, width)
    batch_all = batch_ids.reshape(blocks, 1, width)
    batch_own = batch_ids.reshape(groups, 1, share)
    klw = jnp.broadcast_to(kl_weight.reshape(1, 1), (8, 128))

    own_block = pl.BlockSpec((1, 1, share), lambda i, m: (m[0], 0, 0))
    own_lanes = lambda rows: pl.BlockSpec((rows, share), lambda i, m: (0, m[0]))
    lane_block = lambda rows: pl.BlockSpec((rows, width), lambda i, *_: (0, i))

    enc_pieces, dec_pieces = call(
        prep_kernel,
        (1,),
        [(enc_b_t, whole((hidden, kinds))), (dec_b_t, whole((hidden, kinds))), (lat_t, whole((hidden, 16)))],
        [((3 * hidden, kinds), BF, whole((3 * hidden, kinds))), ((3 * hidden, kinds + 48), BF, whole((3 * hidden, kinds + 48)))],
    )

    keep_part, send_part = call(
        enc_kernel,
        (groups,),
        [
            (me if fast else me & 1, None),
            (x_t, pl.BlockSpec((genes, share), lambda i, m: (0, i ^ m[0]))),
            (enc_low, whole((hidden, genes))),
        ],
        [
            ((groups // 2, hidden, share), F32, pl.BlockSpec((1, hidden, share), lambda i, m: (i // 2, 0, 0))),
            ((groups // 2, hidden, share), BF, pl.BlockSpec((1, hidden, share), lambda i, m: (i // 2, 0, 0))),
        ],
        scalars=1,
        flops=2 * rows_all * genes * hidden,
        moved=2 * rows_all * genes,
    )
    got = swap(send_part, "genes", 1)
    slot = pl.BlockSpec((1, hidden, share), lambda i, m: (0, 0, 0))
    if fast:
        far = []
        for k in (2, 3, 1):
            mine = (keep_part[k : k + 1] + got[k : k + 1].astype(F32)).astype(BF)
            far.append(swap(mine, "genes", 2 * k))
        kept = keep_part
    else:
        summed = keep_part + got.astype(F32)
        summed = lax.psum_scatter(
            summed,
            "genes",
            scatter_dimension=0,
            axis_index_groups=[list(range(c, groups, 2)) for c in range(2)],
            tiled=True,
        )
        zero = jnp.zeros((1, hidden, share), BF)
        kept, got, far = summed, zero, [zero] * 3
    pre_enc, stat_enc = call(
        own_kernel,
        (1,),
        [(me, None), (kept, slot), (got, slot)]
        + [(part, slot) for part in far]
        + [(batch_own, own_block), (enc_pieces, whole((3 * hidden, kinds)))],
        [((hidden, share), F32, whole((hidden, share))), ((8, hidden), F32, whole((8, hidden)))],
        scalars=1,
        flops=2 * share * hidden * kinds * 3,
        moved=share * hidden * 16,
    )
    logc, gam_cell, dig_acc = call(
        lambda *refs: counts_kernel(chunk, *refs),
        (blocks,),
        [
            (x_t, lane_block(genes)),
            (lg_tab, whole((COUNT_TOP, genes, 128))),
            (dg_tab, whole((COUNT_TOP, genes, 128))),
        ],
        [
            ((genes, rows_all), BF, lane_block(genes)),
            ((blocks, width), F32, whole((blocks, width))),
            ((genes, 128), F32, whole((genes, 128))),
        ],
        flops=rows_all * genes * 30,
        moved=4 * rows_all * genes,
    )
    stat_enc = total(total(stat_enc, "genes"), "cells")

    stat8 = whole((8, hidden))
    z_own, head_out, kl_row = call(
        lambda *refs: latent_kernel(cells, latent, *refs),
        (1,),
        [
            (me, None),
            (pre_enc, whole((hidden, share))),
            (stat_enc, stat8),
            (norm_t, whole((hidden, 4))),
            (head_rows, whole((32, hidden))),
            (head_bias, whole((32, 128))),
            (noise_t, own_lanes(16)),
            (batch_own, own_block),
            (dec_pieces, whole((3 * hidden, kinds + 48))),
            (enc_b_t, whole((hidden, kinds))),
        ],
        [
            ((16, share), F32, whole((16, share))),
            ((32, share), F32, whole((32, share))),
            ((1, share), F32, whole((1, share))),
        ],
        scalars=1,
    )
    if fast:
        column = jnp.stack([z_own] + [swap(z_own, "genes", 2 * k) for k in (1, 2, 3)])
        z_all = jnp.concatenate([column, swap(column, "genes", 1)])
        stat_dec = jnp.sum(z_all[:, 8:, :hidden], axis=0)
        where_z = me
        z_spec = pl.BlockSpec((1, 16, width), lambda i, m: (((i ^ m[0]) % 2) * 4 + (i ^ m[0]) // 2, 0, 0))
    else:
        z_all = lax.all_gather(z_own, "genes", axis=0)
        stat_dec = jnp.sum(z_all[:, 8:, :hidden], axis=0)
        z_all = z_all.transpose(1, 0, 2).reshape(16, blocks, width).transpose(1, 0, 2)
        where_z = me
        z_spec = pl.BlockSpec((1, 16, width), lambda i, m: (i, 0, 0))
    stat_dec = total(stat_dec, "cells")

    batch_spec = pl.BlockSpec((1, 1, width), lambda i, *_: (i, 0, 0))
    hid, phat_dec, lse = call(
        lambda *refs: decode_kernel(cells, latent, *refs),
        (blocks,),
        [
            (where_z, None),
            (z_all, z_spec),
            (batch_all, batch_spec),
            (stat_dec, stat8),
            (norm_t, whole((hidden, 4))),
            (dec_pieces, whole((3 * hidden, kinds + 48))),
            (enc_b_t, whole((hidden, kinds))),
            (dec_t, pl.BlockSpec((genes, hidden), lambda i, m: (0, 0))),
            (par, pl.BlockSpec((None, genes, 128), lambda i, m: (0, 0, 0))),
        ],
        [
            ((hidden, rows_all), BF, lane_block(hidden)),
            ((hidden, rows_all), F32, lane_block(hidden)),
            ((blocks, width), F32, whole((blocks, width))),
        ],
        scratch=[pltpu.VMEM((genes, width), F32)],
        scalars=1,
        flops=2 * rows_all * genes * hidden,
        moved=rows_all * hidden * 6,
    )
    lse = log_total_of(lse, "genes")

    full8 = whole((blocks, width))
    gm, gd, rt, mass, recon, gene_acc = call(
        lambda *refs: zinb_kernel(chunk, min(256, width), *refs),
        (blocks,),
        [
            (hid, lane_block(hidden)),
            (dec_t, whole((2 * genes, hidden))),
            (x_t, lane_block(genes)),
            (keep_bf, whole((genes, 128))),
            (par, whole((6, genes, 128))),
            (lib8, full8),
            (lse, full8),
            (gam_cell, full8),
        ],
        [
            ((genes, rows_all), BF, lane_block(genes)),
            ((genes, rows_all), BF, lane_block(genes)),
            ((genes, rows_all), BF, lane_block(genes)),
            ((blocks, width), F32, full8),
            ((blocks, width), F32, full8),
            ((3, genes, 128), F32, whole((3, genes, 128))),
        ],
        scratch=[pltpu.VMEM((2 * genes, width), F32)],
        flops=rows_all * genes * 200,
        moved=8 * rows_all * genes,
    )
    mass = total(mass, "genes")
    part_a, part_r, dec_acc = call(
        back_kernel,
        (blocks,),
        [
            (gm, lane_block(genes)),
            (gd, lane_block(genes)),
            (rt, lane_block(genes)),
            (hid, lane_block(hidden)),
            (dec_n, whole((hidden, 2 * genes))),
        ],
        [
            ((hidden, rows_all), F32, lane_block(hidden)),
            ((hidden, rows_all), F32, lane_block(hidden)),
            ((2 * genes, hidden), F32, whole((2 * genes, hidden))),
        ],
        flops=2 * rows_all * genes * hidden * 5,
        moved=8 * rows_all * genes,
    )

    if fast:
        where_d = me
    else:
        where_d = jnp.zeros_like(me)
    half = whole((blocks // 2, 16, width))
    dy_dec, keep_d, send_d = call(
        lambda *refs: hidden_grad_kernel(cells, latent, *refs),
        (blocks,),
        [
            (where_d, None),
            (part_a, lane_block(hidden)),
            (part_r, lane_block(hidden)),
            (mass, full8),
            (hid, lane_block(hidden)),
            (phat_dec, lane_block(hidden)),
            (stat_dec, stat8),
            (norm_par, whole((4, hidden))),
            (lat_row, whole((16, hidden))),
            (recon, full8),
        ],
        [
            ((hidden, rows_all), F32, lane_block(hidden)),
            ((blocks // 2, 16, width), F32, half),
            ((blocks // 2, 16, width), F32, half),
        ],
        scratch=[pltpu.VMEM((2, hidden, 128), F32)],
        scalars=1,
    )
    slot_d = pl.BlockSpec((1, 16, share), lambda i, m: (0, 0, 0))
    if fast:
        got_d = swap(send_d, "genes", 1)
        pieces = [swap(keep_d[k : k + 1] + got_d[k : k + 1], "genes", 2 * k) for k in (1, 2, 3)]
        own_d = [keep_d, got_d] + pieces
    else:
        both = jnp.stack([keep_d, send_d], axis=1).reshape(blocks, 16, width)
        stat_part = both[0, 8:, :hidden]
        both = both.transpose(1, 0, 2).reshape(16, groups, share).transpose(1, 0, 2)
        mine = lax.psum_scatter(both, "genes", scatter_dimension=0, tiled=True)
        zero = jnp.zeros_like(mine)
        own_d = [mine, zero, zero, zero, zero]
    if fast:
        sums_dec = sum(part[0, 8:, :hidden] for part in own_d)
    else:
        sums_dec = lax.psum(stat_part, "genes")
    sums_dec = total(sums_dec, "cells")
    dec_part, oh_part = call(
        lambda *refs: dec_grad_kernel(cells, latent, *refs),
        (blocks,),
        [
            (where_z, None),
            (rt, lane_block(genes)),
            (hid, lane_block(hidden)),
            (mass, full8),
            (dy_dec, lane_block(hidden)),
            (z_all, z_spec),
            (batch_all, batch_spec),
            (dec_acc, whole((2 * genes, hidden))),
            (gene_acc, whole((3, genes, 128))),
            (dig_acc, whole((genes, 128))),
            (par, pl.BlockSpec((None, genes, 128), lambda i, m: (3, 0, 0))),
        ],
        [
            ((2 * genes + 8 * (-(-genes // 128)), hidden), F32, whole((2 * genes + 8 * (-(-genes // 128)), hidden))),
            ((kinds + 16, hidden), F32, whole((kinds + 16, hidden))),
        ],
        scratch=[pltpu.VMEM((genes, hidden + 16), F32)],
        scalars=1,
    )

    dy_enc, g_head, loss, stat_back = call(
        lambda *refs: head_grad_kernel(cells, latent, *refs),
        (1,),
        [(me, None)]
        + [(part, slot_d) for part in own_d]
        + [
            (sums_dec, stat8),
            (phat_dec, own_lanes(hidden)),
            (stat_dec, stat8),
            (norm_par, whole((4, hidden))),
            (lat_row, whole((16, hidden))),
            (head_out, whole((32, share))),
            (noise_t, own_lanes(16)),
            (kl_row, whole((1, share))),
            (klw, whole((8, 128))),
            (pre_enc, whole((hidden, share))),
            (stat_enc, stat8),
            (norm_t, whole((hidden, 4))),
            (head_cols, whole((hidden, 32))),
        ],
        [
            ((hidden, share), F32, whole((hidden, share))),
            ((32, share), F32, whole((32, share))),
            ((1, share), F32, whole((1, share))),
            ((8, hidden), F32, stat8),
        ],
        scalars=1,
    )
    stat_back = total(total(stat_back, "genes"), "cells")
    pre_grad, pre_low = call(
        lambda *refs: pre_grad_kernel(cells, *refs),
        (1,),
        [
            (dy_enc, whole((hidden, share))),
            (pre_enc, whole((hidden, share))),
            (stat_enc, stat8),
            (norm_t, whole((hidden, 4))),
            (stat_back, stat8),
        ],
        [((hidden, share), F32, whole((hidden, share))), ((hidden, share), BF, whole((hidden, share)))],
    )
    pre_all = lax.all_gather(pre_low, "genes", axis=0)
    small_rows = 2 * kinds + 16 + 64
    (small_part,) = call(
        lambda *refs: small_grad_kernel(cells, latent, *refs),
        (1,),
        [
            (me, None),
            (pre_grad, whole((hidden, share))),
            (g_head, whole((32, share))),
            (pre_enc, whole((hidden, share))),
            (stat_enc, stat8),
            (norm_t, whole((hidden, 4))),
            (batch_own, own_block),
            (phat_dec, own_lanes(hidden)),
            (z_own, whole((16, share))),
            (oh_part, whole((kinds + 16, hidden))),
            (sums_dec, stat8),
            (stat_dec, stat8),
            (norm_par, whole((4, hidden))),
        ],
        [((small_rows, hidden), F32, whole((small_rows, hidden)))],
        scalars=1,
    )
    small_g = total(total(small_part, "genes"), "cells")
    dec_g = total(dec_part, "cells")
    (enc_part,) = call(
        enc_grad_kernel,
        (blocks,),
        [
            (logc, lane_block(genes)),
            (pre_all, pl.BlockSpec((groups // blocks, hidden, share), lambda i: (i, 0, 0))),
        ],
        [((genes, hidden), F32, whole((genes, hidden)))],
        flops=2 * rows_all * genes * hidden,
        moved=2 * rows_all * genes,
    )
    enc_g = total(enc_part, "cells")

    (square,) = call(
        square_kernel,
        (1,),
        [(enc_g, whole(enc_g.shape)), (dec_g, whole(dec_g.shape))],
        [((8, 128), F32, whole((8, 128)))],
    )
    square = total(square, "genes")

    def turn(value):
        return value.transpose(0, 2, 1)

    state = [
        enc_w, enc_m, enc_v, turn(dec_w), turn(dec_m), turn(dec_v), gene_par, gene_m, gene_v,
        small_w, small_m, small_v, head_w.T, head_m.T, head_v.T, norm_par, norm_m, norm_v,
    ]
    ins = [square, enc_g, dec_g, small_g, stat_back, sums_dec] + state
    outs = []
    for index in range(6):
        one = state[3 * index]
        outs += [(one.shape, F32)] * 3
        if index < 2:
            outs.append((one.shape, BF))
    outs.append(((8, 128), F32))
    res = call(
        lambda *refs: update_kernel(latent, *refs),
        (1,),
        [(array, whole(array.shape)) for array in ins],
        [(shape, dtype, whole(shape)) for shape, dtype in outs],
        scratch=[pltpu.VMEM((24, 2 * hidden), F32)],
    )
    enc_res, dec_res = res[0:4], [turn(part) for part in res[4:8]]
    head_res = [part.T for part in res[14:17]]
    return (
        *enc_res,
        *dec_res,
        *res[8:14],
        *head_res,
        *res[17:20],
        res[20][0, 0],
        loss.reshape(share),
    )


def solution(mesh):
    placed = (
        P("cells", "genes"), P("cells"), P("cells", None), P("cells"), P("genes"), P(),
        P("genes", None), P("genes", None), P("genes", None),
        P(None, None, "genes"), P(None, None, "genes"), P(None, None, "genes"),
        P(None, "genes"), P(None, "genes"), P(None, "genes"),
        P(), P(), P(), P(), P(), P(), P(), P(), P(),
    )
    return jax.shard_map(
        per_device,
        mesh=mesh,
        in_specs=placed,
        out_specs=(
            P("genes", None), P("genes", None), P("genes", None), P("genes", None),
            P(None, None, "genes"), P(None, None, "genes"), P(None, None, "genes"), P(None, None, "genes"),
            P(None, "genes"), P(None, "genes"), P(None, "genes"),
            P(), P(), P(), P(), P(), P(), P(), P(), P(), P(),
            P(("cells", "genes")),
        ),
        check_vma=False,
    )
```

time: 1110 us -> 335 us (0.30)
  other arithmetic: 396 us -> 19.9 us
  blocking collectives: 278 us -> 0 us
  waiting for transfers between devices: 290 us -> 62.1 us
  Pallas kernels: 0 us -> 146 us
  starting transfers between devices: 0.97 us -> 73.1 us
  local copies, waits for them, and re-layouts: 69.4 us -> 16.6 us
  matrix products: 42.9 us -> 0 us
    reduce_sum x21 -> x1, other arithmetic: 329 us -> 0.01 us  [per_device(): stat_dec = jnp.sum(z_all[:, 8:, :hidden], axis=0)]
    psum x8 -> x0, blocking collectives: 250 us -> none  [the longest x4 159 us: wide_sum(): return lax.psum((values[0], values[1]), ('cells', 'genes'))]
    psum x2 -> x0, waiting for transfers between devices: 153 us -> none  [the longest x1 106 us: per_device(): lax.psum((grad_small, grad_head), ('cells', 'genes'))]
    pallas_call x0 -> x16, Pallas kernels: none -> 146 us  [call(): pl.pallas_call(kernel, out_shape=[jax.ShapeDtypeStruct(shape, dtype) for...]
    reduce_scatter x2 -> x0, waiting for transfers between devices: 99.3 us -> none  [the longest x1 51.9 us: per_device(): lax.psum_scatter(jnp.dot(cell_rows, enc_low, preferred_element_type=jnp.f...]
    ppermute x0 -> x57, starting transfers between devices: none -> 73.1 us  [swap(): return lax.ppermute(value, axis, [(i, i ^ bit) for i in range(count)])]
    ppermute x0 -> x57, waiting for transfers between devices: none -> 56.4 us  [swap(): return lax.ppermute(value, axis, [(i, i ^ bit) for i in range(count)])]
    dot_general x15 -> x0, matrix products: 42.9 us -> none  [the longest x2 16.2 us: plain_inner(): lax.dot_general(left, right, (((0,), (0,)), ((), ())), preferred_element_...]
  transfers between devices with their start and end apart: 6 -> 58, of which waited for: 6 -> 34; matrix products, arithmetic and copies ran while one was open for 3% -> 5% of each run, Pallas kernels for 0% -> 16%
where the time goes in v1:
time: 335 us; the launch traced here: 333 us
  Pallas kernels  146 us (44%)
  starting transfers between devices  73.1 us (22%)
  waiting for transfers between devices  62.1 us (19%)
  other arithmetic  19.9 us (6%)
  local copies, waits for them, and re-layouts  16.6 us (5%)
  between operations  15.2 us (5%)
    pallas_call x16, Pallas kernels, call(): pl.pallas_call(kernel, out_shape=[jax.ShapeDtypeStruct(shape, dtype) for...  146 us
    ppermute x57, starting transfers between devices, swap(): return lax.ppermute(value, axis, [(i, i ^ bit) for i in range(count)])  73.1 us
    ppermute x57, waiting for transfers between devices, swap(): return lax.ppermute(value, axis, [(i, i ^ bit) for i in range(count)])  56.4 us
    add x12, other arithmetic, total(): value + swap(value, axis, low) + (swap(value, axis, high) + swap(value, a...  6.81 us
  transfers between devices with their start and end apart: 58, of which 34 were waited for; matrix products, arithmetic and copies ran while one was open for 5% of the time, Pallas kernels for 16%

profile of v1, /device:TPU:0, one launch (start us, length us, event | category | flops | bytes accessed | tf_op | source)
XLA Modules:
  0.0 333.4 jit_solution(12790383665107719092)
XLA Ops:
  9.0 8.5 %shard_map.400 = (f32[4,128,1024]{2,1,0:T(8,128)}, bf16[4,128,1024]{2,1,0:T(8,128)(2,1)}) custom-call(s32[1]{0:T(128)} %bitcast.1.me_ref.refs_0_, bf16[320,8192]{1,0:T(8,128)(2,1)} %bitcast.46, bf16[128,320]{1,0:T(8,128)(2,1)} %bitcast.68), custom_call_target="tpu_custom_call" | custom-call | flops 671088640 | bytes 5242880 | tf_op jit(solution)/shard_map/pallas_call | solution.py:46
  20.4 2.7 add_convert_fusion
  23.2 4.0 %collective-permute-start.1 = (bf16[1,128,1024]{2,1,0:T(8,128)(2,1)}, bf16[1,128,1024]{2,1,0:T(8,128)(2,1)S(1)}, u32[]{:S(2)}, u32[]{:S(2)}) collective-permute-start(bf16[1,128,1024]{2,1,0:T(8,128)(2,1)} %get-tuple-element.170), channel_id=1, source_target_pairs={{0,4},{1,5},{2,6},{3,7},{4,0},{5,1},{6,2},{7,3},{8,12},{9,13},{10,... | collective-permute-start | bytes 786440 | tf_op jit(solution)/shard_map/ppermute | solution.py:63
  33.9 11.8 %collective-permute-done.1.one_ref = bf16[1,128,1024]{2,1,0:T(8,128)(2,1)S(1)} collective-permute-done((bf16[1,128,1024]{2,1,0:T(8,128)(2,1)}, bf16[1,128,1024]{2,1,0:T(8,128)(2,1)S(1)}, u32[]{:S(2)}, u32[]{:S(2)}) %collective-permute-start.1) | collective-permute-done | bytes 262176 | tf_op jit(solution)/shard_map/ppermute | solution.py:63
  47.0 3.2 shard_map.402
  52.3 5.3 %collective-permute-start.5 = (f32[8,128]{1,0:T(8,128)S(1)}, f32[8,128]{1,0:T(8,128)S(1)}, u32[]{:S(2)}, u32[]{:S(2)}) collective-permute-start(f32[8,128]{1,0:T(8,128)S(1)} %add.293), channel_id=1, source_target_pairs={{0,2},{1,3},{2,0},{3,1},{4,6},{5,7},{6,4},{7,5},{8,10},{9,11},{10,... | collective-permute-start | bytes 12296 | tf_op jit(solution)/shard_map/ppermute | solution.py:63
  62.1 2.8 collective-permute-done.7
  64.9 2.4 collective-permute-start.10
  72.8 3.7 %shard_map.403 = (f32[16,1024]{1,0:T(8,128)}, f32[32,1024]{1,0:T(8,128)}, f32[1,1024]{1,0:T(1,128)}) custom-call(s32[1]{0:T(128)} %bitcast.1.me_ref.refs_0_, f32[128,1024]{1,0:T(8,128)} %get-tuple-element.82.refs_1_.refs_15_.refs_3_, f32[8,128]{1,0:T(8,128)} %add_add_fusion.10.refs_2_.refs_16_.refs_4_, f32[128,4]{1,0:T(8,128)} %bitcast.51, ...), custom_call_target="tpu_custom_call" | custom-call | tf_op jit(solution)/shard_map/pallas_call | solution.py:46
  78.5 2.4 collective-permute-start.13
  82.0 2.7 collective-permute-done.13
  95.7 15.5 %shard_map.404 = (bf16[128,8192]{1,0:T(8,128)(2,1)}, f32[128,8192]{1,0:T(8,128)}, f32[8,1024]{1,0:T(8,128)}) custom-call(s32[1]{0:T(128)} %bitcast.1.me_ref.refs_0_, f32[8,16,1024]{2,1,0:T(8,128)} %copy-done.3, s32[8,1,1024]{2,1,0:T(1,128)} %bitcast.64, f32[8,128]{1,0:T(8,128)} %add_add_fusion.9.refs_3_.refs_6_.refs_8_.refs_11_, f32[128,4]{1,0:T(8,128)} %bitcast.52, ...), custom_call_target="tpu_custom_call" | custom-call | flops 671088640 | bytes 6291456 | tf_op jit(solution)/shard_map/pallas_call | solution.py:46
  113.5 2.9 collective-permute-start.20
  121.7 14.7 %shard_map.399 = (bf16[320,8192]{1,0:T(8,128)(2,1)}, f32[8,1024]{1,0:T(8,128)}, f32[320,128]{1,0:T(8,128)}) custom-call(bf16[320,8192]{1,0:T(8,128)(2,1)} %bitcast.47, f32[8,320,128]{2,1,0:T(8,128)} %broadcast_in_dim.64.refs_1_, f32[8,320,128]{2,1,0:T(8,128)} %broadcast_in_dim.65.refs_2_), custom_call_target="tpu_custom_call" | custom-call | flops 78643200 | bytes 10485760 | tf_op jit(solution)/shard_map/pallas_call | solution.py:46
  137.8 42.1 %shard_map.405 = (bf16[320,8192]{1,0:T(8,128)(2,1)}, bf16[320,8192]{1,0:T(8,128)(2,1)}, bf16[320,8192]{1,0:T(8,128)(2,1)}, f32[8,1024]{1,0:T(8,128)}, f32[8,1024]{1,0:T(8,128)}, /*index=5*/f32[3,320,128]{2,1,0:T(8,128)}) custom-call(bf16[128,8192]{1,0:T(8,128)(2,1)} %get-tuple-element.86.refs_0_.hid_ref.refs_4_.refs_2_, bf16[640,128]{1,0:T(8,128)(2,1)} %bitcast.57, ...), custom_call_target="tpu_custom_call" | custom-call | flops 524288000 | bytes 20971520 | tf_op jit(solution)/shard_map/pallas_call | solution.py:46
  182.1 2.9 collective-permute-start.24
  186.5 13.2 %shard_map.406 = (f32[128,8192]{1,0:T(8,128)}, f32[128,8192]{1,0:T(8,128)}, f32[640,128]{1,0:T(8,128)}) custom-call(bf16[320,8192]{1,0:T(8,128)(2,1)} %get-tuple-element.89.gm_ref, bf16[320,8192]{1,0:T(8,128)(2,1)} %get-tuple-element.90.gd_ref, bf16[320,8192]{1,0:T(8,128)(2,1)} %get-tuple-element.91.rt_ref.refs_1_, ...), custom_call_target="tpu_custom_call" | custom-call | flops 3355443200 | bytes 20971520 | tf_op jit(solution)/shard_map/pallas_call | solution.py:46
  200.4 10.5 %shard_map.407 = (f32[128,8192]{1,0:T(8,128)}, f32[4,16,1024]{2,1,0:T(8,128)}, f32[4,16,1024]{2,1,0:T(8,128)}) custom-call(s32[1]{0:T(128)} %bitcast.1.me_ref.refs_0_, f32[128,8192]{1,0:T(8,128)} %get-tuple-element.92.refs_1_, f32[128,8192]{1,0:T(8,128)} %get-tuple-element.93.refs_2_, f32[8,1024]{1,0:T(8,128)} %add_add_fusion.4.refs_3_, ...), custom_call_target="tpu_custom_call" | custom-call | tf_op jit(solution)/shard_map/pallas_call | solution.py:46
  213.8 2.9 collective-permute-start.28
  219.1 2.4 collective-permute-done.28.refs_4_
  231.3 3.8 %shard_map.408 = (f32[128,1024]{1,0:T(8,128)}, f32[32,1024]{1,0:T(8,128)}, f32[1,1024]{1,0:T(1,128)}, f32[8,128]{1,0:T(8,128)}) custom-call(s32[1]{0:T(128)} %bitcast.1.me_ref.refs_0_, f32[4,16,1024]{2,1,0:T(8,128)} %get-tuple-element.97.refs_1_, f32[4,16,1024]{2,1,0:T(8,128)} %copy-done.2, f32[1,16,1024]{2,1,0:T(8,128)} %copy-done.11, ...), custom_call_target="tpu_custom_call" | custom-call | tf_op jit(solution)/shard_map/pallas_call | solution.py:46
  242.6 2.4 collective-permute-done.36
  252.1 2.6 shard_map.409
  254.8 10.6 %shard_map.411 = (f32[664,128]{1,0:T(8,128)}, f32[144,128]{1,0:T(8,128)}) custom-call(s32[1]{0:T(128)} %bitcast.1.me_ref.refs_0_, bf16[320,8192]{1,0:T(8,128)(2,1)} %get-tuple-element.91.rt_ref.refs_1_, bf16[128,8192]{1,0:T(8,128)(2,1)} %get-tuple-element.86.refs_0_.hid_ref.refs_4_.refs_2_, f32[8,1024]{1,0:T(8,128)} %add_add_fusion.4.refs_3_, ...), custom_call_target="tpu_custom_call" | custom-call | tf_op jit(solution)/shard_map/pallas_call | solution.py:46
  269.0 3.7 %shard_map.413 = f32[336,128]{1,0:T(8,128)} custom-call(s32[1]{0:T(128)} %bitcast.1.me_ref.refs_0_, f32[128,1024]{1,0:T(8,128)} %get-tuple-element.109.refs_1_, f32[32,1024]{1,0:T(8,128)} %get-tuple-element.110.refs_2_, f32[128,1024]{1,0:T(8,128)} %get-tuple-element.82.refs_1_.refs_15_.refs_3_, f32[8,128]{1,0:T(8,128)} %add_add_fusion.10.refs_2_.refs_16_.refs_4_, ...), custom_call_target="tpu_custom_call" | custom-call | tf_op jit(solution)/shard_map/pallas_call | solution.py:46
  275.3 2.5 collective-permute-start.52
  281.3 5.6 %all-gather.3.cloned.1.call-done = bf16[1024,1024]{1,0:T(8,128)(2,1)} async-done(((bf16[128,1024]{1,0:T(8,128)(2,1)}), bf16[1024,1024]{1,0:T(8,128)(2,1)}) %all-gather.3.cloned.1.call-update) | async-done | bytes 2097168 | tf_op jit(solution)/shard_map/all_gather | solution.py:1000
  286.9 7.2 %shard_map.410 = f32[320,128]{1,0:T(8,128)} custom-call(bf16[320,8192]{1,0:T(8,128)(2,1)} %get-tuple-element.78.logc_ref, bf16[8,128,1024]{2,1,0:T(8,128)(2,1)} %bitcast.50), custom_call_target="tpu_custom_call" | custom-call | flops 671088640 | bytes 5242880 | tf_op jit(solution)/shard_map/pallas_call | solution.py:46
  301.3 2.8 collective-permute-start.56
  304.1 2.7 collective-permute-done.41
  318.1 3.0 collective-permute-done.49
  321.7 3.7 %shard_map.414 = (f32[320,128]{1,0:T(8,128)}, f32[320,128]{1,0:T(8,128)}, f32[320,128]{1,0:T(8,128)}, bf16[320,128]{1,0:T(8,128)(2,1)}, f32[2,320,128]{2,1,0:T(8...) custom-call(f32[8,128]{1,0:T(8,128)} %add_add_fusion.5.refs_0_, ...), custom_call_target="tpu_custom_call" | custom-call | tf_op jit(solution)/shard_map/pallas_call | solution.py:46
  (221 shorter events, 110.9 us)
Async XLA Ops:
  7.2 279.7 %all-gather.3.cloned.1.call-start = ((), (), s32[]{:S(2)}) async-start(), calls=%async_computation | async-start | bytes 2359296 | tf_op jit(solution)/shard_map/all_gather | solution.py:1000
  23.2 22.5 %collective-permute-start.1 = (bf16[1,128,1024]{2,1,0:T(8,128)(2,1)}, bf16[1,128,1024]{2,1,0:T(8,128)(2,1)S(1)}, u32[]{:S(2)}, u32[]{:S(2)}) collective-permute-start(bf16[1,128,1024]{2,1,0:T(8,128)(2,1)} %get-tuple-element.170), channel_id=1, source_target_pairs={{0,4},{1,5},{2,6},{3,7},{4,0},{5,1},{6,2},{7,3},{8,12},{9,13},{10,... | collective-permute-start | bytes 786440 | tf_op jit(solution)/shard_map/ppermute | solution.py:63
  27.1 18.6 %collective-permute-start.2 = (bf16[1,128,1024]{2,1,0:T(8,128)(2,1)S(1)}, bf16[1,128,1024]{2,1,0:T(8,128)(2,1)S(1)}, u32[]{:S(2)}, u32[]{:S(2)}) collective-permute-start(bf16[1,128,1024]{2,1,0:T(8,128)(2,1)S(1)} %get-tuple-element.169), channel_id=1, source_target_pairs={{0,6},{1,7},{2,4},{3,5},{4,2},{5,3},{6,0},{7,1},{8,14},{9,15},{10,... | collective-permute-start | bytes 786440 | tf_op jit(solution)/shard_map/ppermute | solution.py:63
  28.4 17.9 %collective-permute-start.3 = (bf16[1,128,1024]{2,1,0:T(8,128)(2,1)S(1)}, bf16[1,128,1024]{2,1,0:T(8,128)(2,1)S(1)}, u32[]{:S(2)}, u32[]{:S(2)}) collective-permute-start(bf16[1,128,1024]{2,1,0:T(8,128)(2,1)S(1)} %get-tuple-element.168), channel_id=1, source_target_pairs={{0,2},{1,3},{2,0},{3,1},{4,6},{5,7},{6,4},{7,5},{8,10},{9,11},{10,... | collective-permute-start | bytes 786440 | tf_op jit(solution)/shard_map/ppermute | solution.py:63
  52.3 8.7 %collective-permute-start.5 = (f32[8,128]{1,0:T(8,128)S(1)}, f32[8,128]{1,0:T(8,128)S(1)}, u32[]{:S(2)}, u32[]{:S(2)}) collective-permute-start(f32[8,128]{1,0:T(8,128)S(1)} %add.293), channel_id=1, source_target_pairs={{0,2},{1,3},{2,0},{3,1},{4,6},{5,7},{6,4},{7,5},{8,10},{9,11},{10,... | collective-permute-start | bytes 12296 | tf_op jit(solution)/shard_map/ppermute | solution.py:63
  59.5 5.4 %collective-permute-start.7 = (f32[8,128]{1,0:T(8,128)S(1)}, f32[8,128]{1,0:T(8,128)S(1)}, u32[]{:S(2)}, u32[]{:S(2)}) collective-permute-start(f32[8,128]{1,0:T(8,128)S(1)} %add.293), channel_id=1, source_target_pairs={{0,6},{1,7},{2,4},{3,5},{4,2},{5,3},{6,0},{7,1},{8,14},{9,15},{10,... | collective-permute-start | bytes 12296 | tf_op jit(solution)/shard_map/ppermute | solution.py:63
  76.4 5.3 %collective-permute-start.11 = (f32[16,1024]{1,0:T(8,128)}, f32[16,1024]{1,0:T(8,128)S(1)}, u32[]{:S(2)}, u32[]{:S(2)}) collective-permute-start(f32[16,1024]{1,0:T(8,128)} %get-tuple-element.85.refs_8_), channel_id=1, source_target_pairs={{0,2},{1,3},{2,0},{3,1},{4,6},{5,7},{6,4},{7,5},{8,10},{9,11},{10,... | collective-permute-start | bytes 196616 | tf_op jit(solution)/shard_map/ppermute | solution.py:63
  76.7 5.4 %collective-permute-start.12 = (f32[16,1024]{1,0:T(8,128)}, f32[16,1024]{1,0:T(8,128)S(1)}, u32[]{:S(2)}, u32[]{:S(2)}) collective-permute-start(f32[16,1024]{1,0:T(8,128)} %get-tuple-element.85.refs_8_), channel_id=1, source_target_pairs={{0,4},{1,5},{2,6},{3,7},{4,0},{5,1},{6,2},{7,3},{8,12},{9,13},{10,... | collective-permute-start | bytes 196616 | tf_op jit(solution)/shard_map/ppermute | solution.py:63
  78.5 6.3 %collective-permute-start.13 = (f32[16,1024]{1,0:T(8,128)}, f32[16,1024]{1,0:T(8,128)S(1)}, u32[]{:S(2)}, u32[]{:S(2)}) collective-permute-start(f32[16,1024]{1,0:T(8,128)} %get-tuple-element.85.refs_8_), channel_id=1, source_target_pairs={{0,6},{1,7},{2,4},{3,5},{4,2},{5,3},{6,0},{7,1},{8,14},{9,15},{10,... | collective-permute-start | bytes 196616 | tf_op jit(solution)/shard_map/ppermute | solution.py:63
  113.4 23.0 %collective-permute-start.19 = (f32[8,1024]{1,0:T(8,128)S(1)}, f32[8,1024]{1,0:T(8,128)S(1)}, u32[]{:S(2)}, u32[]{:S(2)}) collective-permute-start(f32[8,1024]{1,0:T(8,128)S(1)} %log_add_fusion.1), channel_id=1, source_target_pairs={{0,2},{1,3},{2,0},{3,1},{4,6},{5,7},{6,4},{7,5},{8,10},{9,11},{10,... | collective-permute-start | bytes 98312 | tf_op jit(solution)/shard_map/ppermute | solution.py:63
  113.5 22.9 %collective-permute-start.20 = (f32[8,1024]{1,0:T(8,128)S(1)}, f32[8,1024]{1,0:T(8,128)S(1)}, u32[]{:S(2)}, u32[]{:S(2)}) collective-permute-start(f32[8,1024]{1,0:T(8,128)S(1)} %log_add_fusion.1), channel_id=1, source_target_pairs={{0,4},{1,5},{2,6},{3,7},{4,0},{5,1},{6,2},{7,3},{8,12},{9,13},{10,... | collective-permute-start | bytes 98312 | tf_op jit(solution)/shard_map/ppermute | solution.py:63
  116.4 20.0 %collective-permute-start.21 = (f32[8,1024]{1,0:T(8,128)S(1)}, f32[8,1024]{1,0:T(8,128)S(1)}, u32[]{:S(2)}, u32[]{:S(2)}) collective-permute-start(f32[8,1024]{1,0:T(8,128)S(1)} %log_add_fusion.1), channel_id=1, source_target_pairs={{0,6},{1,7},{2,4},{3,5},{4,2},{5,3},{6,0},{7,1},{8,14},{9,15},{10,... | collective-permute-start | bytes 98312 | tf_op jit(solution)/shard_map/ppermute | solution.py:63
  182.1 17.6 %collective-permute-start.23 = (f32[8,1024]{1,0:T(8,128)S(1)}, f32[8,1024]{1,0:T(8,128)S(1)}, u32[]{:S(2)}, u32[]{:S(2)}) collective-permute-start(f32[8,1024]{1,0:T(8,128)S(1)} %add.311), channel_id=1, source_target_pairs={{0,2},{1,3},{2,0},{3,1},{4,6},{5,7},{6,4},{7,5},{8,10},{9,11},{10,... | collective-permute-start | bytes 98312 | tf_op jit(solution)/shard_map/ppermute | solution.py:63
  182.1 17.6 %collective-permute-start.24 = (f32[8,1024]{1,0:T(8,128)S(1)}, f32[8,1024]{1,0:T(8,128)S(1)}, u32[]{:S(2)}, u32[]{:S(2)}) collective-permute-start(f32[8,1024]{1,0:T(8,128)S(1)} %add.311), channel_id=1, source_target_pairs={{0,4},{1,5},{2,6},{3,7},{4,0},{5,1},{6,2},{7,3},{8,12},{9,13},{10,... | collective-permute-start | bytes 98312 | tf_op jit(solution)/shard_map/ppermute | solution.py:63
  185.0 14.7 %collective-permute-start.25 = (f32[8,1024]{1,0:T(8,128)S(1)}, f32[8,1024]{1,0:T(8,128)S(1)}, u32[]{:S(2)}, u32[]{:S(2)}) collective-permute-start(f32[8,1024]{1,0:T(8,128)S(1)} %add.311), channel_id=1, source_target_pairs={{0,6},{1,7},{2,4},{3,5},{4,2},{5,3},{6,0},{7,1},{8,14},{9,15},{10,... | collective-permute-start | bytes 98312 | tf_op jit(solution)/shard_map/ppermute | solution.py:63
  213.7 5.4 %collective-permute-start.27 = (f32[1,16,1024]{2,1,0:T(8,128)S(1)}, f32[1,16,1024]{2,1,0:T(8,128)S(1)}, u32[]{:S(2)}, u32[]{:S(2)}) collective-permute-start(f32[1,16,1024]{2,1,0:T(8,128)S(1)} %get-tuple-element.173), channel_id=1, source_target_pairs={{0,2},{1,3},{2,0},{3,1},{4,6},{5,7},{6,4},{7,5},{8,10},{9,11},{10,... | collective-permute-start | bytes 196616 | tf_op jit(solution)/shard_map/ppermute | solution.py:63
  213.8 7.7 %collective-permute-start.28 = (f32[1,16,1024]{2,1,0:T(8,128)S(1)}, f32[1,16,1024]{2,1,0:T(8,128)S(1)}, u32[]{:S(2)}, u32[]{:S(2)}) collective-permute-start(f32[1,16,1024]{2,1,0:T(8,128)S(1)} %get-tuple-element.172), channel_id=1, source_target_pairs={{0,4},{1,5},{2,6},{3,7},{4,0},{5,1},{6,2},{7,3},{8,12},{9,13},{10,... | collective-permute-start | bytes 196616 | tf_op jit(solution)/shard_map/ppermute | solution.py:63
  216.7 6.2 %collective-permute-start.29 = (f32[1,16,1024]{2,1,0:T(8,128)S(1)}, f32[1,16,1024]{2,1,0:T(8,128)S(1)}, u32[]{:S(2)}, u32[]{:S(2)}) collective-permute-start(f32[1,16,1024]{2,1,0:T(8,128)S(1)} %get-tuple-element.171), channel_id=1, source_target_pairs={{0,6},{1,7},{2,4},{3,5},{4,2},{5,3},{6,0},{7,1},{8,14},{9,15},{10,... | collective-permute-start | bytes 196616 | tf_op jit(solution)/shard_map/ppermute | solution.py:63
  239.6 5.4 %collective-permute-start.36 = (f32[8,128]{1,0:T(8,128)S(1)}, f32[8,128]{1,0:T(8,128)S(1)}, u32[]{:S(2)}, u32[]{:S(2)}) collective-permute-start(f32[8,128]{1,0:T(8,128)S(1)} %add.326), channel_id=1, source_target_pairs={{0,6},{1,7},{2,4},{3,5},{4,2},{5,3},{6,0},{7,1},{8,14},{9,15},{10,... | collective-permute-start | bytes 12296 | tf_op jit(solution)/shard_map/ppermute | solution.py:63
  265.4 12.4 %collective-permute-start.43 = (f32[664,128]{1,0:T(8,128)}, f32[664,128]{1,0:T(8,128)S(1)}, u32[]{:S(2)}, u32[]{:S(2)}) collective-permute-start(f32[664,128]{1,0:T(8,128)} %get-tuple-element.108), channel_id=1, source_target_pairs={{0,8},{8,0},{16,24},{24,16},{1,9},{9,1},{17,25},{25,17},{2,10},{10... | collective-permute-start | bytes 1019912 | tf_op jit(solution)/shard_map/ppermute | solution.py:63
  266.0 13.8 %collective-permute-start.44 = (f32[664,128]{1,0:T(8,128)}, f32[664,128]{1,0:T(8,128)S(1)}, u32[]{:S(2)}, u32[]{:S(2)}) collective-permute-start(f32[664,128]{1,0:T(8,128)} %get-tuple-element.108), channel_id=1, source_target_pairs={{0,16},{8,24},{16,0},{24,8},{1,17},{9,25},{17,1},{25,9},{2,18},{10... | collective-permute-start | bytes 1019912 | tf_op jit(solution)/shard_map/ppermute | solution.py:63
  267.5 13.0 %collective-permute-start.45 = (f32[664,128]{1,0:T(8,128)}, f32[664,128]{1,0:T(8,128)S(1)}, u32[]{:S(2)}, u32[]{:S(2)}) collective-permute-start(f32[664,128]{1,0:T(8,128)} %get-tuple-element.108), channel_id=1, source_target_pairs={{0,24},{8,16},{16,8},{24,0},{1,25},{9,17},{17,9},{25,1},{2,26},{10... | collective-permute-start | bytes 1019912 | tf_op jit(solution)/shard_map/ppermute | solution.py:63
  275.3 22.2 %collective-permute-start.51 = (f32[336,128]{1,0:T(8,128)S(1)}, f32[336,128]{1,0:T(8,128)S(1)}, u32[]{:S(2)}, u32[]{:S(2)}) collective-permute-start(f32[336,128]{1,0:T(8,128)S(1)} %add.343), channel_id=1, source_target_pairs={{0,2},{1,3},{2,0},{3,1},{4,6},{5,7},{6,4},{7,5},{8,10},{9,11},{10,... | collective-permute-start | bytes 516104 | tf_op jit(solution)/shard_map/ppermute | solution.py:63
  275.3 22.3 %collective-permute-start.52 = (f32[336,128]{1,0:T(8,128)S(1)}, f32[336,128]{1,0:T(8,128)S(1)}, u32[]{:S(2)}, u32[]{:S(2)}) collective-permute-start(f32[336,128]{1,0:T(8,128)S(1)} %add.343), channel_id=1, source_target_pairs={{0,4},{1,5},{2,6},{3,7},{4,0},{5,1},{6,2},{7,3},{8,12},{9,13},{10,... | collective-permute-start | bytes 516104 | tf_op jit(solution)/shard_map/ppermute | solution.py:63
  277.8 19.8 %collective-permute-start.53 = (f32[336,128]{1,0:T(8,128)S(1)}, f32[336,128]{1,0:T(8,128)S(1)}, u32[]{:S(2)}, u32[]{:S(2)}) collective-permute-start(f32[336,128]{1,0:T(8,128)S(1)} %add.343), channel_id=1, source_target_pairs={{0,6},{1,7},{2,4},{3,5},{4,2},{5,3},{6,0},{7,1},{8,14},{9,15},{10,... | collective-permute-start | bytes 516104 | tf_op jit(solution)/shard_map/ppermute | solution.py:63
  294.1 7.2 %collective-permute-start.40 = (f32[320,128]{1,0:T(8,128)}, f32[320,128]{1,0:T(8,128)S(1)}, u32[]{:S(2)}, u32[]{:S(2)}) collective-permute-start(f32[320,128]{1,0:T(8,128)} %shard_map.410), channel_id=1, source_target_pairs={{0,8},{8,0},{16,24},{24,16},{1,9},{9,1},{17,25},{25,17},{2,10},{10... | collective-permute-start | bytes 491528 | tf_op jit(solution)/shard_map/ppermute | solution.py:63
  296.1 10.8 %collective-permute-start.41 = (f32[320,128]{1,0:T(8,128)}, f32[320,128]{1,0:T(8,128)S(1)}, u32[]{:S(2)}, u32[]{:S(2)}) collective-permute-start(f32[320,128]{1,0:T(8,128)} %shard_map.410), channel_id=1, source_target_pairs={{0,16},{8,24},{16,0},{24,8},{1,17},{9,25},{17,1},{25,9},{2,18},{10... | collective-permute-start | bytes 491528 | tf_op jit(solution)/shard_map/ppermute | solution.py:63
  297.5 9.4 %collective-permute-start.42 = (f32[320,128]{1,0:T(8,128)}, f32[320,128]{1,0:T(8,128)S(1)}, u32[]{:S(2)}, u32[]{:S(2)}) collective-permute-start(f32[320,128]{1,0:T(8,128)} %shard_map.410), channel_id=1, source_target_pairs={{0,24},{8,16},{16,8},{24,0},{1,25},{9,17},{17,9},{25,1},{2,26},{10... | collective-permute-start | bytes 491528 | tf_op jit(solution)/shard_map/ppermute | solution.py:63
  297.7 18.0 %collective-permute-start.54 = (f32[336,128]{1,0:T(8,128)S(1)}, f32[336,128]{1,0:T(8,128)S(1)}, u32[]{:S(2)}, u32[]{:S(2)}) collective-permute-start(f32[336,128]{1,0:T(8,128)S(1)} %add_add_fusion.2), channel_id=1, source_target_pairs={{0,8},{8,0},{16,24},{24,16},{1,9},{9,1},{17,25},{25,17},{2,10},{10... | collective-permute-start | bytes 516104 | tf_op jit(solution)/shard_map/ppermute | solution.py:63
  299.7 17.1 %collective-permute-start.55 = (f32[336,128]{1,0:T(8,128)S(1)}, f32[336,128]{1,0:T(8,128)S(1)}, u32[]{:S(2)}, u32[]{:S(2)}) collective-permute-start(f32[336,128]{1,0:T(8,128)S(1)} %add_add_fusion.2), channel_id=1, source_target_pairs={{0,16},{8,24},{16,0},{24,8},{1,17},{9,25},{17,1},{25,9},{2,18},{10... | collective-permute-start | bytes 516104 | tf_op jit(solution)/shard_map/ppermute | solution.py:63
  301.3 15.4 %collective-permute-start.56 = (f32[336,128]{1,0:T(8,128)S(1)}, f32[336,128]{1,0:T(8,128)S(1)}, u32[]{:S(2)}, u32[]{:S(2)}) collective-permute-start(f32[336,128]{1,0:T(8,128)S(1)} %add_add_fusion.2), channel_id=1, source_target_pairs={{0,24},{8,16},{16,8},{24,0},{1,25},{9,17},{17,9},{25,1},{2,26},{10... | collective-permute-start | bytes 516104 | tf_op jit(solution)/shard_map/ppermute | solution.py:63
  315.7 5.4 %collective-permute-start.49 = (f32[8,128]{1,0:T(8,128)S(1)}, f32[8,128]{1,0:T(8,128)S(1)}, u32[]{:S(2)}, u32[]{:S(2)}) collective-permute-start(f32[8,128]{1,0:T(8,128)S(1)} %add.339), channel_id=1, source_target_pairs={{0,6},{1,7},{2,4},{3,5},{4,2},{5,3},{6,0},{7,1},{8,14},{9,15},{10,... | collective-permute-start | bytes 12296 | tf_op jit(solution)/shard_map/ppermute | solution.py:63
  (46 other events, 485.7 us)
Sparse Core Ops, SparseCore 0:
  254.9 32.0 all-gather.2

commit v2 on v1

v2 whole, which is shorter than its diff:
```python
import jax
import jax.numpy as jnp
from jax import lax
from jax.experimental import pallas as pl
from jax.experimental.pallas import tpu as pltpu
from jax.sharding import PartitionSpec as P

norm_epsilon = 0.001
zinb_epsilon = 1e-08
beta_one = 0.9
beta_two = 0.999
step_number = 5.0
decay_rate = 0.01
rate_genes = 0.03
rate_small = 0.2
max_norm = 0.1

F32 = jnp.float32
BF = jnp.bfloat16
HI = lax.Precision.HIGHEST
COUNT_TOP = 8
LOG2_E = 1.4426950408889634


def nn(left, right, precision=None):
    return lax.dot_general(
        left, right, (((1,), (0,)), ((), ())), precision=precision, preferred_element_type=F32
    )


def nt(left, right, precision=None):
    return lax.dot_general(
        left, right, (((1,), (1,)), ((), ())), precision=precision, preferred_element_type=F32
    )


def whole(shape):
    return pl.BlockSpec(shape, lambda *_: (0,) * len(shape))


def call(kernel, grid, ins, outs, scratch=(), scalars=0, flops=0, moved=0, mib=12):
    return pl.pallas_call(
        kernel,
        out_shape=[jax.ShapeDtypeStruct(shape, dtype) for shape, dtype, _ in outs],
        grid_spec=pltpu.PrefetchScalarGridSpec(
            num_scalar_prefetch=scalars,
            grid=grid,
            in_specs=[spec for _, spec in ins[scalars:]],
            out_specs=[spec for _, _, spec in outs],
            scratch_shapes=list(scratch),
        ),
        compiler_params=pltpu.CompilerParams(vmem_limit_bytes=mib * 1024 * 1024),
        cost_estimate=pl.CostEstimate(flops=flops, bytes_accessed=moved, transcendentals=0),
    )(*[array for array, _ in ins])


def swap(value, axis, bit):
    count = lax.axis_size(axis)
    return lax.ppermute(value, axis, [(i, i ^ bit) for i in range(count)])


def bit_groups(axis):
    count = lax.axis_size(axis)
    if axis == "genes":
        groups, bit = [[1]], 2
    else:
        groups, bit = [], 1
    while bit < count:
        groups.append([bit, 2 * bit] if 2 * bit < count else [bit])
        bit *= 4
    return groups


def total(value, axis):
    for group in bit_groups(axis):
        if len(group) == 1:
            value = value + swap(value, axis, group[0])
        else:
            low, high = group
            value = (value + swap(value, axis, low)) + (
                swap(value, axis, high) + swap(value, axis, low ^ high)
            )
    return value


def log_total_of(value, axis):
    for group in bit_groups(axis):
        if len(group) == 1:
            parts = [value, swap(value, axis, group[0])]
        else:
            low, high = group
            parts = [value] + [swap(value, axis, k) for k in (low, high, low ^ high)]
        top = parts[0]
        for part in parts[1:]:
            top = jnp.maximum(top, part)
        mass = sum(jnp.exp(part - top) for part in parts)
        value = top + jnp.log(mass)
    return value


def total_by_halves(value, axis, order):
    for bit in order:
        value = value + swap(value, axis, bit)
    return value


def after(value, *others):
    return lax.optimization_barrier((value,) + others)[0]


def three(value):
    high = value.astype(BF)
    rest = value - high.astype(F32)
    mid = rest.astype(BF)
    low = (rest - mid.astype(F32)).astype(BF)
    return high, mid, low


def one_hot(batch_row, kinds):
    ids = lax.broadcasted_iota(jnp.int32, (kinds, batch_row.shape[1]), 0)
    return jnp.where(ids == batch_row, 1.0, 0.0)


def columns(rows):
    return jnp.transpose(rows)


def prep_kernel(gene_ref, mask_ref, dec_ref, small_ref, head_ref, norm_ref, aug_ref, turn_ref, par_ref, lg_ref, dg_ref, enc_out, dec_out, lat_out, head_out, bias_out, cols_out, norm_out):
    genes = gene_ref.shape[1]
    hidden = norm_ref.shape[1]
    latent = head_ref.shape[0] // 2
    kinds = (small_ref.shape[0] - latent) // 2
    padded = pl.cdiv(genes, 128) * 128
    keep = mask_ref[...] > 0
    score_b = jnp.where(keep, gene_ref[0:1], -1e30)
    drop_b = jnp.where(keep, gene_ref[1:2], 1e30)
    th = jnp.exp(gene_ref[2:3])
    kept = jnp.where(keep, 1.0, 0.0)
    rows = jnp.concatenate((score_b, drop_b, th, kept, th, th, th, th), axis=0)
    if padded > genes:
        rows = jnp.concatenate((rows, jnp.ones((8, padded - genes), F32)), axis=1)
    turned = jnp.transpose(rows)[:genes]
    lane = lax.broadcasted_iota(jnp.int32, (genes, 16), 1)
    for half in range(2):
        at = slice(half * genes, (half + 1) * genes)
        aug_ref[at, 0:hidden] = dec_ref[half].astype(BF)
        high, mid, low = (jnp.broadcast_to(part.astype(F32), (genes, 16)) for part in three(turned[:, half : half + 1]))
        tail = jnp.where(lane == 0, high, jnp.where(lane == 1, mid, jnp.where(lane == 2, low, 0.0)))
        if half == 0:
            tail = jnp.where((lane >= 3) & (lane < 6), 1.0, tail)
        aug_ref[at, hidden : hidden + 16] = tail.astype(BF)
        turn_ref[:, at] = jnp.transpose(dec_ref[half]).astype(BF)
    th_w = jnp.broadcast_to(turned[:, 2:3], (genes, 128))
    keep_w = jnp.broadcast_to(turned[:, 3:4], (genes, 128))
    the_w = th_w + zinb_epsilon
    par_ref[0] = the_w
    par_ref[1] = th_w
    par_ref[2] = jnp.log(the_w)
    par_ref[3] = th_w / the_w
    par_ref[4] = keep_w
    gam = jnp.zeros_like(th_w)
    dig = jnp.zeros_like(th_w)
    for k in range(COUNT_TOP):
        more = th_w + float(k)
        gam = gam + keep_w * jnp.log(more * (1.0 / (1.0 + k)))
        dig = dig + keep_w / more
        lg_ref[k] = gam
        dg_ref[k] = dig
    for index, piece in enumerate(three(jnp.transpose(small_ref[0:kinds, :]))):
        enc_out[index * hidden : (index + 1) * hidden, :] = piece
    row = lax.broadcasted_iota(jnp.int32, (16, hidden), 0)
    lat_row = jnp.zeros((16, hidden), F32)
    for index in range(latent):
        lat_row = jnp.where(row == index, small_ref[2 * kinds + index : 2 * kinds + index + 1, :], lat_row)
    lat_out[...] = lat_row
    batch_pieces = three(jnp.transpose(small_ref[kinds : 2 * kinds, :]))
    lat = three(jnp.transpose(lat_row))
    zero = jnp.zeros_like(lat[0])
    tails = ((lat[0], lat[0], lat[0]), (lat[1], lat[1], zero), (lat[2], zero, zero))
    for index in range(3):
        at = slice(index * hidden, (index + 1) * hidden)
        dec_out[at, :] = jnp.concatenate((batch_pieces[index],) + tails[index], axis=1)
    full = lax.broadcasted_iota(jnp.int32, (32, hidden), 0)
    head = jnp.zeros((32, hidden), F32)
    bias = jnp.zeros((32, 1), F32)
    for index in range(2 * latent):
        to = index if index < latent else index - latent + 16
        head = jnp.where(full == to, head_ref[index : index + 1, 0:hidden], head)
        bias = jnp.where(full[:, 0:1] == to, head_ref[index : index + 1, hidden : hidden + 1], bias)
    head_out[...] = head
    bias_out[...] = jnp.broadcast_to(bias, (32, 128))
    high, mid, _ = three(jnp.transpose(head))
    cols_out[0:hidden, :] = jnp.concatenate((high, high), axis=1)
    cols_out[hidden : 2 * hidden, :] = jnp.concatenate((mid, jnp.zeros_like(mid)), axis=1)
    norm_out[...] = jnp.transpose(jnp.concatenate((norm_ref[...], norm_ref[...]), axis=0))


def exact_rows(stacked, table):
    out = nn(stacked, table)
    hidden = out.shape[0] // 3
    return out[:hidden] + out[hidden : 2 * hidden] + out[2 * hidden :]


def dec_table(z, batch_row, kinds):
    high, mid, low = three(z)
    return jnp.concatenate((one_hot(batch_row, kinds).astype(BF), high, mid, low), axis=0)


def row_sums(value):
    return nt(jnp.ones((8, value.shape[1]), F32), value, HI)


def stat_rows(first, second, at):
    sums, squares = row_sums(first), row_sums(second)
    row = lax.broadcasted_iota(jnp.int32, sums.shape, 0)
    return jnp.where(row == at, sums, jnp.where(row == at + 1, squares, 0.0))


def enc_kernel(me_ref, x_ref, w_ref, keep_ref, send_ref, turn_ref):
    step = pl.program_id(0)

    @pl.when(step == 0)
    def _():
        turn_ref[...] = jnp.transpose(w_ref[...]).astype(BF)

    log_counts = jnp.log(1.0 + x_ref[...].astype(F32)).astype(BF)
    part = nn(turn_ref[...], log_counts)
    odd = lax.rem(step, 2)

    @pl.when(odd == 0)
    def _():
        keep_ref[0] = part

    @pl.when(odd == 1)
    def _():
        send_ref[0] = part.astype(BF)


def lines(rows8, count):
    wide = rows8.shape[1]
    if wide < 128 * count:
        rows8 = jnp.concatenate((rows8, jnp.zeros((8, 128 * count - wide), F32)), axis=1)
    return jnp.concatenate([rows8[:, i * 128 : (i + 1) * 128] for i in range(count)], axis=0)


def counts_kernel(rows, span, x_ref, lg_ref, dg_ref, keep_ref, logc_ref, mask_ref, cell_ref, disp_ref, line_ref, sum_ref):
    step = pl.program_id(0)
    genes, width = x_ref.shape

    @pl.when(step == 0)
    def _():
        disp_ref[...] = jnp.zeros_like(disp_ref)
        sum_ref[...] = jnp.zeros_like(sum_ref)

    tiles = span // 128
    done = []
    for first in range(0, width, span):
        lanes = [slice(first + tile * 128, first + (tile + 1) * 128) for tile in range(tiles)]

        def chunk(g, cell):
            at = pl.ds(pl.multiple_of(g * rows, rows), rows)
            keep = keep_ref[at, :]
            xs = [x_ref[at, lanes[tile]].astype(F32) for tile in range(tiles)]
            logs = [jnp.log(1.0 + x) for x in xs]
            for tile in range(tiles):
                logc_ref[at, lanes[tile]] = logs[tile].astype(BF)
                mask_ref[at, lanes[tile]] = (xs[tile] * keep).astype(BF)
            sum_ref[at, :] += sum(part.astype(BF).astype(F32) for part in logs)
            gams = [jnp.zeros_like(xs[0]) for _ in range(tiles)]
            digs = [jnp.zeros_like(xs[0]) for _ in range(tiles)]
            for k in range(COUNT_TOP):
                lg, dg = lg_ref[k, at, :], dg_ref[k, at, :]
                for tile in range(tiles):
                    more = xs[tile] > (k + 0.5)
                    gams[tile] = jnp.where(more, lg, gams[tile])
                    digs[tile] = jnp.where(more, dg, digs[tile])
            disp_ref[at, :] += sum(digs)
            out = []
            for tile in range(tiles):
                folded = cell[tile]
                for part in range(rows // 8):
                    folded = folded + gams[tile][part * 8 : (part + 1) * 8]
                out.append(folded)
            return tuple(out)

        zero = tuple(jnp.zeros((8, 128), F32) for _ in range(tiles))
        done += list(lax.fori_loop(0, genes // rows, chunk, zero))
    cell_ref[pl.ds(step, 1), :] = jnp.sum(jnp.concatenate(done, axis=1), axis=0, keepdims=True)

    @pl.when(step == pl.num_programs(0) - 1)
    def _():
        line_ref[...] = lines(row_sums(sum_ref[...]), line_ref.shape[0] // 8)


def own_kernel(me_ref, keep_ref, got_ref, one_ref, two_ref, six_ref, batch_ref, enc_b_ref, pre_ref, stat_ref):
    kinds = enc_b_ref.shape[1]
    gathered = (keep_ref[0] + got_ref[0].astype(F32) + one_ref[0].astype(F32)) + (
        two_ref[0].astype(F32) + six_ref[0].astype(F32)
    )
    table = one_hot(batch_ref[0], kinds).astype(BF)
    pre = gathered + exact_rows(enc_b_ref[...], table)
    pre_ref[...] = pre
    stat_ref[...] = stat_rows(pre, pre * pre, 0)


def norm_columns(stat, first, cells):
    turned = jnp.transpose(stat)
    mean = turned[:, first : first + 1] / cells
    var = turned[:, first + 1 : first + 2] / cells - mean * mean
    return mean, lax.rsqrt(var + norm_epsilon)


def norm_rows(stat, first, cells):
    mean = stat[first : first + 1] / cells
    var = stat[first + 1 : first + 2] / cells - mean * mean
    return mean, lax.rsqrt(var + norm_epsilon)


def latent_kernel(cells, latent, me_ref, pre_ref, stat_ref, norm_ref, head_ref, bias_ref, noise_ref, batch_ref, dec_b_ref, pack_ref, aff_ref, kl_ref):
    kinds = dec_b_ref.shape[1] - 48
    mean, inv = norm_columns(stat_ref[...], 0, cells)
    phat = (pre_ref[...] - mean) * inv
    affine = norm_ref[:, 0:1] * phat + norm_ref[:, 1:2]
    aff_ref[...] = affine.astype(BF)
    out = nn(head_ref[...], jnp.maximum(affine, 0.0), HI) + bias_ref[:, 0:1]
    lat_mean, lat_logvar = out[:latent], out[16 : 16 + latent]
    var = jnp.exp(lat_logvar) + 0.0001
    z = lat_mean + jnp.sqrt(var) * noise_ref[...]
    terms = var + lat_mean * lat_mean - 1.0 - jnp.log(var)
    kl_ref[...] = 0.5 * jnp.sum(terms, axis=0, keepdims=True)
    pre_dec = exact_rows(dec_b_ref[...], dec_table(latent_rows(z), batch_ref[0], kinds))
    hidden = pre_dec.shape[0]
    stat = stat_rows(pre_dec, pre_dec * pre_dec, 0)
    pack_ref[0:latent, :] = lat_mean
    pack_ref[latent : latent + 6, :] = jnp.zeros((6, z.shape[1]), F32)
    pack_ref[latent : latent + 1, 0:hidden] = stat[0:1]
    pack_ref[latent + 1 : latent + 2, 0:hidden] = stat[1:2]
    pack_ref[16 : 16 + latent, :] = lat_logvar
    pack_ref[16 + latent : 32, :] = jnp.zeros((16 - latent, z.shape[1]), F32)


def latent_rows(z):
    if z.shape[0] == 16:
        return z
    return jnp.concatenate((z, jnp.zeros((16 - z.shape[0], z.shape[1]), F32)), axis=0)


def draw(latent, pack, noise):
    lat_mean, lat_logvar = pack[0:latent], pack[16 : 16 + latent]
    return lat_mean, lat_logvar, lat_mean + jnp.sqrt(jnp.exp(lat_logvar) + 0.0001) * noise


def pick(step, me_ref, fast, near_ref, far_ref):
    if not fast:
        return near_ref[0]
    return jnp.where(lax.rem(step ^ me_ref[0], 2) == 0, near_ref[0], far_ref[0])


def decode_kernel(cells, latent, fast, me_ref, near_ref, far_ref, noise_ref, batch_ref, stat_ref, norm_ref, dec_b_ref, w_ref, hid_ref, phat_ref, lse_ref, z_ref, score_ref):
    kinds = dec_b_ref.shape[1] - 48
    step = pl.program_id(0)
    genes = score_ref.shape[0]
    mean, inv = norm_columns(stat_ref[...], latent - 8, cells)
    _, _, z = draw(latent, pick(step, me_ref, fast, near_ref, far_ref), noise_ref[...])
    z = latent_rows(z)
    z_ref[...] = z
    pre_dec = exact_rows(dec_b_ref[...], dec_table(z, batch_ref[0], kinds))
    phat = (pre_dec - mean) * inv
    phat_ref[...] = phat
    hidden = jnp.maximum(norm_ref[:, 2:3] * phat + norm_ref[:, 3:4], 0.0).astype(BF)
    hid_ref[...] = hidden
    width = score_ref.shape[1]
    row = lax.broadcasted_iota(jnp.int32, (16, width), 0)
    table = jnp.concatenate((hidden, jnp.where(row < 3, 1.0, 0.0).astype(BF)), axis=0)
    score_ref[...] = nn(w_ref[...], table)
    tiles = width // 128
    rows = 32

    def top(g, best):
        at = pl.ds(pl.multiple_of(g * rows, rows), rows)
        new = []
        for tile in range(tiles):
            value = score_ref[at, slice(tile * 128, (tile + 1) * 128)]
            part = best[tile]
            for index in range(rows // 8):
                part = jnp.maximum(part, value[index * 8 : (index + 1) * 8])
            new.append(part)
        return tuple(new)

    best = lax.fori_loop(0, genes // rows, top, tuple(jnp.full((8, 128), -3e38, F32) for _ in range(tiles)))
    high = [jnp.max(part, axis=0, keepdims=True) for part in best]
    wide = [jnp.broadcast_to(part, (8, 128)) for part in high]

    def mass(g, sums):
        at = pl.ds(pl.multiple_of(g * rows, rows), rows)
        new = []
        for tile in range(tiles):
            value = score_ref[at, slice(tile * 128, (tile + 1) * 128)]
            part = sums[tile]
            for index in range(rows // 8):
                part = part + jnp.exp(value[index * 8 : (index + 1) * 8] - wide[tile])
            new.append(part)
        return tuple(new)

    sums = lax.fori_loop(0, genes // rows, mass, tuple(jnp.zeros((8, 128), F32) for _ in range(tiles)))
    lse = [high[tile] + jnp.log(jnp.sum(sums[tile], axis=0, keepdims=True)) for tile in range(tiles)]
    lse_ref[pl.ds(step, 1), :] = jnp.concatenate(lse, axis=1)


def enc_sums_kernel(fast, me_ref, logc_ref, near_ref, far_ref, batch_ref, lines_ref, out_ref):
    step = pl.program_id(0)
    genes = logc_ref.shape[0]
    kinds = out_ref.shape[0] - genes - lines_ref.shape[0] - 8

    @pl.when(step == 0)
    def _():
        out_ref[...] = jnp.zeros_like(out_ref)
        out_ref[genes + kinds : genes + kinds + lines_ref.shape[0], :] = lines_ref[...]

    affine = pick(step, me_ref, fast, near_ref, far_ref)
    table = one_hot(batch_ref[0], kinds)
    out_ref[0:genes, :] += nt(logc_ref[...], affine)
    out_ref[genes : genes + kinds, :] += nt(table.astype(BF), affine)
    out_ref[genes + kinds + lines_ref.shape[0] :, :] += row_sums(table)


def zinb_kernel(rows, span, hid_ref, w_ref, x_ref, par_ref, lib_ref, lse_ref, gam_ref, gm_ref, gd_ref, rt_ref, mass_ref, recon_ref, acc_ref, sc_ref):
    step = pl.program_id(0)
    genes, width = x_ref.shape

    @pl.when(step == 0)
    def _():
        acc_ref[...] = jnp.zeros_like(acc_ref)

    one_row = pl.ds(step, 1)
    gam_row = gam_ref[one_row, :]
    shift = lib_ref[one_row, :] - lse_ref[one_row, :]
    row = lax.broadcasted_iota(jnp.int32, (16, width), 0)
    hi, mid, lo = three(shift)
    extra = jnp.where(row < 3, 1.0, jnp.where(row == 3, hi.astype(F32), jnp.where(row == 4, mid.astype(F32), jnp.where(row == 5, lo.astype(F32), 0.0))))
    table = jnp.concatenate((hid_ref[...], extra.astype(BF)), axis=0)
    sc_ref[...] = nn(w_ref[...], table)
    tiles = span // 128
    mass_out, recon_out = [], []
    for first in range(0, width, span):
        lanes = [slice(first + tile * 128, first + (tile + 1) * 128) for tile in range(tiles)]
        def chunk(g, state):
            at = pl.ds(pl.multiple_of(g * rows, rows), rows)
            at_drop = pl.ds(pl.multiple_of(genes + g * rows, rows), rows)
            the, th, log_the, part_th = (par_ref[i, at, :] for i in range(4))
            sums = [acc_ref[i, at, :] for i in range(3)]
            new = []
            for tile in range(tiles):
                rec, prod, back = state[tile]
                x = x_ref[at, lanes[tile]].astype(F32)
                mu = jnp.exp(sc_ref[at, lanes[tile]])
                drop = sc_ref[at_drop, lanes[tile]]
                both = mu + the
                r = 1.0 / both
                log_both = jnp.log(both)
                gap = log_the - log_both
                th_gap = th * gap
                u = jnp.where(x < 0.5, th_gap - drop, 1e30)
                eu = jnp.exp2(jnp.abs(u) * (-LOG2_E))
                ed = jnp.exp2(jnp.abs(drop) * (-LOG2_E))
                den = 1.0 + eu
                mu_eps = mu + zinb_epsilon
                rd = 1.0 / (1.0 + ed)
                w0 = jnp.where(u >= 0.0, 1.0, eu) * (1.0 / den)
                term = (th_gap - jnp.maximum(drop, 0.0)) + (x * (jnp.log(mu_eps) - log_both) - jnp.minimum(u, 0.0))
                factor = den * rd
                y = (x + w0 * th) * r
                g_mean = mu * (x * (1.0 / mu_eps) - y)
                g_drop = jnp.where(drop >= 0.0, ed, 1.0) * rd - w0
                g_disp = w0 * (gap + part_th) - y
                gm_ref[at, lanes[tile]] = g_mean.astype(BF)
                gd_ref[at, lanes[tile]] = g_drop.astype(BF)
                rt_ref[at, lanes[tile]] = mu.astype(BF)
                sums = [a + b for a, b in zip(sums, (g_mean, g_drop, g_disp))]
                for part in range(rows // 8):
                    sub = slice(part * 8, (part + 1) * 8)
                    rec = rec + term[sub]
                    prod = prod * factor[sub]
                    back = back + g_mean[sub]
                new.append((rec, prod, back))
            for i in range(3):
                acc_ref[i, at, :] = sums[i]
            return tuple(new)
        zero = jnp.zeros((8, 128), F32)
        state = tuple((zero, zero + 1.0, zero) for _ in range(tiles))
        state = lax.fori_loop(0, genes // rows, chunk, state)
        for tile in range(tiles):
            rec, prod, back = state[tile]
            mass_out.append(jnp.sum(back, axis=0, keepdims=True))
            recon_out.append(jnp.sum(rec + jnp.log(prod), axis=0, keepdims=True))
    mass_ref[one_row, :] = jnp.concatenate(mass_out, axis=1)
    recon_ref[one_row, :] = jnp.concatenate(recon_out, axis=1) + gam_row


def back_kernel(gm_ref, gd_ref, rt_ref, hid_ref, w_ref, a_ref, r_ref, g_ref):
    genes = gm_ref.shape[0]

    @pl.when(pl.program_id(0) == 0)
    def _():
        g_ref[...] = jnp.zeros_like(g_ref)

    gm, gd, rt, hid = gm_ref[...], gd_ref[...], rt_ref[...], hid_ref[...]
    scale_w = w_ref[:, :genes]
    a_ref[...] = nn(scale_w, gm) + nn(w_ref[:, genes:], gd)
    r_ref[...] = nn(scale_w, rt)
    g_ref[:genes, :] += nt(gm, hid)
    g_ref[genes:, :] += nt(gd, hid)


def hidden_grad_kernel(cells, latent, me_ref, a_ref, r_ref, mass_ref, hid_ref, phat_ref, lib_ref, stat_ref, gain_ref, lat_ref, recon_ref, dy_ref, keep_ref, send_ref, sum_ref):
    step = pl.program_id(0)
    steps = pl.num_programs(0)
    place = step ^ me_ref[0]

    @pl.when(step == 0)
    def _():
        sum_ref[...] = jnp.zeros_like(sum_ref)

    back = mass_ref[pl.ds(step, 1), :] * jnp.exp(-lib_ref[pl.ds(step, 1), :])
    dy = jnp.where(hid_ref[...] > 0, (a_ref[...] - back * r_ref[...]) * (-1.0 / cells), 0.0)
    dy_ref[...] = dy
    hidden, width = dy.shape
    weighted = dy * phat_ref[...]
    first, second = dy[:, :128], weighted[:, :128]
    for tile in range(1, width // 128):
        lanes = slice(tile * 128, (tile + 1) * 128)
        first = first + dy[:, lanes]
        second = second + weighted[:, lanes]
    sum_ref[0] += first
    sum_ref[1] += second
    _, inv = norm_rows(stat_ref[...], latent - 8, cells)
    lat = lat_ref[...] * (gain_ref[2:3] * inv)
    lat_high, lat_mid, _ = three(lat)
    dy_high, dy_mid, _ = three(dy)
    table = jnp.concatenate((dy_high, dy_mid), axis=0)
    left = jnp.concatenate(
        (
            jnp.concatenate((lat_high, lat_high), axis=1),
            jnp.concatenate((lat_mid, jnp.zeros_like(lat_mid)), axis=1),
        ),
        axis=0,
    )
    both = nn(left, table)
    block = both[:16] + both[16:]
    row = lax.broadcasted_iota(jnp.int32, block.shape, 0)
    block = jnp.where(row == latent, recon_ref[pl.ds(step, 1), :], block)
    slot = lax.div(place, 2)

    @pl.when(lax.rem(place, 2) == 0)
    def _():
        keep_ref[slot] = block

    @pl.when(lax.rem(place, 2) == 1)
    def _():
        send_ref[slot] = block

    @pl.when(step == steps - 1)
    def _():
        one, two = row_sums(sum_ref[0]), row_sums(sum_ref[1])
        for ref in (keep_ref, send_ref):
            for index in range(ref.shape[0]):
                ref[index, latent + 1 : latent + 2, 0:hidden] = one[0:1]
                ref[index, latent + 2 : latent + 3, 0:hidden] = two[0:1]


def dec_grad_kernel(cells, rt_ref, hid_ref, mass_ref, lib_ref, dy_ref, z_ref, batch_ref, g_ref, acc_ref, dig_ref, th_ref, dec_ref, oh_ref, mix_ref):
    step = pl.program_id(0)
    steps = pl.num_programs(0)
    genes = rt_ref.shape[0]
    hidden = hid_ref.shape[0]
    kinds = oh_ref.shape[0] - 16

    @pl.when(step == 0)
    def _():
        mix_ref[...] = jnp.zeros_like(mix_ref)
        oh_ref[...] = jnp.zeros_like(oh_ref)

    back = mass_ref[pl.ds(step, 1), :] * jnp.exp(-lib_ref[pl.ds(step, 1), :])
    back_high, back_mid, back_low = three(back)
    row = lax.broadcasted_iota(jnp.int32, (16, back.shape[1]), 0)
    extra = jnp.where(row == 0, back_high.astype(F32), jnp.where(row == 1, back_mid.astype(F32), 0.0))
    scaled = (hid_ref[...].astype(F32) * back).astype(BF)
    mix_ref[...] += nt(rt_ref[...], jnp.concatenate((scaled, extra.astype(BF)), axis=0))
    z_high, z_mid, _ = three(z_ref[...])
    left = jnp.concatenate((one_hot(batch_ref[0], kinds).astype(BF), z_high, z_mid), axis=0)
    dy_high, dy_mid, _ = three(dy_ref[...])
    part = nt(left, dy_high) + nt(left, dy_mid)
    oh_ref[:kinds, :] += part[:kinds]
    oh_ref[kinds:, :] += part[kinds : kinds + 16] + part[kinds + 16 :]

    @pl.when(step == steps - 1)
    def _():
        scale = -1.0 / cells
        mix = mix_ref[...]
        dec_ref[:genes, :] = (g_ref[:genes, :] - mix[:, :hidden]) * scale
        dec_ref[genes : 2 * genes, :] = g_ref[genes:, :] * scale
        pick = jnp.where(lax.broadcasted_iota(jnp.int32, (8, 16), 1) < 2, 1.0, 0.0)
        score_row = row_sums(acc_ref[0]) - nt(pick, mix[:, hidden:], HI)
        drop_row = row_sums(acc_ref[1])
        disp_row = row_sums((acc_ref[2] + dig_ref[...]) * th_ref[...])
        line = lax.broadcasted_iota(jnp.int32, score_row.shape, 0)
        gene_rows = scale * jnp.where(
            line == 0, score_row, jnp.where(line == 1, drop_row, jnp.where(line == 2, disp_row, 0.0))
        )
        dec_ref[2 * genes :, :] = lines(gene_rows, pl.cdiv(genes, 128))


def enc_back_kernel(cells, latent, fast, me_ref, dnear_ref, dfar_ref, phat_ref, sums_ref, stat_ref, gain_ref, lat_ref, near_ref, far_ref, noise_ref, klw_ref, anear_ref, afar_ref, batch_ref, logc_ref, cols_ref, z_ref, enc_ref, rest_ref, lane_ref):
    step = pl.program_id(0)
    genes, width = logc_ref.shape
    hidden = phat_ref.shape[0]
    kinds = (rest_ref.shape[0] - 32 - 16 - 16) // 2

    @pl.when(step == 0)
    def _():
        enc_ref[...] = jnp.zeros_like(enc_ref)
        rest_ref[...] = jnp.zeros_like(rest_ref)
        lane_ref[...] = jnp.zeros_like(lane_ref)

    block = pick(step, me_ref, fast, dnear_ref, dfar_ref)
    _, inv = norm_rows(stat_ref[...], latent - 8, cells)
    scaled = gain_ref[2:3] * inv
    lat = lat_ref[...] * scaled
    at = latent + 1 - 8
    m_one = sums_ref[at : at + 1] * (1.0 / cells)
    m_two = sums_ref[at + 1 : at + 2] * (1.0 / cells)
    fixed = jnp.sum(lat * m_one, axis=1, keepdims=True)
    left_high, left_mid, _ = three(lat * m_two)
    phat_high, phat_mid, _ = three(phat_ref[...])
    both = nn(
        jnp.concatenate(
            (
                jnp.concatenate((left_high, left_high), axis=1),
                jnp.concatenate((left_mid, jnp.zeros_like(left_mid)), axis=1),
            ),
            axis=0,
        ),
        jnp.concatenate((phat_high, phat_mid), axis=0),
    )
    grad_z = (block - fixed - (both[:16] + both[16:]))[:latent]
    noise = noise_ref[...]
    lat_mean, lat_logvar, _ = draw(latent, pick(step, me_ref, fast, near_ref, far_ref), noise)
    spread = jnp.exp(lat_logvar)
    var = spread + 0.0001
    scale = klw_ref[0:1, 0:1] * (1.0 / cells)
    g_mean = latent_rows(grad_z + scale * lat_mean)
    g_var = latent_rows(
        grad_z * noise * 0.5 * spread * lax.rsqrt(var) + scale * 0.5 * (spread - spread / var)
    )
    g_head = jnp.concatenate((g_mean, g_var), axis=0)
    head_high, head_mid, _ = three(g_head)
    spread_out = nn(cols_ref[...], jnp.concatenate((head_high, head_mid), axis=0))
    affine = pick(step, me_ref, fast, anear_ref, afar_ref)
    wide = affine.astype(F32)
    dy = jnp.where(wide > 0, spread_out[:hidden] + spread_out[hidden:], 0.0)
    weighted = dy * wide
    first, second = dy[:, :128], weighted[:, :128]
    for tile in range(1, width // 128):
        lanes = slice(tile * 128, (tile + 1) * 128)
        first = first + dy[:, lanes]
        second = second + weighted[:, lanes]
    lane_ref[0] += first
    lane_ref[1] += second
    dy_low = dy.astype(BF)
    table = one_hot(batch_ref[0], kinds)
    hidden_low = jnp.maximum(wide, 0.0).astype(BF)
    enc_ref[...] += nt(logc_ref[...], dy_low)
    rest_ref[0:kinds, :] += nt(table.astype(BF), dy_low)
    rest_ref[kinds : kinds + 32, :] += nt(head_high, hidden_low) + nt(head_mid, hidden_low)
    base = kinds + 32
    z_high, z_mid, _ = three(z_ref[...])
    left = jnp.concatenate((table.astype(BF), z_high, z_mid), axis=0)
    part = nt(left, phat_high) + nt(left, phat_mid)
    held = jnp.sum(jnp.concatenate((table, z_ref[...]), axis=0), axis=1, keepdims=True)
    product = jnp.concatenate((part[:kinds], part[kinds : kinds + 16] + part[kinds + 16 :]), axis=0)
    rest_ref[base + 16 :, :] -= held * m_one + product * m_two
    bias = row_sums(g_head)
    rest_ref[base + 8 : base + 16, 0:32] += bias

    @pl.when(step == pl.num_programs(0) - 1)
    def _():
        one, two = row_sums(lane_ref[0]), row_sums(lane_ref[1])
        row = lax.broadcasted_iota(jnp.int32, one.shape, 0)
        rest_ref[base : base + 8, :] = jnp.where(row == 0, one, jnp.where(row == 1, two, 0.0))


def finish_kernel(cells, latent, enc_ref, rest_ref, dec_ref, fixed_ref, stat_enc_ref, stat_dec_ref, sums_ref, norm_ref, kl_ref, klw_ref, own_ref, enc_out, small_out, head_out, norm_out, square_out, loss_out):
    genes, hidden = enc_ref.shape
    kinds = (rest_ref.shape[0] - 32 - 16 - 16) // 2
    count = pl.cdiv(genes, 128)
    loss_out[...] = klw_ref[0:1, 0:1] * kl_ref[...] - own_ref[latent : latent + 1, :]
    gain, shift = norm_ref[0:1], norm_ref[1:2]
    _, inv = norm_rows(stat_enc_ref[...], 0, cells)
    base = kinds + 32
    n_one = rest_ref[base : base + 1]
    n_two = (rest_ref[base + 1 : base + 2] - shift * n_one) / gain
    one, two = n_one * (1.0 / cells), n_two * (1.0 / cells)
    lines_at = genes + kinds
    logs = jnp.concatenate([fixed_ref[lines_at + 8 * i : lines_at + 8 * (i + 1), :] for i in range(count)], axis=1)
    log_sum = jnp.transpose(logs)[:genes, 0:1]
    batch_sum = jnp.transpose(fixed_ref[lines_at + 8 * count : lines_at + 8 * count + 8, :])[:kinds, 0:1]

    def whole_gradient(part, product, plain):
        return (gain * inv) * (part - plain * one - ((product - plain * shift) / gain) * two)

    enc = whole_gradient(enc_ref[...], fixed_ref[0:genes, :], log_sum)
    enc_out[...] = enc
    dec = dec_ref[...]
    lane = jnp.sum(enc * enc, axis=0, keepdims=True) + jnp.sum(dec * dec, axis=0, keepdims=True)
    square_out[...] = jnp.broadcast_to(jnp.sum(lane, axis=1, keepdims=True), square_out.shape)
    small_out[0:kinds, :] = whole_gradient(rest_ref[0:kinds, :], fixed_ref[genes : genes + kinds, :], batch_sum)
    _, inv_dec = norm_rows(stat_dec_ref[...], latent - 8, cells)
    small_out[kinds:, :] = (norm_ref[2:3] * inv_dec) * rest_ref[base + 16 :, :]
    bias = jnp.transpose(rest_ref[base + 8 : base + 16, :])
    for half in range(2):
        rows = slice(half * latent, (half + 1) * latent)
        head_out[rows, 0:hidden] = rest_ref[kinds + 16 * half : kinds + 16 * half + latent, :]
        head_out[rows, hidden : hidden + 1] = bias[16 * half : 16 * half + latent, 0:1]
    at = latent + 1 - 8
    norm_out[0:1] = n_two
    norm_out[1:2] = n_one
    norm_out[2:3] = sums_ref[at + 1 : at + 2]
    norm_out[3:4] = sums_ref[at : at + 1]


def step_of(weight, gradient, first, second, rate):
    first = beta_one * first + (1.0 - beta_one) * gradient
    second = beta_two * second + (1.0 - beta_two) * gradient * gradient
    fixed_one = first * (1.0 / (1.0 - beta_one**step_number))
    fixed_two = second * (1.0 / (1.0 - beta_two**step_number))
    update = fixed_one / (jnp.sqrt(fixed_two) + 1e-08) + decay_rate * weight
    return weight - rate * update, first, second


def update_kernel(latent, square_ref, enc_g_ref, dec_g_ref, small_g_ref, head_g_ref, norm_g_ref, *refs):
    ins, outs = refs[:18], refs[18:]
    enc, dec, gene, small, head, norm = (ins[3 * i : 3 * i + 3] for i in range(6))
    genes = enc[0].shape[0]
    rows = small[0].shape[0]
    small_square = jnp.zeros((1, 1), F32)
    for part in (small_g_ref[0:rows, :], head_g_ref[...], norm_g_ref[...]):
        small_square = small_square + jnp.sum(jnp.sum(part * part, axis=0, keepdims=True), axis=1, keepdims=True)
    value = jnp.sqrt(square_ref[0:1, 0:1] + small_square)
    factor = jnp.minimum(1.0, max_norm / value)
    (enc_n, enc_m, enc_v, enc_l, dec_n, dec_m, dec_v, dec_l, gene_n, gene_m, gene_v, small_n, small_m, small_v, head_n, head_m, head_v, norm_n, norm_m, norm_v, norm_out) = outs
    norm_out[...] = jnp.broadcast_to(value, norm_out.shape)
    new, first, second = step_of(enc[0][...], enc_g_ref[...] * factor, enc[1][...], enc[2][...], rate_genes)
    enc_n[...], enc_m[...], enc_v[...], enc_l[...] = new, first, second, new.astype(BF)
    for index in range(2):
        gradient = dec_g_ref[index * genes : (index + 1) * genes, :] * factor
        new, first, second = step_of(dec[0][index], gradient, dec[1][index], dec[2][index], rate_genes)
        dec_n[index], dec_m[index], dec_v[index], dec_l[index] = new, first, second, new.astype(BF)
    for index in range(pl.cdiv(genes, 128)):
        span = slice(index * 128, min(genes, (index + 1) * 128))
        gradient = dec_g_ref[2 * genes + index * 8 : 2 * genes + index * 8 + 3, 0 : span.stop - span.start] * factor
        new, first, second = step_of(gene[0][:, span], gradient, gene[1][:, span], gene[2][:, span], rate_small)
        gene_n[:, span], gene_m[:, span], gene_v[:, span] = new, first, second
    new, first, second = step_of(small[0][...], small_g_ref[0:rows, :] * factor, small[1][...], small[2][...], rate_small)
    small_n[...], small_m[...], small_v[...] = new, first, second
    new, first, second = step_of(head[0][...], head_g_ref[...] * factor, head[1][...], head[2][...], rate_small)
    head_n[...], head_m[...], head_v[...] = new, first, second
    new, first, second = step_of(norm[0][...], norm_g_ref[...] * factor, norm[1][...], norm[2][...], rate_small)
    norm_n[...], norm_m[...], norm_v[...] = new, first, second


def gather_genes(value, fast, blocks, width):
    if fast:
        near = jnp.stack([value] + [swap(value, "genes", 2 * k) for k in (1, 2, 3)])
        return near, swap(near, "genes", 1)
    rows = value.shape[0]
    whole_rows = lax.all_gather(value, "genes", axis=0).transpose(1, 0, 2)
    near = whole_rows.reshape(rows, blocks, width).transpose(1, 0, 2)
    return near, near


def per_device(counts, library, noise, batch_ids, gene_mask, kl_weight, enc_w, enc_m, enc_v, dec_w, dec_m, dec_v, gene_par, gene_m, gene_v, small_w, small_m, small_v, head_w, head_m, head_v, norm_par, norm_m, norm_v):
    rows_all, genes = counts.shape
    cells = float(rows_all * lax.axis_size("cells"))
    groups = lax.axis_size("genes")
    hidden = enc_w.shape[1]
    latent = head_w.shape[1] // 2
    kinds = (small_w.shape[0] - latent) // 2
    share = rows_all // groups
    width = min(1024, rows_all)
    blocks = rows_all // width
    fast = groups == 8 and blocks == 8
    me = lax.axis_index("genes").astype(jnp.int32).reshape(1)
    gene_lines = -(-genes // 128)

    def turn(value):
        return value.transpose(0, 2, 1)

    x_t = counts.T
    noise_t = noise.T
    dec_t = turn(dec_w)
    head_t = head_w.T
    lib8 = library.reshape(blocks, width)
    batch_all = batch_ids.reshape(blocks, 1, width)
    batch_own = batch_ids.reshape(groups, 1, share)
    klw = jnp.broadcast_to(kl_weight.reshape(1, 1), (8, 128))

    own_block = pl.BlockSpec((1, 1, share), lambda i, m: (m[0], 0, 0))
    own_lanes = lambda rows: pl.BlockSpec((rows, share), lambda i, m: (0, m[0]))
    lane_block = lambda rows: pl.BlockSpec((rows, width), lambda i, *_: (0, i))
    full = lambda array: (array, whole(array.shape))
    new = lambda shape, dtype=F32: (shape, dtype, whole(shape))
    if fast:
        from_all = lambda rows: pl.BlockSpec((1, rows, width), lambda i, m: ((i ^ m[0]) // 2, 0, 0))
    else:
        from_all = lambda rows: pl.BlockSpec((1, rows, width), lambda i, m: (i, 0, 0))

    keep_part, send_part = call(
        enc_kernel,
        (groups,),
        [
            (me if fast else me & 1, None),
            (x_t, pl.BlockSpec((genes, share), lambda i, m: (0, i ^ m[0]))),
            full(enc_w),
        ],
        [
            ((groups // 2, hidden, share), F32, pl.BlockSpec((1, hidden, share), lambda i, m: (i // 2, 0, 0))),
            ((groups // 2, hidden, share), BF, pl.BlockSpec((1, hidden, share), lambda i, m: (i // 2, 0, 0))),
        ],
        scratch=[pltpu.VMEM((hidden, genes), BF)],
        scalars=1,
        flops=2 * rows_all * genes * hidden,
        moved=2 * rows_all * genes,
    )
    got = swap(send_part, "genes", 1)
    slot = pl.BlockSpec((1, hidden, share), lambda i, m: (0, 0, 0))
    if fast:
        mine = [(keep_part[k : k + 1] + got[k : k + 1].astype(F32)).astype(BF) for k in (2, 3, 1)]
        far = [swap(part, "genes", 2 * k) for part, k in zip(mine, (2, 3, 1))]
        kept = keep_part
        ready = mine[2]
    else:
        summed = lax.psum_scatter(
            keep_part + got.astype(F32),
            "genes",
            scatter_dimension=0,
            axis_index_groups=[list(range(c, groups, 2)) for c in range(2)],
            tiled=True,
        )
        zero = jnp.zeros((1, hidden, share), BF)
        kept, got, far = summed, zero, [zero] * 3
        ready = keep_part

    mask_late = after(gene_mask.reshape(1, genes), ready)
    aug, dec_n, par, lg_tab, dg_tab, enc_pieces, dec_pieces, lat_row, head_rows, head_bias, head_cols, norm_t = call(
        prep_kernel,
        (1,),
        [full(gene_par), full(mask_late), full(dec_t), full(small_w), full(head_t), full(norm_par)],
        [
            new((2 * genes, hidden + 16), BF),
            new((hidden, 2 * genes), BF),
            new((5, genes, 128)),
            new((COUNT_TOP, genes, 128)),
            new((COUNT_TOP, genes, 128)),
            new((3 * hidden, kinds), BF),
            new((3 * hidden, kinds + 48), BF),
            new((16, hidden)),
            new((32, hidden)),
            new((32, 128)),
            new((2 * hidden, 64), BF),
            new((hidden, 8)),
        ],
    )
    logc, x_kept, gam_cell, dig_acc, log_lines = call(
        lambda *refs: counts_kernel(16, min(512, width), *refs),
        (blocks,),
        [
            (x_t, lane_block(genes)),
            full(lg_tab),
            full(dg_tab),
            (par, pl.BlockSpec((None, genes, 128), lambda i: (4, 0, 0))),
        ],
        [
            ((genes, rows_all), BF, lane_block(genes)),
            ((genes, rows_all), BF, lane_block(genes)),
            new((blocks, width)),
            new((genes, 128)),
            new((8 * gene_lines, 128)),
        ],
        scratch=[pltpu.VMEM((genes, 128), F32)],
        flops=rows_all * genes * 30,
        moved=4 * rows_all * genes,
        mib=16,
    )
    enc_late = after(enc_pieces, log_lines)
    stat8 = whole((8, hidden))
    pre_enc, stat_enc = call(
        own_kernel,
        (1,),
        [(me, None), (kept, slot), (got, slot)]
        + [(part, slot) for part in far]
        + [(batch_own, own_block), full(enc_late)],
        [new((hidden, share)), new((8, hidden))],
        scalars=1,
        flops=2 * share * hidden * kinds * 3,
        moved=share * hidden * 16,
    )
    stat_enc = total(total(stat_enc, "genes"), "cells")

    pack, aff_own, kl_row = call(
        lambda *refs: latent_kernel(cells, latent, *refs),
        (1,),
        [
            (me, None),
            full(pre_enc),
            full(stat_enc),
            full(norm_t),
            full(head_rows),
            full(head_bias),
            (noise_t, own_lanes(latent)),
            (batch_own, own_block),
            full(dec_pieces),
        ],
        [new((32, share)), new((hidden, share), BF), new((1, share))],
        scalars=1,
    )
    near, far_pack = gather_genes(pack, fast, blocks, width)
    if fast:
        stat_dec = jnp.sum(near[:, 8:16, :hidden], axis=0) + jnp.sum(far_pack[:, 8:16, :hidden], axis=0)
    else:
        stat_dec = lax.psum(pack[8:16, :hidden], "genes")
    stat_dec = total(stat_dec, "cells")

    batch_spec = pl.BlockSpec((1, 1, width), lambda i, *_: (i, 0, 0))
    hid, phat_dec, lse, z_all = call(
        lambda *refs: decode_kernel(cells, latent, fast, *refs),
        (blocks,),
        [
            (me, None),
            (near, from_all(32)),
            (far_pack, from_all(32)),
            (noise_t, lane_block(latent)),
            (batch_all, batch_spec),
            full(stat_dec),
            full(norm_t),
            full(dec_pieces),
            (aug, pl.BlockSpec((genes, hidden + 16), lambda i, m: (0, 0))),
        ],
        [
            ((hidden, rows_all), BF, lane_block(hidden)),
            ((hidden, rows_all), F32, lane_block(hidden)),
            new((blocks, width)),
            ((16, rows_all), F32, lane_block(16)),
        ],
        scratch=[pltpu.VMEM((genes, width), F32)],
        scalars=1,
        flops=2 * rows_all * genes * hidden,
        moved=rows_all * hidden * 6,
    )
    lse_all = log_total_of(lse, "genes")

    aff_near, aff_far = gather_genes(after(aff_own, stat_dec), fast, blocks, width)
    fixed_rows = genes + kinds + 8 * gene_lines + 8
    (fixed,) = call(
        lambda *refs: enc_sums_kernel(fast, *refs),
        (blocks,),
        [
            (me, None),
            (logc, lane_block(genes)),
            (aff_near, from_all(hidden)),
            (aff_far, from_all(hidden)),
            (batch_all, batch_spec),
            full(log_lines),
        ],
        [new((fixed_rows, hidden))],
        scalars=1,
    )
    fixed = total_by_halves(fixed, "cells", (1, 2))

    full8 = whole((blocks, width))
    gm, gd, rt, mass, recon, gene_acc = call(
        lambda *refs: zinb_kernel(32, min(512, width), *refs),
        (blocks,),
        [
            (hid, lane_block(hidden)),
            full(aug),
            (x_kept, lane_block(genes)),
            (par, pl.BlockSpec((4, genes, 128), lambda i: (0, 0, 0))),
            full(lib8),
            full(lse_all),
            full(gam_cell),
        ],
        [((genes, rows_all), BF, lane_block(genes))] * 3
        + [new((blocks, width)), new((blocks, width)), new((3, genes, 128))],
        scratch=[pltpu.VMEM((2 * genes, width), F32)],
        flops=rows_all * genes * 200,
        moved=8 * rows_all * genes,
        mib=20,
    )
    mass = total(mass, "genes")
    part_a, part_r, dec_acc = call(
        back_kernel,
        (blocks,),
        [
            (gm, lane_block(genes)),
            (gd, lane_block(genes)),
            (rt, lane_block(genes)),
            (hid, lane_block(hidden)),
            full(dec_n),
        ],
        [
            ((hidden, rows_all), F32, lane_block(hidden)),
            ((hidden, rows_all), F32, lane_block(hidden)),
            new((2 * genes, hidden)),
        ],
        flops=2 * rows_all * genes * hidden * 5,
        moved=8 * rows_all * genes,
        mib=16,
    )

    dy_dec, keep_d, send_d = call(
        lambda *refs: hidden_grad_kernel(cells, latent, *refs),
        (blocks,),
        [
            (me if fast else jnp.zeros_like(me), None),
            (part_a, lane_block(hidden)),
            (part_r, lane_block(hidden)),
            (mass, full8),
            (hid, lane_block(hidden)),
            (phat_dec, lane_block(hidden)),
            full(lib8),
            full(stat_dec),
            full(norm_par),
            full(lat_row),
            full(recon),
        ],
        [
            ((hidden, rows_all), F32, lane_block(hidden)),
            new((blocks // 2, 16, width)),
            new((blocks // 2, 16, width)),
        ],
        scratch=[pltpu.VMEM((2, hidden, 128), F32)],
        scalars=1,
    )
    if fast:
        got_d = swap(send_d, "genes", 1)
        pieces = [swap(keep_d[k] + got_d[k], "genes", 2 * k) for k in (1, 2, 3)]
        own_d = (keep_d[0] + got_d[0] + pieces[0]) + (pieces[1] + pieces[2])
        sums_dec = own_d[8:, :hidden]
    else:
        both = jnp.stack([keep_d, send_d], axis=1).reshape(blocks, 16, width)
        sums_dec = lax.psum(both[0, 8:, :hidden], "genes")
        both = both.transpose(1, 0, 2).reshape(16, groups, share).transpose(1, 0, 2)
        own_d = lax.psum_scatter(both, "genes", scatter_dimension=0, tiled=True)[0]
    sums_dec = total(sums_dec, "cells")
    d_near, d_far = gather_genes(own_d, fast, blocks, width)
    dec_part, oh_part = call(
        lambda *refs: dec_grad_kernel(cells, *refs),
        (blocks,),
        [
            (rt, lane_block(genes)),
            (hid, lane_block(hidden)),
            (mass, full8),
            full(lib8),
            (dy_dec, lane_block(hidden)),
            (z_all, lane_block(16)),
            (batch_all, batch_spec),
            full(dec_acc),
            full(gene_acc),
            full(dig_acc),
            (par, pl.BlockSpec((None, genes, 128), lambda i: (1, 0, 0))),
        ],
        [new((2 * genes + 8 * gene_lines, hidden)), new((kinds + 16, hidden))],
        scratch=[pltpu.VMEM((genes, hidden + 16), F32)],
    )
    oh_part = total(oh_part, "genes")
    dec_g = total_by_halves(dec_part, "cells", (2, 1))

    rest_rows = 2 * kinds + 16 + 32 + 16
    enc_part, rest = call(
        lambda *refs: enc_back_kernel(cells, latent, fast, *refs),
        (blocks,),
        [
            (me, None),
            (d_near, from_all(16)),
            (d_far, from_all(16)),
            (phat_dec, lane_block(hidden)),
            full(sums_dec),
            full(stat_dec),
            full(norm_par),
            full(lat_row),
            (near, from_all(32)),
            (far_pack, from_all(32)),
            (noise_t, lane_block(latent)),
            full(klw),
            (aff_near, from_all(hidden)),
            (aff_far, from_all(hidden)),
            (batch_all, batch_spec),
            (logc, lane_block(genes)),
            full(head_cols),
            (z_all, lane_block(16)),
        ],
        [new((genes, hidden)), new((rest_rows, hidden))],
        scratch=[pltpu.VMEM((2, hidden, 128), F32)],
        scalars=1,
        flops=2 * rows_all * genes * hidden,
        moved=2 * rows_all * genes,
    )
    rest = jnp.concatenate([rest[: kinds + 48], rest[kinds + 48 :] + oh_part])
    enc_sum = total_by_halves(enc_part, "cells", (1, 2))
    rest = total_by_halves(rest, "cells", (2, 1))

    enc_g, small_g, head_g, norm_g, square, loss = call(
        lambda *refs: finish_kernel(cells, latent, *refs),
        (1,),
        [full(a) for a in (enc_sum, rest, dec_g, fixed, stat_enc, stat_dec, sums_dec, norm_par, kl_row, klw, own_d)],
        [
            new((genes, hidden)),
            new((2 * kinds + 16, hidden)),
            new((2 * latent, hidden + 1)),
            new((4, hidden)),
            new((8, 128)),
            new((1, share)),
        ],
    )
    square = total(square, "genes")

    state = [
        enc_w, enc_m, enc_v, dec_t, turn(dec_m), turn(dec_v), gene_par, gene_m, gene_v,
        small_w, small_m, small_v, head_t, head_m.T, head_v.T, norm_par, norm_m, norm_v,
    ]
    ins = [square, enc_g, dec_g, small_g, head_g, norm_g] + state
    outs = []
    for index in range(6):
        one = state[3 * index]
        outs += [(one.shape, F32)] * 3
        if index < 2:
            outs.append((one.shape, BF))
    outs.append(((8, 128), F32))
    res = call(
        lambda *refs: update_kernel(latent, *refs),
        (1,),
        [full(array) for array in ins],
        [new(shape, dtype) for shape, dtype in outs],
        mib=16,
    )
    enc_res, dec_res = res[0:4], [turn(part) for part in res[4:8]]
    head_res = [part.T for part in res[14:17]]
    return (
        *enc_res,
        *dec_res,
        *res[8:14],
        *head_res,
        *res[17:20],
        res[20][0, 0],
        loss.reshape(share),
    )


def solution(mesh):
    placed = (
        P("cells", "genes"), P("cells"), P("cells", None), P("cells"), P("genes"), P(),
        P("genes", None), P("genes", None), P("genes", None),
        P(None, None, "genes"), P(None, None, "genes"), P(None, None, "genes"),
        P(None, "genes"), P(None, "genes"), P(None, "genes"),
        P(), P(), P(), P(), P(), P(), P(), P(), P(),
    )
    return jax.shard_map(
        per_device,
        mesh=mesh,
        in_specs=placed,
        out_specs=(
            P("genes", None), P("genes", None), P("genes", None), P("genes", None),
            P(None, None, "genes"), P(None, None, "genes"), P(None, None, "genes"), P(None, None, "genes"),
            P(None, "genes"), P(None, "genes"), P(None, "genes"),
            P(), P(), P(), P(), P(), P(), P(), P(), P(), P(),
            P(("cells", "genes")),
        ),
        check_vma=False,
    )
```

time: 335 us -> 248 us (0.74)
  Pallas kernels: 146 us -> 104 us
  other arithmetic: 19.9 us -> 2.32 us
  between operations: 15.2 us -> 2.18 us
  starting transfers between devices: 73.1 us -> 62.2 us
    pallas_call x16 -> x14, Pallas kernels: 146 us -> 104 us  [call(): pl.pallas_call(kernel, out_shape=[jax.ShapeDtypeStruct(shape, dtype) for...]
    unnamed x46 -> x106, local copies, waits for them, and re-layouts: 4.04 us -> 15 us
    ppermute x57, starting transfers between devices: 73.1 us -> 62.2 us  [swap(): return lax.ppermute(value, axis, [(i, i ^ bit) for i in range(count)])]
    add x12 -> x6, other arithmetic: 6.81 us -> 0.04 us  [total(): value + swap(value, axis, low) + (swap(value, axis, high) + swap(value, a...]
    all_gather x1 -> x0, waiting for transfers between devices: 5.65 us -> none  [per_device(): pre_all = lax.all_gather(pre_low, 'genes', axis=0)]
    broadcast_in_dim x5 -> x0, local copies, waits for them, and re-layouts: 5.6 us -> none  [the longest x4 4.92 us: tall(): return jnp.broadcast_to(row[..., None], row.shape + (128,))]
    ppermute x57, waiting for transfers between devices: 56.4 us -> 61.2 us  [swap(): return lax.ppermute(value, axis, [(i, i ^ bit) for i in range(count)])]
    convert_element_type x4 -> x1, other arithmetic: 4.34 us -> 0.26 us  [per_device(): (keep_part[k:k + 1] + got[k:k + 1].astype(F32)).astype(BF)]
  transfers between devices with their start and end apart: 58 -> 57, of which waited for: 34 -> 29; matrix products, arithmetic and copies ran while one was open for 5% -> 1% of each run, Pallas kernels for 16% -> 23%
where the time goes in v2:
time: 248 us
  Pallas kernels  104 us (42%)
  starting transfers between devices  62.2 us (25%)
  waiting for transfers between devices  61.2 us (25%)
  local copies, waits for them, and re-layouts  16.3 us (7%)
    pallas_call x14, Pallas kernels, call(): pl.pallas_call(kernel, out_shape=[jax.ShapeDtypeStruct(shape, dtype) for...  104 us
    ppermute x57, starting transfers between devices, swap(): return lax.ppermute(value, axis, [(i, i ^ bit) for i in range(count)])  62.2 us
    ppermute x57, waiting for transfers between devices, swap(): return lax.ppermute(value, axis, [(i, i ^ bit) for i in range(count)])  61.2 us
    unnamed x106, local copies, waits for them, and re-layouts  15 us
  transfers between devices with their start and end apart: 57, of which 29 were waited for; matrix products, arithmetic and copies ran while one was open for 1% of the time, Pallas kernels for 23%

profile of v2, /device:TPU:0, one launch (start us, length us, event | category | flops | bytes accessed | tf_op | source)
XLA Modules:
  0.0 247.8 jit_solution(17382308984311795826)
XLA Ops:
  0.7 2.5 copy-done
  4.1 4.0 %shard_map.399 = (f32[4,128,1024]{2,1,0:T(8,128)S(1)}, bf16[4,128,1024]{2,1,0:T(8,128)(2,1)S(1)}) custom-call(s32[1]{0:T(128)} %bitcast.me_ref.refs_0_, bf16[320,8192]{1,0:T(8,128)(2,1)S(1)} %bitcast.45, f32[320,128]{1,0:T(8,128)S(1)} %copy-done.14), custom_call_target="tpu_custom_call" | custom-call | flops 671088640 | bytes 5242880 | tf_op jit(solution)/shard_map/pallas_call | solution.py:42
  8.6 2.3 collective-permute-done.got_ref
  11.2 4.0 %collective-permute-start.1 = (bf16[1,128,1024]{2,1,0:T(8,128)(2,1)S(1)}, bf16[1,128,1024]{2,1,0:T(8,128)(2,1)S(1)}, u32[]{:S(2)}, u32[]{:S(2)}) collective-permute-start(bf16[1,128,1024]{2,1,0:T(8,128)(2,1)S(1)} %get-tuple-element.172), channel_id=1, source_target_pairs={{0,4},{1,5},{2,6},{3,7},{4,0},{5,1},{6,2},{7,3},{8,12},{9,13},{10,... | collective-permute-start | bytes 786440 | tf_op jit(solution)/shard_map/ppermute | solution.py:59
  19.2 15.8 %shard_map.401 = (bf16[320,8192]{1,0:T(8,128)(2,1)S(1)}, bf16[320,8192]{1,0:T(8,128)(2,1)S(1)}, f32[8,1024]{1,0:T(8,128)S(1)}, f32[320,128]{1,0:T(8,128)S(1)}, f32[24,128]{1,0:T(8,128)S(1)}) custom-call(bf16[320,8192]{1,0:T(8,128)(2,1)S(1)} %bitcast.46, f32[8,320,128]{2,1,0:T(8,128)S(1)} %get-tuple-element.100.refs_1_, ...), custom_call_target="tpu_custom_call" | custom-call | flops 78643200 | bytes 10485760 | tf_op jit(solution)/shard_map/pallas_call | solution.py:42
  35.0 2.4 copy-done.2
  39.8 4.0 %collective-permute-start.6 = (f32[8,128]{1,0:T(8,128)S(1)}, f32[8,128]{1,0:T(8,128)S(1)}, u32[]{:S(2)}, u32[]{:S(2)}) collective-permute-start(f32[8,128]{1,0:T(8,128)S(1)} %add.168), channel_id=1, source_target_pairs={{0,4},{1,5},{2,6},{3,7},{4,0},{5,1},{6,2},{7,3},{8,12},{9,13},{10,... | collective-permute-start | bytes 12296 | tf_op jit(solution)/shard_map/ppermute | solution.py:59
  45.4 3.8 %collective-permute-done.7 = f32[8,128]{1,0:T(8,128)S(1)} collective-permute-done((f32[8,128]{1,0:T(8,128)S(1)}, f32[8,128]{1,0:T(8,128)S(1)}, u32[]{:S(2)}, u32[]{:S(2)}) %collective-permute-start.7) | collective-permute-done | bytes 4128 | tf_op jit(solution)/shard_map/ppermute | solution.py:59
  52.9 2.4 collective-permute-done.10
  60.3 2.4 collective-permute-start.11
  62.7 3.0 %collective-permute-done.13 = f32[32,1024]{1,0:T(8,128)S(1)} collective-permute-done((f32[32,1024]{1,0:T(8,128)S(1)}, f32[32,1024]{1,0:T(8,128)S(1)}, u32[]{:S(2)}, u32[]{:S(2)}) %collective-permute-start.13) | collective-permute-done | bytes 131104 | tf_op jit(solution)/shard_map/ppermute | solution.py:59
  65.7 4.0 %collective-permute-done.12 = f32[32,1024]{1,0:T(8,128)S(1)} collective-permute-done((f32[32,1024]{1,0:T(8,128)S(1)}, f32[32,1024]{1,0:T(8,128)S(1)}, u32[]{:S(2)}, u32[]{:S(2)}) %collective-permute-start.12) | collective-permute-done | bytes 131104 | tf_op jit(solution)/shard_map/ppermute | solution.py:59
  75.4 2.4 collective-permute-done.17
  78.0 9.5 %shard_map.404 = (bf16[128,8192]{1,0:T(8,128)(2,1)S(1)}, f32[128,8192]{1,0:T(8,128)S(1)}, f32[8,1024]{1,0:T(8,128)S(1)}, f32[16,8192]{1,0:T(8,128)S(1)}) custom-call(s32[1]{0:T(128)} %bitcast.me_ref.refs_0_, f32[4,32,1024]{2,1,0:T(8,128)S(1)} %pad_maximum_fusion.1.refs_1_.refs_8_, f32[4,32,1024]{2,1,0:T(8,128)S(1)} %collective-permute-done.14.refs_2_.refs_9_, ...), custom_call_target="tpu_custom_call" | custom-call | flops 671088640 | bytes 6291456 | tf_op jit(solution)/shard_map/pallas_call | solution.py:42
  93.9 2.6 %collective-permute-start.19 = (f32[8,1024]{1,0:T(8,128)}, f32[8,1024]{1,0:T(8,128)}, u32[]{:S(2)}, u32[]{:S(2)}) collective-permute-start(f32[8,1024]{1,0:T(8,128)} %log_add_fusion.1), channel_id=1, source_target_pairs={{0,2},{1,3},{2,0},{3,1},{4,6},{5,7},{6,4},{7,5},{8,10},{9,11},{10,... | collective-permute-start | bytes 98312 | tf_op jit(solution)/shard_map/ppermute | solution.py:59
  100.2 2.5 copy-done.6
  104.4 28.3 %shard_map.405 = (bf16[320,8192]{1,0:T(8,128)(2,1)S(1)}, bf16[320,8192]{1,0:T(8,128)(2,1)S(1)}, bf16[320,8192]{1,0:T(8,128)(2,1)S(1)}, f32[8,1024]{1,0:T(8,128)S...) custom-call(bf16[128,8192]{1,0:T(8,128)(2,1)S(1)} %get-tuple-element.113.refs_0_.hid_ref.refs_4_.refs_1_, ...), custom_call_target="tpu_custom_call" | custom-call | flops 524288000 | bytes 20971520 | tf_op jit(solution)/shard_map/pallas_call | solution.py:42
  135.8 2.0 collective-permute-start.24
  137.8 2.0 collective-permute-start.25
  139.8 9.5 %shard_map.406 = (f32[128,8192]{1,0:T(8,128)S(1)}, f32[128,8192]{1,0:T(8,128)S(1)}, f32[640,128]{1,0:T(8,128)S(1)}) custom-call(bf16[320,8192]{1,0:T(8,128)(2,1)S(1)} %get-tuple-element.117.gm_ref, bf16[320,8192]{1,0:T(8,128)(2,1)S(1)} %get-tuple-element.118.gd_ref, bf16[320,8192]{1,0:T(8,128)(2,1)S(1)} %get-tuple-element.119.rt_ref.refs_0_, ...), custom_call_target="tpu_custom_call" | custom-call | flops 3355443200 | bytes 20971520 | tf_op jit(solution)/shard_map/pallas_call | solution.py:42
  149.3 12.5 %collective-permute-done.24 = f32[8,1024]{1,0:T(8,128)S(1)} collective-permute-done((f32[8,1024]{1,0:T(8,128)S(1)}, f32[8,1024]{1,0:T(8,128)S(1)}, u32[]{:S(2)}, u32[]{:S(2)}) %collective-permute-start.24) | collective-permute-done | bytes 32800 | tf_op jit(solution)/shard_map/ppermute | solution.py:59
  161.8 4.7 %shard_map.407 = (f32[128,8192]{1,0:T(8,128)S(1)}, f32[4,16,1024]{2,1,0:T(8,128)S(1)}, f32[4,16,1024]{2,1,0:T(8,128)S(1)}) custom-call(s32[1]{0:T(128)} %bitcast.me_ref.refs_0_, f32[128,8192]{1,0:T(8,128)S(1)} %get-tuple-element.121.refs_1_, f32[128,8192]{1,0:T(8,128)S(1)} %get-tuple-element.122.refs_2_, f32[8,1024]{1,0:T(8,128)S(1)} %add_add_fusion.1.refs_3_.refs_2_, ...), custom_call_target="tpu_custom_call" | custom-call | tf_op jit(solution)/shard_map/pallas_call | solution.py:42
  166.6 2.6 %collective-permute-done.37 = bf16[128,1024]{1,0:T(8,128)(2,1)S(1)} collective-permute-done((bf16[128,1024]{1,0:T(8,128)(2,1)S(1)}, bf16[128,1024]{1,0:T(8,128)(2,1)S(1)}, u32[]{:S(2)}, u32[]{:S(2)}) %collective-permute-start.37) | collective-permute-done | bytes 262176 | tf_op jit(solution)/shard_map/ppermute | solution.py:59
  171.9 2.1 collective-permute-start.29
  174.7 3.8 %collective-permute-done.28 = f32[16,1024]{1,0:T(8,128)S(1)} collective-permute-done((f32[16,1024]{1,0:T(8,128)S(1)}, f32[16,1024]{1,0:T(8,128)S(1)}, u32[]{:S(2)}, u32[]{:S(2)}) %collective-permute-start.28) | collective-permute-done | bytes 65568 | tf_op jit(solution)/shard_map/ppermute | solution.py:59
  178.6 2.0 collective-permute-start.32
  183.1 6.2 %shard_map.409 = (f32[664,128]{1,0:T(8,128)S(1)}, f32[144,128]{1,0:T(8,128)S(1)}) custom-call(bf16[320,8192]{1,0:T(8,128)(2,1)S(1)} %get-tuple-element.119.rt_ref.refs_0_, bf16[128,8192]{1,0:T(8,128)(2,1)S(1)} %get-tuple-element.113.refs_0_.hid_ref.refs_4_.refs_1_, f32[8,1024]{1,0:T(8,128)S(1)} %add_add_fusion.1.refs_3_.refs_2_, ...), custom_call_target="tpu_custom_call" | custom-call | tf_op jit(solution)/shard_map/pallas_call | solution.py:42
  198.5 11.8 %shard_map.408 = (f32[320,128]{1,0:T(8,128)S(1)}, f32[320,128]{1,0:T(8,128)S(1)}) custom-call(s32[1]{0:T(128)} %bitcast.me_ref.refs_0_, f32[4,16,1024]{2,1,0:T(8,128)S(1)} %pad_maximum_fusion.2.refs_1_, f32[4,16,1024]{2,1,0:T(8,128)S(1)} %collective-permute-done.33.refs_2_, f32[128,8192]{1,0:T(8,128)S(1)} %copy-done.4, ...), custom_call_target="tpu_custom_call" | custom-call | flops 671088640 | bytes 5242880 | tf_op jit(solution)/shard_map/pallas_call | solution.py:42
  212.0 7.1 %shard_map.410 = f32[480,128]{1,0:T(8,128)S(1)} custom-call(s32[1]{0:T(128)} %bitcast.me_ref.refs_0_, bf16[320,8192]{1,0:T(8,128)(2,1)S(1)} %bitcast.48, bf16[4,128,1024]{2,1,0:T(8,128)(2,1)S(1)} %pad_maximum_fusion.refs_12_.refs_2_, bf16[4,128,1024]{2,1,0:T(8,128)(2,1)S(1)} %collective-permute-done.40.refs_13_.refs_3_, s32[8,1,1024]{2,1,0:T(1,128)S(1)} %bitcast.59, ...), custom_call_target="tpu_custom_call" | custom-call | tf_op jit(solution)/shard_map/pallas_call | solution.py:42
  223.8 4.5 %collective-permute-done.51 = f32[480,128]{1,0:T(8,128)S(1)} collective-permute-done((f32[480,128]{1,0:T(8,128)S(1)}, f32[480,128]{1,0:T(8,128)S(1)}, u32[]{:S(2)}, u32[]{:S(2)}) %collective-permute-start.51) | collective-permute-done | bytes 245792 | tf_op jit(solution)/shard_map/ppermute | solution.py:59
  230.1 4.1 %collective-permute-done.50 = f32[664,128]{1,0:T(8,128)S(1)} collective-permute-done((f32[664,128]{1,0:T(8,128)S(1)}, f32[664,128]{1,0:T(8,128)S(1)}, u32[]{:S(2)}, u32[]{:S(2)}) %collective-permute-start.50) | collective-permute-done | bytes 340000 | tf_op jit(solution)/shard_map/ppermute | solution.py:59
  242.5 2.6 %collective-permute-done.56 = f32[8,128]{1,0:T(8,128)S(1)} collective-permute-done((f32[8,128]{1,0:T(8,128)S(1)}, f32[8,128]{1,0:T(8,128)S(1)}, u32[]{:S(2)}, u32[]{:S(2)}) %collective-permute-start.56) | collective-permute-done | bytes 4128 | tf_op jit(solution)/shard_map/ppermute | solution.py:59
  (240 shorter events, 72.5 us)
Async XLA Ops:
  11.2 26.2 %collective-permute-start.1 = (bf16[1,128,1024]{2,1,0:T(8,128)(2,1)S(1)}, bf16[1,128,1024]{2,1,0:T(8,128)(2,1)S(1)}, u32[]{:S(2)}, u32[]{:S(2)}) collective-permute-start(bf16[1,128,1024]{2,1,0:T(8,128)(2,1)S(1)} %get-tuple-element.172), channel_id=1, source_target_pairs={{0,4},{1,5},{2,6},{3,7},{4,0},{5,1},{6,2},{7,3},{8,12},{9,13},{10,... | collective-permute-start | bytes 786440 | tf_op jit(solution)/shard_map/ppermute | solution.py:59
  15.2 22.2 %collective-permute-start.2 = (bf16[1,128,1024]{2,1,0:T(8,128)(2,1)S(1)}, bf16[1,128,1024]{2,1,0:T(8,128)(2,1)S(1)}, u32[]{:S(2)}, u32[]{:S(2)}) collective-permute-start(bf16[1,128,1024]{2,1,0:T(8,128)(2,1)S(1)} %get-tuple-element.171), channel_id=1, source_target_pairs={{0,6},{1,7},{2,4},{3,5},{4,2},{5,3},{6,0},{7,1},{8,14},{9,15},{10,... | collective-permute-start | bytes 786440 | tf_op jit(solution)/shard_map/ppermute | solution.py:59
  16.6 20.8 %collective-permute-start.3 = (bf16[1,128,1024]{2,1,0:T(8,128)(2,1)S(1)}, bf16[1,128,1024]{2,1,0:T(8,128)(2,1)S(1)}, u32[]{:S(2)}, u32[]{:S(2)}) collective-permute-start(bf16[1,128,1024]{2,1,0:T(8,128)(2,1)S(1)} %get-tuple-element.170), channel_id=1, source_target_pairs={{0,2},{1,3},{2,0},{3,1},{4,6},{5,7},{6,4},{7,5},{8,10},{9,11},{10,... | collective-permute-start | bytes 786440 | tf_op jit(solution)/shard_map/ppermute | solution.py:59
  39.8 5.5 %collective-permute-start.6 = (f32[8,128]{1,0:T(8,128)S(1)}, f32[8,128]{1,0:T(8,128)S(1)}, u32[]{:S(2)}, u32[]{:S(2)}) collective-permute-start(f32[8,128]{1,0:T(8,128)S(1)} %add.168), channel_id=1, source_target_pairs={{0,4},{1,5},{2,6},{3,7},{4,0},{5,1},{6,2},{7,3},{8,12},{9,13},{10,... | collective-permute-start | bytes 12296 | tf_op jit(solution)/shard_map/ppermute | solution.py:59
  58.3 7.4 %collective-permute-start.13 = (f32[32,1024]{1,0:T(8,128)S(1)}, f32[32,1024]{1,0:T(8,128)S(1)}, u32[]{:S(2)}, u32[]{:S(2)}) collective-permute-start(f32[32,1024]{1,0:T(8,128)S(1)} %get-tuple-element.111), channel_id=1, source_target_pairs={{0,6},{1,7},{2,4},{3,5},{4,2},{5,3},{6,0},{7,1},{8,14},{9,15},{10,... | collective-permute-start | bytes 393224 | tf_op jit(solution)/shard_map/ppermute | solution.py:59
  60.3 9.4 %collective-permute-start.12 = (f32[32,1024]{1,0:T(8,128)S(1)}, f32[32,1024]{1,0:T(8,128)S(1)}, u32[]{:S(2)}, u32[]{:S(2)}) collective-permute-start(f32[32,1024]{1,0:T(8,128)S(1)} %get-tuple-element.111), channel_id=1, source_target_pairs={{0,4},{1,5},{2,6},{3,7},{4,0},{5,1},{6,2},{7,3},{8,12},{9,13},{10,... | collective-permute-start | bytes 393224 | tf_op jit(solution)/shard_map/ppermute | solution.py:59
  60.3 9.4 %collective-permute-start.11 = (f32[32,1024]{1,0:T(8,128)S(1)}, f32[32,1024]{1,0:T(8,128)S(1)}, u32[]{:S(2)}, u32[]{:S(2)}) collective-permute-start(f32[32,1024]{1,0:T(8,128)S(1)} %get-tuple-element.111), channel_id=1, source_target_pairs={{0,2},{1,3},{2,0},{3,1},{4,6},{5,7},{6,4},{7,5},{8,10},{9,11},{10,... | collective-permute-start | bytes 393224 | tf_op jit(solution)/shard_map/ppermute | solution.py:59
  92.2 6.0 %collective-permute-start.21 = (f32[8,1024]{1,0:T(8,128)}, f32[8,1024]{1,0:T(8,128)}, u32[]{:S(2)}, u32[]{:S(2)}) collective-permute-start(f32[8,1024]{1,0:T(8,128)} %log_add_fusion.1), channel_id=1, source_target_pairs={{0,6},{1,7},{2,4},{3,5},{4,2},{5,3},{6,0},{7,1},{8,14},{9,15},{10,... | collective-permute-start | bytes 98312 | tf_op jit(solution)/shard_map/ppermute | solution.py:59
  132.9 33.7 %collective-permute-start.39 = (bf16[128,1024]{1,0:T(8,128)(2,1)S(1)}, bf16[128,1024]{1,0:T(8,128)(2,1)S(1)}, u32[]{:S(2)}, u32[]{:S(2)}) collective-permute-start(bf16[128,1024]{1,0:T(8,128)(2,1)S(1)} %copy-done.25), channel_id=1, source_target_pairs={{0,6},{1,7},{2,4},{3,5},{4,2},{5,3},{6,0},{7,1},{8,14},{9,15},{10,... | collective-permute-start | bytes 786440 | tf_op jit(solution)/shard_map/ppermute | solution.py:59
  134.8 31.9 %collective-permute-start.38 = (bf16[128,1024]{1,0:T(8,128)(2,1)S(1)}, bf16[128,1024]{1,0:T(8,128)(2,1)S(1)}, u32[]{:S(2)}, u32[]{:S(2)}) collective-permute-start(bf16[128,1024]{1,0:T(8,128)(2,1)S(1)} %copy-done.25), channel_id=1, source_target_pairs={{0,4},{1,5},{2,6},{3,7},{4,0},{5,1},{6,2},{7,3},{8,12},{9,13},{10,... | collective-permute-start | bytes 786440 | tf_op jit(solution)/shard_map/ppermute | solution.py:59
  135.8 25.9 %collective-permute-start.24 = (f32[8,1024]{1,0:T(8,128)S(1)}, f32[8,1024]{1,0:T(8,128)S(1)}, u32[]{:S(2)}, u32[]{:S(2)}) collective-permute-start(f32[8,1024]{1,0:T(8,128)S(1)} %add.185), channel_id=1, source_target_pairs={{0,4},{1,5},{2,6},{3,7},{4,0},{5,1},{6,2},{7,3},{8,12},{9,13},{10,... | collective-permute-start | bytes 98312 | tf_op jit(solution)/shard_map/ppermute | solution.py:59
  137.8 24.0 %collective-permute-start.25 = (f32[8,1024]{1,0:T(8,128)S(1)}, f32[8,1024]{1,0:T(8,128)S(1)}, u32[]{:S(2)}, u32[]{:S(2)}) collective-permute-start(f32[8,1024]{1,0:T(8,128)S(1)} %add.185), channel_id=1, source_target_pairs={{0,6},{1,7},{2,4},{3,5},{4,2},{5,3},{6,0},{7,1},{8,14},{9,15},{10,... | collective-permute-start | bytes 98312 | tf_op jit(solution)/shard_map/ppermute | solution.py:59
  139.8 22.0 %collective-permute-start.23 = (f32[8,1024]{1,0:T(8,128)S(1)}, f32[8,1024]{1,0:T(8,128)S(1)}, u32[]{:S(2)}, u32[]{:S(2)}) collective-permute-start(f32[8,1024]{1,0:T(8,128)S(1)} %add.185), channel_id=1, source_target_pairs={{0,2},{1,3},{2,0},{3,1},{4,6},{5,7},{6,4},{7,5},{8,10},{9,11},{10,... | collective-permute-start | bytes 98312 | tf_op jit(solution)/shard_map/ppermute | solution.py:59
  161.7 7.5 %collective-permute-start.37 = (bf16[128,1024]{1,0:T(8,128)(2,1)S(1)}, bf16[128,1024]{1,0:T(8,128)(2,1)S(1)}, u32[]{:S(2)}, u32[]{:S(2)}) collective-permute-start(bf16[128,1024]{1,0:T(8,128)(2,1)S(1)} %copy-done.25), channel_id=1, source_target_pairs={{0,2},{1,3},{2,0},{3,1},{4,6},{5,7},{6,4},{7,5},{8,10},{9,11},{10,... | collective-permute-start | bytes 786440 | tf_op jit(solution)/shard_map/ppermute | solution.py:59
  169.4 29.1 %collective-permute-start.40 = (bf16[4,128,1024]{2,1,0:T(8,128)(2,1)S(1)}, bf16[4,128,1024]{2,1,0:T(8,128)(2,1)S(1)}, u32[]{:S(2)}, u32[]{:S(2)}) collective-permute-start(bf16[4,128,1024]{2,1,0:T(8,128)(2,1)S(1)} %pad_maximum_fusion.refs_12_.refs_2_), channel_id=1, source_target_pairs={{0,1},{1,0},{2,3},{3,2},{4,5},{5,4},{6,7},{7,6},{8,9},{9,8},{10,11... | collective-permute-start | bytes 3145736 | tf_op jit(solution)/shard_map/ppermute | solution.py:59
  170.2 8.3 %collective-permute-start.28 = (f32[16,1024]{1,0:T(8,128)S(1)}, f32[16,1024]{1,0:T(8,128)S(1)}, u32[]{:S(2)}, u32[]{:S(2)}) collective-permute-start(f32[16,1024]{1,0:T(8,128)S(1)} %get-tuple-element.174), channel_id=1, source_target_pairs={{0,4},{1,5},{2,6},{3,7},{4,0},{5,1},{6,2},{7,3},{8,12},{9,13},{10,... | collective-permute-start | bytes 196616 | tf_op jit(solution)/shard_map/ppermute | solution.py:59
  171.9 6.6 %collective-permute-start.29 = (f32[16,1024]{1,0:T(8,128)S(1)}, f32[16,1024]{1,0:T(8,128)S(1)}, u32[]{:S(2)}, u32[]{:S(2)}) collective-permute-start(f32[16,1024]{1,0:T(8,128)S(1)} %get-tuple-element.173), channel_id=1, source_target_pairs={{0,6},{1,7},{2,4},{3,5},{4,2},{5,3},{6,0},{7,1},{8,14},{9,15},{10,... | collective-permute-start | bytes 196616 | tf_op jit(solution)/shard_map/ppermute | solution.py:59
  178.6 10.7 %collective-permute-start.32 = (f32[16,1024]{1,0:T(8,128)S(1)}, f32[16,1024]{1,0:T(8,128)S(1)}, u32[]{:S(2)}, u32[]{:S(2)}) collective-permute-start(f32[16,1024]{1,0:T(8,128)S(1)} %fusion.5.refs_10_), channel_id=1, source_target_pairs={{0,6},{1,7},{2,4},{3,5},{4,2},{5,3},{6,0},{7,1},{8,14},{9,15},{10,... | collective-permute-start | bytes 196616 | tf_op jit(solution)/shard_map/ppermute | solution.py:59
  180.6 8.7 %collective-permute-start.31 = (f32[16,1024]{1,0:T(8,128)S(1)}, f32[16,1024]{1,0:T(8,128)S(1)}, u32[]{:S(2)}, u32[]{:S(2)}) collective-permute-start(f32[16,1024]{1,0:T(8,128)S(1)} %fusion.5.refs_10_), channel_id=1, source_target_pairs={{0,4},{1,5},{2,6},{3,7},{4,0},{5,1},{6,2},{7,3},{8,12},{9,13},{10,... | collective-permute-start | bytes 196616 | tf_op jit(solution)/shard_map/ppermute | solution.py:59
  181.3 7.9 %collective-permute-start.30 = (f32[16,1024]{1,0:T(8,128)S(1)}, f32[16,1024]{1,0:T(8,128)S(1)}, u32[]{:S(2)}, u32[]{:S(2)}) collective-permute-start(f32[16,1024]{1,0:T(8,128)S(1)} %fusion.5.refs_10_), channel_id=1, source_target_pairs={{0,2},{1,3},{2,0},{3,1},{4,6},{5,7},{6,4},{7,5},{8,10},{9,11},{10,... | collective-permute-start | bytes 196616 | tf_op jit(solution)/shard_map/ppermute | solution.py:59
  189.3 8.3 %collective-permute-start.33 = (f32[4,16,1024]{2,1,0:T(8,128)S(1)}, f32[4,16,1024]{2,1,0:T(8,128)S(1)}, u32[]{:S(2)}, u32[]{:S(2)}) collective-permute-start(f32[4,16,1024]{2,1,0:T(8,128)S(1)} %pad_maximum_fusion.2.refs_1_), channel_id=1, source_target_pairs={{0,1},{1,0},{2,3},{3,2},{4,5},{5,4},{6,7},{7,6},{8,9},{9,8},{10,11... | collective-permute-start | bytes 786440 | tf_op jit(solution)/shard_map/ppermute | solution.py:59
  194.1 25.3 %collective-permute-start.45 = (f32[144,128]{1,0:T(8,128)S(1)}, f32[144,128]{1,0:T(8,128)S(1)}, u32[]{:S(2)}, u32[]{:S(2)}) collective-permute-start(f32[144,128]{1,0:T(8,128)S(1)} %add.205), channel_id=1, source_target_pairs={{0,4},{1,5},{2,6},{3,7},{4,0},{5,1},{6,2},{7,3},{8,12},{9,13},{10,... | collective-permute-start | bytes 221192 | tf_op jit(solution)/shard_map/ppermute | solution.py:59
  195.2 24.6 %collective-permute-start.46 = (f32[144,128]{1,0:T(8,128)S(1)}, f32[144,128]{1,0:T(8,128)S(1)}, u32[]{:S(2)}, u32[]{:S(2)}) collective-permute-start(f32[144,128]{1,0:T(8,128)S(1)} %add.205), channel_id=1, source_target_pairs={{0,6},{1,7},{2,4},{3,5},{4,2},{5,3},{6,0},{7,1},{8,14},{9,15},{10,... | collective-permute-start | bytes 221192 | tf_op jit(solution)/shard_map/ppermute | solution.py:59
  197.1 22.6 %collective-permute-start.44 = (f32[144,128]{1,0:T(8,128)S(1)}, f32[144,128]{1,0:T(8,128)S(1)}, u32[]{:S(2)}, u32[]{:S(2)}) collective-permute-start(f32[144,128]{1,0:T(8,128)S(1)} %add.205), channel_id=1, source_target_pairs={{0,2},{1,3},{2,0},{3,1},{4,6},{5,7},{6,4},{7,5},{8,10},{9,11},{10,... | collective-permute-start | bytes 221192 | tf_op jit(solution)/shard_map/ppermute | solution.py:59
  197.6 23.5 %collective-permute-start.49 = (f32[664,128]{1,0:T(8,128)S(1)}, f32[664,128]{1,0:T(8,128)S(1)}, u32[]{:S(2)}, u32[]{:S(2)}) collective-permute-start(f32[664,128]{1,0:T(8,128)S(1)} %get-tuple-element.141), channel_id=1, source_target_pairs={{0,16},{8,24},{16,0},{24,8},{1,17},{9,25},{17,1},{25,9},{2,18},{10... | collective-permute-start | bytes 1019912 | tf_op jit(solution)/shard_map/ppermute | solution.py:59
  210.3 12.0 %collective-permute-start.41 = (f32[320,128]{1,0:T(8,128)S(1)}, f32[320,128]{1,0:T(8,128)S(1)}, u32[]{:S(2)}, u32[]{:S(2)}) collective-permute-start(f32[320,128]{1,0:T(8,128)S(1)} %get-tuple-element.134), channel_id=1, source_target_pairs={{0,8},{8,0},{16,24},{24,16},{1,9},{9,1},{17,25},{25,17},{2,10},{10... | collective-permute-start | bytes 491528 | tf_op jit(solution)/shard_map/ppermute | solution.py:59
  219.3 9.0 %collective-permute-start.51 = (f32[480,128]{1,0:T(8,128)S(1)}, f32[480,128]{1,0:T(8,128)S(1)}, u32[]{:S(2)}, u32[]{:S(2)}) collective-permute-start(f32[480,128]{1,0:T(8,128)S(1)} %shard_map.410), channel_id=1, source_target_pairs={{0,8},{8,0},{16,24},{24,16},{1,9},{9,1},{17,25},{25,17},{2,10},{10... | collective-permute-start | bytes 737288 | tf_op jit(solution)/shard_map/ppermute | solution.py:59
  219.8 9.3 %collective-permute-start.47 = (f32[320,128]{1,0:T(8,128)S(1)}, f32[320,128]{1,0:T(8,128)S(1)}, u32[]{:S(2)}, u32[]{:S(2)}) collective-permute-start(f32[320,128]{1,0:T(8,128)S(1)} %pad_maximum_fusion.3), channel_id=1, source_target_pairs={{0,16},{8,24},{16,0},{24,8},{1,17},{9,25},{17,1},{25,9},{2,18},{10... | collective-permute-start | bytes 491528 | tf_op jit(solution)/shard_map/ppermute | solution.py:59
  221.2 13.0 %collective-permute-start.50 = (f32[664,128]{1,0:T(8,128)S(1)}, f32[664,128]{1,0:T(8,128)S(1)}, u32[]{:S(2)}, u32[]{:S(2)}) collective-permute-start(f32[664,128]{1,0:T(8,128)S(1)} %add.212), channel_id=1, source_target_pairs={{0,8},{8,0},{16,24},{24,16},{1,9},{9,1},{17,25},{25,17},{2,10},{10... | collective-permute-start | bytes 1019912 | tf_op jit(solution)/shard_map/ppermute | solution.py:59
  222.4 11.8 %collective-permute-start.42 = (f32[320,128]{1,0:T(8,128)S(1)}, f32[320,128]{1,0:T(8,128)S(1)}, u32[]{:S(2)}, u32[]{:S(2)}) collective-permute-start(f32[320,128]{1,0:T(8,128)S(1)} %add.203), channel_id=1, source_target_pairs={{0,16},{8,24},{16,0},{24,8},{1,17},{9,25},{17,1},{25,9},{2,18},{10... | collective-permute-start | bytes 491528 | tf_op jit(solution)/shard_map/ppermute | solution.py:59
  228.3 7.6 %collective-permute-start.52 = (f32[480,128]{1,0:T(8,128)S(1)}, f32[480,128]{1,0:T(8,128)S(1)}, u32[]{:S(2)}, u32[]{:S(2)}) collective-permute-start(f32[480,128]{1,0:T(8,128)S(1)} %add.214), channel_id=1, source_target_pairs={{0,16},{8,24},{16,0},{24,8},{1,17},{9,25},{17,1},{25,9},{2,18},{10... | collective-permute-start | bytes 737288 | tf_op jit(solution)/shard_map/ppermute | solution.py:59
  229.1 6.8 %collective-permute-start.48 = (f32[320,128]{1,0:T(8,128)S(1)}, f32[320,128]{1,0:T(8,128)S(1)}, u32[]{:S(2)}, u32[]{:S(2)}) collective-permute-start(f32[320,128]{1,0:T(8,128)S(1)} %fusion.7), channel_id=1, source_target_pairs={{0,8},{8,0},{16,24},{24,16},{1,9},{9,1},{17,25},{25,17},{2,10},{10... | collective-permute-start | bytes 491528 | tf_op jit(solution)/shard_map/ppermute | solution.py:59
  (78 other events, 1151.9 us)

commit v3 on v2

--- a/solution.py
+++ b/solution.py
@@ -38,7 +38,7 @@
     return pl.BlockSpec(shape, lambda *_: (0,) * len(shape))
 
 
-def call(kernel, grid, ins, outs, scratch=(), scalars=0, flops=0, moved=0, mib=12):
+def call(kernel, grid, ins, outs, scratch=(), scalars=0, us=2.0, mib=12):
     return pl.pallas_call(
         kernel,
         out_shape=[jax.ShapeDtypeStruct(shape, dtype) for shape, dtype, _ in outs],
@@ -50,7 +50,7 @@
             scratch_shapes=list(scratch),
         ),
         compiler_params=pltpu.CompilerParams(vmem_limit_bytes=mib * 1024 * 1024),
-        cost_estimate=pl.CostEstimate(flops=flops, bytes_accessed=moved, transcendentals=0),
+        cost_estimate=pl.CostEstimate(flops=0, bytes_accessed=int(us * 3.69e6), transcendentals=0),
     )(*[array for array, _ in ins])
 
 
@@ -318,25 +318,23 @@
 
 def latent_kernel(cells, latent, me_ref, pre_ref, stat_ref, norm_ref, head_ref, bias_ref, noise_ref, batch_ref, dec_b_ref, pack_ref, aff_ref, kl_ref):
     kinds = dec_b_ref.shape[1] - 48
+    hidden = pre_ref.shape[0]
     mean, inv = norm_columns(stat_ref[...], 0, cells)
     phat = (pre_ref[...] - mean) * inv
     affine = norm_ref[:, 0:1] * phat + norm_ref[:, 1:2]
-    aff_ref[...] = affine.astype(BF)
     out = nn(head_ref[...], jnp.maximum(affine, 0.0), HI) + bias_ref[:, 0:1]
     lat_mean, lat_logvar = out[:latent], out[16 : 16 + latent]
+    high, mid, low = three(latent_rows(lat_logvar))
+    aff_ref[...] = jnp.concatenate((affine.astype(BF), high, mid, low), axis=0)
     var = jnp.exp(lat_logvar) + 0.0001
-    z = lat_mean + jnp.sqrt(var) * noise_ref[...]
+    z = latent_rows(lat_mean + jnp.sqrt(var) * noise_ref[...])
     terms = var + lat_mean * lat_mean - 1.0 - jnp.log(var)
     kl_ref[...] = 0.5 * jnp.sum(terms, axis=0, keepdims=True)
-    pre_dec = exact_rows(dec_b_ref[...], dec_table(latent_rows(z), batch_ref[0], kinds))
-    hidden = pre_dec.shape[0]
+    pre_dec = exact_rows(dec_b_ref[...], dec_table(z, batch_ref[0], kinds))
     stat = stat_rows(pre_dec, pre_dec * pre_dec, 0)
-    pack_ref[0:latent, :] = lat_mean
-    pack_ref[latent : latent + 6, :] = jnp.zeros((6, z.shape[1]), F32)
+    pack_ref[...] = z
     pack_ref[latent : latent + 1, 0:hidden] = stat[0:1]
     pack_ref[latent + 1 : latent + 2, 0:hidden] = stat[1:2]
-    pack_ref[16 : 16 + latent, :] = lat_logvar
-    pack_ref[16 + latent : 32, :] = jnp.zeros((16 - latent, z.shape[1]), F32)
 
 
 def latent_rows(z):
@@ -345,24 +343,19 @@
     return jnp.concatenate((z, jnp.zeros((16 - z.shape[0], z.shape[1]), F32)), axis=0)
 
 
-def draw(latent, pack, noise):
-    lat_mean, lat_logvar = pack[0:latent], pack[16 : 16 + latent]
-    return lat_mean, lat_logvar, lat_mean + jnp.sqrt(jnp.exp(lat_logvar) + 0.0001) * noise
-
-
 def pick(step, me_ref, fast, near_ref, far_ref):
     if not fast:
         return near_ref[0]
     return jnp.where(lax.rem(step ^ me_ref[0], 2) == 0, near_ref[0], far_ref[0])
 
 
-def decode_kernel(cells, latent, fast, me_ref, near_ref, far_ref, noise_ref, batch_ref, stat_ref, norm_ref, dec_b_ref, w_ref, hid_ref, phat_ref, lse_ref, z_ref, score_ref):
+def decode_kernel(cells, latent, fast, me_ref, near_ref, far_ref, batch_ref, stat_ref, norm_ref, dec_b_ref, w_ref, hid_ref, phat_ref, lse_ref, z_ref, score_ref):
     kinds = dec_b_ref.shape[1] - 48
     step = pl.program_id(0)
     genes = score_ref.shape[0]
     mean, inv = norm_columns(stat_ref[...], latent - 8, cells)
-    _, _, z = draw(latent, pick(step, me_ref, fast, near_ref, far_ref), noise_ref[...])
-    z = latent_rows(z)
+    z = pick(step, me_ref, fast, near_ref, far_ref)
+    z = jnp.where(lax.broadcasted_iota(jnp.int32, z.shape, 0) < latent, z, 0.0)
     z_ref[...] = z
     pre_dec = exact_rows(dec_b_ref[...], dec_table(z, batch_ref[0], kinds))
     phat = (pre_dec - mean) * inv
@@ -417,11 +410,11 @@
         out_ref[...] = jnp.zeros_like(out_ref)
         out_ref[genes + kinds : genes + kinds + lines_ref.shape[0], :] = lines_ref[...]
 
-    affine = pick(step, me_ref, fast, near_ref, far_ref)
-    table = one_hot(batch_ref[0], kinds)
+    affine = pick(step, me_ref, fast, near_ref, far_ref)[: out_ref.shape[1]]
+    table = one_hot(batch_ref[0], kinds).astype(BF)
     out_ref[0:genes, :] += nt(logc_ref[...], affine)
-    out_ref[genes : genes + kinds, :] += nt(table.astype(BF), affine)
-    out_ref[genes + kinds + lines_ref.shape[0] :, :] += row_sums(table)
+    out_ref[genes : genes + kinds, :] += nt(table, affine)
+    out_ref[genes + kinds + lines_ref.shape[0] :, :] += nt(jnp.ones((8, table.shape[1]), BF), table)
 
 
 def zinb_kernel(rows, span, hid_ref, w_ref, x_ref, par_ref, lib_ref, lse_ref, gam_ref, gm_ref, gd_ref, rt_ref, mass_ref, recon_ref, acc_ref, sc_ref):
@@ -512,7 +505,7 @@
     g_ref[genes:, :] += nt(gd, hid)
 
 
-def hidden_grad_kernel(cells, latent, me_ref, a_ref, r_ref, mass_ref, hid_ref, phat_ref, lib_ref, stat_ref, gain_ref, lat_ref, recon_ref, dy_ref, keep_ref, send_ref, sum_ref):
+def hidden_grad_kernel(cells, latent, me_ref, a_ref, r_ref, mass_ref, hid_ref, phat_ref, lib_ref, stat_ref, gain_ref, lat_ref, recon_ref, z_ref, batch_ref, keep_ref, send_ref, sum_ref, oh_ref):
     step = pl.program_id(0)
     steps = pl.num_programs(0)
     place = step ^ me_ref[0]
@@ -520,10 +513,10 @@
     @pl.when(step == 0)
     def _():
         sum_ref[...] = jnp.zeros_like(sum_ref)
+        oh_ref[...] = jnp.zeros_like(oh_ref)
 
     back = mass_ref[pl.ds(step, 1), :] * jnp.exp(-lib_ref[pl.ds(step, 1), :])
     dy = jnp.where(hid_ref[...] > 0, (a_ref[...] - back * r_ref[...]) * (-1.0 / cells), 0.0)
-    dy_ref[...] = dy
     hidden, width = dy.shape
     weighted = dy * phat_ref[...]
     first, second = dy[:, :128], weighted[:, :128]
@@ -545,6 +538,13 @@
         ),
         axis=0,
     )
+    kinds = oh_ref.shape[0] - 16
+    z_high, z_mid, _ = three(z_ref[...])
+    held = jnp.concatenate((one_hot(batch_ref[0], kinds).astype(BF), z_high, z_mid), axis=0)
+    product = nt(held, table)
+    product = product[:, :hidden] + product[:, hidden:]
+    oh_ref[:kinds, :] += product[:kinds]
+    oh_ref[kinds:, :] += product[kinds : kinds + 16] + product[kinds + 16 :]
     both = nn(left, table)
     block = both[:16] + both[16:]
     row = lax.broadcasted_iota(jnp.int32, block.shape, 0)
@@ -562,23 +562,27 @@
     @pl.when(step == steps - 1)
     def _():
         one, two = row_sums(sum_ref[0]), row_sums(sum_ref[1])
-        for ref in (keep_ref, send_ref):
+        part = oh_ref.shape[0] // steps
+        for core, ref in enumerate((keep_ref, send_ref)):
             for index in range(ref.shape[0]):
                 ref[index, latent + 1 : latent + 2, 0:hidden] = one[0:1]
                 ref[index, latent + 2 : latent + 3, 0:hidden] = two[0:1]
-
-
-def dec_grad_kernel(cells, rt_ref, hid_ref, mass_ref, lib_ref, dy_ref, z_ref, batch_ref, g_ref, acc_ref, dig_ref, th_ref, dec_ref, oh_ref, mix_ref):
+                owner = me_ref[0] ^ (2 * index + core)
+                for k in range(part):
+                    line = latent + 3 + k // 8
+                    lanes = slice((k % 8) * hidden, (k % 8 + 1) * hidden)
+                    ref[index, line : line + 1, lanes] = oh_ref[pl.ds(owner * part + k, 1), :]
+
+
+def dec_grad_kernel(cells, rt_ref, hid_ref, mass_ref, lib_ref, g_ref, acc_ref, dig_ref, th_ref, dec_ref, mix_ref):
     step = pl.program_id(0)
     steps = pl.num_programs(0)
     genes = rt_ref.shape[0]
     hidden = hid_ref.shape[0]
-    kinds = oh_ref.shape[0] - 16
 
     @pl.when(step == 0)
     def _():
         mix_ref[...] = jnp.zeros_like(mix_ref)
-        oh_ref[...] = jnp.zeros_like(oh_ref)
 
     back = mass_ref[pl.ds(step, 1), :] * jnp.exp(-lib_ref[pl.ds(step, 1), :])
     back_high, back_mid, back_low = three(back)
@@ -586,12 +590,6 @@
     extra = jnp.where(row == 0, back_high.astype(F32), jnp.where(row == 1, back_mid.astype(F32), 0.0))
     scaled = (hid_ref[...].astype(F32) * back).astype(BF)
     mix_ref[...] += nt(rt_ref[...], jnp.concatenate((scaled, extra.astype(BF)), axis=0))
-    z_high, z_mid, _ = three(z_ref[...])
-    left = jnp.concatenate((one_hot(batch_ref[0], kinds).astype(BF), z_high, z_mid), axis=0)
-    dy_high, dy_mid, _ = three(dy_ref[...])
-    part = nt(left, dy_high) + nt(left, dy_mid)
-    oh_ref[:kinds, :] += part[:kinds]
-    oh_ref[kinds:, :] += part[kinds : kinds + 16] + part[kinds + 16 :]
 
     @pl.when(step == steps - 1)
     def _():
@@ -610,15 +608,16 @@
         dec_ref[2 * genes :, :] = lines(gene_rows, pl.cdiv(genes, 128))
 
 
-def enc_back_kernel(cells, latent, fast, me_ref, dnear_ref, dfar_ref, phat_ref, sums_ref, stat_ref, gain_ref, lat_ref, near_ref, far_ref, noise_ref, klw_ref, anear_ref, afar_ref, batch_ref, logc_ref, cols_ref, z_ref, enc_ref, rest_ref, lane_ref):
+def enc_back_kernel(cells, latent, fast, me_ref, own_ref, dnear_ref, dfar_ref, phat_ref, sums_ref, stat_ref, gain_ref, lat_ref, noise_ref, klw_ref, anear_ref, afar_ref, batch_ref, logc_ref, cols_ref, z_ref, out_ref, rest_ref, lane_ref):
     step = pl.program_id(0)
     genes, width = logc_ref.shape
     hidden = phat_ref.shape[0]
-    kinds = (rest_ref.shape[0] - 32 - 16 - 16) // 2
+    kinds = (rest_ref.shape[0] - 64) // 2
+    steps = pl.num_programs(0)
 
     @pl.when(step == 0)
     def _():
-        enc_ref[...] = jnp.zeros_like(enc_ref)
+        out_ref[...] = jnp.zeros_like(out_ref)
         rest_ref[...] = jnp.zeros_like(rest_ref)
         lane_ref[...] = jnp.zeros_like(lane_ref)
 
@@ -644,9 +643,12 @@
     )
     grad_z = (block - fixed - (both[:16] + both[16:]))[:latent]
     noise = noise_ref[...]
-    lat_mean, lat_logvar, _ = draw(latent, pick(step, me_ref, fast, near_ref, far_ref), noise)
+    rows = pick(step, me_ref, fast, anear_ref, afar_ref)
+    pieces = rows[hidden:].astype(F32)
+    lat_logvar = (pieces[:latent] + pieces[16 : 16 + latent]) + pieces[32 : 32 + latent]
     spread = jnp.exp(lat_logvar)
     var = spread + 0.0001
+    lat_mean = z_ref[0:latent, :] - jnp.sqrt(var) * noise
     scale = klw_ref[0:1, 0:1] * (1.0 / cells)
     g_mean = latent_rows(grad_z + scale * lat_mean)
     g_var = latent_rows(
@@ -655,8 +657,7 @@
     g_head = jnp.concatenate((g_mean, g_var), axis=0)
     head_high, head_mid, _ = three(g_head)
     spread_out = nn(cols_ref[...], jnp.concatenate((head_high, head_mid), axis=0))
-    affine = pick(step, me_ref, fast, anear_ref, afar_ref)
-    wide = affine.astype(F32)
+    wide = rows[:hidden].astype(F32)
     dy = jnp.where(wide > 0, spread_out[:hidden] + spread_out[hidden:], 0.0)
     weighted = dy * wide
     first, second = dy[:, :128], weighted[:, :128]
@@ -669,63 +670,59 @@
     dy_low = dy.astype(BF)
     table = one_hot(batch_ref[0], kinds)
     hidden_low = jnp.maximum(wide, 0.0).astype(BF)
-    enc_ref[...] += nt(logc_ref[...], dy_low)
+    out_ref[0:genes, :] += nt(logc_ref[...], dy_low)
     rest_ref[0:kinds, :] += nt(table.astype(BF), dy_low)
     rest_ref[kinds : kinds + 32, :] += nt(head_high, hidden_low) + nt(head_mid, hidden_low)
-    base = kinds + 32
+    rest_ref[kinds + 32 : kinds + 40, 0:32] += row_sums(g_head)
+    base = kinds + 40
     z_high, z_mid, _ = three(z_ref[...])
     left = jnp.concatenate((table.astype(BF), z_high, z_mid), axis=0)
-    part = nt(left, phat_high) + nt(left, phat_mid)
+    part = nt(left, jnp.concatenate((phat_high, phat_mid), axis=0))
+    part = part[:, :hidden] + part[:, hidden:]
     held = jnp.sum(jnp.concatenate((table, z_ref[...]), axis=0), axis=1, keepdims=True)
     product = jnp.concatenate((part[:kinds], part[kinds : kinds + 16] + part[kinds + 16 :]), axis=0)
-    rest_ref[base + 16 :, :] -= held * m_one + product * m_two
-    bias = row_sums(g_head)
-    rest_ref[base + 8 : base + 16, 0:32] += bias
-
-    @pl.when(step == pl.num_programs(0) - 1)
+    rest_ref[base : base + kinds + 16, :] -= held * m_one + product * m_two
+    count = (kinds + 16) // steps
+    for k in range(count):
+        line = latent + 3 + k // 8
+        rest_ref[pl.ds(base + step * count + k, 1), :] += block[line : line + 1, (k % 8) * hidden : (k % 8 + 1) * hidden]
+
+    @pl.when(step == steps - 1)
     def _():
         one, two = row_sums(lane_ref[0]), row_sums(lane_ref[1])
         row = lax.broadcasted_iota(jnp.int32, one.shape, 0)
-        rest_ref[base : base + 8, :] = jnp.where(row == 0, one, jnp.where(row == 1, two, 0.0))
-
-
-def finish_kernel(cells, latent, enc_ref, rest_ref, dec_ref, fixed_ref, stat_enc_ref, stat_dec_ref, sums_ref, norm_ref, kl_ref, klw_ref, own_ref, enc_out, small_out, head_out, norm_out, square_out, loss_out):
-    genes, hidden = enc_ref.shape
-    kinds = (rest_ref.shape[0] - 32 - 16 - 16) // 2
+        out_ref[genes : genes + 8, :] = jnp.where(row == 0, one, jnp.where(row == 1, two, 0.0))
+        size = rest_ref.shape[0] // 8
+        out_ref[genes + 8 :, :] = rest_ref[pl.ds(pl.multiple_of((own_ref[0] & 7) * size, 8), size), :]
+
+
+def whole_gradient(part, product, plain, gain, shift, inv, one, two):
+    return (gain * inv) * (part - plain * one - ((product - plain * shift) / gain) * two)
+
+
+def norm_sums(rows, norm_ref):
+    return rows[0:1], (rows[1:2] - norm_ref[1:2] * rows[0:1]) / norm_ref[0:1]
+
+
+def finish_kernel(cells, latent, sum_ref, dec_ref, fixed_ref, stat_enc_ref, norm_ref, kl_ref, klw_ref, own_ref, enc_out, tail_out, loss_out):
+    genes = enc_out.shape[0]
+    size = tail_out.shape[0] - 8
     count = pl.cdiv(genes, 128)
+    kinds = fixed_ref.shape[0] - genes - 8 * count - 8
     loss_out[...] = klw_ref[0:1, 0:1] * kl_ref[...] - own_ref[latent : latent + 1, :]
-    gain, shift = norm_ref[0:1], norm_ref[1:2]
     _, inv = norm_rows(stat_enc_ref[...], 0, cells)
-    base = kinds + 32
-    n_one = rest_ref[base : base + 1]
-    n_two = (rest_ref[base + 1 : base + 2] - shift * n_one) / gain
-    one, two = n_one * (1.0 / cells), n_two * (1.0 / cells)
-    lines_at = genes + kinds
-    logs = jnp.concatenate([fixed_ref[lines_at + 8 * i : lines_at + 8 * (i + 1), :] for i in range(count)], axis=1)
+    n_one, n_two = norm_sums(sum_ref[genes : genes + 8, :], norm_ref)
+    at = genes + kinds
+    logs = jnp.concatenate([fixed_ref[at + 8 * i : at + 8 * (i + 1), :] for i in range(count)], axis=1)
     log_sum = jnp.transpose(logs)[:genes, 0:1]
-    batch_sum = jnp.transpose(fixed_ref[lines_at + 8 * count : lines_at + 8 * count + 8, :])[:kinds, 0:1]
-
-    def whole_gradient(part, product, plain):
-        return (gain * inv) * (part - plain * one - ((product - plain * shift) / gain) * two)
-
-    enc = whole_gradient(enc_ref[...], fixed_ref[0:genes, :], log_sum)
+    enc = whole_gradient(
+        sum_ref[0:genes, :], fixed_ref[0:genes, :], log_sum, norm_ref[0:1], norm_ref[1:2], inv, n_one * (1.0 / cells), n_two * (1.0 / cells)
+    )
     enc_out[...] = enc
     dec = dec_ref[...]
     lane = jnp.sum(enc * enc, axis=0, keepdims=True) + jnp.sum(dec * dec, axis=0, keepdims=True)
-    square_out[...] = jnp.broadcast_to(jnp.sum(lane, axis=1, keepdims=True), square_out.shape)
-    small_out[0:kinds, :] = whole_gradient(rest_ref[0:kinds, :], fixed_ref[genes : genes + kinds, :], batch_sum)
-    _, inv_dec = norm_rows(stat_dec_ref[...], latent - 8, cells)
-    small_out[kinds:, :] = (norm_ref[2:3] * inv_dec) * rest_ref[base + 16 :, :]
-    bias = jnp.transpose(rest_ref[base + 8 : base + 16, :])
-    for half in range(2):
-        rows = slice(half * latent, (half + 1) * latent)
-        head_out[rows, 0:hidden] = rest_ref[kinds + 16 * half : kinds + 16 * half + latent, :]
-        head_out[rows, hidden : hidden + 1] = bias[16 * half : 16 * half + latent, 0:1]
-    at = latent + 1 - 8
-    norm_out[0:1] = n_two
-    norm_out[1:2] = n_one
-    norm_out[2:3] = sums_ref[at + 1 : at + 2]
-    norm_out[3:4] = sums_ref[at : at + 1]
+    tail_out[0:size, :] = sum_ref[genes + 8 :, :]
+    tail_out[size:, :] = jnp.broadcast_to(jnp.sum(lane, axis=1, keepdims=True), (8, tail_out.shape[1]))
 
 
 def step_of(weight, gradient, first, second, rate):
@@ -737,15 +734,48 @@
     return weight - rate * update, first, second
 
 
-def update_kernel(latent, square_ref, enc_g_ref, dec_g_ref, small_g_ref, head_g_ref, norm_g_ref, *refs):
-    ins, outs = refs[:18], refs[18:]
+def update_kernel(cells, latent, me_ref, near_ref, far_ref, enc_g_ref, dec_g_ref, sum_ref, fixed_ref, stat_enc_ref, stat_dec_ref, sums_ref, *refs):
+    ins, outs, (rest_ref, small_g_ref, head_g_ref, norm_g_ref) = refs[:18], refs[18:-4], refs[-4:]
     enc, dec, gene, small, head, norm = (ins[3 * i : 3 * i + 3] for i in range(6))
-    genes = enc[0].shape[0]
+    genes, hidden = enc[0].shape
     rows = small[0].shape[0]
+    kinds = (rows - latent) // 2
+    count = pl.cdiv(genes, 128)
+    size = near_ref.shape[1]
+    for core, ref in enumerate((near_ref, far_ref)):
+        for index in range(ref.shape[0]):
+            owner = me_ref[0] ^ (2 * index + core)
+            rest_ref[pl.ds(pl.multiple_of(owner * size, 8), size), :] = ref[index]
+    whole_rest = [rest_ref[i * size : i * size + size - 8, :] for i in range(8)]
+    square = jnp.zeros((1, 1), F32)
+    for i in range(8):
+        square = square + rest_ref[(i + 1) * size - 8 : (i + 1) * size - 7, 0:1]
+    rest = jnp.concatenate(whole_rest, axis=0)
+    gains = norm[0]
+    gain, shift = gains[0:1], gains[1:2]
+    n_one, n_two = norm_sums(sum_ref[genes : genes + 8, :], gains)
+    _, inv = norm_rows(stat_enc_ref[...], 0, cells)
+    _, inv_dec = norm_rows(stat_dec_ref[...], latent - 8, cells)
+    at = genes + kinds + 8 * count
+    batch_sum = jnp.transpose(fixed_ref[at : at + 8, :])[:kinds, 0:1]
+    small_g_ref[0:kinds, :] = whole_gradient(
+        rest[0:kinds], fixed_ref[genes : genes + kinds, :], batch_sum, gain, shift, inv, n_one * (1.0 / cells), n_two * (1.0 / cells)
+    )
+    small_g_ref[kinds:, :] = (gains[2:3] * inv_dec) * rest[kinds + 40 : 2 * kinds + 56]
+    bias = jnp.transpose(rest[kinds + 32 : kinds + 40])
+    for half in range(2):
+        into = slice(half * latent, (half + 1) * latent)
+        head_g_ref[into, 0:hidden] = rest[kinds + 16 * half : kinds + 16 * half + latent]
+        head_g_ref[into, hidden : hidden + 1] = bias[16 * half : 16 * half + latent, 0:1]
+    at = latent + 1 - 8
+    norm_g_ref[0:1] = n_two
+    norm_g_ref[1:2] = n_one
+    norm_g_ref[2:3] = sums_ref[at + 1 : at + 2]
+    norm_g_ref[3:4] = sums_ref[at : at + 1]
     small_square = jnp.zeros((1, 1), F32)
     for part in (small_g_ref[0:rows, :], head_g_ref[...], norm_g_ref[...]):
         small_square = small_square + jnp.sum(jnp.sum(part * part, axis=0, keepdims=True), axis=1, keepdims=True)
-    value = jnp.sqrt(square_ref[0:1, 0:1] + small_square)
+    value = jnp.sqrt(square + small_square)
     factor = jnp.minimum(1.0, max_norm / value)
     (enc_n, enc_m, enc_v, enc_l, dec_n, dec_m, dec_v, dec_l, gene_n, gene_m, gene_v, small_n, small_m, small_v, head_n, head_m, head_v, norm_n, norm_m, norm_v, norm_out) = outs
     norm_out[...] = jnp.broadcast_to(value, norm_out.shape)
@@ -768,9 +798,10 @@
     norm_n[...], norm_m[...], norm_v[...] = new, first, second
 
 
-def gather_genes(value, fast, blocks, width):
+def gather_genes(value, fast, blocks, width, late=None):
     if fast:
         near = jnp.stack([value] + [swap(value, "genes", 2 * k) for k in (1, 2, 3)])
+        near = near if late is None else after(near, late)
         return near, swap(near, "genes", 1)
     rows = value.shape[0]
     whole_rows = lax.all_gather(value, "genes", axis=0).transpose(1, 0, 2)
@@ -810,9 +841,9 @@
     full = lambda array: (array, whole(array.shape))
     new = lambda shape, dtype=F32: (shape, dtype, whole(shape))
     if fast:
-        from_all = lambda rows: pl.BlockSpec((1, rows, width), lambda i, m: ((i ^ m[0]) // 2, 0, 0))
+        from_all = lambda rows: pl.BlockSpec((1, rows, width), lambda i, m, *_: ((i ^ m[0]) // 2, 0, 0))
     else:
-        from_all = lambda rows: pl.BlockSpec((1, rows, width), lambda i, m: (i, 0, 0))
+        from_all = lambda rows: pl.BlockSpec((1, rows, width), lambda i, m, *_: (i, 0, 0))
 
     keep_part, send_part = call(
         enc_kernel,
@@ -828,8 +859,7 @@
         ],
         scratch=[pltpu.VMEM((hidden, genes), BF)],
         scalars=1,
-        flops=2 * rows_all * genes * hidden,
-        moved=2 * rows_all * genes,
+        us=4.0,
     )
     got = swap(send_part, "genes", 1)
     slot = pl.BlockSpec((1, hidden, share), lambda i, m: (0, 0, 0))
@@ -887,9 +917,8 @@
             new((8 * gene_lines, 128)),
         ],
         scratch=[pltpu.VMEM((genes, 128), F32)],
-        flops=rows_all * genes * 30,
-        moved=4 * rows_all * genes,
         mib=16,
+        us=15.0,
     )
     enc_late = after(enc_pieces, log_lines)
     stat8 = whole((8, hidden))
@@ -901,8 +930,6 @@
         + [(batch_own, own_block), full(enc_late)],
         [new((hidden, share)), new((8, hidden))],
         scalars=1,
-        flops=2 * share * hidden * kinds * 3,
-        moved=share * hidden * 16,
     )
     stat_enc = total(total(stat_enc, "genes"), "cells")
 
@@ -920,7 +947,7 @@
             (batch_own, own_block),
             full(dec_pieces),
         ],
-        [new((32, share)), new((hidden, share), BF), new((1, share))],
+        [new((16, share)), new((hidden + 48, share), BF), new((1, share))],
         scalars=1,
     )
     near, far_pack = gather_genes(pack, fast, blocks, width)
@@ -936,9 +963,8 @@
         (blocks,),
         [
             (me, None),
-            (near, from_all(32)),
-            (far_pack, from_all(32)),
-            (noise_t, lane_block(latent)),
+            (near, from_all(16)),
+            (far_pack, from_all(16)),
             (batch_all, batch_spec),
             full(stat_dec),
             full(norm_t),
@@ -953,28 +979,9 @@
         ],
         scratch=[pltpu.VMEM((genes, width), F32)],
         scalars=1,
-        flops=2 * rows_all * genes * hidden,
-        moved=rows_all * hidden * 6,
+        us=8.0,
     )
     lse_all = log_total_of(lse, "genes")
-
-    aff_near, aff_far = gather_genes(after(aff_own, stat_dec), fast, blocks, width)
-    fixed_rows = genes + kinds + 8 * gene_lines + 8
-    (fixed,) = call(
-        lambda *refs: enc_sums_kernel(fast, *refs),
-        (blocks,),
-        [
-            (me, None),
-            (logc, lane_block(genes)),
-            (aff_near, from_all(hidden)),
-            (aff_far, from_all(hidden)),
-            (batch_all, batch_spec),
-            full(log_lines),
-        ],
-        [new((fixed_rows, hidden))],
-        scalars=1,
-    )
-    fixed = total_by_halves(fixed, "cells", (1, 2))
 
     full8 = whole((blocks, width))
     gm, gd, rt, mass, recon, gene_acc = call(
@@ -992,11 +999,10 @@
         [((genes, rows_all), BF, lane_block(genes))] * 3
         + [new((blocks, width)), new((blocks, width)), new((3, genes, 128))],
         scratch=[pltpu.VMEM((2 * genes, width), F32)],
-        flops=rows_all * genes * 200,
-        moved=8 * rows_all * genes,
         mib=20,
-    )
-    mass = total(mass, "genes")
+        us=28.0,
+    )
+    mass_own, mass = mass, total(mass, "genes")
     part_a, part_r, dec_acc = call(
         back_kernel,
         (blocks,),
@@ -1012,12 +1018,30 @@
             ((hidden, rows_all), F32, lane_block(hidden)),
             new((2 * genes, hidden)),
         ],
-        flops=2 * rows_all * genes * hidden * 5,
-        moved=8 * rows_all * genes,
         mib=16,
-    )
-
-    dy_dec, keep_d, send_d = call(
+        us=9.0,
+    )
+
+    aff_near, aff_far = gather_genes(after(aff_own, lse_all), fast, blocks, width, mass_own)
+    fixed_rows = genes + kinds + 8 * gene_lines + 8
+    (fixed,) = call(
+        lambda *refs: enc_sums_kernel(fast, *refs),
+        (blocks,),
+        [
+            (me, None),
+            (logc, lane_block(genes)),
+            (aff_near, from_all(hidden + 48)),
+            (aff_far, from_all(hidden + 48)),
+            (batch_all, batch_spec),
+            full(log_lines),
+        ],
+        [new((fixed_rows, hidden))],
+        scalars=1,
+        us=4.0,
+    )
+    fixed = total_by_halves(fixed, "cells", (1, 2))
+
+    keep_d, send_d = call(
         lambda *refs: hidden_grad_kernel(cells, latent, *refs),
         (blocks,),
         [
@@ -1032,14 +1056,16 @@
             full(norm_par),
             full(lat_row),
             full(recon),
-        ],
-        [
-            ((hidden, rows_all), F32, lane_block(hidden)),
+            (z_all, lane_block(16)),
+            (batch_all, batch_spec),
+        ],
+        [
             new((blocks // 2, 16, width)),
             new((blocks // 2, 16, width)),
         ],
-        scratch=[pltpu.VMEM((2, hidden, 128), F32)],
+        scratch=[pltpu.VMEM((2, hidden, 128), F32), pltpu.VMEM((kinds + 16, hidden), F32)],
         scalars=1,
+        us=5.0,
     )
     if fast:
         got_d = swap(send_d, "genes", 1)
@@ -1053,7 +1079,7 @@
         own_d = lax.psum_scatter(both, "genes", scatter_dimension=0, tiled=True)[0]
     sums_dec = total(sums_dec, "cells")
     d_near, d_far = gather_genes(own_d, fast, blocks, width)
-    dec_part, oh_part = call(
+    (dec_part,) = call(
         lambda *refs: dec_grad_kernel(cells, *refs),
         (blocks,),
         [
@@ -1061,25 +1087,23 @@
             (hid, lane_block(hidden)),
             (mass, full8),
             full(lib8),
-            (dy_dec, lane_block(hidden)),
-            (z_all, lane_block(16)),
-            (batch_all, batch_spec),
             full(dec_acc),
             full(gene_acc),
             full(dig_acc),
             (par, pl.BlockSpec((None, genes, 128), lambda i: (1, 0, 0))),
         ],
-        [new((2 * genes + 8 * gene_lines, hidden)), new((kinds + 16, hidden))],
+        [new((2 * genes + 8 * gene_lines, hidden))],
         scratch=[pltpu.VMEM((genes, hidden + 16), F32)],
-    )
-    oh_part = total(oh_part, "genes")
+        us=5.0,
+    )
     dec_g = total_by_halves(dec_part, "cells", (2, 1))
 
-    rest_rows = 2 * kinds + 16 + 32 + 16
-    enc_part, rest = call(
+    size = (2 * kinds + 64) // 8
+    (enc_part,) = call(
         lambda *refs: enc_back_kernel(cells, latent, fast, *refs),
         (blocks,),
         [
+            (me, None),
             (me, None),
             (d_near, from_all(16)),
             (d_far, from_all(16)),
@@ -1088,47 +1112,41 @@
             full(stat_dec),
             full(norm_par),
             full(lat_row),
-            (near, from_all(32)),
-            (far_pack, from_all(32)),
             (noise_t, lane_block(latent)),
             full(klw),
-            (aff_near, from_all(hidden)),
-            (aff_far, from_all(hidden)),
+            (aff_near, from_all(hidden + 48)),
+            (aff_far, from_all(hidden + 48)),
             (batch_all, batch_spec),
             (logc, lane_block(genes)),
             full(head_cols),
             (z_all, lane_block(16)),
         ],
-        [new((genes, hidden)), new((rest_rows, hidden))],
-        scratch=[pltpu.VMEM((2, hidden, 128), F32)],
-        scalars=1,
-        flops=2 * rows_all * genes * hidden,
-        moved=2 * rows_all * genes,
-    )
-    rest = jnp.concatenate([rest[: kinds + 48], rest[kinds + 48 :] + oh_part])
+        [new((genes + 8 + size, hidden))],
+        scratch=[pltpu.VMEM((2 * kinds + 64, hidden), F32), pltpu.VMEM((2, hidden, 128), F32)],
+        scalars=2,
+        us=11.0,
+    )
     enc_sum = total_by_halves(enc_part, "cells", (1, 2))
-    rest = total_by_halves(rest, "cells", (2, 1))
-
-    enc_g, small_g, head_g, norm_g, square, loss = call(
+    enc_g, tail, loss = call(
         lambda *refs: finish_kernel(cells, latent, *refs),
         (1,),
-        [full(a) for a in (enc_sum, rest, dec_g, fixed, stat_enc, stat_dec, sums_dec, norm_par, kl_row, klw, own_d)],
-        [
-            new((genes, hidden)),
-            new((2 * kinds + 16, hidden)),
-            new((2 * latent, hidden + 1)),
-            new((4, hidden)),
-            new((8, 128)),
-            new((1, share)),
-        ],
-    )
-    square = total(square, "genes")
+        [full(a) for a in (enc_sum, dec_g, fixed, stat_enc, norm_par, kl_row, klw, own_d)],
+        [new((genes, hidden)), new((size + 8, hidden)), new((1, share))],
+    )
+    if fast:
+        tail_near = jnp.stack([tail] + [swap(tail, "genes", 2 * k) for k in (1, 2, 3)])
+        tail_far = swap(tail_near, "genes", 1)
+    else:
+        tails = lax.all_gather(tail, "genes", axis=0)
+        square = jnp.sum(tails[:, size:], axis=0)
+        tails = tails[:8].at[:, size:].set(0.0).at[0, size:].set(square)
+        tail_near, tail_far = tails[0::2], tails[1::2]
 
     state = [
         enc_w, enc_m, enc_v, dec_t, turn(dec_m), turn(dec_v), gene_par, gene_m, gene_v,
         small_w, small_m, small_v, head_t, head_m.T, head_v.T, norm_par, norm_m, norm_v,
     ]
-    ins = [square, enc_g, dec_g, small_g, head_g, norm_g] + state
+    ins = [tail_near, tail_far, enc_g, dec_g, enc_sum, fixed, stat_enc, stat_dec, sums_dec] + state
     outs = []
     for index in range(6):
         one = state[3 * index]
@@ -1137,10 +1155,17 @@
             outs.append((one.shape, BF))
     outs.append(((8, 128), F32))
     res = call(
-        lambda *refs: update_kernel(latent, *refs),
+        lambda *refs: update_kernel(cells, latent, *refs),
         (1,),
-        [full(array) for array in ins],
+        [(me if fast else jnp.zeros_like(me), None)] + [full(array) for array in ins],
         [new(shape, dtype) for shape, dtype in outs],
+        scratch=[
+            pltpu.VMEM((8 * (size + 8), hidden), F32),
+            pltpu.VMEM((2 * kinds + 16, hidden), F32),
+            pltpu.VMEM((2 * latent, hidden + 1), F32),
+            pltpu.VMEM((4, hidden), F32),
+        ],
+        scalars=1,
         mib=16,
     )
     enc_res, dec_res = res[0:4], [turn(part) for part in res[4:8]]

time: 248 us -> 224 us (0.903)
  waiting for transfers between devices: 61.2 us -> 44.9 us
  starting transfers between devices: 62.2 us -> 57.8 us
  Pallas kernels: 104 us -> 100 us
    ppermute x57 -> x51, waiting for transfers between devices: 61.2 us -> 44.9 us  [swap(): return lax.ppermute(value, axis, [(i, i ^ bit) for i in range(count)])]
    ppermute x57 -> x51, starting transfers between devices: 62.2 us -> 57.8 us  [swap(): return lax.ppermute(value, axis, [(i, i ^ bit) for i in range(count)])]
    pallas_call x14, Pallas kernels: 104 us -> 100 us  [call(): pl.pallas_call(kernel, out_shape=[jax.ShapeDtypeStruct(shape, dtype) for...]
    unnamed x106 -> x102, local copies, waits for them, and re-layouts: 15 us -> 14.8 us
  transfers between devices with their start and end apart: 57 -> 51, of which waited for: 29 -> 24; matrix products, arithmetic and copies ran while one was open for 1% -> 0% of each run, Pallas kernels for 23% -> 36%
where the time goes in v3:
time: 224 us; the launch traced here: 223 us
  Pallas kernels  100 us (45%)
  starting transfers between devices  57.8 us (26%)
  waiting for transfers between devices  44.9 us (20%)
  local copies, waits for them, and re-layouts  16.1 us (7%)
    pallas_call x14, Pallas kernels, call(): pl.pallas_call(kernel, out_shape=[jax.ShapeDtypeStruct(shape, dtype) for...  100 us
    ppermute x51, starting transfers between devices, swap(): return lax.ppermute(value, axis, [(i, i ^ bit) for i in range(count)])  57.8 us
    ppermute x51, waiting for transfers between devices, swap(): return lax.ppermute(value, axis, [(i, i ^ bit) for i in range(count)])  44.9 us
    unnamed x102, local copies, waits for them, and re-layouts  14.8 us
  transfers between devices with their start and end apart: 51, of which 24 were waited for; matrix products, arithmetic and copies ran while one was open for 0% of the time, Pallas kernels for 36%

profile of v3, /device:TPU:0, one launch (start us, length us, event | category | flops | bytes accessed | tf_op | source)
XLA Modules:
  0.0 223.2 jit_solution(2719955724802656947)
XLA Ops:
  0.7 2.5 %copy-done = bf16[8192,320]{0,1:T(8,128)(2,1)S(1)} copy-done((bf16[8192,320]{0,1:T(8,128)(2,1)S(1)}, bf16[8192,320]{0,1:T(8,128)(2,1)}, u32[]{:S(2)}) %copy-start) | copy-done | bytes 5242904
  4.1 4.0 %shard_map.399 = (f32[4,128,1024]{2,1,0:T(8,128)S(1)}, bf16[4,128,1024]{2,1,0:T(8,128)(2,1)S(1)}) custom-call(s32[1]{0:T(128)} %bitcast.me_ref.refs_0_.refs_1_, bf16[320,8192]{1,0:T(8,128)(2,1)S(1)} %bitcast.49, f32[320,128]{1,0:T(8,128)S(1)} %copy-done.15), custom_call_target="tpu_custom_call" | custom-call | bytes 14760000 | tf_op jit(solution)/shard_map/pallas_call | solution.py:42
  8.7 2.3 %collective-permute-done.got_ref = bf16[4,128,1024]{2,1,0:T(8,128)(2,1)S(1)} collective-permute-done((bf16[4,128,1024]{2,1,0:T(8,128)(2,1)S(1)}, bf16[4,128,1024]{2,1,0:T(8,128)(2,1)S(1)}, u32[]{:S(2)}, u32[]{:S(2)}) %collective-permute-start) | collective-permute-done | bytes 1048608 | tf_op jit(solution)/shard_map/ppermute | solution.py:59
  11.2 4.0 %collective-permute-start.1 = (bf16[1,128,1024]{2,1,0:T(8,128)(2,1)S(1)}, bf16[1,128,1024]{2,1,0:T(8,128)(2,1)S(1)}, u32[]{:S(2)}, u32[]{:S(2)}) collective-permute-start(bf16[1,128,1024]{2,1,0:T(8,128)(2,1)S(1)} %get-tuple-element.158), channel_id=1, source_target_pairs={{0,4},{1,5},{2,6},{3,7},{4,0},{5,1},{6,2},{7,3},{8,12},{9,13},{10,... | collective-permute-start | bytes 786440 | tf_op jit(solution)/shard_map/ppermute | solution.py:59
  19.8 15.8 %shard_map.401 = (bf16[320,8192]{1,0:T(8,128)(2,1)S(1)}, bf16[320,8192]{1,0:T(8,128)(2,1)S(1)}, f32[8,1024]{1,0:T(8,128)S(1)}, f32[320,128]{1,0:T(8,128)S(1)}, f32[24,128]{1,0:T(8,128)S(1)}) custom-call(bf16[320,8192]{1,0:T(8,128)(2,1)S(1)} %bitcast.50, f32[8,320,128]{2,1,0:T(8,128)S(1)} %get-tuple-element.93.refs_1_, ...), custom_call_target="tpu_custom_call" | custom-call | bytes 55350000 | tf_op jit(solution)/shard_map/pallas_call | solution.py:42
  35.6 2.4 %copy-done.2 = bf16[320,8192]{1,0:T(8,128)(2,1)} copy-done((bf16[320,8192]{1,0:T(8,128)(2,1)}, bf16[320,8192]{1,0:T(8,128)(2,1)S(1)}, u32[]{:S(2)}) %copy-start.2) | copy-done | bytes 5242904
  40.4 3.4 %collective-permute-start.6 = (f32[8,128]{1,0:T(8,128)S(1)}, f32[8,128]{1,0:T(8,128)S(1)}, u32[]{:S(2)}, u32[]{:S(2)}) collective-permute-start(f32[8,128]{1,0:T(8,128)S(1)} %add.135), channel_id=1, source_target_pairs={{0,4},{1,5},{2,6},{3,7},{4,0},{5,1},{6,2},{7,3},{8,12},{9,13},{10,... | collective-permute-start | bytes 12296 | tf_op jit(solution)/shard_map/ppermute | solution.py:59
  45.4 3.8 %collective-permute-done.7 = f32[8,128]{1,0:T(8,128)S(1)} collective-permute-done((f32[8,128]{1,0:T(8,128)S(1)}, f32[8,128]{1,0:T(8,128)S(1)}, u32[]{:S(2)}, u32[]{:S(2)}) %collective-permute-start.7) | collective-permute-done | bytes 4128 | tf_op jit(solution)/shard_map/ppermute | solution.py:59
  52.9 2.4 %collective-permute-done.10 = f32[8,128]{1,0:T(8,128)S(1)} collective-permute-done((f32[8,128]{1,0:T(8,128)S(1)}, f32[8,128]{1,0:T(8,128)S(1)}, u32[]{:S(2)}, u32[]{:S(2)}) %collective-permute-start.10) | collective-permute-done | bytes 4128 | tf_op jit(solution)/shard_map/ppermute | solution.py:59
  57.7 2.0 collective-permute-start.13
  59.7 2.4 %collective-permute-start.11 = (f32[16,1024]{1,0:T(8,128)S(1)}, f32[16,1024]{1,0:T(8,128)S(1)}, u32[]{:S(2)}, u32[]{:S(2)}) collective-permute-start(f32[16,1024]{1,0:T(8,128)S(1)} %get-tuple-element.104), channel_id=1, source_target_pairs={{0,2},{1,3},{2,0},{3,1},{4,6},{5,7},{6,4},{7,5},{8,10},{9,11},{10,... | collective-permute-start | bytes 196616 | tf_op jit(solution)/shard_map/ppermute | solution.py:59
  70.5 2.4 %collective-permute-done.17 = f32[8,128]{1,0:T(8,128)S(1)} collective-permute-done((f32[8,128]{1,0:T(8,128)S(1)}, f32[8,128]{1,0:T(8,128)S(1)}, u32[]{:S(2)}, u32[]{:S(2)}) %collective-permute-start.17) | collective-permute-done | bytes 4128 | tf_op jit(solution)/shard_map/ppermute | solution.py:59
  73.0 9.3 %shard_map.404 = (bf16[128,8192]{1,0:T(8,128)(2,1)S(1)}, f32[128,8192]{1,0:T(8,128)S(1)}, f32[8,1024]{1,0:T(8,128)S(1)}, f32[16,8192]{1,0:T(8,128)S(1)}) custom-call(s32[1]{0:T(128)} %bitcast.me_ref.refs_0_.refs_1_, f32[4,16,1024]{2,1,0:T(8,128)S(1)} %pad_maximum_fusion.1.refs_1_, f32[4,16,1024]{2,1,0:T(8,128)S(1)} %collective-permute-done.14.refs_2_, ...), custom_call_target="tpu_custom_call" | custom-call | bytes 29520000 | tf_op jit(solution)/shard_map/pallas_call | solution.py:42
  82.3 1.9 copy-done.3
  86.3 2.0 collective-permute-start.21
  93.3 2.0 collective-permute-start.39
  98.6 2.5 %copy-done.6 = bf16[320,8192]{1,0:T(8,128)(2,1)S(1)} copy-done((bf16[320,8192]{1,0:T(8,128)(2,1)S(1)}, bf16[320,8192]{1,0:T(8,128)(2,1)}, u32[]{:S(2)}) %copy-start.6) | copy-done | bytes 5242904
  102.8 28.5 %shard_map.405 = (bf16[320,8192]{1,0:T(8,128)(2,1)S(1)}, bf16[320,8192]{1,0:T(8,128)(2,1)S(1)}, bf16[320,8192]{1,0:T(8,128)(2,1)S(1)}, f32[8,1024]{1,0:T(8,128)S...) custom-call(bf16[128,8192]{1,0:T(8,128)(2,1)S(1)} %get-tuple-element.106.refs_0_.hid_ref.refs_4_.refs_1_, ...), custom_call_target="tpu_custom_call" | custom-call | bytes 103320000 | tf_op jit(solution)/shard_map/pallas_call | solution.py:42
  133.5 2.8 %collective-permute-done.22 = f32[8,1024]{1,0:T(8,128)S(1)} collective-permute-done((f32[8,1024]{1,0:T(8,128)S(1)}, f32[8,1024]{1,0:T(8,128)S(1)}, u32[]{:S(2)}, u32[]{:S(2)}) %collective-permute-start.22) | collective-permute-done | bytes 32800 | tf_op jit(solution)/shard_map/ppermute | solution.py:59
  139.7 9.6 %shard_map.406 = (f32[128,8192]{1,0:T(8,128)S(1)}, f32[128,8192]{1,0:T(8,128)S(1)}, f32[640,128]{1,0:T(8,128)S(1)}) custom-call(bf16[320,8192]{1,0:T(8,128)(2,1)S(1)} %get-tuple-element.110.gm_ref, bf16[320,8192]{1,0:T(8,128)(2,1)S(1)} %get-tuple-element.111.gd_ref, bf16[320,8192]{1,0:T(8,128)(2,1)S(1)} %get-tuple-element.112.rt_ref.refs_0_, ...), custom_call_target="tpu_custom_call" | custom-call | bytes 33210000 | tf_op jit(solution)/shard_map/pallas_call | solution.py:42
  149.5 5.6 %shard_map.407 = (f32[4,16,1024]{2,1,0:T(8,128)S(1)}, f32[4,16,1024]{2,1,0:T(8,128)S(1)}) custom-call(s32[1]{0:T(128)} %bitcast.me_ref.refs_0_.refs_1_, f32[128,8192]{1,0:T(8,128)S(1)} %get-tuple-element.114.refs_1_, f32[128,8192]{1,0:T(8,128)S(1)} %get-tuple-element.115.refs_2_, f32[8,1024]{1,0:T(8,128)S(1)} %add_add_fusion.refs_3_.refs_2_, ...), custom_call_target="tpu_custom_call" | custom-call | bytes 18450000 | tf_op jit(solution)/shard_map/pallas_call | solution.py:42
  161.1 5.1 %collective-permute-done.28 = f32[16,1024]{1,0:T(8,128)S(1)} collective-permute-done((f32[16,1024]{1,0:T(8,128)S(1)}, f32[16,1024]{1,0:T(8,128)S(1)}, u32[]{:S(2)}, u32[]{:S(2)}) %collective-permute-start.28) | collective-permute-done | bytes 65568 | tf_op jit(solution)/shard_map/ppermute | solution.py:59
  166.3 2.0 collective-permute-start.32
  170.8 4.4 %shard_map.409 = f32[664,128]{1,0:T(8,128)S(1)} custom-call(bf16[320,8192]{1,0:T(8,128)(2,1)S(1)} %get-tuple-element.112.rt_ref.refs_0_, bf16[128,8192]{1,0:T(8,128)(2,1)S(1)} %get-tuple-element.106.refs_0_.hid_ref.refs_4_.refs_1_, f32[8,1024]{1,0:T(8,128)S(1)} %add_add_fusion.refs_3_.refs_2_, f32[8,1024]{1,0:T(8,128)S(1)} %reshape.69.refs_4_.refs_6_.refs_3_, ...), custom_call_target="tpu_custom_call" | custom-call | bytes 18450000 | tf_op jit(solution)/shard_map/pallas_call | solution.py:42
  177.4 2.0 collective-permute-start.36
  180.7 4.2 %shard_map.410 = f32[480,128]{1,0:T(8,128)S(1)} custom-call(s32[1]{0:T(128)} %bitcast.me_ref.refs_0_.refs_1_, bf16[320,8192]{1,0:T(8,128)(2,1)S(1)} %bitcast.52, bf16[4,176,1024]{2,1,0:T(8,128)(2,1)S(1)} %pad_maximum_fusion.refs_11_.refs_2_, bf16[4,176,1024]{2,1,0:T(8,128)(2,1)S(1)} %collective-permute-done.40.refs_12_.refs_3_, s32[8,1,1024]{2,1,0:T(1,128)S(1)} %bitcast.61, ...), custom_call_target="tpu_custom_call" | custom-call | bytes 14760000 | tf_op jit(solution)/shard_map/pallas_call | solution.py:42
  186.5 11.6 %shard_map.408 = f32[368,128]{1,0:T(8,128)S(1)} custom-call(s32[1]{0:T(128)} %bitcast.me_ref.refs_0_.refs_1_, s32[1]{0:T(128)} %bitcast.me_ref.refs_0_.refs_1_, f32[4,16,1024]{2,1,0:T(8,128)S(1)} %pad_maximum_fusion.2.refs_2_, f32[4,16,1024]{2,1,0:T(8,128)S(1)} %collective-permute-done.33.refs_3_, f32[128,8192]{1,0:T(8,128)S(1)} %copy-done.4, ...), custom_call_target="tpu_custom_call" | custom-call | bytes 40590000 | tf_op jit(solution)/shard_map/pallas_call | solution.py:42
  201.0 4.7 %collective-permute-done.41 = f32[368,128]{1,0:T(8,128)S(1)} collective-permute-done((f32[368,128]{1,0:T(8,128)S(1)}, f32[368,128]{1,0:T(8,128)S(1)}, u32[]{:S(2)}, u32[]{:S(2)}) %collective-permute-start.41) | collective-permute-done | bytes 188448 | tf_op jit(solution)/shard_map/ppermute | solution.py:59
  206.3 5.0 %collective-permute-done.44 = f32[664,128]{1,0:T(8,128)S(1)} collective-permute-done((f32[664,128]{1,0:T(8,128)S(1)}, f32[664,128]{1,0:T(8,128)S(1)}, u32[]{:S(2)}, u32[]{:S(2)}) %collective-permute-start.44) | collective-permute-done | bytes 340000 | tf_op jit(solution)/shard_map/ppermute | solution.py:59
  212.2 2.0 collective-permute-start.49
  214.2 2.4 %collective-permute-start.47 = (f32[48,128]{1,0:T(8,128)S(1)}, f32[48,128]{1,0:T(8,128)S(1)}, u32[]{:S(2)}, u32[]{:S(2)}) collective-permute-start(f32[48,128]{1,0:T(8,128)S(1)} %get-tuple-element.132), channel_id=1, source_target_pairs={{0,2},{1,3},{2,0},{3,1},{4,6},{5,7},{6,4},{7,5},{8,10},{9,11},{10,... | collective-permute-start | bytes 73736 | tf_op jit(solution)/shard_map/ppermute | solution.py:59
  220.5 2.2 shard_map.412
  (217 shorter events, 63.7 us)
Async XLA Ops:
  11.2 26.8 %collective-permute-start.1 = (bf16[1,128,1024]{2,1,0:T(8,128)(2,1)S(1)}, bf16[1,128,1024]{2,1,0:T(8,128)(2,1)S(1)}, u32[]{:S(2)}, u32[]{:S(2)}) collective-permute-start(bf16[1,128,1024]{2,1,0:T(8,128)(2,1)S(1)} %get-tuple-element.158), channel_id=1, source_target_pairs={{0,4},{1,5},{2,6},{3,7},{4,0},{5,1},{6,2},{7,3},{8,12},{9,13},{10,... | collective-permute-start | bytes 786440 | tf_op jit(solution)/shard_map/ppermute | solution.py:59
  15.2 22.8 %collective-permute-start.2 = (bf16[1,128,1024]{2,1,0:T(8,128)(2,1)S(1)}, bf16[1,128,1024]{2,1,0:T(8,128)(2,1)S(1)}, u32[]{:S(2)}, u32[]{:S(2)}) collective-permute-start(bf16[1,128,1024]{2,1,0:T(8,128)(2,1)S(1)} %get-tuple-element.157), channel_id=1, source_target_pairs={{0,6},{1,7},{2,4},{3,5},{4,2},{5,3},{6,0},{7,1},{8,14},{9,15},{10,... | collective-permute-start | bytes 786440 | tf_op jit(solution)/shard_map/ppermute | solution.py:59
  16.6 21.4 %collective-permute-start.3 = (bf16[1,128,1024]{2,1,0:T(8,128)(2,1)S(1)}, bf16[1,128,1024]{2,1,0:T(8,128)(2,1)S(1)}, u32[]{:S(2)}, u32[]{:S(2)}) collective-permute-start(bf16[1,128,1024]{2,1,0:T(8,128)(2,1)S(1)} %get-tuple-element.156), channel_id=1, source_target_pairs={{0,2},{1,3},{2,0},{3,1},{4,6},{5,7},{6,4},{7,5},{8,10},{9,11},{10,... | collective-permute-start | bytes 786440 | tf_op jit(solution)/shard_map/ppermute | solution.py:59
  40.4 5.0 %collective-permute-start.6 = (f32[8,128]{1,0:T(8,128)S(1)}, f32[8,128]{1,0:T(8,128)S(1)}, u32[]{:S(2)}, u32[]{:S(2)}) collective-permute-start(f32[8,128]{1,0:T(8,128)S(1)} %add.135), channel_id=1, source_target_pairs={{0,4},{1,5},{2,6},{3,7},{4,0},{5,1},{6,2},{7,3},{8,12},{9,13},{10,... | collective-permute-start | bytes 12296 | tf_op jit(solution)/shard_map/ppermute | solution.py:59
  43.8 5.4 %collective-permute-start.7 = (f32[8,128]{1,0:T(8,128)S(1)}, f32[8,128]{1,0:T(8,128)S(1)}, u32[]{:S(2)}, u32[]{:S(2)}) collective-permute-start(f32[8,128]{1,0:T(8,128)S(1)} %add.135), channel_id=1, source_target_pairs={{0,6},{1,7},{2,4},{3,5},{4,2},{5,3},{6,0},{7,1},{8,14},{9,15},{10,... | collective-permute-start | bytes 12296 | tf_op jit(solution)/shard_map/ppermute | solution.py:59
  57.7 6.1 %collective-permute-start.13 = (f32[16,1024]{1,0:T(8,128)S(1)}, f32[16,1024]{1,0:T(8,128)S(1)}, u32[]{:S(2)}, u32[]{:S(2)}) collective-permute-start(f32[16,1024]{1,0:T(8,128)S(1)} %get-tuple-element.104), channel_id=1, source_target_pairs={{0,6},{1,7},{2,4},{3,5},{4,2},{5,3},{6,0},{7,1},{8,14},{9,15},{10,... | collective-permute-start | bytes 196616 | tf_op jit(solution)/shard_map/ppermute | solution.py:59
  59.7 5.5 %collective-permute-start.12 = (f32[16,1024]{1,0:T(8,128)S(1)}, f32[16,1024]{1,0:T(8,128)S(1)}, u32[]{:S(2)}, u32[]{:S(2)}) collective-permute-start(f32[16,1024]{1,0:T(8,128)S(1)} %get-tuple-element.104), channel_id=1, source_target_pairs={{0,4},{1,5},{2,6},{3,7},{4,0},{5,1},{6,2},{7,3},{8,12},{9,13},{10,... | collective-permute-start | bytes 196616 | tf_op jit(solution)/shard_map/ppermute | solution.py:59
  59.7 5.5 %collective-permute-start.11 = (f32[16,1024]{1,0:T(8,128)S(1)}, f32[16,1024]{1,0:T(8,128)S(1)}, u32[]{:S(2)}, u32[]{:S(2)}) collective-permute-start(f32[16,1024]{1,0:T(8,128)S(1)} %get-tuple-element.104), channel_id=1, source_target_pairs={{0,2},{1,3},{2,0},{3,1},{4,6},{5,7},{6,4},{7,5},{8,10},{9,11},{10,... | collective-permute-start | bytes 196616 | tf_op jit(solution)/shard_map/ppermute | solution.py:59
  86.3 5.9 %collective-permute-start.21 = (f32[8,1024]{1,0:T(8,128)S(1)}, f32[8,1024]{1,0:T(8,128)S(1)}, u32[]{:S(2)}, u32[]{:S(2)}) collective-permute-start(f32[8,1024]{1,0:T(8,128)S(1)} %log_add_fusion.1), channel_id=1, source_target_pairs={{0,6},{1,7},{2,4},{3,5},{4,2},{5,3},{6,0},{7,1},{8,14},{9,15},{10,... | collective-permute-start | bytes 98312 | tf_op jit(solution)/shard_map/ppermute | solution.py:59
  93.3 38.0 %collective-permute-start.39 = (bf16[176,1024]{1,0:T(8,128)(2,1)}, bf16[176,1024]{1,0:T(8,128)(2,1)}, u32[]{:S(2)}, u32[]{:S(2)}) collective-permute-start(bf16[176,1024]{1,0:T(8,128)(2,1)} %get-tuple-element.124), channel_id=1, source_target_pairs={{0,6},{1,7},{2,4},{3,5},{4,2},{5,3},{6,0},{7,1},{8,14},{9,15},{10,... | collective-permute-start | bytes 1081352 | tf_op jit(solution)/shard_map/ppermute | solution.py:59
  95.3 36.0 %collective-permute-start.38 = (bf16[176,1024]{1,0:T(8,128)(2,1)}, bf16[176,1024]{1,0:T(8,128)(2,1)}, u32[]{:S(2)}, u32[]{:S(2)}) collective-permute-start(bf16[176,1024]{1,0:T(8,128)(2,1)} %get-tuple-element.124), channel_id=1, source_target_pairs={{0,4},{1,5},{2,6},{3,7},{4,0},{5,1},{6,2},{7,3},{8,12},{9,13},{10,... | collective-permute-start | bytes 1081352 | tf_op jit(solution)/shard_map/ppermute | solution.py:59
  96.2 35.1 %collective-permute-start.37 = (bf16[176,1024]{1,0:T(8,128)(2,1)}, bf16[176,1024]{1,0:T(8,128)(2,1)}, u32[]{:S(2)}, u32[]{:S(2)}) collective-permute-start(bf16[176,1024]{1,0:T(8,128)(2,1)} %get-tuple-element.124), channel_id=1, source_target_pairs={{0,2},{1,3},{2,0},{3,1},{4,6},{5,7},{6,4},{7,5},{8,10},{9,11},{10,... | collective-permute-start | bytes 1081352 | tf_op jit(solution)/shard_map/ppermute | solution.py:59
  132.9 46.5 %collective-permute-start.40 = (bf16[4,176,1024]{2,1,0:T(8,128)(2,1)S(1)}, bf16[4,176,1024]{2,1,0:T(8,128)(2,1)S(1)}, u32[]{:S(2)}, u32[]{:S(2)}) collective-permute-start(bf16[4,176,1024]{2,1,0:T(8,128)(2,1)S(1)} %pad_maximum_fusion.refs_11_.refs_2_), channel_id=1, source_target_pairs={{0,1},{1,0},{2,3},{3,2},{4,5},{5,4},{6,7},{7,6},{8,9},{9,8},{10,11... | collective-permute-start | bytes 4325384 | tf_op jit(solution)/shard_map/ppermute | solution.py:59
  136.2 13.1 %collective-permute-start.24 = (f32[8,1024]{1,0:T(8,128)S(1)}, f32[8,1024]{1,0:T(8,128)S(1)}, u32[]{:S(2)}, u32[]{:S(2)}) collective-permute-start(f32[8,1024]{1,0:T(8,128)S(1)} %add.152), channel_id=1, source_target_pairs={{0,4},{1,5},{2,6},{3,7},{4,0},{5,1},{6,2},{7,3},{8,12},{9,13},{10,... | collective-permute-start | bytes 98312 | tf_op jit(solution)/shard_map/ppermute | solution.py:59
  137.2 12.2 %collective-permute-start.25 = (f32[8,1024]{1,0:T(8,128)S(1)}, f32[8,1024]{1,0:T(8,128)S(1)}, u32[]{:S(2)}, u32[]{:S(2)}) collective-permute-start(f32[8,1024]{1,0:T(8,128)S(1)} %add.152), channel_id=1, source_target_pairs={{0,6},{1,7},{2,4},{3,5},{4,2},{5,3},{6,0},{7,1},{8,14},{9,15},{10,... | collective-permute-start | bytes 98312 | tf_op jit(solution)/shard_map/ppermute | solution.py:59
  139.1 10.3 %collective-permute-start.23 = (f32[8,1024]{1,0:T(8,128)S(1)}, f32[8,1024]{1,0:T(8,128)S(1)}, u32[]{:S(2)}, u32[]{:S(2)}) collective-permute-start(f32[8,1024]{1,0:T(8,128)S(1)} %add.152), channel_id=1, source_target_pairs={{0,2},{1,3},{2,0},{3,1},{4,6},{5,7},{6,4},{7,5},{8,10},{9,11},{10,... | collective-permute-start | bytes 98312 | tf_op jit(solution)/shard_map/ppermute | solution.py:59
  158.1 8.1 %collective-permute-start.28 = (f32[16,1024]{1,0:T(8,128)S(1)}, f32[16,1024]{1,0:T(8,128)S(1)}, u32[]{:S(2)}, u32[]{:S(2)}) collective-permute-start(f32[16,1024]{1,0:T(8,128)S(1)} %get-tuple-element.160), channel_id=1, source_target_pairs={{0,4},{1,5},{2,6},{3,7},{4,0},{5,1},{6,2},{7,3},{8,12},{9,13},{10,... | collective-permute-start | bytes 196616 | tf_op jit(solution)/shard_map/ppermute | solution.py:59
  159.3 7.0 %collective-permute-start.29 = (f32[16,1024]{1,0:T(8,128)S(1)}, f32[16,1024]{1,0:T(8,128)S(1)}, u32[]{:S(2)}, u32[]{:S(2)}) collective-permute-start(f32[16,1024]{1,0:T(8,128)S(1)} %get-tuple-element.159), channel_id=1, source_target_pairs={{0,6},{1,7},{2,4},{3,5},{4,2},{5,3},{6,0},{7,1},{8,14},{9,15},{10,... | collective-permute-start | bytes 196616 | tf_op jit(solution)/shard_map/ppermute | solution.py:59
  166.3 10.0 %collective-permute-start.32 = (f32[16,1024]{1,0:T(8,128)S(1)}, f32[16,1024]{1,0:T(8,128)S(1)}, u32[]{:S(2)}, u32[]{:S(2)}) collective-permute-start(f32[16,1024]{1,0:T(8,128)S(1)} %fusion.5.refs_7_), channel_id=1, source_target_pairs={{0,6},{1,7},{2,4},{3,5},{4,2},{5,3},{6,0},{7,1},{8,14},{9,15},{10,... | collective-permute-start | bytes 196616 | tf_op jit(solution)/shard_map/ppermute | solution.py:59
  168.3 7.9 %collective-permute-start.31 = (f32[16,1024]{1,0:T(8,128)S(1)}, f32[16,1024]{1,0:T(8,128)S(1)}, u32[]{:S(2)}, u32[]{:S(2)}) collective-permute-start(f32[16,1024]{1,0:T(8,128)S(1)} %fusion.5.refs_7_), channel_id=1, source_target_pairs={{0,4},{1,5},{2,6},{3,7},{4,0},{5,1},{6,2},{7,3},{8,12},{9,13},{10,... | collective-permute-start | bytes 196616 | tf_op jit(solution)/shard_map/ppermute | solution.py:59
  169.2 7.1 %collective-permute-start.30 = (f32[16,1024]{1,0:T(8,128)S(1)}, f32[16,1024]{1,0:T(8,128)S(1)}, u32[]{:S(2)}, u32[]{:S(2)}) collective-permute-start(f32[16,1024]{1,0:T(8,128)S(1)} %fusion.5.refs_7_), channel_id=1, source_target_pairs={{0,2},{1,3},{2,0},{3,1},{4,6},{5,7},{6,4},{7,5},{8,10},{9,11},{10,... | collective-permute-start | bytes 196616 | tf_op jit(solution)/shard_map/ppermute | solution.py:59
  175.2 23.5 %collective-permute-start.43 = (f32[664,128]{1,0:T(8,128)S(1)}, f32[664,128]{1,0:T(8,128)S(1)}, u32[]{:S(2)}, u32[]{:S(2)}) collective-permute-start(f32[664,128]{1,0:T(8,128)S(1)} %shard_map.409), channel_id=1, source_target_pairs={{0,16},{8,24},{16,0},{24,8},{1,17},{9,25},{17,1},{25,9},{2,18},{10... | collective-permute-start | bytes 1019912 | tf_op jit(solution)/shard_map/ppermute | solution.py:59
  176.3 10.2 %collective-permute-start.33 = (f32[4,16,1024]{2,1,0:T(8,128)S(1)}, f32[4,16,1024]{2,1,0:T(8,128)S(1)}, u32[]{:S(2)}, u32[]{:S(2)}) collective-permute-start(f32[4,16,1024]{2,1,0:T(8,128)S(1)} %pad_maximum_fusion.2.refs_2_), channel_id=1, source_target_pairs={{0,1},{1,0},{2,3},{3,2},{4,5},{5,4},{6,7},{7,6},{8,9},{9,8},{10,11... | collective-permute-start | bytes 786440 | tf_op jit(solution)/shard_map/ppermute | solution.py:59
  176.4 8.5 %collective-permute-start.35 = (f32[8,128]{1,0:T(8,128)S(1)}, f32[8,128]{1,0:T(8,128)S(1)}, u32[]{:S(2)}, u32[]{:S(2)}) collective-permute-start(f32[8,128]{1,0:T(8,128)S(1)} %slice.81), channel_id=1, source_target_pairs={{0,16},{8,24},{16,0},{24,8},{1,17},{9,25},{17,1},{25,9},{2,18},{10... | collective-permute-start | bytes 12296 | tf_op jit(solution)/shard_map/ppermute | solution.py:59
  177.4 9.0 %collective-permute-start.36 = (f32[8,128]{1,0:T(8,128)S(1)}, f32[8,128]{1,0:T(8,128)S(1)}, u32[]{:S(2)}, u32[]{:S(2)}) collective-permute-start(f32[8,128]{1,0:T(8,128)S(1)} %slice.81), channel_id=1, source_target_pairs={{0,24},{8,16},{16,8},{24,0},{1,25},{9,17},{17,9},{25,1},{2,26},{10... | collective-permute-start | bytes 12296 | tf_op jit(solution)/shard_map/ppermute | solution.py:59
  179.4 7.1 %collective-permute-start.34 = (f32[8,128]{1,0:T(8,128)S(1)}, f32[8,128]{1,0:T(8,128)S(1)}, u32[]{:S(2)}, u32[]{:S(2)}) collective-permute-start(f32[8,128]{1,0:T(8,128)S(1)} %slice.81), channel_id=1, source_target_pairs={{0,8},{8,0},{16,24},{24,16},{1,9},{9,1},{17,25},{25,17},{2,10},{10... | collective-permute-start | bytes 12296 | tf_op jit(solution)/shard_map/ppermute | solution.py:59
  184.9 15.3 %collective-permute-start.45 = (f32[480,128]{1,0:T(8,128)S(1)}, f32[480,128]{1,0:T(8,128)S(1)}, u32[]{:S(2)}, u32[]{:S(2)}) collective-permute-start(f32[480,128]{1,0:T(8,128)S(1)} %shard_map.410), channel_id=1, source_target_pairs={{0,8},{8,0},{16,24},{24,16},{1,9},{9,1},{17,25},{25,17},{2,10},{10... | collective-permute-start | bytes 737288 | tf_op jit(solution)/shard_map/ppermute | solution.py:59
  198.1 7.7 %collective-permute-start.41 = (f32[368,128]{1,0:T(8,128)S(1)}, f32[368,128]{1,0:T(8,128)S(1)}, u32[]{:S(2)}, u32[]{:S(2)}) collective-permute-start(f32[368,128]{1,0:T(8,128)S(1)} %shard_map.408), channel_id=1, source_target_pairs={{0,8},{8,0},{16,24},{24,16},{1,9},{9,1},{17,25},{25,17},{2,10},{10... | collective-permute-start | bytes 565256 | tf_op jit(solution)/shard_map/ppermute | solution.py:59
  198.7 12.6 %collective-permute-start.44 = (f32[664,128]{1,0:T(8,128)S(1)}, f32[664,128]{1,0:T(8,128)S(1)}, u32[]{:S(2)}, u32[]{:S(2)}) collective-permute-start(f32[664,128]{1,0:T(8,128)S(1)} %add.172), channel_id=1, source_target_pairs={{0,8},{8,0},{16,24},{24,16},{1,9},{9,1},{17,25},{25,17},{2,10},{10... | collective-permute-start | bytes 1019912 | tf_op jit(solution)/shard_map/ppermute | solution.py:59
  200.5 11.0 %collective-permute-start.46 = (f32[480,128]{1,0:T(8,128)S(1)}, f32[480,128]{1,0:T(8,128)S(1)}, u32[]{:S(2)}, u32[]{:S(2)}) collective-permute-start(f32[480,128]{1,0:T(8,128)S(1)} %add.174), channel_id=1, source_target_pairs={{0,16},{8,24},{16,0},{24,8},{1,17},{9,25},{17,1},{25,9},{2,18},{10... | collective-permute-start | bytes 737288 | tf_op jit(solution)/shard_map/ppermute | solution.py:59
  205.8 5.6 %collective-permute-start.42 = (f32[368,128]{1,0:T(8,128)S(1)}, f32[368,128]{1,0:T(8,128)S(1)}, u32[]{:S(2)}, u32[]{:S(2)}) collective-permute-start(f32[368,128]{1,0:T(8,128)S(1)} %add.170), channel_id=1, source_target_pairs={{0,16},{8,24},{16,0},{24,8},{1,17},{9,25},{17,1},{25,9},{2,18},{10... | collective-permute-start | bytes 565256 | tf_op jit(solution)/shard_map/ppermute | solution.py:59
  212.2 5.6 %collective-permute-start.49 = (f32[48,128]{1,0:T(8,128)S(1)}, f32[48,128]{1,0:T(8,128)S(1)}, u32[]{:S(2)}, u32[]{:S(2)}) collective-permute-start(f32[48,128]{1,0:T(8,128)S(1)} %get-tuple-element.132), channel_id=1, source_target_pairs={{0,6},{1,7},{2,4},{3,5},{4,2},{5,3},{6,0},{7,1},{8,14},{9,15},{10,... | collective-permute-start | bytes 73736 | tf_op jit(solution)/shard_map/ppermute | solution.py:59
  (70 other events, 750.0 us)

commit v4 on v3

--- a/solution.py
+++ b/solution.py
@@ -38,15 +38,19 @@
     return pl.BlockSpec(shape, lambda *_: (0,) * len(shape))
 
 
+def in_hbm(array):
+    return pltpu.with_memory_space_constraint(array, pltpu.HBM)
+
+
 def call(kernel, grid, ins, outs, scratch=(), scalars=0, us=2.0, mib=12):
     return pl.pallas_call(
         kernel,
-        out_shape=[jax.ShapeDtypeStruct(shape, dtype) for shape, dtype, _ in outs],
+        out_shape=[pltpu.HBM(out[0], out[1]) if len(out) == 4 else jax.ShapeDtypeStruct(out[0], out[1]) for out in outs],
         grid_spec=pltpu.PrefetchScalarGridSpec(
             num_scalar_prefetch=scalars,
             grid=grid,
             in_specs=[spec for _, spec in ins[scalars:]],
-            out_specs=[spec for _, _, spec in outs],
+            out_specs=[out[2] for out in outs],
             scratch_shapes=list(scratch),
         ),
         compiler_params=pltpu.CompilerParams(vmem_limit_bytes=mib * 1024 * 1024),
@@ -125,7 +129,7 @@
     return jnp.transpose(rows)
 
 
-def prep_kernel(gene_ref, mask_ref, dec_ref, small_ref, head_ref, norm_ref, aug_ref, turn_ref, par_ref, lg_ref, dg_ref, enc_out, dec_out, lat_out, head_out, bias_out, cols_out, norm_out):
+def prep_kernel(gene_ref, mask_ref, dec_ref, small_ref, head_ref, norm_ref, aug_ref, turn_ref, par_ref, lg_ref, dg_ref, enc_out, dec_out, plain_out, lat_out, head_out, bias_out, cols_out, norm_out):
     genes = gene_ref.shape[1]
     hidden = norm_ref.shape[1]
     latent = head_ref.shape[0] // 2
@@ -173,8 +177,10 @@
     for index in range(latent):
         lat_row = jnp.where(row == index, small_ref[2 * kinds + index : 2 * kinds + index + 1, :], lat_row)
     lat_out[...] = lat_row
-    batch_pieces = three(jnp.transpose(small_ref[kinds : 2 * kinds, :]))
-    lat = three(jnp.transpose(lat_row))
+    batch_turned, lat_turned = jnp.transpose(small_ref[kinds : 2 * kinds, :]), jnp.transpose(lat_row)
+    plain_out[...] = jnp.concatenate((batch_turned, lat_turned), axis=1)
+    batch_pieces = three(batch_turned)
+    lat = three(lat_turned)
     zero = jnp.zeros_like(lat[0])
     tails = ((lat[0], lat[0], lat[0]), (lat[1], lat[1], zero), (lat[2], zero, zero))
     for index in range(3):
@@ -190,8 +196,7 @@
     head_out[...] = head
     bias_out[...] = jnp.broadcast_to(bias, (32, 128))
     high, mid, _ = three(jnp.transpose(head))
-    cols_out[0:hidden, :] = jnp.concatenate((high, high), axis=1)
-    cols_out[hidden : 2 * hidden, :] = jnp.concatenate((mid, jnp.zeros_like(mid)), axis=1)
+    cols_out[...] = jnp.concatenate((high, high, mid), axis=1)
     norm_out[...] = jnp.transpose(jnp.concatenate((norm_ref[...], norm_ref[...]), axis=0))
 
 
@@ -216,24 +221,30 @@
     return jnp.where(row == at, sums, jnp.where(row == at + 1, squares, 0.0))
 
 
-def enc_kernel(me_ref, x_ref, w_ref, keep_ref, send_ref, turn_ref):
-    step = pl.program_id(0)
-
-    @pl.when(step == 0)
-    def _():
-        turn_ref[...] = jnp.transpose(w_ref[...]).astype(BF)
-
-    log_counts = jnp.log(1.0 + x_ref[...].astype(F32)).astype(BF)
-    part = nn(turn_ref[...], log_counts)
-    odd = lax.rem(step, 2)
-
-    @pl.when(odd == 0)
-    def _():
-        keep_ref[0] = part
-
-    @pl.when(odd == 1)
-    def _():
-        send_ref[0] = part.astype(BF)
+def enc_kernel(low, me_ref, x_ref, w_ref, keep_ref, send_ref, buffer_ref, turn_ref, arrived):
+    count, _, share = buffer_ref.shape
+
+    def block(i):
+        at = pl.multiple_of(((low + i) ^ me_ref[0]) * share, share)
+        return pltpu.make_async_copy(x_ref.at[:, pl.ds(at, share)], buffer_ref.at[i], arrived.at[i])
+
+    for i in range(count):
+        block(i).start()
+    turn_ref[...] = jnp.transpose(w_ref[...]).astype(BF)
+
+    def pair(half, carry):
+        for odd in range(2):
+            i = 2 * half + odd
+            block(i).wait()
+            log_counts = jnp.log(1.0 + buffer_ref[i].astype(F32)).astype(BF)
+            part = nn(turn_ref[...], log_counts)
+            if odd:
+                send_ref[half] = part.astype(BF)
+            else:
+                keep_ref[half] = part
+        return carry
+
+    lax.fori_loop(0, count // 2, pair, 0)
 
 
 def lines(rows8, count):
@@ -243,7 +254,7 @@
     return jnp.concatenate([rows8[:, i * 128 : (i + 1) * 128] for i in range(count)], axis=0)
 
 
-def counts_kernel(rows, span, x_ref, lg_ref, dg_ref, keep_ref, logc_ref, mask_ref, cell_ref, disp_ref, line_ref, sum_ref):
+def counts_kernel(rows, span, x_ref, lg_ref, dg_ref, keep_ref, batch_ref, logc_ref, mask_ref, side_ref, cell_ref, disp_ref, line_ref, held_ref, sum_ref):
     step = pl.program_id(0)
     genes, width = x_ref.shape
 
@@ -251,7 +262,14 @@
     def _():
         disp_ref[...] = jnp.zeros_like(disp_ref)
         sum_ref[...] = jnp.zeros_like(sum_ref)
-
+        held_ref[...] = jnp.zeros_like(held_ref)
+
+    kinds = held_ref.shape[0]
+    table = one_hot(batch_ref[0], kinds)
+    held_ref[...] += sum(table[:, t : t + 128] for t in range(0, width, 128))
+    row = lax.broadcasted_iota(jnp.int32, (16, width), 0)
+    side_ref[0:kinds, :] = table.astype(BF)
+    side_ref[kinds:, :] = jnp.where(row == 0, 1.0, 0.0).astype(BF)
     tiles = span // 128
     done = []
     for first in range(0, width, span):
@@ -289,7 +307,9 @@
 
     @pl.when(step == pl.num_programs(0) - 1)
     def _():
-        line_ref[...] = lines(row_sums(sum_ref[...]), line_ref.shape[0] // 8)
+        most = line_ref.shape[0] - 8
+        line_ref[0:most, :] = lines(row_sums(sum_ref[...]), most // 8)
+        line_ref[most:, :] = row_sums(held_ref[...])
 
 
 def own_kernel(me_ref, keep_ref, got_ref, one_ref, two_ref, six_ref, batch_ref, enc_b_ref, pre_ref, stat_ref):
@@ -343,29 +363,54 @@
     return jnp.concatenate((z, jnp.zeros((16 - z.shape[0], z.shape[1]), F32)), axis=0)
 
 
+def part_of(step, width):
+    return pl.ds(pl.multiple_of(step * width, 128), width)
+
+
+def relu_low(affine):
+    return jnp.maximum(affine, jnp.zeros_like(affine))
+
+
 def pick(step, me_ref, fast, near_ref, far_ref):
     if not fast:
-        return near_ref[0]
-    return jnp.where(lax.rem(step ^ me_ref[0], 2) == 0, near_ref[0], far_ref[0])
-
-
-def decode_kernel(cells, latent, fast, me_ref, near_ref, far_ref, batch_ref, stat_ref, norm_ref, dec_b_ref, w_ref, hid_ref, phat_ref, lse_ref, z_ref, score_ref):
-    kinds = dec_b_ref.shape[1] - 48
+        return near_ref[step]
+    place = step ^ me_ref[0]
+    return jnp.where(lax.rem(place, 2) == 0, near_ref[lax.div(place, 2)], far_ref[lax.div(place, 2)])
+
+
+def decode_kernel(cells, latent, fast, me_ref, near_ref, far_ref, side_ref, stat_ref, norm_ref, plain_ref, w_ref, aff_ref, lse_ref, z_ref, score_ref, left_ref):
+    kinds = plain_ref.shape[1] - 16
     step = pl.program_id(0)
+    cells_at = part_of(step, score_ref.shape[1])
     genes = score_ref.shape[0]
-    mean, inv = norm_columns(stat_ref[...], latent - 8, cells)
+    hidden_rows = aff_ref.shape[0]
+
+    @pl.when(step == 0)
+    def _():
+        mean, inv = norm_columns(stat_ref[...], latent - 8, cells)
+        scaled = norm_ref[:, 2:3] * inv
+        weights = plain_ref[...] * scaled
+        high, mid, _ = three(weights)
+        lane = lax.broadcasted_iota(jnp.int32, (hidden_rows, 16), 1)
+        shift = jnp.broadcast_to(norm_ref[:, 3:4] - scaled * mean, (hidden_rows, 16))
+        one, two, rest = (part.astype(F32) for part in three(shift))
+        tail = jnp.where(lane == 0, one, jnp.where(lane == 1, two, jnp.where(lane == 2, rest, 0.0))).astype(BF)
+        zero = jnp.zeros_like(tail)
+        left_ref[:hidden_rows, :] = jnp.concatenate((high, high[:, kinds:], tail), axis=1)
+        left_ref[hidden_rows:, :] = jnp.concatenate((mid, zero, zero), axis=1)
+
     z = pick(step, me_ref, fast, near_ref, far_ref)
     z = jnp.where(lax.broadcasted_iota(jnp.int32, z.shape, 0) < latent, z, 0.0)
-    z_ref[...] = z
-    pre_dec = exact_rows(dec_b_ref[...], dec_table(z, batch_ref[0], kinds))
-    phat = (pre_dec - mean) * inv
-    phat_ref[...] = phat
-    hidden = jnp.maximum(norm_ref[:, 2:3] * phat + norm_ref[:, 3:4], 0.0).astype(BF)
-    hid_ref[...] = hidden
+    z_ref[:, cells_at] = z
+    z_high, z_mid, _ = three(z)
+    ones = jnp.where(lax.broadcasted_iota(jnp.int32, z.shape, 0) < 3, 1.0, 0.0).astype(BF)
+    table = jnp.concatenate((side_ref[0:kinds, cells_at], z_high, z_mid, ones), axis=0)
+    both = nn(left_ref[...], table)
+    affine = (both[:hidden_rows] + both[hidden_rows:]).astype(BF)
+    aff_ref[:, cells_at] = affine
+    hidden = relu_low(affine)
     width = score_ref.shape[1]
-    row = lax.broadcasted_iota(jnp.int32, (16, width), 0)
-    table = jnp.concatenate((hidden, jnp.where(row < 3, 1.0, 0.0).astype(BF)), axis=0)
-    score_ref[...] = nn(w_ref[...], table)
+    score_ref[...] = nn(w_ref[...], jnp.concatenate((hidden, ones), axis=0))
     tiles = width // 128
     rows = 32
 
@@ -380,7 +425,7 @@
             new.append(part)
         return tuple(new)
 
-    best = lax.fori_loop(0, genes // rows, top, tuple(jnp.full((8, 128), -3e38, F32) for _ in range(tiles)))
+    best = lax.fori_loop(0, genes // rows, top, tuple(jnp.full((8, 128), -3e38, F32) for _ in range(tiles)), unroll=5)
     high = [jnp.max(part, axis=0, keepdims=True) for part in best]
     wide = [jnp.broadcast_to(part, (8, 128)) for part in high]
 
@@ -395,29 +440,28 @@
             new.append(part)
         return tuple(new)
 
-    sums = lax.fori_loop(0, genes // rows, mass, tuple(jnp.zeros((8, 128), F32) for _ in range(tiles)))
+    sums = lax.fori_loop(0, genes // rows, mass, tuple(jnp.zeros((8, 128), F32) for _ in range(tiles)), unroll=5)
     lse = [high[tile] + jnp.log(jnp.sum(sums[tile], axis=0, keepdims=True)) for tile in range(tiles)]
     lse_ref[pl.ds(step, 1), :] = jnp.concatenate(lse, axis=1)
 
 
-def enc_sums_kernel(fast, me_ref, logc_ref, near_ref, far_ref, batch_ref, lines_ref, out_ref):
+def enc_sums_kernel(fast, me_ref, logc_ref, near_ref, far_ref, side_ref, lines_ref, out_ref):
     step = pl.program_id(0)
     genes = logc_ref.shape[0]
-    kinds = out_ref.shape[0] - genes - lines_ref.shape[0] - 8
+    kinds = side_ref.shape[0] - 16
 
     @pl.when(step == 0)
     def _():
         out_ref[...] = jnp.zeros_like(out_ref)
-        out_ref[genes + kinds : genes + kinds + lines_ref.shape[0], :] = lines_ref[...]
-
+        out_ref[genes + kinds :, :] = lines_ref[...]
+
+    cells_at = part_of(step, near_ref.shape[2])
     affine = pick(step, me_ref, fast, near_ref, far_ref)[: out_ref.shape[1]]
-    table = one_hot(batch_ref[0], kinds).astype(BF)
-    out_ref[0:genes, :] += nt(logc_ref[...], affine)
-    out_ref[genes : genes + kinds, :] += nt(table, affine)
-    out_ref[genes + kinds + lines_ref.shape[0] :, :] += nt(jnp.ones((8, table.shape[1]), BF), table)
-
-
-def zinb_kernel(rows, span, hid_ref, w_ref, x_ref, par_ref, lib_ref, lse_ref, gam_ref, gm_ref, gd_ref, rt_ref, mass_ref, recon_ref, acc_ref, sc_ref):
+    out_ref[0:genes, :] += nt(logc_ref[:, cells_at], affine)
+    out_ref[genes : genes + kinds, :] += nt(side_ref[0:kinds, cells_at], affine)
+
+
+def zinb_kernel(rows, span, hid_ref, w_ref, x_ref, par_ref, lib_ref, lse_ref, gam_ref, g_ref, rt_ref, mass_ref, recon_ref, acc_ref, sc_ref):
     step = pl.program_id(0)
     genes, width = x_ref.shape
 
@@ -431,12 +475,13 @@
     row = lax.broadcasted_iota(jnp.int32, (16, width), 0)
     hi, mid, lo = three(shift)
     extra = jnp.where(row < 3, 1.0, jnp.where(row == 3, hi.astype(F32), jnp.where(row == 4, mid.astype(F32), jnp.where(row == 5, lo.astype(F32), 0.0))))
-    table = jnp.concatenate((hid_ref[...], extra.astype(BF)), axis=0)
+    table = jnp.concatenate((relu_low(hid_ref[:, part_of(step, width)]), extra.astype(BF)), axis=0)
     sc_ref[...] = nn(w_ref[...], table)
     tiles = span // 128
     mass_out, recon_out = [], []
     for first in range(0, width, span):
         lanes = [slice(first + tile * 128, first + (tile + 1) * 128) for tile in range(tiles)]
+        far_lanes = [pl.ds(pl.multiple_of(step * width + first + tile * 128, 128), 128) for tile in range(tiles)]
         def chunk(g, state):
             at = pl.ds(pl.multiple_of(g * rows, rows), rows)
             at_drop = pl.ds(pl.multiple_of(genes + g * rows, rows), rows)
@@ -466,9 +511,9 @@
                 g_mean = mu * (x * (1.0 / mu_eps) - y)
                 g_drop = jnp.where(drop >= 0.0, ed, 1.0) * rd - w0
                 g_disp = w0 * (gap + part_th) - y
-                gm_ref[at, lanes[tile]] = g_mean.astype(BF)
-                gd_ref[at, lanes[tile]] = g_drop.astype(BF)
-                rt_ref[at, lanes[tile]] = mu.astype(BF)
+                g_ref[at, far_lanes[tile]] = g_mean.astype(BF)
+                g_ref[at_drop, far_lanes[tile]] = g_drop.astype(BF)
+                rt_ref[at, far_lanes[tile]] = mu.astype(BF)
                 sums = [a + b for a, b in zip(sums, (g_mean, g_drop, g_disp))]
                 for part in range(rows // 8):
                     sub = slice(part * 8, (part + 1) * 8)
@@ -490,62 +535,43 @@
     recon_ref[one_row, :] = jnp.concatenate(recon_out, axis=1) + gam_row
 
 
-def back_kernel(gm_ref, gd_ref, rt_ref, hid_ref, w_ref, a_ref, r_ref, g_ref):
-    genes = gm_ref.shape[0]
-
-    @pl.when(pl.program_id(0) == 0)
+def back_kernel(width, g_in_ref, rt_ref, aff_ref, w_ref, a_ref, r_ref, g_ref):
+    genes = rt_ref.shape[0]
+    step = pl.program_id(0)
+    cells_at = part_of(step, width)
+
+    @pl.when(step == 0)
     def _():
         g_ref[...] = jnp.zeros_like(g_ref)
 
-    gm, gd, rt, hid = gm_ref[...], gd_ref[...], rt_ref[...], hid_ref[...]
-    scale_w = w_ref[:, :genes]
-    a_ref[...] = nn(scale_w, gm) + nn(w_ref[:, genes:], gd)
-    r_ref[...] = nn(scale_w, rt)
-    g_ref[:genes, :] += nt(gm, hid)
-    g_ref[genes:, :] += nt(gd, hid)
-
-
-def hidden_grad_kernel(cells, latent, me_ref, a_ref, r_ref, mass_ref, hid_ref, phat_ref, lib_ref, stat_ref, gain_ref, lat_ref, recon_ref, z_ref, batch_ref, keep_ref, send_ref, sum_ref, oh_ref):
+    a_ref[:, cells_at] = nn(w_ref[...], g_in_ref[:, cells_at])
+    r_ref[:, cells_at] = nn(w_ref[:, :genes], rt_ref[:, cells_at])
+    g_ref[...] += nt(g_in_ref[:, cells_at], relu_low(aff_ref[:, cells_at]))
+
+
+def hidden_grad_kernel(cells, latent, me_ref, a_ref, r_ref, mass_ref, aff_ref, lib_ref, stat_ref, gain_ref, lat_ref, recon_ref, z_ref, side_ref, keep_ref, send_ref, lane_ref, oh_ref):
     step = pl.program_id(0)
     steps = pl.num_programs(0)
     place = step ^ me_ref[0]
+    hidden, width = a_ref.shape[0], mass_ref.shape[1]
+    cells_at = part_of(step, width)
+    kinds = side_ref.shape[0] - 16
 
     @pl.when(step == 0)
     def _():
-        sum_ref[...] = jnp.zeros_like(sum_ref)
+        lane_ref[...] = jnp.zeros_like(lane_ref)
         oh_ref[...] = jnp.zeros_like(oh_ref)
 
     back = mass_ref[pl.ds(step, 1), :] * jnp.exp(-lib_ref[pl.ds(step, 1), :])
-    dy = jnp.where(hid_ref[...] > 0, (a_ref[...] - back * r_ref[...]) * (-1.0 / cells), 0.0)
-    hidden, width = dy.shape
-    weighted = dy * phat_ref[...]
-    first, second = dy[:, :128], weighted[:, :128]
-    for tile in range(1, width // 128):
-        lanes = slice(tile * 128, (tile + 1) * 128)
-        first = first + dy[:, lanes]
-        second = second + weighted[:, lanes]
-    sum_ref[0] += first
-    sum_ref[1] += second
+    wide = aff_ref[:, cells_at].astype(F32)
+    dy = jnp.where(wide > 0, a_ref[:, cells_at] - back * r_ref[:, cells_at], 0.0)
+    weighted = dy * wide
+    lane_ref[...] += sum(weighted[:, t : t + 128] for t in range(0, width, 128))
+    dy_low = dy.astype(BF)
+    oh_ref[...] += nt(jnp.concatenate((side_ref[:, cells_at], z_ref[:, cells_at].astype(BF)), axis=0), dy_low)
     _, inv = norm_rows(stat_ref[...], latent - 8, cells)
-    lat = lat_ref[...] * (gain_ref[2:3] * inv)
-    lat_high, lat_mid, _ = three(lat)
-    dy_high, dy_mid, _ = three(dy)
-    table = jnp.concatenate((dy_high, dy_mid), axis=0)
-    left = jnp.concatenate(
-        (
-            jnp.concatenate((lat_high, lat_high), axis=1),
-            jnp.concatenate((lat_mid, jnp.zeros_like(lat_mid)), axis=1),
-        ),
-        axis=0,
-    )
-    kinds = oh_ref.shape[0] - 16
-    z_high, z_mid, _ = three(z_ref[...])
-    held = jnp.concatenate((one_hot(batch_ref[0], kinds).astype(BF), z_high, z_mid), axis=0)
-    product = nt(held, table)
-    product = product[:, :hidden] + product[:, hidden:]
-    oh_ref[:kinds, :] += product[:kinds]
-    oh_ref[kinds:, :] += product[kinds : kinds + 16] + product[kinds + 16 :]
-    both = nn(left, table)
+    lat_high, lat_mid, _ = three(lat_ref[...] * (gain_ref[2:3] * inv) * (-1.0 / cells))
+    both = nn(jnp.concatenate((lat_high, lat_mid), axis=0), dy_low)
     block = both[:16] + both[16:]
     row = lax.broadcasted_iota(jnp.int32, block.shape, 0)
     block = jnp.where(row == latent, recon_ref[pl.ds(step, 1), :], block)
@@ -561,23 +587,26 @@
 
     @pl.when(step == steps - 1)
     def _():
-        one, two = row_sums(sum_ref[0]), row_sums(sum_ref[1])
-        part = oh_ref.shape[0] // steps
+        scale = -1.0 / cells
+        one, two = oh_ref[kinds : kinds + 1, :] * scale, row_sums(lane_ref[...])[0:1] * scale
+        oh_ref[kinds : kinds + 16, :] = oh_ref[kinds + 16 :, :]
+        part = (kinds + 16) // steps
         for core, ref in enumerate((keep_ref, send_ref)):
             for index in range(ref.shape[0]):
-                ref[index, latent + 1 : latent + 2, 0:hidden] = one[0:1]
-                ref[index, latent + 2 : latent + 3, 0:hidden] = two[0:1]
+                ref[index, latent + 1 : latent + 2, 0:hidden] = one
+                ref[index, latent + 2 : latent + 3, 0:hidden] = two
                 owner = me_ref[0] ^ (2 * index + core)
                 for k in range(part):
                     line = latent + 3 + k // 8
                     lanes = slice((k % 8) * hidden, (k % 8 + 1) * hidden)
-                    ref[index, line : line + 1, lanes] = oh_ref[pl.ds(owner * part + k, 1), :]
+                    ref[index, line : line + 1, lanes] = oh_ref[pl.ds(owner * part + k, 1), :] * scale
 
 
 def dec_grad_kernel(cells, rt_ref, hid_ref, mass_ref, lib_ref, g_ref, acc_ref, dig_ref, th_ref, dec_ref, mix_ref):
     step = pl.program_id(0)
     steps = pl.num_programs(0)
     genes = rt_ref.shape[0]
+    cells_at = part_of(step, mass_ref.shape[1])
     hidden = hid_ref.shape[0]
 
     @pl.when(step == 0)
@@ -588,8 +617,8 @@
     back_high, back_mid, back_low = three(back)
     row = lax.broadcasted_iota(jnp.int32, (16, back.shape[1]), 0)
     extra = jnp.where(row == 0, back_high.astype(F32), jnp.where(row == 1, back_mid.astype(F32), 0.0))
-    scaled = (hid_ref[...].astype(F32) * back).astype(BF)
-    mix_ref[...] += nt(rt_ref[...], jnp.concatenate((scaled, extra.astype(BF)), axis=0))
+    scaled = (relu_low(hid_ref[:, cells_at]).astype(F32) * back).astype(BF)
+    mix_ref[...] += nt(rt_ref[:, cells_at], jnp.concatenate((scaled, extra.astype(BF)), axis=0))
 
     @pl.when(step == steps - 1)
     def _():
@@ -608,90 +637,94 @@
         dec_ref[2 * genes :, :] = lines(gene_rows, pl.cdiv(genes, 128))
 
 
-def enc_back_kernel(cells, latent, fast, me_ref, own_ref, dnear_ref, dfar_ref, phat_ref, sums_ref, stat_ref, gain_ref, lat_ref, noise_ref, klw_ref, anear_ref, afar_ref, batch_ref, logc_ref, cols_ref, z_ref, out_ref, rest_ref, lane_ref):
+def enc_back_kernel(cells, latent, fast, span, me_ref, own_ref, dnear_ref, dfar_ref, aff_dec_ref, sums_ref, stat_ref, gain_ref, lat_ref, noise_ref, klw_ref, anear_ref, afar_ref, side_ref, held_ref, logc_ref, cols_ref, z_ref, out_ref, rest_ref, lane_ref, left_ref, fixed_ref, one_ref, kept_ref, sum_ref):
     step = pl.program_id(0)
-    genes, width = logc_ref.shape
-    hidden = phat_ref.shape[0]
+    steps = kept_ref.shape[0]
+    genes, width = logc_ref.shape[0], dnear_ref.shape[2]
+    hidden = aff_dec_ref.shape[0]
+    cells_at = part_of(step, width)
+    place = (step ^ me_ref[0]) if fast else step
     kinds = (rest_ref.shape[0] - 64) // 2
-    steps = pl.num_programs(0)
+    at = latent + 1 - 8
+    m_one, m_two = norm_sums(sums_ref[at : at + 2], gain_ref, 2)
+    m_two = m_two / gain_ref[2:3] * (1.0 / cells)
+    m_one = m_one * (1.0 / cells) - m_two * gain_ref[3:4]
 
     @pl.when(step == 0)
     def _():
         out_ref[...] = jnp.zeros_like(out_ref)
         rest_ref[...] = jnp.zeros_like(rest_ref)
         lane_ref[...] = jnp.zeros_like(lane_ref)
-
-    block = pick(step, me_ref, fast, dnear_ref, dfar_ref)
-    _, inv = norm_rows(stat_ref[...], latent - 8, cells)
-    scaled = gain_ref[2:3] * inv
-    lat = lat_ref[...] * scaled
-    at = latent + 1 - 8
-    m_one = sums_ref[at : at + 1] * (1.0 / cells)
-    m_two = sums_ref[at + 1 : at + 2] * (1.0 / cells)
-    fixed = jnp.sum(lat * m_one, axis=1, keepdims=True)
-    left_high, left_mid, _ = three(lat * m_two)
-    phat_high, phat_mid, _ = three(phat_ref[...])
-    both = nn(
-        jnp.concatenate(
-            (
-                jnp.concatenate((left_high, left_high), axis=1),
-                jnp.concatenate((left_mid, jnp.zeros_like(left_mid)), axis=1),
-            ),
-            axis=0,
-        ),
-        jnp.concatenate((phat_high, phat_mid), axis=0),
-    )
-    grad_z = (block - fixed - (both[:16] + both[16:]))[:latent]
-    noise = noise_ref[...]
-    rows = pick(step, me_ref, fast, anear_ref, afar_ref)
-    pieces = rows[hidden:].astype(F32)
+        sum_ref[...] = jnp.zeros_like(sum_ref)
+        _, inv = norm_rows(stat_ref[...], latent - 8, cells)
+        lat = lat_ref[...] * (gain_ref[2:3] * inv)
+        fixed_ref[...] = jnp.broadcast_to(jnp.sum(lat * m_one, axis=1, keepdims=True), fixed_ref.shape)
+        high, mid, _ = three(lat * m_two)
+        left_ref[...] = jnp.concatenate((high, mid), axis=0)
+
+    index = lax.div(place, 2) if fast else place
+    near = (lax.rem(place, 2) == 0) if fast else None
+
+    def take(near_ref, far_ref, rows, lanes):
+        if not fast:
+            return near_ref[index, rows, lanes]
+        return jnp.where(near, near_ref[index, rows, lanes], far_ref[index, rows, lanes])
+
+    every = slice(0, width)
+    scale = klw_ref[0:1, 0:1] * (1.0 / cells)
+    affine_dec = aff_dec_ref[:, cells_at]
+    both = nn(left_ref[...], affine_dec)
+    block = take(dnear_ref, dfar_ref, slice(0, 16), every)
+    kept_ref[step] = block[8:]
+    grad_z = (block - fixed_ref[:, 0:1] - (both[:16] + both[16:]))[:latent]
+    noise = noise_ref[:, cells_at]
+    pieces = take(anear_ref, afar_ref, slice(hidden, hidden + 48), every).astype(F32)
     lat_logvar = (pieces[:latent] + pieces[16 : 16 + latent]) + pieces[32 : 32 + latent]
     spread = jnp.exp(lat_logvar)
     var = spread + 0.0001
-    lat_mean = z_ref[0:latent, :] - jnp.sqrt(var) * noise
-    scale = klw_ref[0:1, 0:1] * (1.0 / cells)
+    inv_std = lax.rsqrt(var)
+    z = z_ref[:, cells_at]
+    lat_mean = z[0:latent] - var * inv_std * noise
     g_mean = latent_rows(grad_z + scale * lat_mean)
-    g_var = latent_rows(
-        grad_z * noise * 0.5 * spread * lax.rsqrt(var) + scale * 0.5 * (spread - spread / var)
-    )
+    g_var = latent_rows(spread * (grad_z * noise * (0.5 * inv_std) + (0.5 * scale) * (1.0 - inv_std * inv_std)))
     g_head = jnp.concatenate((g_mean, g_var), axis=0)
+    sum_ref[0:32, :] += sum(g_head[:, t : t + 128] for t in range(0, width, 128))
+    sum_ref[32:, :] += sum(z[:, t : t + 128] for t in range(0, width, 128))
     head_high, head_mid, _ = three(g_head)
-    spread_out = nn(cols_ref[...], jnp.concatenate((head_high, head_mid), axis=0))
-    wide = rows[:hidden].astype(F32)
-    dy = jnp.where(wide > 0, spread_out[:hidden] + spread_out[hidden:], 0.0)
-    weighted = dy * wide
-    first, second = dy[:, :128], weighted[:, :128]
-    for tile in range(1, width // 128):
-        lanes = slice(tile * 128, (tile + 1) * 128)
-        first = first + dy[:, lanes]
-        second = second + weighted[:, lanes]
-    lane_ref[0] += first
-    lane_ref[1] += second
-    dy_low = dy.astype(BF)
-    table = one_hot(batch_ref[0], kinds)
-    hidden_low = jnp.maximum(wide, 0.0).astype(BF)
-    out_ref[0:genes, :] += nt(logc_ref[...], dy_low)
-    rest_ref[0:kinds, :] += nt(table.astype(BF), dy_low)
-    rest_ref[kinds : kinds + 32, :] += nt(head_high, hidden_low) + nt(head_mid, hidden_low)
-    rest_ref[kinds + 32 : kinds + 40, 0:32] += row_sums(g_head)
+    heads = jnp.concatenate((head_high, head_mid, head_high), axis=0)
+    for begin in range(0, width, span):
+        lanes = slice(begin, begin + span)
+        affine = take(anear_ref, afar_ref, slice(0, hidden), lanes)
+        one_ref[hidden:, lanes] = relu_low(affine)
+        wide = affine.astype(F32)
+        dy = jnp.where(wide > 0, nn(cols_ref[...], heads[:, lanes]), 0.0)
+        one_ref[0:hidden, lanes] = dy.astype(BF)
+        weighted = dy * wide
+        lane_ref[...] += sum(weighted[:, t : t + 128] for t in range(0, span, 128))
+    dy_low = one_ref[0:hidden, :]
+    side = side_ref[:, cells_at]
+    out_ref[0:genes, :] += nt(logc_ref[:, cells_at], dy_low)
+    mixed = nt(side, dy_low)
+    rest_ref[0:kinds, :] += mixed[:kinds]
+    out_ref[genes : genes + 1, :] += mixed[kinds : kinds + 1]
+    rest_ref[kinds : kinds + 32, :] += nt(head_high, one_ref[hidden:, :])
     base = kinds + 40
-    z_high, z_mid, _ = three(z_ref[...])
-    left = jnp.concatenate((table.astype(BF), z_high, z_mid), axis=0)
-    part = nt(left, jnp.concatenate((phat_high, phat_mid), axis=0))
-    part = part[:, :hidden] + part[:, hidden:]
-    held = jnp.sum(jnp.concatenate((table, z_ref[...]), axis=0), axis=1, keepdims=True)
-    product = jnp.concatenate((part[:kinds], part[kinds : kinds + 16] + part[kinds + 16 :]), axis=0)
-    rest_ref[base : base + kinds + 16, :] -= held * m_one + product * m_two
-    count = (kinds + 16) // steps
-    for k in range(count):
-        line = latent + 3 + k // 8
-        rest_ref[pl.ds(base + step * count + k, 1), :] += block[line : line + 1, (k % 8) * hidden : (k % 8 + 1) * hidden]
+    product = nt(jnp.concatenate((side, z.astype(BF)), axis=0), affine_dec)
+    rest_ref[base : base + kinds, :] -= product[:kinds] * m_two
+    rest_ref[base + kinds : base + kinds + 16, :] -= product[kinds + 16 :] * m_two
 
     @pl.when(step == steps - 1)
     def _():
-        one, two = row_sums(lane_ref[0]), row_sums(lane_ref[1])
-        row = lax.broadcasted_iota(jnp.int32, one.shape, 0)
-        out_ref[genes : genes + 8, :] = jnp.where(row == 0, one, jnp.where(row == 1, two, 0.0))
+        out_ref[genes + 1 : genes + 2, :] = row_sums(lane_ref[...])[0:1]
+        rest_ref[kinds + 32 : kinds + 40, 0:32] = row_sums(sum_ref[0:32, :])
+        held = jnp.concatenate((held_ref[...], sum_ref[32:, :]), axis=0)
+        rest_ref[base : base + kinds + 16, :] -= jnp.sum(held, axis=1, keepdims=True) * m_one
+        count = (kinds + 16) // steps
+        for owner in range(steps):
+            for k in range(count):
+                line = latent + 3 + k // 8 - 8
+                at = slice(base + owner * count + k, base + owner * count + k + 1)
+                rest_ref[at, :] += kept_ref[owner, line : line + 1, (k % 8) * hidden : (k % 8 + 1) * hidden]
         size = rest_ref.shape[0] // 8
         out_ref[genes + 8 :, :] = rest_ref[pl.ds(pl.multiple_of((own_ref[0] & 7) * size, 8), size), :]
 
@@ -700,8 +733,8 @@
     return (gain * inv) * (part - plain * one - ((product - plain * shift) / gain) * two)
 
 
-def norm_sums(rows, norm_ref):
-    return rows[0:1], (rows[1:2] - norm_ref[1:2] * rows[0:1]) / norm_ref[0:1]
+def norm_sums(rows, norm_ref, at):
+    return rows[0:1], (rows[1:2] - norm_ref[at + 1 : at + 2] * rows[0:1]) / norm_ref[at : at + 1]
 
 
 def finish_kernel(cells, latent, sum_ref, dec_ref, fixed_ref, stat_enc_ref, norm_ref, kl_ref, klw_ref, own_ref, enc_out, tail_out, loss_out):
@@ -711,7 +744,7 @@
     kinds = fixed_ref.shape[0] - genes - 8 * count - 8
     loss_out[...] = klw_ref[0:1, 0:1] * kl_ref[...] - own_ref[latent : latent + 1, :]
     _, inv = norm_rows(stat_enc_ref[...], 0, cells)
-    n_one, n_two = norm_sums(sum_ref[genes : genes + 8, :], norm_ref)
+    n_one, n_two = norm_sums(sum_ref[genes : genes + 8, :], norm_ref, 0)
     at = genes + kinds
     logs = jnp.concatenate([fixed_ref[at + 8 * i : at + 8 * (i + 1), :] for i in range(count)], axis=1)
     log_sum = jnp.transpose(logs)[:genes, 0:1]
@@ -753,7 +786,7 @@
     rest = jnp.concatenate(whole_rest, axis=0)
     gains = norm[0]
     gain, shift = gains[0:1], gains[1:2]
-    n_one, n_two = norm_sums(sum_ref[genes : genes + 8, :], gains)
+    n_one, n_two = norm_sums(sum_ref[genes : genes + 8, :], gains, 0)
     _, inv = norm_rows(stat_enc_ref[...], 0, cells)
     _, inv_dec = norm_rows(stat_dec_ref[...], latent - 8, cells)
     at = genes + kinds + 8 * count
@@ -770,8 +803,9 @@
     at = latent + 1 - 8
     norm_g_ref[0:1] = n_two
     norm_g_ref[1:2] = n_one
-    norm_g_ref[2:3] = sums_ref[at + 1 : at + 2]
-    norm_g_ref[3:4] = sums_ref[at : at + 1]
+    m_one, m_two = norm_sums(sums_ref[at : at + 2], gains, 2)
+    norm_g_ref[2:3] = m_two
+    norm_g_ref[3:4] = m_one
     small_square = jnp.zeros((1, 1), F32)
     for part in (small_g_ref[0:rows, :], head_g_ref[...], norm_g_ref[...]):
         small_square = small_square + jnp.sum(jnp.sum(part * part, axis=0, keepdims=True), axis=1, keepdims=True)
@@ -839,36 +873,45 @@
     own_lanes = lambda rows: pl.BlockSpec((rows, share), lambda i, m: (0, m[0]))
     lane_block = lambda rows: pl.BlockSpec((rows, width), lambda i, *_: (0, i))
     full = lambda array: (array, whole(array.shape))
+    here = pl.BlockSpec(memory_space=pltpu.VMEM)
     new = lambda shape, dtype=F32: (shape, dtype, whole(shape))
-    if fast:
-        from_all = lambda rows: pl.BlockSpec((1, rows, width), lambda i, m, *_: ((i ^ m[0]) // 2, 0, 0))
-    else:
-        from_all = lambda rows: pl.BlockSpec((1, rows, width), lambda i, m, *_: (i, 0, 0))
-
-    keep_part, send_part = call(
-        enc_kernel,
-        (groups,),
-        [
-            (me if fast else me & 1, None),
-            (x_t, pl.BlockSpec((genes, share), lambda i, m: (0, i ^ m[0]))),
-            full(enc_w),
-        ],
-        [
-            ((groups // 2, hidden, share), F32, pl.BlockSpec((1, hidden, share), lambda i, m: (i // 2, 0, 0))),
-            ((groups // 2, hidden, share), BF, pl.BlockSpec((1, hidden, share), lambda i, m: (i // 2, 0, 0))),
-        ],
-        scratch=[pltpu.VMEM((hidden, genes), BF)],
-        scalars=1,
-        us=4.0,
-    )
-    got = swap(send_part, "genes", 1)
+
+    def encode(low, count, weight):
+        return call(
+            lambda *refs: enc_kernel(low, *refs),
+            (1,),
+            [
+                (me if fast else me & 1, None),
+                (in_hbm(x_t), pl.BlockSpec(memory_space=pl.ANY)),
+                full(weight),
+            ],
+            [new((count // 2, hidden, share)), new((count // 2, hidden, share), BF)],
+            scratch=[
+                pltpu.VMEM((count, genes, share), BF),
+                pltpu.VMEM((hidden, genes), BF),
+                pltpu.SemaphoreType.DMA((count,)),
+            ],
+            scalars=1,
+            us=3.0,
+            mib=20,
+        )
+
     slot = pl.BlockSpec((1, hidden, share), lambda i, m: (0, 0, 0))
     if fast:
-        mine = [(keep_part[k : k + 1] + got[k : k + 1].astype(F32)).astype(BF) for k in (2, 3, 1)]
-        far = [swap(part, "genes", 2 * k) for part, k in zip(mine, (2, 3, 1))]
-        kept = keep_part
-        ready = mine[2]
+        keep_far, send_far = encode(4, 4, enc_w)
+        got_far = swap(send_far, "genes", 1)
+        keep_near, send_near = encode(0, 4, after(enc_w, send_far))
+        far = [
+            swap((keep_far[k : k + 1] + got_far[k : k + 1].astype(F32)).astype(BF), "genes", 4 + 2 * k)
+            for k in range(2)
+        ]
+        got = swap(send_near, "genes", 1)
+        ready = (keep_near[1:2] + got[1:2].astype(F32)).astype(BF)
+        far.append(swap(ready, "genes", 2))
+        kept = keep_near
     else:
+        keep_part, send_part = encode(0, groups, enc_w)
+        got = swap(send_part, "genes", 1)
         summed = lax.psum_scatter(
             keep_part + got.astype(F32),
             "genes",
@@ -881,7 +924,7 @@
         ready = keep_part
 
     mask_late = after(gene_mask.reshape(1, genes), ready)
-    aug, dec_n, par, lg_tab, dg_tab, enc_pieces, dec_pieces, lat_row, head_rows, head_bias, head_cols, norm_t = call(
+    aug, dec_n, par, lg_tab, dg_tab, enc_pieces, dec_pieces, dec_plain, lat_row, head_rows, head_bias, head_cols, norm_t = call(
         prep_kernel,
         (1,),
         [full(gene_par), full(mask_late), full(dec_t), full(small_w), full(head_t), full(norm_par)],
@@ -893,14 +936,16 @@
             new((COUNT_TOP, genes, 128)),
             new((3 * hidden, kinds), BF),
             new((3 * hidden, kinds + 48), BF),
+            new((hidden, kinds + 16)),
             new((16, hidden)),
             new((32, hidden)),
             new((32, 128)),
-            new((2 * hidden, 64), BF),
+            new((hidden, 96), BF),
             new((hidden, 8)),
         ],
     )
-    logc, x_kept, gam_cell, dig_acc, log_lines = call(
+    batch_spec = pl.BlockSpec((1, 1, width), lambda i, *_: (i, 0, 0))
+    logc, x_kept, side, gam_cell, dig_acc, log_lines, held = call(
         lambda *refs: counts_kernel(16, min(512, width), *refs),
         (blocks,),
         [
@@ -908,13 +953,16 @@
             full(lg_tab),
             full(dg_tab),
             (par, pl.BlockSpec((None, genes, 128), lambda i: (4, 0, 0))),
-        ],
-        [
-            ((genes, rows_all), BF, lane_block(genes)),
-            ((genes, rows_all), BF, lane_block(genes)),
+            (batch_all, batch_spec),
+        ],
+        [
+            ((genes, rows_all), BF, lane_block(genes), True),
+            ((genes, rows_all), BF, lane_block(genes), True),
+            ((kinds + 16, rows_all), BF, lane_block(kinds + 16)),
             new((blocks, width)),
             new((genes, 128)),
-            new((8 * gene_lines, 128)),
+            new((8 * gene_lines + 8, 128)),
+            new((kinds, 128)),
         ],
         scratch=[pltpu.VMEM((genes, 128), F32)],
         mib=16,
@@ -957,46 +1005,44 @@
         stat_dec = lax.psum(pack[8:16, :hidden], "genes")
     stat_dec = total(stat_dec, "cells")
 
-    batch_spec = pl.BlockSpec((1, 1, width), lambda i, *_: (i, 0, 0))
-    hid, phat_dec, lse, z_all = call(
+    aff_dec, lse, z_all = call(
         lambda *refs: decode_kernel(cells, latent, fast, *refs),
         (blocks,),
         [
             (me, None),
-            (near, from_all(16)),
-            (far_pack, from_all(16)),
-            (batch_all, batch_spec),
+            (near, here),
+            (far_pack, here),
+            (side, here),
             full(stat_dec),
             full(norm_t),
-            full(dec_pieces),
+            full(dec_plain),
             (aug, pl.BlockSpec((genes, hidden + 16), lambda i, m: (0, 0))),
         ],
         [
-            ((hidden, rows_all), BF, lane_block(hidden)),
-            ((hidden, rows_all), F32, lane_block(hidden)),
+            ((hidden, rows_all), BF, here),
             new((blocks, width)),
-            ((16, rows_all), F32, lane_block(16)),
-        ],
-        scratch=[pltpu.VMEM((genes, width), F32)],
+            ((16, rows_all), F32, here),
+        ],
+        scratch=[pltpu.VMEM((genes, width), F32), pltpu.VMEM((2 * hidden, kinds + 48), BF)],
         scalars=1,
         us=8.0,
     )
     lse_all = log_total_of(lse, "genes")
 
     full8 = whole((blocks, width))
-    gm, gd, rt, mass, recon, gene_acc = call(
-        lambda *refs: zinb_kernel(32, min(512, width), *refs),
+    g_both, rt, mass, recon, gene_acc = call(
+        lambda *refs: zinb_kernel(64, min(512, width), *refs),
         (blocks,),
         [
-            (hid, lane_block(hidden)),
+            (aff_dec, here),
             full(aug),
-            (x_kept, lane_block(genes)),
+            (in_hbm(x_kept), lane_block(genes)),
             (par, pl.BlockSpec((4, genes, 128), lambda i: (0, 0, 0))),
             full(lib8),
             full(lse_all),
             full(gam_cell),
         ],
-        [((genes, rows_all), BF, lane_block(genes))] * 3
+        [((2 * genes, rows_all), BF, here), ((genes, rows_all), BF, here)]
         + [new((blocks, width)), new((blocks, width)), new((3, genes, 128))],
         scratch=[pltpu.VMEM((2 * genes, width), F32)],
         mib=20,
@@ -1004,18 +1050,17 @@
     )
     mass_own, mass = mass, total(mass, "genes")
     part_a, part_r, dec_acc = call(
-        back_kernel,
+        lambda *refs: back_kernel(width, *refs),
         (blocks,),
         [
-            (gm, lane_block(genes)),
-            (gd, lane_block(genes)),
-            (rt, lane_block(genes)),
-            (hid, lane_block(hidden)),
+            (g_both, here),
+            (rt, here),
+            (aff_dec, here),
             full(dec_n),
         ],
         [
-            ((hidden, rows_all), F32, lane_block(hidden)),
-            ((hidden, rows_all), F32, lane_block(hidden)),
+            ((hidden, rows_all), F32, here),
+            ((hidden, rows_all), F32, here),
             new((2 * genes, hidden)),
         ],
         mib=16,
@@ -1029,10 +1074,10 @@
         (blocks,),
         [
             (me, None),
-            (logc, lane_block(genes)),
-            (aff_near, from_all(hidden + 48)),
-            (aff_far, from_all(hidden + 48)),
-            (batch_all, batch_spec),
+            (logc, here),
+            (aff_near, here),
+            (aff_far, here),
+            (side, here),
             full(log_lines),
         ],
         [new((fixed_rows, hidden))],
@@ -1046,24 +1091,23 @@
         (blocks,),
         [
             (me if fast else jnp.zeros_like(me), None),
-            (part_a, lane_block(hidden)),
-            (part_r, lane_block(hidden)),
+            (part_a, here),
+            (part_r, here),
             (mass, full8),
-            (hid, lane_block(hidden)),
-            (phat_dec, lane_block(hidden)),
+            (aff_dec, here),
             full(lib8),
             full(stat_dec),
             full(norm_par),
             full(lat_row),
             full(recon),
-            (z_all, lane_block(16)),
-            (batch_all, batch_spec),
+            (z_all, here),
+            (side, here),
         ],
         [
             new((blocks // 2, 16, width)),
             new((blocks // 2, 16, width)),
         ],
-        scratch=[pltpu.VMEM((2, hidden, 128), F32), pltpu.VMEM((kinds + 16, hidden), F32)],
+        scratch=[pltpu.VMEM((hidden, 128), F32), pltpu.VMEM((kinds + 32, hidden), F32)],
         scalars=1,
         us=5.0,
     )
@@ -1083,8 +1127,8 @@
         lambda *refs: dec_grad_kernel(cells, *refs),
         (blocks,),
         [
-            (rt, lane_block(genes)),
-            (hid, lane_block(hidden)),
+            (rt, here),
+            (aff_dec, here),
             (mass, full8),
             full(lib8),
             full(dec_acc),
@@ -1100,29 +1144,38 @@
 
     size = (2 * kinds + 64) // 8
     (enc_part,) = call(
-        lambda *refs: enc_back_kernel(cells, latent, fast, *refs),
+        lambda *refs: enc_back_kernel(cells, latent, fast, min(256, width), *refs),
         (blocks,),
         [
             (me, None),
             (me, None),
-            (d_near, from_all(16)),
-            (d_far, from_all(16)),
-            (phat_dec, lane_block(hidden)),
+            (d_near, here),
+            (d_far, here),
+            (aff_dec, here),
             full(sums_dec),
             full(stat_dec),
             full(norm_par),
             full(lat_row),
-            (noise_t, lane_block(latent)),
+            (noise_t, here),
             full(klw),
-            (aff_near, from_all(hidden + 48)),
-            (aff_far, from_all(hidden + 48)),
-            (batch_all, batch_spec),
-            (logc, lane_block(genes)),
+            (aff_near, here),
+            (aff_far, here),
+            (side, here),
+            full(held),
+            (logc, here),
             full(head_cols),
-            (z_all, lane_block(16)),
+            (z_all, here),
         ],
         [new((genes + 8 + size, hidden))],
-        scratch=[pltpu.VMEM((2 * kinds + 64, hidden), F32), pltpu.VMEM((2, hidden, 128), F32)],
+        scratch=[
+            pltpu.VMEM((2 * kinds + 64, hidden), F32),
+            pltpu.VMEM((hidden, 128), F32),
+            pltpu.VMEM((32, hidden), BF),
+            pltpu.VMEM((16, 128), F32),
+            pltpu.VMEM((2 * hidden, width), BF),
+            pltpu.VMEM((blocks, 8, width), F32),
+            pltpu.VMEM((48, 128), F32),
+        ],
         scalars=2,
         us=11.0,
     )

time: 224 us -> 204 us (0.911)
  local copies, waits for them, and re-layouts: 16.1 us -> 5.65 us
  Pallas kernels: 100 us -> 91.1 us
    unnamed x102 -> x94, local copies, waits for them, and re-layouts: 14.8 us -> 4.36 us
    pallas_call x14 -> x15, Pallas kernels: 100 us -> 91.1 us  [call(): pl.pallas_call(kernel, out_shape=[pltpu.HBM(out[0], out[1]) if len(out) =...]
    ppermute x51 -> x52, starting transfers between devices: 57.8 us -> 59.9 us  [swap(): return lax.ppermute(value, axis, [(i, i ^ bit) for i in range(count)])]
    ppermute x51 -> x52, waiting for transfers between devices: 44.9 us -> 42.9 us  [swap(): return lax.ppermute(value, axis, [(i, i ^ bit) for i in range(count)])]
  transfers between devices with their start and end apart: 51 -> 52, of which waited for: 24 -> 22; matrix products, arithmetic and copies ran while one was open for 0% -> 1% of each run, Pallas kernels for 36% -> 37%
where the time goes in v4:
time: 204 us
  Pallas kernels  91.1 us (45%)
  starting transfers between devices  59.9 us (29%)
  waiting for transfers between devices  42.9 us (21%)
  local copies, waits for them, and re-layouts  5.65 us (3%)
  between operations  2.2 us (1%)
  other arithmetic  2.15 us (1%)
    pallas_call x15, Pallas kernels, call(): pl.pallas_call(kernel, out_shape=[pltpu.HBM(out[0], out[1]) if len(out) =...  91.1 us
    ppermute x52, starting transfers between devices, swap(): return lax.ppermute(value, axis, [(i, i ^ bit) for i in range(count)])  59.9 us
    ppermute x52, waiting for transfers between devices, swap(): return lax.ppermute(value, axis, [(i, i ^ bit) for i in range(count)])  42.9 us
    unnamed x94, local copies, waits for them, and re-layouts  4.36 us
  transfers between devices with their start and end apart: 52, of which 22 were waited for; matrix products, arithmetic and copies ran while one was open for 1% of the time, Pallas kernels for 37%

profile of v4, /device:TPU:0, one launch (start us, length us, event | category | flops | bytes accessed | tf_op | source)
XLA Modules:
  0.0 203.9 jit_solution(18108112428248669837)
XLA Ops:
  1.6 2.9 %shard_map.399 = (f32[2,128,1024]{2,1,0:T(8,128)S(1)}, bf16[2,128,1024]{2,1,0:T(8,128)(2,1)S(1)}) custom-call(s32[1]{0:T(128)} %bitcast.refs_0_.me_ref.refs_1_, bf16[320,8192]{1,0:T(8,128)(2,1)} %bitcast.49, f32[320,128]{1,0:T(8,128)S(1)} %copy-done.5), custom_call_target="tpu_custom_call" | custom-call | bytes 11070000 | tf_op jit(solution)/shard_map/pallas_call | solution.py:46
  5.0 2.8 %shard_map.400 = (f32[2,128,1024]{2,1,0:T(8,128)S(1)}, bf16[2,128,1024]{2,1,0:T(8,128)(2,1)S(1)}) custom-call(s32[1]{0:T(128)} %bitcast.refs_0_.me_ref.refs_1_, bf16[320,8192]{1,0:T(8,128)(2,1)} %bitcast.50, f32[320,128]{1,0:T(8,128)S(1)} %copy-done.5), custom_call_target="tpu_custom_call" | custom-call | bytes 11070000 | tf_op jit(solution)/shard_map/pallas_call | solution.py:46
  8.2 4.0 %collective-permute-start.2 = (bf16[1,128,1024]{2,1,0:T(8,128)(2,1)S(1)}, bf16[1,128,1024]{2,1,0:T(8,128)(2,1)S(1)}, u32[]{:S(2)}, u32[]{:S(2)}) collective-permute-start(bf16[1,128,1024]{2,1,0:T(8,128)(2,1)S(1)} %get-tuple-element.165), channel_id=1, source_target_pairs={{0,4},{1,5},{2,6},{3,7},{4,0},{5,1},{6,2},{7,3},{8,12},{9,13},{10,... | collective-permute-start | bytes 786440 | tf_op jit(solution)/shard_map/ppermute | solution.py:63
  15.7 17.1 %shard_map.402 = (bf16[320,8192]{1,0:T(8,128)(2,1)}, bf16[320,8192]{1,0:T(8,128)(2,1)}, bf16[144,8192]{1,0:T(8,128)(2,1)S(1)}, f32[8,1024]{1,0:T(8,128)S(1)}, f3...) custom-call(bf16[320,8192]{1,0:T(8,128)(2,1)S(1)} %bitcast.53, ...), custom_call_target="tpu_custom_call" | custom-call | bytes 55350000 | tf_op jit(solution)/shard_map/pallas_call | solution.py:46
  35.4 5.4 %collective-permute-start.7 = (f32[8,128]{1,0:T(8,128)S(1)}, f32[8,128]{1,0:T(8,128)S(1)}, u32[]{:S(2)}, u32[]{:S(2)}) collective-permute-start(f32[8,128]{1,0:T(8,128)S(1)} %add.135), channel_id=1, source_target_pairs={{0,4},{1,5},{2,6},{3,7},{4,0},{5,1},{6,2},{7,3},{8,12},{9,13},{10,... | collective-permute-start | bytes 12296 | tf_op jit(solution)/shard_map/ppermute | solution.py:63
  42.3 3.8 %collective-permute-done.8 = f32[8,128]{1,0:T(8,128)S(1)} collective-permute-done((f32[8,128]{1,0:T(8,128)S(1)}, f32[8,128]{1,0:T(8,128)S(1)}, u32[]{:S(2)}, u32[]{:S(2)}) %collective-permute-start.8) | collective-permute-done | bytes 4128 | tf_op jit(solution)/shard_map/ppermute | solution.py:63
  49.8 2.4 %collective-permute-done.11 = f32[8,128]{1,0:T(8,128)S(1)} collective-permute-done((f32[8,128]{1,0:T(8,128)S(1)}, f32[8,128]{1,0:T(8,128)S(1)}, u32[]{:S(2)}, u32[]{:S(2)}) %collective-permute-start.11) | collective-permute-done | bytes 4128 | tf_op jit(solution)/shard_map/ppermute | solution.py:63
  52.8 1.8 shard_map.404
  54.6 2.0 collective-permute-start.14
  56.6 2.4 %collective-permute-start.12 = (f32[16,1024]{1,0:T(8,128)S(1)}, f32[16,1024]{1,0:T(8,128)S(1)}, u32[]{:S(2)}, u32[]{:S(2)}) collective-permute-start(f32[16,1024]{1,0:T(8,128)S(1)} %get-tuple-element.111), channel_id=1, source_target_pairs={{0,2},{1,3},{2,0},{3,1},{4,6},{5,7},{6,4},{7,5},{8,10},{9,11},{10,... | collective-permute-start | bytes 196616 | tf_op jit(solution)/shard_map/ppermute | solution.py:63
  67.5 2.4 %collective-permute-done.18 = f32[8,128]{1,0:T(8,128)S(1)} collective-permute-done((f32[8,128]{1,0:T(8,128)S(1)}, f32[8,128]{1,0:T(8,128)S(1)}, u32[]{:S(2)}, u32[]{:S(2)}) %collective-permute-start.18) | collective-permute-done | bytes 4128 | tf_op jit(solution)/shard_map/ppermute | solution.py:63
  69.9 7.0 %shard_map.405 = (bf16[128,8192]{1,0:T(8,128)(2,1)S(1)}, f32[8,1024]{1,0:T(8,128)S(1)}, f32[16,8192]{1,0:T(8,128)S(1)}) custom-call(s32[1]{0:T(128)} %bitcast.refs_0_.me_ref.refs_1_, f32[4,16,1024]{2,1,0:T(8,128)S(1)} %pad_maximum_fusion.1.refs_1_, f32[4,16,1024]{2,1,0:T(8,128)S(1)} %collective-permute-done.15.refs_2_, ...), custom_call_target="tpu_custom_call" | custom-call | bytes 29520000 | tf_op jit(solution)/shard_map/pallas_call | solution.py:46
  79.0 2.0 collective-permute-start.22
  81.7 1.7 collective-permute-start.20
  86.0 2.0 collective-permute-start.40
  93.0 28.5 %shard_map.406 = (bf16[640,8192]{1,0:T(8,128)(2,1)S(1)}, bf16[320,8192]{1,0:T(8,128)(2,1)S(1)}, f32[8,1024]{1,0:T(8,128)S(1)}, f32[8,1024]{1,0:T(8,128)S(1)}, f32[3,320,128]{2,1,0:T(8,128)S(1)}) custom-call(bf16[128,8192]{1,0:T(8,128)(2,1)S(1)} %get-tuple-element.115.refs_0_.refs_2_.refs_4_.refs_1_, bf16[640,144]{1,0:T(8,128)(2,1)S(1)} %copy-done.8, ...), custom_call_target="tpu_custom_call" | custom-call | bytes 103320000 | tf_op jit(solution)/shard_map/pallas_call | solution.py:46
  123.6 2.8 %collective-permute-done.23 = f32[8,1024]{1,0:T(8,128)S(1)} collective-permute-done((f32[8,1024]{1,0:T(8,128)S(1)}, f32[8,1024]{1,0:T(8,128)S(1)}, u32[]{:S(2)}, u32[]{:S(2)}) %collective-permute-start.23) | collective-permute-done | bytes 32800 | tf_op jit(solution)/shard_map/ppermute | solution.py:63
  127.4 1.9 collective-permute-start.26
  129.9 6.9 %shard_map.407 = (f32[128,8192]{1,0:T(8,128)S(1)}, f32[128,8192]{1,0:T(8,128)S(1)}, f32[640,128]{1,0:T(8,128)S(1)}) custom-call(bf16[640,8192]{1,0:T(8,128)(2,1)S(1)} %get-tuple-element.119.refs_0_, bf16[320,8192]{1,0:T(8,128)(2,1)S(1)} %get-tuple-element.120.refs_1_.refs_0_, bf16[128,8192]{1,0:T(8,128)(2,1)S(1)} %get-tuple-element.115.refs_0_.refs_2_.refs_4_.refs_1_, ...), custom_call_target="tpu_custom_call" | custom-call | bytes 33210000 | tf_op jit(solution)/shard_map/pallas_call | solution.py:46
  136.9 3.4 %shard_map.408 = (f32[4,16,1024]{2,1,0:T(8,128)S(1)}, f32[4,16,1024]{2,1,0:T(8,128)S(1)}) custom-call(s32[1]{0:T(128)} %bitcast.refs_0_.me_ref.refs_1_, f32[128,8192]{1,0:T(8,128)S(1)} %get-tuple-element.122.refs_1_, f32[128,8192]{1,0:T(8,128)S(1)} %get-tuple-element.123.refs_2_, f32[8,1024]{1,0:T(8,128)S(1)} %add_add_fusion.refs_3_.refs_2_, ...), custom_call_target="tpu_custom_call" | custom-call | bytes 18450000 | tf_op jit(solution)/shard_map/pallas_call | solution.py:46
  144.5 1.9 collective-permute-start.30
  146.4 5.1 %collective-permute-done.29 = f32[16,1024]{1,0:T(8,128)S(1)} collective-permute-done((f32[16,1024]{1,0:T(8,128)S(1)}, f32[16,1024]{1,0:T(8,128)S(1)}, u32[]{:S(2)}, u32[]{:S(2)}) %collective-permute-start.29) | collective-permute-done | bytes 65568 | tf_op jit(solution)/shard_map/ppermute | solution.py:63
  151.5 2.0 %collective-permute-start.33 = (f32[16,1024]{1,0:T(8,128)S(1)}, f32[16,1024]{1,0:T(8,128)S(1)}, u32[]{:S(2)}, u32[]{:S(2)}) collective-permute-start(f32[16,1024]{1,0:T(8,128)S(1)} %fusion.5.refs_7_), channel_id=1, source_target_pairs={{0,6},{1,7},{2,4},{3,5},{4,2},{5,3},{6,0},{7,1},{8,14},{9,15},{10,... | collective-permute-start | bytes 196616 | tf_op jit(solution)/shard_map/ppermute | solution.py:63
  156.0 3.9 %shard_map.410 = f32[664,128]{1,0:T(8,128)S(1)} custom-call(bf16[320,8192]{1,0:T(8,128)(2,1)S(1)} %get-tuple-element.120.refs_1_.refs_0_, bf16[128,8192]{1,0:T(8,128)(2,1)S(1)} %get-tuple-element.115.refs_0_.refs_2_.refs_4_.refs_1_, f32[8,1024]{1,0:T(8,128)S(1)} %add_add_fusion.refs_3_.refs_2_, f32[8,1024]{1,0:T(8,128)S(1)} %reshape.69.refs_4_.refs_5_.refs_3_, ...), custom_call_target="tpu_custom_call" | custom-call | bytes 18450000 | tf_op jit(solution)/shard_map/pallas_call | solution.py:46
  162.1 2.0 collective-permute-start.37
  165.4 3.4 %shard_map.411 = f32[480,128]{1,0:T(8,128)S(1)} custom-call(s32[1]{0:T(128)} %bitcast.refs_0_.me_ref.refs_1_, bf16[320,8192]{1,0:T(8,128)(2,1)S(1)} %bitcast.55, bf16[4,176,1024]{2,1,0:T(8,128)(2,1)S(1)} %pad_maximum_fusion.refs_11_.refs_2_, bf16[4,176,1024]{2,1,0:T(8,128)(2,1)S(1)} %collective-permute-done.41.refs_12_.refs_3_, ...), custom_call_target="tpu_custom_call" | custom-call | bytes 14760000 | tf_op jit(solution)/shard_map/pallas_call | solution.py:46
  170.4 8.2 %shard_map.409 = f32[368,128]{1,0:T(8,128)S(1)} custom-call(s32[1]{0:T(128)} %bitcast.refs_0_.me_ref.refs_1_, s32[1]{0:T(128)} %bitcast.refs_0_.me_ref.refs_1_, f32[4,16,1024]{2,1,0:T(8,128)S(1)} %pad_maximum_fusion.2.refs_2_, f32[4,16,1024]{2,1,0:T(8,128)S(1)} %collective-permute-done.34.refs_3_, ...), custom_call_target="tpu_custom_call" | custom-call | bytes 40590000 | tf_op jit(solution)/shard_map/pallas_call | solution.py:46
  181.4 4.9 %collective-permute-done.42 = f32[368,128]{1,0:T(8,128)S(1)} collective-permute-done((f32[368,128]{1,0:T(8,128)S(1)}, f32[368,128]{1,0:T(8,128)S(1)}, u32[]{:S(2)}, u32[]{:S(2)}) %collective-permute-start.42) | collective-permute-done | bytes 188448 | tf_op jit(solution)/shard_map/ppermute | solution.py:63
  186.9 5.0 %collective-permute-done.45 = f32[664,128]{1,0:T(8,128)S(1)} collective-permute-done((f32[664,128]{1,0:T(8,128)S(1)}, f32[664,128]{1,0:T(8,128)S(1)}, u32[]{:S(2)}, u32[]{:S(2)}) %collective-permute-start.45) | collective-permute-done | bytes 340000 | tf_op jit(solution)/shard_map/ppermute | solution.py:63
  192.9 2.0 collective-permute-start.50
  194.9 2.4 %collective-permute-start.48 = (f32[48,128]{1,0:T(8,128)S(1)}, f32[48,128]{1,0:T(8,128)S(1)}, u32[]{:S(2)}, u32[]{:S(2)}) collective-permute-start(f32[48,128]{1,0:T(8,128)S(1)} %get-tuple-element.140), channel_id=1, source_target_pairs={{0,2},{1,3},{2,0},{3,1},{4,6},{5,7},{6,4},{7,5},{8,10},{9,11},{10,... | collective-permute-start | bytes 73736 | tf_op jit(solution)/shard_map/ppermute | solution.py:63
  201.2 2.2 %shard_map.413 = (f32[320,128]{1,0:T(8,128)}, f32[320,128]{1,0:T(8,128)}, f32[320,128]{1,0:T(8,128)}, bf16[320,128]{1,0:T(8,128)(2,1)}, f32[2,320,128]{2,1,0:T(8...) custom-call(s32[1]{0:T(128)} %bitcast.refs_0_.me_ref.refs_1_, ...), custom_call_target="tpu_custom_call" | custom-call | bytes 7380000 | tf_op jit(solution)/shard_map/pallas_call | solution.py:46
  (214 shorter events, 55.4 us)
Async XLA Ops:
  7.8 5.8 %collective-permute-start = (bf16[2,128,1024]{2,1,0:T(8,128)(2,1)S(1)}, bf16[2,128,1024]{2,1,0:T(8,128)(2,1)S(1)}, u32[]{:S(2)}, u32[]{:S(2)}) collective-permute-start(bf16[2,128,1024]{2,1,0:T(8,128)(2,1)S(1)} %get-tuple-element.96), channel_id=1, source_target_pairs={{0,1},{1,0},{2,3},{3,2},{4,5},{5,4},{6,7},{7,6},{8,9},{9,8},{10,11... | collective-permute-start | bytes 1572872 | tf_op jit(solution)/shard_map/ppermute | solution.py:63
  8.2 24.7 %collective-permute-start.2 = (bf16[1,128,1024]{2,1,0:T(8,128)(2,1)S(1)}, bf16[1,128,1024]{2,1,0:T(8,128)(2,1)S(1)}, u32[]{:S(2)}, u32[]{:S(2)}) collective-permute-start(bf16[1,128,1024]{2,1,0:T(8,128)(2,1)S(1)} %get-tuple-element.165), channel_id=1, source_target_pairs={{0,4},{1,5},{2,6},{3,7},{4,0},{5,1},{6,2},{7,3},{8,12},{9,13},{10,... | collective-permute-start | bytes 786440 | tf_op jit(solution)/shard_map/ppermute | solution.py:63
  12.2 20.7 %collective-permute-start.3 = (bf16[1,128,1024]{2,1,0:T(8,128)(2,1)S(1)}, bf16[1,128,1024]{2,1,0:T(8,128)(2,1)S(1)}, u32[]{:S(2)}, u32[]{:S(2)}) collective-permute-start(bf16[1,128,1024]{2,1,0:T(8,128)(2,1)S(1)} %get-tuple-element.164), channel_id=1, source_target_pairs={{0,6},{1,7},{2,4},{3,5},{4,2},{5,3},{6,0},{7,1},{8,14},{9,15},{10,... | collective-permute-start | bytes 786440 | tf_op jit(solution)/shard_map/ppermute | solution.py:63
  13.6 19.3 %collective-permute-start.4 = (bf16[1,128,1024]{2,1,0:T(8,128)(2,1)S(1)}, bf16[1,128,1024]{2,1,0:T(8,128)(2,1)S(1)}, u32[]{:S(2)}, u32[]{:S(2)}) collective-permute-start(bf16[1,128,1024]{2,1,0:T(8,128)(2,1)S(1)} %add_convert_fusion), channel_id=1, source_target_pairs={{0,2},{1,3},{2,0},{3,1},{4,6},{5,7},{6,4},{7,5},{8,10},{9,11},{10,... | collective-permute-start | bytes 786440 | tf_op jit(solution)/shard_map/ppermute | solution.py:63
  35.4 6.9 %collective-permute-start.7 = (f32[8,128]{1,0:T(8,128)S(1)}, f32[8,128]{1,0:T(8,128)S(1)}, u32[]{:S(2)}, u32[]{:S(2)}) collective-permute-start(f32[8,128]{1,0:T(8,128)S(1)} %add.135), channel_id=1, source_target_pairs={{0,4},{1,5},{2,6},{3,7},{4,0},{5,1},{6,2},{7,3},{8,12},{9,13},{10,... | collective-permute-start | bytes 12296 | tf_op jit(solution)/shard_map/ppermute | solution.py:63
  54.6 6.1 %collective-permute-start.14 = (f32[16,1024]{1,0:T(8,128)S(1)}, f32[16,1024]{1,0:T(8,128)S(1)}, u32[]{:S(2)}, u32[]{:S(2)}) collective-permute-start(f32[16,1024]{1,0:T(8,128)S(1)} %get-tuple-element.111), channel_id=1, source_target_pairs={{0,6},{1,7},{2,4},{3,5},{4,2},{5,3},{6,0},{7,1},{8,14},{9,15},{10,... | collective-permute-start | bytes 196616 | tf_op jit(solution)/shard_map/ppermute | solution.py:63
  56.6 5.5 %collective-permute-start.13 = (f32[16,1024]{1,0:T(8,128)S(1)}, f32[16,1024]{1,0:T(8,128)S(1)}, u32[]{:S(2)}, u32[]{:S(2)}) collective-permute-start(f32[16,1024]{1,0:T(8,128)S(1)} %get-tuple-element.111), channel_id=1, source_target_pairs={{0,4},{1,5},{2,6},{3,7},{4,0},{5,1},{6,2},{7,3},{8,12},{9,13},{10,... | collective-permute-start | bytes 196616 | tf_op jit(solution)/shard_map/ppermute | solution.py:63
  56.6 5.5 %collective-permute-start.12 = (f32[16,1024]{1,0:T(8,128)S(1)}, f32[16,1024]{1,0:T(8,128)S(1)}, u32[]{:S(2)}, u32[]{:S(2)}) collective-permute-start(f32[16,1024]{1,0:T(8,128)S(1)} %get-tuple-element.111), channel_id=1, source_target_pairs={{0,2},{1,3},{2,0},{3,1},{4,6},{5,7},{6,4},{7,5},{8,10},{9,11},{10,... | collective-permute-start | bytes 196616 | tf_op jit(solution)/shard_map/ppermute | solution.py:63
  79.0 5.9 %collective-permute-start.22 = (f32[8,1024]{1,0:T(8,128)S(1)}, f32[8,1024]{1,0:T(8,128)S(1)}, u32[]{:S(2)}, u32[]{:S(2)}) collective-permute-start(f32[8,1024]{1,0:T(8,128)S(1)} %log_add_fusion.1), channel_id=1, source_target_pairs={{0,6},{1,7},{2,4},{3,5},{4,2},{5,3},{6,0},{7,1},{8,14},{9,15},{10,... | collective-permute-start | bytes 98312 | tf_op jit(solution)/shard_map/ppermute | solution.py:63
  86.0 35.5 %collective-permute-start.40 = (bf16[176,1024]{1,0:T(8,128)(2,1)}, bf16[176,1024]{1,0:T(8,128)(2,1)}, u32[]{:S(2)}, u32[]{:S(2)}) collective-permute-start(bf16[176,1024]{1,0:T(8,128)(2,1)} %get-tuple-element.131), channel_id=1, source_target_pairs={{0,6},{1,7},{2,4},{3,5},{4,2},{5,3},{6,0},{7,1},{8,14},{9,15},{10,... | collective-permute-start | bytes 1081352 | tf_op jit(solution)/shard_map/ppermute | solution.py:63
  88.0 33.5 %collective-permute-start.39 = (bf16[176,1024]{1,0:T(8,128)(2,1)}, bf16[176,1024]{1,0:T(8,128)(2,1)}, u32[]{:S(2)}, u32[]{:S(2)}) collective-permute-start(bf16[176,1024]{1,0:T(8,128)(2,1)} %get-tuple-element.131), channel_id=1, source_target_pairs={{0,4},{1,5},{2,6},{3,7},{4,0},{5,1},{6,2},{7,3},{8,12},{9,13},{10,... | collective-permute-start | bytes 1081352 | tf_op jit(solution)/shard_map/ppermute | solution.py:63
  88.9 32.6 %collective-permute-start.38 = (bf16[176,1024]{1,0:T(8,128)(2,1)}, bf16[176,1024]{1,0:T(8,128)(2,1)}, u32[]{:S(2)}, u32[]{:S(2)}) collective-permute-start(bf16[176,1024]{1,0:T(8,128)(2,1)} %get-tuple-element.131), channel_id=1, source_target_pairs={{0,2},{1,3},{2,0},{3,1},{4,6},{5,7},{6,4},{7,5},{8,10},{9,11},{10,... | collective-permute-start | bytes 1081352 | tf_op jit(solution)/shard_map/ppermute | solution.py:63
  123.1 41.1 %collective-permute-start.41 = (bf16[4,176,1024]{2,1,0:T(8,128)(2,1)S(1)}, bf16[4,176,1024]{2,1,0:T(8,128)(2,1)S(1)}, u32[]{:S(2)}, u32[]{:S(2)}) collective-permute-start(bf16[4,176,1024]{2,1,0:T(8,128)(2,1)S(1)} %pad_maximum_fusion.refs_11_.refs_2_), channel_id=1, source_target_pairs={{0,1},{1,0},{2,3},{3,2},{4,5},{5,4},{6,7},{7,6},{8,9},{9,8},{10,11... | collective-permute-start | bytes 4325384 | tf_op jit(solution)/shard_map/ppermute | solution.py:63
  126.4 10.4 %collective-permute-start.25 = (f32[8,1024]{1,0:T(8,128)S(1)}, f32[8,1024]{1,0:T(8,128)S(1)}, u32[]{:S(2)}, u32[]{:S(2)}) collective-permute-start(f32[8,1024]{1,0:T(8,128)S(1)} %add.152), channel_id=1, source_target_pairs={{0,4},{1,5},{2,6},{3,7},{4,0},{5,1},{6,2},{7,3},{8,12},{9,13},{10,... | collective-permute-start | bytes 98312 | tf_op jit(solution)/shard_map/ppermute | solution.py:63
  127.4 9.5 %collective-permute-start.26 = (f32[8,1024]{1,0:T(8,128)S(1)}, f32[8,1024]{1,0:T(8,128)S(1)}, u32[]{:S(2)}, u32[]{:S(2)}) collective-permute-start(f32[8,1024]{1,0:T(8,128)S(1)} %add.152), channel_id=1, source_target_pairs={{0,6},{1,7},{2,4},{3,5},{4,2},{5,3},{6,0},{7,1},{8,14},{9,15},{10,... | collective-permute-start | bytes 98312 | tf_op jit(solution)/shard_map/ppermute | solution.py:63
  129.2 7.6 %collective-permute-start.24 = (f32[8,1024]{1,0:T(8,128)S(1)}, f32[8,1024]{1,0:T(8,128)S(1)}, u32[]{:S(2)}, u32[]{:S(2)}) collective-permute-start(f32[8,1024]{1,0:T(8,128)S(1)} %add.152), channel_id=1, source_target_pairs={{0,2},{1,3},{2,0},{3,1},{4,6},{5,7},{6,4},{7,5},{8,10},{9,11},{10,... | collective-permute-start | bytes 98312 | tf_op jit(solution)/shard_map/ppermute | solution.py:63
  143.4 8.1 %collective-permute-start.29 = (f32[16,1024]{1,0:T(8,128)S(1)}, f32[16,1024]{1,0:T(8,128)S(1)}, u32[]{:S(2)}, u32[]{:S(2)}) collective-permute-start(f32[16,1024]{1,0:T(8,128)S(1)} %get-tuple-element.167), channel_id=1, source_target_pairs={{0,4},{1,5},{2,6},{3,7},{4,0},{5,1},{6,2},{7,3},{8,12},{9,13},{10,... | collective-permute-start | bytes 196616 | tf_op jit(solution)/shard_map/ppermute | solution.py:63
  144.5 7.0 %collective-permute-start.30 = (f32[16,1024]{1,0:T(8,128)S(1)}, f32[16,1024]{1,0:T(8,128)S(1)}, u32[]{:S(2)}, u32[]{:S(2)}) collective-permute-start(f32[16,1024]{1,0:T(8,128)S(1)} %get-tuple-element.166), channel_id=1, source_target_pairs={{0,6},{1,7},{2,4},{3,5},{4,2},{5,3},{6,0},{7,1},{8,14},{9,15},{10,... | collective-permute-start | bytes 196616 | tf_op jit(solution)/shard_map/ppermute | solution.py:63
  151.5 9.5 %collective-permute-start.33 = (f32[16,1024]{1,0:T(8,128)S(1)}, f32[16,1024]{1,0:T(8,128)S(1)}, u32[]{:S(2)}, u32[]{:S(2)}) collective-permute-start(f32[16,1024]{1,0:T(8,128)S(1)} %fusion.5.refs_7_), channel_id=1, source_target_pairs={{0,6},{1,7},{2,4},{3,5},{4,2},{5,3},{6,0},{7,1},{8,14},{9,15},{10,... | collective-permute-start | bytes 196616 | tf_op jit(solution)/shard_map/ppermute | solution.py:63
  153.6 7.4 %collective-permute-start.32 = (f32[16,1024]{1,0:T(8,128)S(1)}, f32[16,1024]{1,0:T(8,128)S(1)}, u32[]{:S(2)}, u32[]{:S(2)}) collective-permute-start(f32[16,1024]{1,0:T(8,128)S(1)} %fusion.5.refs_7_), channel_id=1, source_target_pairs={{0,4},{1,5},{2,6},{3,7},{4,0},{5,1},{6,2},{7,3},{8,12},{9,13},{10,... | collective-permute-start | bytes 196616 | tf_op jit(solution)/shard_map/ppermute | solution.py:63
  154.4 6.6 %collective-permute-start.31 = (f32[16,1024]{1,0:T(8,128)S(1)}, f32[16,1024]{1,0:T(8,128)S(1)}, u32[]{:S(2)}, u32[]{:S(2)}) collective-permute-start(f32[16,1024]{1,0:T(8,128)S(1)} %fusion.5.refs_7_), channel_id=1, source_target_pairs={{0,2},{1,3},{2,0},{3,1},{4,6},{5,7},{6,4},{7,5},{8,10},{9,11},{10,... | collective-permute-start | bytes 196616 | tf_op jit(solution)/shard_map/ppermute | solution.py:63
  159.9 19.3 %collective-permute-start.44 = (f32[664,128]{1,0:T(8,128)S(1)}, f32[664,128]{1,0:T(8,128)S(1)}, u32[]{:S(2)}, u32[]{:S(2)}) collective-permute-start(f32[664,128]{1,0:T(8,128)S(1)} %shard_map.410), channel_id=1, source_target_pairs={{0,16},{8,24},{16,0},{24,8},{1,17},{9,25},{17,1},{25,9},{2,18},{10... | collective-permute-start | bytes 1019912 | tf_op jit(solution)/shard_map/ppermute | solution.py:63
  161.0 9.4 %collective-permute-start.34 = (f32[4,16,1024]{2,1,0:T(8,128)S(1)}, f32[4,16,1024]{2,1,0:T(8,128)S(1)}, u32[]{:S(2)}, u32[]{:S(2)}) collective-permute-start(f32[4,16,1024]{2,1,0:T(8,128)S(1)} %pad_maximum_fusion.2.refs_2_), channel_id=1, source_target_pairs={{0,1},{1,0},{2,3},{3,2},{4,5},{5,4},{6,7},{7,6},{8,9},{9,8},{10,11... | collective-permute-start | bytes 786440 | tf_op jit(solution)/shard_map/ppermute | solution.py:63
  161.1 7.7 %collective-permute-start.36 = (f32[8,128]{1,0:T(8,128)S(1)}, f32[8,128]{1,0:T(8,128)S(1)}, u32[]{:S(2)}, u32[]{:S(2)}) collective-permute-start(f32[8,128]{1,0:T(8,128)S(1)} %slice.81), channel_id=1, source_target_pairs={{0,16},{8,24},{16,0},{24,8},{1,17},{9,25},{17,1},{25,9},{2,18},{10... | collective-permute-start | bytes 12296 | tf_op jit(solution)/shard_map/ppermute | solution.py:63
  162.1 8.3 %collective-permute-start.37 = (f32[8,128]{1,0:T(8,128)S(1)}, f32[8,128]{1,0:T(8,128)S(1)}, u32[]{:S(2)}, u32[]{:S(2)}) collective-permute-start(f32[8,128]{1,0:T(8,128)S(1)} %slice.81), channel_id=1, source_target_pairs={{0,24},{8,16},{16,8},{24,0},{1,25},{9,17},{17,9},{25,1},{2,26},{10... | collective-permute-start | bytes 12296 | tf_op jit(solution)/shard_map/ppermute | solution.py:63
  164.1 6.2 %collective-permute-start.35 = (f32[8,128]{1,0:T(8,128)S(1)}, f32[8,128]{1,0:T(8,128)S(1)}, u32[]{:S(2)}, u32[]{:S(2)}) collective-permute-start(f32[8,128]{1,0:T(8,128)S(1)} %slice.81), channel_id=1, source_target_pairs={{0,8},{8,0},{16,24},{24,16},{1,9},{9,1},{17,25},{25,17},{2,10},{10... | collective-permute-start | bytes 12296 | tf_op jit(solution)/shard_map/ppermute | solution.py:63
  168.8 12.0 %collective-permute-start.46 = (f32[480,128]{1,0:T(8,128)S(1)}, f32[480,128]{1,0:T(8,128)S(1)}, u32[]{:S(2)}, u32[]{:S(2)}) collective-permute-start(f32[480,128]{1,0:T(8,128)S(1)} %shard_map.411), channel_id=1, source_target_pairs={{0,8},{8,0},{16,24},{24,16},{1,9},{9,1},{17,25},{25,17},{2,10},{10... | collective-permute-start | bytes 737288 | tf_op jit(solution)/shard_map/ppermute | solution.py:63
  178.6 7.7 %collective-permute-start.42 = (f32[368,128]{1,0:T(8,128)S(1)}, f32[368,128]{1,0:T(8,128)S(1)}, u32[]{:S(2)}, u32[]{:S(2)}) collective-permute-start(f32[368,128]{1,0:T(8,128)S(1)} %shard_map.409), channel_id=1, source_target_pairs={{0,8},{8,0},{16,24},{24,16},{1,9},{9,1},{17,25},{25,17},{2,10},{10... | collective-permute-start | bytes 565256 | tf_op jit(solution)/shard_map/ppermute | solution.py:63
  179.2 12.7 %collective-permute-start.45 = (f32[664,128]{1,0:T(8,128)S(1)}, f32[664,128]{1,0:T(8,128)S(1)}, u32[]{:S(2)}, u32[]{:S(2)}) collective-permute-start(f32[664,128]{1,0:T(8,128)S(1)} %add.172), channel_id=1, source_target_pairs={{0,8},{8,0},{16,24},{24,16},{1,9},{9,1},{17,25},{25,17},{2,10},{10... | collective-permute-start | bytes 1019912 | tf_op jit(solution)/shard_map/ppermute | solution.py:63
  180.8 11.4 %collective-permute-start.47 = (f32[480,128]{1,0:T(8,128)S(1)}, f32[480,128]{1,0:T(8,128)S(1)}, u32[]{:S(2)}, u32[]{:S(2)}) collective-permute-start(f32[480,128]{1,0:T(8,128)S(1)} %add.174), channel_id=1, source_target_pairs={{0,16},{8,24},{16,0},{24,8},{1,17},{9,25},{17,1},{25,9},{2,18},{10... | collective-permute-start | bytes 737288 | tf_op jit(solution)/shard_map/ppermute | solution.py:63
  186.3 5.8 %collective-permute-start.43 = (f32[368,128]{1,0:T(8,128)S(1)}, f32[368,128]{1,0:T(8,128)S(1)}, u32[]{:S(2)}, u32[]{:S(2)}) collective-permute-start(f32[368,128]{1,0:T(8,128)S(1)} %add.170), channel_id=1, source_target_pairs={{0,16},{8,24},{16,0},{24,8},{1,17},{9,25},{17,1},{25,9},{2,18},{10... | collective-permute-start | bytes 565256 | tf_op jit(solution)/shard_map/ppermute | solution.py:63
  192.9 5.6 %collective-permute-start.50 = (f32[48,128]{1,0:T(8,128)S(1)}, f32[48,128]{1,0:T(8,128)S(1)}, u32[]{:S(2)}, u32[]{:S(2)}) collective-permute-start(f32[48,128]{1,0:T(8,128)S(1)} %get-tuple-element.140), channel_id=1, source_target_pairs={{0,6},{1,7},{2,4},{3,5},{4,2},{5,3},{6,0},{7,1},{8,14},{9,15},{10,... | collective-permute-start | bytes 73736 | tf_op jit(solution)/shard_map/ppermute | solution.py:63
  (67 other events, 583.3 us)

commit v5 on v4

--- a/solution.py
+++ b/solution.py
@@ -75,8 +75,8 @@
     return groups
 
 
-def total(value, axis):
-    for group in bit_groups(axis):
+def total(value, axis, done=0):
+    for group in bit_groups(axis)[done:]:
         if len(group) == 1:
             value = value + swap(value, axis, group[0])
         else:
@@ -221,23 +221,32 @@
     return jnp.where(row == at, sums, jnp.where(row == at + 1, squares, 0.0))
 
 
-def enc_kernel(low, me_ref, x_ref, w_ref, keep_ref, send_ref, buffer_ref, turn_ref, arrived):
-    count, _, share = buffer_ref.shape
-
-    def block(i):
-        at = pl.multiple_of(((low + i) ^ me_ref[0]) * share, share)
-        return pltpu.make_async_copy(x_ref.at[:, pl.ds(at, share)], buffer_ref.at[i], arrived.at[i])
-
-    for i in range(count):
-        block(i).start()
-    turn_ref[...] = jnp.transpose(w_ref[...]).astype(BF)
+def enc_kernel(low, count, share, near, me_ref, x_ref, w_ref, keep_ref, send_ref, weight_ref, turn_ref, arrived, *buffers):
+    def at(i):
+        return pl.ds(pl.multiple_of(((low + i) ^ me_ref[0]) * share, share), share)
+
+    weight = pltpu.make_async_copy(w_ref, weight_ref, arrived.at[count])
+    weight.start()
+    if not near:
+        (buffer_ref,) = buffers
+
+        def block(i):
+            return pltpu.make_async_copy(x_ref.at[:, at(i)], buffer_ref.at[i], arrived.at[i])
+
+        for i in range(count):
+            block(i).start()
+    weight.wait()
+    turn_ref[...] = jnp.transpose(weight_ref[...]).astype(BF)
 
     def pair(half, carry):
         for odd in range(2):
             i = 2 * half + odd
-            block(i).wait()
-            log_counts = jnp.log(1.0 + buffer_ref[i].astype(F32)).astype(BF)
-            part = nn(turn_ref[...], log_counts)
+            if near:
+                x = x_ref[:, at(i)]
+            else:
+                block(i).wait()
+                x = buffer_ref[i]
+            part = nn(turn_ref[...], jnp.log(1.0 + x.astype(F32)).astype(BF))
             if odd:
                 send_ref[half] = part.astype(BF)
             else:
@@ -254,9 +263,9 @@
     return jnp.concatenate([rows8[:, i * 128 : (i + 1) * 128] for i in range(count)], axis=0)
 
 
-def counts_kernel(rows, span, x_ref, lg_ref, dg_ref, keep_ref, batch_ref, logc_ref, mask_ref, side_ref, cell_ref, disp_ref, line_ref, held_ref, sum_ref):
+def counts_kernel(rows, span, x_ref, lg_ref, dg_ref, par_ref, batch_ref, lib_ref, logc_ref, mask_ref, side_ref, lib_out, cell_ref, disp_ref, line_ref, held_ref, sum_ref):
     step = pl.program_id(0)
-    genes, width = x_ref.shape
+    genes, width = mask_ref.shape
 
     @pl.when(step == 0)
     def _():
@@ -268,17 +277,19 @@
     table = one_hot(batch_ref[0], kinds)
     held_ref[...] += sum(table[:, t : t + 128] for t in range(0, width, 128))
     row = lax.broadcasted_iota(jnp.int32, (16, width), 0)
-    side_ref[0:kinds, :] = table.astype(BF)
-    side_ref[kinds:, :] = jnp.where(row == 0, 1.0, 0.0).astype(BF)
+    side_ref[0:kinds, part_of(step, width)] = table.astype(BF)
+    side_ref[kinds:, part_of(step, width)] = jnp.where(row == 0, 1.0, 0.0).astype(BF)
+    lib_out[...] = lib_ref[...]
     tiles = span // 128
     done = []
     for first in range(0, width, span):
         lanes = [slice(first + tile * 128, first + (tile + 1) * 128) for tile in range(tiles)]
+        far_lanes = [pl.ds(pl.multiple_of(step * width + first + tile * 128, 128), 128) for tile in range(tiles)]
 
         def chunk(g, cell):
             at = pl.ds(pl.multiple_of(g * rows, rows), rows)
-            keep = keep_ref[at, :]
-            xs = [x_ref[at, lanes[tile]].astype(F32) for tile in range(tiles)]
+            keep = par_ref[4, at, :]
+            xs = [x_ref[at, far_lanes[tile]].astype(F32) for tile in range(tiles)]
             logs = [jnp.log(1.0 + x) for x in xs]
             for tile in range(tiles):
                 logc_ref[at, lanes[tile]] = logs[tile].astype(BF)
@@ -378,7 +389,7 @@
     return jnp.where(lax.rem(place, 2) == 0, near_ref[lax.div(place, 2)], far_ref[lax.div(place, 2)])
 
 
-def decode_kernel(cells, latent, fast, me_ref, near_ref, far_ref, side_ref, stat_ref, norm_ref, plain_ref, w_ref, aff_ref, lse_ref, z_ref, score_ref, left_ref):
+def decode_kernel(cells, latent, fast, me_ref, near_ref, far_ref, side_ref, stat_ref, norm_ref, plain_ref, w_ref, aff_ref, lse_ref, z_ref, top_ref, mass_ref, score_ref, left_ref):
     kinds = plain_ref.shape[1] - 16
     step = pl.program_id(0)
     cells_at = part_of(step, score_ref.shape[1])
@@ -410,7 +421,7 @@
     aff_ref[:, cells_at] = affine
     hidden = relu_low(affine)
     width = score_ref.shape[1]
-    score_ref[...] = nn(w_ref[...], jnp.concatenate((hidden, ones), axis=0))
+    score_ref[...] = nn(w_ref[0:genes, :], jnp.concatenate((hidden, ones), axis=0))
     tiles = width // 128
     rows = 32
 
@@ -429,18 +440,24 @@
     high = [jnp.max(part, axis=0, keepdims=True) for part in best]
     wide = [jnp.broadcast_to(part, (8, 128)) for part in high]
 
+    far_lanes = [pl.ds(pl.multiple_of(step * width + tile * 128, 128), 128) for tile in range(tiles)]
+
     def mass(g, sums):
         at = pl.ds(pl.multiple_of(g * rows, rows), rows)
         new = []
         for tile in range(tiles):
             value = score_ref[at, slice(tile * 128, (tile + 1) * 128)]
             part = sums[tile]
+            pieces = []
             for index in range(rows // 8):
-                part = part + jnp.exp(value[index * 8 : (index + 1) * 8] - wide[tile])
+                pieces.append(jnp.exp(value[index * 8 : (index + 1) * 8] - wide[tile]))
+                part = part + pieces[-1]
+            mass_ref[at, far_lanes[tile]] = jnp.concatenate(pieces, axis=0)
             new.append(part)
         return tuple(new)
 
     sums = lax.fori_loop(0, genes // rows, mass, tuple(jnp.zeros((8, 128), F32) for _ in range(tiles)), unroll=5)
+    top_ref[pl.ds(step, 1), :] = jnp.concatenate(high, axis=1)
     lse = [high[tile] + jnp.log(jnp.sum(sums[tile], axis=0, keepdims=True)) for tile in range(tiles)]
     lse_ref[pl.ds(step, 1), :] = jnp.concatenate(lse, axis=1)
 
@@ -461,7 +478,7 @@
     out_ref[genes : genes + kinds, :] += nt(side_ref[0:kinds, cells_at], affine)
 
 
-def zinb_kernel(rows, span, hid_ref, w_ref, x_ref, par_ref, lib_ref, lse_ref, gam_ref, g_ref, rt_ref, mass_ref, recon_ref, acc_ref, sc_ref):
+def zinb_kernel(rows, span, hid_ref, e_ref, top_ref, w_ref, x_ref, par_ref, lib_ref, lse_ref, gam_ref, g_ref, rt_ref, mass_ref, recon_ref, acc_ref, sc_ref):
     step = pl.program_id(0)
     genes, width = x_ref.shape
 
@@ -471,17 +488,17 @@
 
     one_row = pl.ds(step, 1)
     gam_row = gam_ref[one_row, :]
-    shift = lib_ref[one_row, :] - lse_ref[one_row, :]
+    level = jnp.exp(top_ref[one_row, :] + (lib_ref[one_row, :] - lse_ref[one_row, :]))
     row = lax.broadcasted_iota(jnp.int32, (16, width), 0)
-    hi, mid, lo = three(shift)
-    extra = jnp.where(row < 3, 1.0, jnp.where(row == 3, hi.astype(F32), jnp.where(row == 4, mid.astype(F32), jnp.where(row == 5, lo.astype(F32), 0.0))))
-    table = jnp.concatenate((relu_low(hid_ref[:, part_of(step, width)]), extra.astype(BF)), axis=0)
-    sc_ref[...] = nn(w_ref[...], table)
+    ones = jnp.where(row < 3, 1.0, 0.0).astype(BF)
+    sc_ref[...] = nn(w_ref[genes:, :], jnp.concatenate((relu_low(hid_ref[:, part_of(step, width)]), ones), axis=0))
     tiles = span // 128
     mass_out, recon_out = [], []
     for first in range(0, width, span):
         lanes = [slice(first + tile * 128, first + (tile + 1) * 128) for tile in range(tiles)]
         far_lanes = [pl.ds(pl.multiple_of(step * width + first + tile * 128, 128), 128) for tile in range(tiles)]
+        scale = [jnp.broadcast_to(level[:, lanes[tile]], (rows, 128)) for tile in range(tiles)]
+
         def chunk(g, state):
             at = pl.ds(pl.multiple_of(g * rows, rows), rows)
             at_drop = pl.ds(pl.multiple_of(genes + g * rows, rows), rows)
@@ -491,8 +508,8 @@
             for tile in range(tiles):
                 rec, prod, back = state[tile]
                 x = x_ref[at, lanes[tile]].astype(F32)
-                mu = jnp.exp(sc_ref[at, lanes[tile]])
-                drop = sc_ref[at_drop, lanes[tile]]
+                mu = e_ref[at, far_lanes[tile]] * scale[tile]
+                drop = sc_ref[at, lanes[tile]]
                 both = mu + the
                 r = 1.0 / both
                 log_both = jnp.log(both)
@@ -602,7 +619,7 @@
                     ref[index, line : line + 1, lanes] = oh_ref[pl.ds(owner * part + k, 1), :] * scale
 
 
-def dec_grad_kernel(cells, rt_ref, hid_ref, mass_ref, lib_ref, g_ref, acc_ref, dig_ref, th_ref, dec_ref, mix_ref):
+def dec_grad_kernel(cells, rt_ref, hid_ref, mass_ref, lib_ref, g_ref, acc_ref, dig_ref, par_ref, dec_ref, mix_ref):
     step = pl.program_id(0)
     steps = pl.num_programs(0)
     genes = rt_ref.shape[0]
@@ -629,7 +646,7 @@
         pick = jnp.where(lax.broadcasted_iota(jnp.int32, (8, 16), 1) < 2, 1.0, 0.0)
         score_row = row_sums(acc_ref[0]) - nt(pick, mix[:, hidden:], HI)
         drop_row = row_sums(acc_ref[1])
-        disp_row = row_sums((acc_ref[2] + dig_ref[...]) * th_ref[...])
+        disp_row = row_sums((acc_ref[2] + dig_ref[...]) * par_ref[1])
         line = lax.broadcasted_iota(jnp.int32, score_row.shape, 0)
         gene_rows = scale * jnp.where(
             line == 0, score_row, jnp.where(line == 1, drop_row, jnp.where(line == 2, disp_row, 0.0))
@@ -812,7 +829,7 @@
     value = jnp.sqrt(square + small_square)
     factor = jnp.minimum(1.0, max_norm / value)
     (enc_n, enc_m, enc_v, enc_l, dec_n, dec_m, dec_v, dec_l, gene_n, gene_m, gene_v, small_n, small_m, small_v, head_n, head_m, head_v, norm_n, norm_m, norm_v, norm_out) = outs
-    norm_out[...] = jnp.broadcast_to(value, norm_out.shape)
+    norm_out[...] = value
     new, first, second = step_of(enc[0][...], enc_g_ref[...] * factor, enc[1][...], enc[2][...], rate_genes)
     enc_n[...], enc_m[...], enc_v[...], enc_l[...] = new, first, second, new.astype(BF)
     for index in range(2):
@@ -872,35 +889,37 @@
     own_block = pl.BlockSpec((1, 1, share), lambda i, m: (m[0], 0, 0))
     own_lanes = lambda rows: pl.BlockSpec((rows, share), lambda i, m: (0, m[0]))
     lane_block = lambda rows: pl.BlockSpec((rows, width), lambda i, *_: (0, i))
-    full = lambda array: (array, whole(array.shape))
     here = pl.BlockSpec(memory_space=pltpu.VMEM)
-    new = lambda shape, dtype=F32: (shape, dtype, whole(shape))
-
-    def encode(low, count, weight):
+    full = lambda array: (array, here)
+    out_of = lambda shape, dtype=F32: (shape, dtype, whole(shape))
+    new = lambda shape, dtype=F32: (shape, dtype, here)
+
+    def encode(low, count, weight, near=False):
         return call(
-            lambda *refs: enc_kernel(low, *refs),
+            lambda *refs: enc_kernel(low, count, share, near, *refs),
             (1,),
             [
                 (me if fast else me & 1, None),
-                (in_hbm(x_t), pl.BlockSpec(memory_space=pl.ANY)),
-                full(weight),
+                (x_t, here) if near else (in_hbm(x_t), pl.BlockSpec(memory_space=pl.ANY)),
+                (in_hbm(weight), pl.BlockSpec(memory_space=pl.ANY)),
             ],
             [new((count // 2, hidden, share)), new((count // 2, hidden, share), BF)],
             scratch=[
-                pltpu.VMEM((count, genes, share), BF),
+                pltpu.VMEM((genes, hidden), F32),
                 pltpu.VMEM((hidden, genes), BF),
-                pltpu.SemaphoreType.DMA((count,)),
-            ],
+                pltpu.SemaphoreType.DMA((count + 1,)),
+            ]
+            + ([] if near else [pltpu.VMEM((count, genes, share), BF)]),
             scalars=1,
-            us=3.0,
-            mib=20,
+            us=2.0 if near else 3.0,
+            mib=16,
         )
 
     slot = pl.BlockSpec((1, hidden, share), lambda i, m: (0, 0, 0))
     if fast:
         keep_far, send_far = encode(4, 4, enc_w)
         got_far = swap(send_far, "genes", 1)
-        keep_near, send_near = encode(0, 4, after(enc_w, send_far))
+        keep_near, send_near = encode(0, 4, after(enc_w, send_far), True)
         far = [
             swap((keep_far[k : k + 1] + got_far[k : k + 1].astype(F32)).astype(BF), "genes", 4 + 2 * k)
             for k in range(2)
@@ -945,20 +964,22 @@
         ],
     )
     batch_spec = pl.BlockSpec((1, 1, width), lambda i, *_: (i, 0, 0))
-    logc, x_kept, side, gam_cell, dig_acc, log_lines, held = call(
+    logc, x_kept, side, lib8, gam_cell, dig_acc, log_lines, held = call(
         lambda *refs: counts_kernel(16, min(512, width), *refs),
         (blocks,),
         [
-            (x_t, lane_block(genes)),
+            (x_t, here),
             full(lg_tab),
             full(dg_tab),
-            (par, pl.BlockSpec((None, genes, 128), lambda i: (4, 0, 0))),
+            full(par),
             (batch_all, batch_spec),
+            full(lib8),
         ],
         [
             ((genes, rows_all), BF, lane_block(genes), True),
             ((genes, rows_all), BF, lane_block(genes), True),
-            ((kinds + 16, rows_all), BF, lane_block(kinds + 16)),
+            ((kinds + 16, rows_all), BF, here),
+            new((blocks, width)),
             new((blocks, width)),
             new((genes, 128)),
             new((8 * gene_lines + 8, 128)),
@@ -1005,7 +1026,7 @@
         stat_dec = lax.psum(pack[8:16, :hidden], "genes")
     stat_dec = total(stat_dec, "cells")
 
-    aff_dec, lse, z_all = call(
+    aff_dec, lse, z_all, top, mass_all = call(
         lambda *refs: decode_kernel(cells, latent, fast, *refs),
         (blocks,),
         [
@@ -1016,12 +1037,14 @@
             full(stat_dec),
             full(norm_t),
             full(dec_plain),
-            (aug, pl.BlockSpec((genes, hidden + 16), lambda i, m: (0, 0))),
+            full(aug),
         ],
         [
             ((hidden, rows_all), BF, here),
             new((blocks, width)),
             ((16, rows_all), F32, here),
+            new((blocks, width)),
+            ((genes, rows_all), F32, here),
         ],
         scratch=[pltpu.VMEM((genes, width), F32), pltpu.VMEM((2 * hidden, kinds + 48), BF)],
         scalars=1,
@@ -1035,20 +1058,23 @@
         (blocks,),
         [
             (aff_dec, here),
+            (mass_all, here),
+            full(top),
             full(aug),
             (in_hbm(x_kept), lane_block(genes)),
-            (par, pl.BlockSpec((4, genes, 128), lambda i: (0, 0, 0))),
+            full(par),
             full(lib8),
             full(lse_all),
             full(gam_cell),
         ],
         [((2 * genes, rows_all), BF, here), ((genes, rows_all), BF, here)]
         + [new((blocks, width)), new((blocks, width)), new((3, genes, 128))],
-        scratch=[pltpu.VMEM((2 * genes, width), F32)],
+        scratch=[pltpu.VMEM((genes, width), F32)],
         mib=20,
         us=28.0,
     )
-    mass_own, mass = mass, total(mass, "genes")
+    mass_low = mass + swap(mass, "genes", 1)
+    mass = total(mass_low, "genes", 1)
     part_a, part_r, dec_acc = call(
         lambda *refs: back_kernel(width, *refs),
         (blocks,),
@@ -1067,7 +1093,7 @@
         us=9.0,
     )
 
-    aff_near, aff_far = gather_genes(after(aff_own, lse_all), fast, blocks, width, mass_own)
+    aff_near, aff_far = gather_genes(after(aff_own, lse_all), fast, blocks, width, mass_low)
     fixed_rows = genes + kinds + 8 * gene_lines + 8
     (fixed,) = call(
         lambda *refs: enc_sums_kernel(fast, *refs),
@@ -1093,7 +1119,7 @@
             (me if fast else jnp.zeros_like(me), None),
             (part_a, here),
             (part_r, here),
-            (mass, full8),
+            (mass, here),
             (aff_dec, here),
             full(lib8),
             full(stat_dec),
@@ -1111,9 +1137,27 @@
         scalars=1,
         us=5.0,
     )
+    (dec_part,) = call(
+        lambda *refs: dec_grad_kernel(cells, *refs),
+        (blocks,),
+        [
+            (rt, here),
+            (aff_dec, here),
+            (mass, here),
+            full(lib8),
+            full(dec_acc),
+            full(gene_acc),
+            full(dig_acc),
+            full(par),
+        ],
+        [new((2 * genes + 8 * gene_lines, hidden))],
+        scratch=[pltpu.VMEM((genes, hidden + 16), F32)],
+        us=5.0,
+    )
     if fast:
         got_d = swap(send_d, "genes", 1)
         pieces = [swap(keep_d[k] + got_d[k], "genes", 2 * k) for k in (1, 2, 3)]
+        pieces = [after(piece, dec_part) for piece in pieces]
         own_d = (keep_d[0] + got_d[0] + pieces[0]) + (pieces[1] + pieces[2])
         sums_dec = own_d[8:, :hidden]
     else:
@@ -1123,23 +1167,6 @@
         own_d = lax.psum_scatter(both, "genes", scatter_dimension=0, tiled=True)[0]
     sums_dec = total(sums_dec, "cells")
     d_near, d_far = gather_genes(own_d, fast, blocks, width)
-    (dec_part,) = call(
-        lambda *refs: dec_grad_kernel(cells, *refs),
-        (blocks,),
-        [
-            (rt, here),
-            (aff_dec, here),
-            (mass, full8),
-            full(lib8),
-            full(dec_acc),
-            full(gene_acc),
-            full(dig_acc),
-            (par, pl.BlockSpec((None, genes, 128), lambda i: (1, 0, 0))),
-        ],
-        [new((2 * genes + 8 * gene_lines, hidden))],
-        scratch=[pltpu.VMEM((genes, hidden + 16), F32)],
-        us=5.0,
-    )
     dec_g = total_by_halves(dec_part, "cells", (2, 1))
 
     size = (2 * kinds + 64) // 8
@@ -1206,12 +1233,12 @@
         outs += [(one.shape, F32)] * 3
         if index < 2:
             outs.append((one.shape, BF))
-    outs.append(((8, 128), F32))
+    outs.append(((1, 1), F32))
     res = call(
         lambda *refs: update_kernel(cells, latent, *refs),
         (1,),
         [(me if fast else jnp.zeros_like(me), None)] + [full(array) for array in ins],
-        [new(shape, dtype) for shape, dtype in outs],
+        [out_of(shape, dtype) for shape, dtype in outs],
         scratch=[
             pltpu.VMEM((8 * (size + 8), hidden), F32),
             pltpu.VMEM((2 * kinds + 16, hidden), F32),
@@ -1229,7 +1256,7 @@
         *res[8:14],
         *head_res,
         *res[17:20],
-        res[20][0, 0],
+        res[20].reshape(()),
         loss.reshape(share),
     )
 

time: 204 us -> 195 us (0.956)
  waiting for transfers between devices: 42.9 us -> 37.8 us
  local copies, waits for them, and re-layouts: 5.65 us -> 2.66 us
    ppermute x52, waiting for transfers between devices: 42.9 us -> 37.8 us  [swap(): return lax.ppermute(value, axis, [(i, i ^ bit) for i in range(count)])]
    unnamed x94 -> x58, local copies, waits for them, and re-layouts: 4.36 us -> 2.64 us
  transfers between devices with their start and end apart: 52 -> 52, of which waited for: 22 -> 25; matrix products, arithmetic and copies ran while one was open for 1% -> 1% of each run, Pallas kernels for 37% -> 37%
where the time goes in v5:
time: 195 us; the launch traced here: 194 us
  Pallas kernels  90.3 us (46%)
  starting transfers between devices  59.2 us (30%)
  waiting for transfers between devices  37.8 us (19%)
  local copies, waits for them, and re-layouts  2.66 us (1%)
  other arithmetic  2.3 us (1%)
  between operations  2.16 us (1%)
    pallas_call x15, Pallas kernels, call(): pl.pallas_call(kernel, out_shape=[pltpu.HBM(out[0], out[1]) if len(out) =...  90.3 us
    ppermute x52, starting transfers between devices, swap(): return lax.ppermute(value, axis, [(i, i ^ bit) for i in range(count)])  59.2 us
    ppermute x52, waiting for transfers between devices, swap(): return lax.ppermute(value, axis, [(i, i ^ bit) for i in range(count)])  37.8 us
  transfers between devices with their start and end apart: 52, of which 25 were waited for; matrix products, arithmetic and copies ran while one was open for 1% of the time, Pallas kernels for 37%

profile of v5, /device:TPU:0, one launch (start us, length us, event | category | flops | bytes accessed | tf_op | source)
XLA Modules:
  0.0 194.4 jit_solution(13704701444474889977)
XLA Ops:
  0.7 3.0 %shard_map.399 = (f32[2,128,1024]{2,1,0:T(8,128)S(1)}, bf16[2,128,1024]{2,1,0:T(8,128)(2,1)S(1)}) custom-call(s32[1]{0:T(128)} %bitcast.refs_0_.me_ref.refs_1_, bf16[320,8192]{1,0:T(8,128)(2,1)} %bitcast.49, f32[320,128]{1,0:T(8,128)} %refs_10_.1), custom_call_target="tpu_custom_call" | custom-call | bytes 11070000 | tf_op jit(solution)/shard_map/pallas_call | solution.py:46
  4.2 2.4 %shard_map.400 = (f32[2,128,1024]{2,1,0:T(8,128)S(1)}, bf16[2,128,1024]{2,1,0:T(8,128)(2,1)S(1)}) custom-call(s32[1]{0:T(128)} %bitcast.refs_0_.me_ref.refs_1_, bf16[320,8192]{1,0:T(8,128)(2,1)S(1)} %bitcast.50, f32[320,128]{1,0:T(8,128)} %refs_10_.1), custom_call_target="tpu_custom_call" | custom-call | bytes 7380000 | tf_op jit(solution)/shard_map/pallas_call | solution.py:46
  7.9 3.8 %collective-permute-start.2 = (bf16[1,128,1024]{2,1,0:T(8,128)(2,1)}, bf16[1,128,1024]{2,1,0:T(8,128)(2,1)S(1)}, u32[]{:S(2)}, u32[]{:S(2)}) collective-permute-start(bf16[1,128,1024]{2,1,0:T(8,128)(2,1)} %get-tuple-element.177), channel_id=1, source_target_pairs={{0,4},{1,5},{2,6},{3,7},{4,0},{5,1},{6,2},{7,3},{8,12},{9,13},{10,... | collective-permute-start | bytes 786440 | tf_op jit(solution)/shard_map/ppermute | solution.py:63
  15.2 2.5 %copy-done.1 = bf16[8192,320]{0,1:T(8,128)(2,1)S(1)} copy-done((bf16[8192,320]{0,1:T(8,128)(2,1)S(1)}, bf16[8192,320]{0,1:T(8,128)(2,1)}, u32[]{:S(2)}) %copy-start.1) | copy-done | bytes 5242904
  17.7 17.4 %shard_map.402 = (bf16[320,8192]{1,0:T(8,128)(2,1)}, bf16[320,8192]{1,0:T(8,128)(2,1)}, bf16[144,8192]{1,0:T(8,128)(2,1)S(1)}, f32[8,1024]{1,0:T(8,128)S(1)}, f3...) custom-call(bf16[320,8192]{1,0:T(8,128)(2,1)S(1)} %bitcast.51, ...), custom_call_target="tpu_custom_call" | custom-call | bytes 55350000 | tf_op jit(solution)/shard_map/pallas_call | solution.py:46
  35.1 2.2 %shard_map.403 = (f32[128,1024]{1,0:T(8,128)S(1)}, f32[8,128]{1,0:T(8,128)S(1)}) custom-call(s32[1]{0:T(128)} %bitcast.refs_0_.me_ref.refs_1_, f32[2,128,1024]{2,1,0:T(8,128)S(1)} %get-tuple-element.101.keep_ref, bf16[2,128,1024]{2,1,0:T(8,128)(2,1)S(1)} %collective-permute-done.got_ref, bf16[1,128,1024]{2,1,0:T(8,128)(2,1)S(1)} %collective-permute-done.2.one_ref, ...), custom_call_target="tpu_custom_call" | custom-call | bytes 7380000 | tf_op jit(solution)/shard_map/pallas_call | solution.py:46
  38.5 3.1 %collective-permute-start.7 = (f32[8,128]{1,0:T(8,128)S(1)}, f32[8,128]{1,0:T(8,128)S(1)}, u32[]{:S(2)}, u32[]{:S(2)}) collective-permute-start(f32[8,128]{1,0:T(8,128)S(1)} %add.135), channel_id=1, source_target_pairs={{0,4},{1,5},{2,6},{3,7},{4,0},{5,1},{6,2},{7,3},{8,12},{9,13},{10,... | collective-permute-start | bytes 12296 | tf_op jit(solution)/shard_map/ppermute | solution.py:63
  43.2 3.8 %collective-permute-done.8 = f32[8,128]{1,0:T(8,128)S(1)} collective-permute-done((f32[8,128]{1,0:T(8,128)S(1)}, f32[8,128]{1,0:T(8,128)S(1)}, u32[]{:S(2)}, u32[]{:S(2)}) %collective-permute-start.8) | collective-permute-done | bytes 4128 | tf_op jit(solution)/shard_map/ppermute | solution.py:63
  50.7 2.4 %collective-permute-done.11 = f32[8,128]{1,0:T(8,128)S(1)} collective-permute-done((f32[8,128]{1,0:T(8,128)S(1)}, f32[8,128]{1,0:T(8,128)S(1)}, u32[]{:S(2)}, u32[]{:S(2)}) %collective-permute-start.11) | collective-permute-done | bytes 4128 | tf_op jit(solution)/shard_map/ppermute | solution.py:63
  53.6 1.8 shard_map.404
  55.4 2.0 %collective-permute-start.14 = (f32[16,1024]{1,0:T(8,128)S(1)}, f32[16,1024]{1,0:T(8,128)S(1)}, u32[]{:S(2)}, u32[]{:S(2)}) collective-permute-start(f32[16,1024]{1,0:T(8,128)S(1)} %get-tuple-element.117), channel_id=1, source_target_pairs={{0,6},{1,7},{2,4},{3,5},{4,2},{5,3},{6,0},{7,1},{8,14},{9,15},{10,... | collective-permute-start | bytes 196616 | tf_op jit(solution)/shard_map/ppermute | solution.py:63
  57.4 2.4 %collective-permute-start.12 = (f32[16,1024]{1,0:T(8,128)S(1)}, f32[16,1024]{1,0:T(8,128)S(1)}, u32[]{:S(2)}, u32[]{:S(2)}) collective-permute-start(f32[16,1024]{1,0:T(8,128)S(1)} %get-tuple-element.117), channel_id=1, source_target_pairs={{0,2},{1,3},{2,0},{3,1},{4,6},{5,7},{6,4},{7,5},{8,10},{9,11},{10,... | collective-permute-start | bytes 196616 | tf_op jit(solution)/shard_map/ppermute | solution.py:63
  68.2 2.4 %collective-permute-done.18 = f32[8,128]{1,0:T(8,128)S(1)} collective-permute-done((f32[8,128]{1,0:T(8,128)S(1)}, f32[8,128]{1,0:T(8,128)S(1)}, u32[]{:S(2)}, u32[]{:S(2)}) %collective-permute-start.18) | collective-permute-done | bytes 4128 | tf_op jit(solution)/shard_map/ppermute | solution.py:63
  70.7 7.6 %shard_map.405 = (bf16[128,8192]{1,0:T(8,128)(2,1)S(1)}, f32[8,1024]{1,0:T(8,128)S(1)}, f32[16,8192]{1,0:T(8,128)S(1)}, f32[8,1024]{1,0:T(8,128)S(1)}, f32[320,8192]{1,0:T(8,128)S(1)}) custom-call(s32[1]{0:T(128)} %bitcast.refs_0_.me_ref.refs_1_, f32[4,16,1024]{2,1,0:T(8,128)S(1)} %pad_maximum_fusion.1.refs_1_, ...), custom_call_target="tpu_custom_call" | custom-call | bytes 29520000 | tf_op jit(solution)/shard_map/pallas_call | solution.py:46
  79.6 2.0 %collective-permute-start.22 = (f32[8,1024]{1,0:T(8,128)S(1)}, f32[8,1024]{1,0:T(8,128)S(1)}, u32[]{:S(2)}, u32[]{:S(2)}) collective-permute-start(f32[8,1024]{1,0:T(8,128)S(1)} %log_add_fusion.1), channel_id=1, source_target_pairs={{0,6},{1,7},{2,4},{3,5},{4,2},{5,3},{6,0},{7,1},{8,14},{9,15},{10,... | collective-permute-start | bytes 98312 | tf_op jit(solution)/shard_map/ppermute | solution.py:63
  82.3 1.7 collective-permute-start.20
  86.6 2.0 %collective-permute-start.40 = (bf16[176,1024]{1,0:T(8,128)(2,1)S(1)}, bf16[176,1024]{1,0:T(8,128)(2,1)S(1)}, u32[]{:S(2)}, u32[]{:S(2)}) collective-permute-start(bf16[176,1024]{1,0:T(8,128)(2,1)S(1)} %get-tuple-element.146), channel_id=1, source_target_pairs={{0,6},{1,7},{2,4},{3,5},{4,2},{5,3},{6,0},{7,1},{8,14},{9,15},{10,... | collective-permute-start | bytes 1081352 | tf_op jit(solution)/shard_map/ppermute | solution.py:63
  91.1 26.4 %shard_map.406 = (bf16[640,8192]{1,0:T(8,128)(2,1)S(1)}, bf16[320,8192]{1,0:T(8,128)(2,1)S(1)}, f32[8,1024]{1,0:T(8,128)S(1)}, f32[8,1024]{1,0:T(8,128)S(1)}, f32[3,320,128]{2,1,0:T(8,128)S(1)}) custom-call(bf16[128,8192]{1,0:T(8,128)(2,1)S(1)} %get-tuple-element.121.refs_0_.refs_2_.refs_4_.refs_1_, f32[320,8192]{1,0:T(8,128)S(1)} %get-tuple-element.122.refs_1_, ...), custom_call_target="tpu_custom_call" | custom-call | bytes 103320000 | tf_op jit(solution)/shard_map/pallas_call | solution.py:46
  120.2 1.9 %collective-permute-start.26 = (f32[8,1024]{1,0:T(8,128)S(1)}, f32[8,1024]{1,0:T(8,128)S(1)}, u32[]{:S(2)}, u32[]{:S(2)}) collective-permute-start(f32[8,1024]{1,0:T(8,128)S(1)} %add.152), channel_id=1, source_target_pairs={{0,6},{1,7},{2,4},{3,5},{4,2},{5,3},{6,0},{7,1},{8,14},{9,15},{10,... | collective-permute-start | bytes 98312 | tf_op jit(solution)/shard_map/ppermute | solution.py:63
  123.6 6.9 %shard_map.407 = (f32[128,8192]{1,0:T(8,128)S(1)}, f32[128,8192]{1,0:T(8,128)S(1)}, f32[640,128]{1,0:T(8,128)S(1)}) custom-call(bf16[640,8192]{1,0:T(8,128)(2,1)S(1)} %get-tuple-element.128.refs_0_, bf16[320,8192]{1,0:T(8,128)(2,1)S(1)} %get-tuple-element.129.refs_1_.refs_0_, bf16[128,8192]{1,0:T(8,128)(2,1)S(1)} %get-tuple-element.121.refs_0_.refs_2_.refs_4_.refs_1_, ...), custom_call_target="tpu_custom_call" | custom-call | bytes 33210000 | tf_op jit(solution)/shard_map/pallas_call | solution.py:46
  130.5 3.4 %shard_map.408 = (f32[4,16,1024]{2,1,0:T(8,128)S(1)}, f32[4,16,1024]{2,1,0:T(8,128)S(1)}) custom-call(s32[1]{0:T(128)} %bitcast.refs_0_.me_ref.refs_1_, f32[128,8192]{1,0:T(8,128)S(1)} %get-tuple-element.131.refs_1_, f32[128,8192]{1,0:T(8,128)S(1)} %get-tuple-element.132.refs_2_, f32[8,1024]{1,0:T(8,128)S(1)} %add_add_fusion.refs_3_.refs_2_, ...), custom_call_target="tpu_custom_call" | custom-call | bytes 18450000 | tf_op jit(solution)/shard_map/pallas_call | solution.py:46
  136.2 1.9 %collective-permute-start.29 = (f32[16,1024]{1,0:T(8,128)S(1)}, f32[16,1024]{1,0:T(8,128)S(1)}, u32[]{:S(2)}, u32[]{:S(2)}) collective-permute-start(f32[16,1024]{1,0:T(8,128)S(1)} %get-tuple-element.179), channel_id=1, source_target_pairs={{0,4},{1,5},{2,6},{3,7},{4,0},{5,1},{6,2},{7,3},{8,12},{9,13},{10,... | collective-permute-start | bytes 196616 | tf_op jit(solution)/shard_map/ppermute | solution.py:63
  138.1 1.9 collective-permute-start.30
  140.0 3.8 %shard_map.409 = f32[664,128]{1,0:T(8,128)S(1)} custom-call(bf16[320,8192]{1,0:T(8,128)(2,1)S(1)} %get-tuple-element.129.refs_1_.refs_0_, bf16[128,8192]{1,0:T(8,128)(2,1)S(1)} %get-tuple-element.121.refs_0_.refs_2_.refs_4_.refs_1_, f32[8,1024]{1,0:T(8,128)S(1)} %add_add_fusion.refs_3_.refs_2_, f32[8,1024]{1,0:T(8,128)S(1)} %get-tuple-element.125.refs_6_.refs_5_.refs_3_, ...), custom_call_target="tpu_custom_call" | custom-call | bytes 18450000 | tf_op jit(solution)/shard_map/pallas_call | solution.py:46
  144.5 2.0 %collective-permute-start.33 = (f32[16,1024]{1,0:T(8,128)S(1)}, f32[16,1024]{1,0:T(8,128)S(1)}, u32[]{:S(2)}, u32[]{:S(2)}) collective-permute-start(f32[16,1024]{1,0:T(8,128)S(1)} %fusion.5.refs_7_), channel_id=1, source_target_pairs={{0,6},{1,7},{2,4},{3,5},{4,2},{5,3},{6,0},{7,1},{8,14},{9,15},{10,... | collective-permute-start | bytes 196616 | tf_op jit(solution)/shard_map/ppermute | solution.py:63
  156.9 3.4 %shard_map.411 = f32[480,128]{1,0:T(8,128)S(1)} custom-call(s32[1]{0:T(128)} %bitcast.refs_0_.me_ref.refs_1_, bf16[320,8192]{1,0:T(8,128)(2,1)S(1)} %bitcast.53, bf16[4,176,1024]{2,1,0:T(8,128)(2,1)S(1)} %pad_maximum_fusion.refs_11_.refs_2_, bf16[4,176,1024]{2,1,0:T(8,128)(2,1)S(1)} %collective-permute-done.41.refs_12_.refs_3_, ...), custom_call_target="tpu_custom_call" | custom-call | bytes 14760000 | tf_op jit(solution)/shard_map/pallas_call | solution.py:46
  161.4 8.1 %shard_map.410 = f32[368,128]{1,0:T(8,128)S(1)} custom-call(s32[1]{0:T(128)} %bitcast.refs_0_.me_ref.refs_1_, s32[1]{0:T(128)} %bitcast.refs_0_.me_ref.refs_1_, f32[4,16,1024]{2,1,0:T(8,128)S(1)} %pad_maximum_fusion.2.refs_2_, f32[4,16,1024]{2,1,0:T(8,128)S(1)} %collective-permute-done.34.refs_3_, ...), custom_call_target="tpu_custom_call" | custom-call | bytes 40590000 | tf_op jit(solution)/shard_map/pallas_call | solution.py:46
  173.3 3.9 %collective-permute-done.42 = f32[368,128]{1,0:T(8,128)S(1)} collective-permute-done((f32[368,128]{1,0:T(8,128)S(1)}, f32[368,128]{1,0:T(8,128)S(1)}, u32[]{:S(2)}, u32[]{:S(2)}) %collective-permute-start.42) | collective-permute-done | bytes 188448 | tf_op jit(solution)/shard_map/ppermute | solution.py:63
  178.8 3.9 %collective-permute-done.45 = f32[664,128]{1,0:T(8,128)S(1)} collective-permute-done((f32[664,128]{1,0:T(8,128)S(1)}, f32[664,128]{1,0:T(8,128)S(1)}, u32[]{:S(2)}, u32[]{:S(2)}) %collective-permute-start.45) | collective-permute-done | bytes 340000 | tf_op jit(solution)/shard_map/ppermute | solution.py:63
  183.8 2.0 %collective-permute-start.50 = (f32[48,128]{1,0:T(8,128)S(1)}, f32[48,128]{1,0:T(8,128)S(1)}, u32[]{:S(2)}, u32[]{:S(2)}) collective-permute-start(f32[48,128]{1,0:T(8,128)S(1)} %get-tuple-element.152), channel_id=1, source_target_pairs={{0,6},{1,7},{2,4},{3,5},{4,2},{5,3},{6,0},{7,1},{8,14},{9,15},{10,... | collective-permute-start | bytes 73736 | tf_op jit(solution)/shard_map/ppermute | solution.py:63
  185.9 2.3 %collective-permute-start.48 = (f32[48,128]{1,0:T(8,128)S(1)}, f32[48,128]{1,0:T(8,128)S(1)}, u32[]{:S(2)}, u32[]{:S(2)}) collective-permute-start(f32[48,128]{1,0:T(8,128)S(1)} %get-tuple-element.152), channel_id=1, source_target_pairs={{0,2},{1,3},{2,0},{3,1},{4,6},{5,7},{6,4},{7,5},{8,10},{9,11},{10,... | collective-permute-start | bytes 73736 | tf_op jit(solution)/shard_map/ppermute | solution.py:63
  192.0 2.2 %shard_map.413 = (f32[320,128]{1,0:T(8,128)}, f32[320,128]{1,0:T(8,128)}, f32[320,128]{1,0:T(8,128)}, bf16[320,128]{1,0:T(8,128)(2,1)}, f32[2,320,128]{2,1,0:T(8...) custom-call(s32[1]{0:T(128)} %bitcast.refs_0_.me_ref.refs_1_, ...), custom_call_target="tpu_custom_call" | custom-call | bytes 7380000 | tf_op jit(solution)/shard_map/pallas_call | solution.py:46
  (176 shorter events, 55.7 us)
Async XLA Ops:
  6.5 6.5 %collective-permute-start = (bf16[2,128,1024]{2,1,0:T(8,128)(2,1)S(1)}, bf16[2,128,1024]{2,1,0:T(8,128)(2,1)S(1)}, u32[]{:S(2)}, u32[]{:S(2)}) collective-permute-start(bf16[2,128,1024]{2,1,0:T(8,128)(2,1)S(1)} %get-tuple-element.102), channel_id=1, source_target_pairs={{0,1},{1,0},{2,3},{3,2},{4,5},{5,4},{6,7},{7,6},{8,9},{9,8},{10,11... | collective-permute-start | bytes 1572872 | tf_op jit(solution)/shard_map/ppermute | solution.py:63
  7.9 27.2 %collective-permute-start.2 = (bf16[1,128,1024]{2,1,0:T(8,128)(2,1)}, bf16[1,128,1024]{2,1,0:T(8,128)(2,1)S(1)}, u32[]{:S(2)}, u32[]{:S(2)}) collective-permute-start(bf16[1,128,1024]{2,1,0:T(8,128)(2,1)} %get-tuple-element.177), channel_id=1, source_target_pairs={{0,4},{1,5},{2,6},{3,7},{4,0},{5,1},{6,2},{7,3},{8,12},{9,13},{10,... | collective-permute-start | bytes 786440 | tf_op jit(solution)/shard_map/ppermute | solution.py:63
  11.7 23.4 %collective-permute-start.3 = (bf16[1,128,1024]{2,1,0:T(8,128)(2,1)}, bf16[1,128,1024]{2,1,0:T(8,128)(2,1)S(1)}, u32[]{:S(2)}, u32[]{:S(2)}) collective-permute-start(bf16[1,128,1024]{2,1,0:T(8,128)(2,1)} %get-tuple-element.176), channel_id=1, source_target_pairs={{0,6},{1,7},{2,4},{3,5},{4,2},{5,3},{6,0},{7,1},{8,14},{9,15},{10,... | collective-permute-start | bytes 786440 | tf_op jit(solution)/shard_map/ppermute | solution.py:63
  13.8 21.3 %collective-permute-start.4 = (bf16[1,128,1024]{2,1,0:T(8,128)(2,1)}, bf16[1,128,1024]{2,1,0:T(8,128)(2,1)}, u32[]{:S(2)}, u32[]{:S(2)}) collective-permute-start(bf16[1,128,1024]{2,1,0:T(8,128)(2,1)} %add_convert_fusion), channel_id=1, source_target_pairs={{0,2},{1,3},{2,0},{3,1},{4,6},{5,7},{6,4},{7,5},{8,10},{9,11},{10,... | collective-permute-start | bytes 786440 | tf_op jit(solution)/shard_map/ppermute | solution.py:63
  41.6 5.4 %collective-permute-start.8 = (f32[8,128]{1,0:T(8,128)S(1)}, f32[8,128]{1,0:T(8,128)S(1)}, u32[]{:S(2)}, u32[]{:S(2)}) collective-permute-start(f32[8,128]{1,0:T(8,128)S(1)} %add.135), channel_id=1, source_target_pairs={{0,6},{1,7},{2,4},{3,5},{4,2},{5,3},{6,0},{7,1},{8,14},{9,15},{10,... | collective-permute-start | bytes 12296 | tf_op jit(solution)/shard_map/ppermute | solution.py:63
  55.4 6.1 %collective-permute-start.14 = (f32[16,1024]{1,0:T(8,128)S(1)}, f32[16,1024]{1,0:T(8,128)S(1)}, u32[]{:S(2)}, u32[]{:S(2)}) collective-permute-start(f32[16,1024]{1,0:T(8,128)S(1)} %get-tuple-element.117), channel_id=1, source_target_pairs={{0,6},{1,7},{2,4},{3,5},{4,2},{5,3},{6,0},{7,1},{8,14},{9,15},{10,... | collective-permute-start | bytes 196616 | tf_op jit(solution)/shard_map/ppermute | solution.py:63
  57.4 5.5 %collective-permute-start.13 = (f32[16,1024]{1,0:T(8,128)S(1)}, f32[16,1024]{1,0:T(8,128)S(1)}, u32[]{:S(2)}, u32[]{:S(2)}) collective-permute-start(f32[16,1024]{1,0:T(8,128)S(1)} %get-tuple-element.117), channel_id=1, source_target_pairs={{0,4},{1,5},{2,6},{3,7},{4,0},{5,1},{6,2},{7,3},{8,12},{9,13},{10,... | collective-permute-start | bytes 196616 | tf_op jit(solution)/shard_map/ppermute | solution.py:63
  57.4 5.5 %collective-permute-start.12 = (f32[16,1024]{1,0:T(8,128)S(1)}, f32[16,1024]{1,0:T(8,128)S(1)}, u32[]{:S(2)}, u32[]{:S(2)}) collective-permute-start(f32[16,1024]{1,0:T(8,128)S(1)} %get-tuple-element.117), channel_id=1, source_target_pairs={{0,2},{1,3},{2,0},{3,1},{4,6},{5,7},{6,4},{7,5},{8,10},{9,11},{10,... | collective-permute-start | bytes 196616 | tf_op jit(solution)/shard_map/ppermute | solution.py:63
  79.6 5.9 %collective-permute-start.22 = (f32[8,1024]{1,0:T(8,128)S(1)}, f32[8,1024]{1,0:T(8,128)S(1)}, u32[]{:S(2)}, u32[]{:S(2)}) collective-permute-start(f32[8,1024]{1,0:T(8,128)S(1)} %log_add_fusion.1), channel_id=1, source_target_pairs={{0,6},{1,7},{2,4},{3,5},{4,2},{5,3},{6,0},{7,1},{8,14},{9,15},{10,... | collective-permute-start | bytes 98312 | tf_op jit(solution)/shard_map/ppermute | solution.py:63
  86.6 32.1 %collective-permute-start.40 = (bf16[176,1024]{1,0:T(8,128)(2,1)S(1)}, bf16[176,1024]{1,0:T(8,128)(2,1)S(1)}, u32[]{:S(2)}, u32[]{:S(2)}) collective-permute-start(bf16[176,1024]{1,0:T(8,128)(2,1)S(1)} %get-tuple-element.146), channel_id=1, source_target_pairs={{0,6},{1,7},{2,4},{3,5},{4,2},{5,3},{6,0},{7,1},{8,14},{9,15},{10,... | collective-permute-start | bytes 1081352 | tf_op jit(solution)/shard_map/ppermute | solution.py:63
  88.6 31.1 %collective-permute-start.39 = (bf16[176,1024]{1,0:T(8,128)(2,1)S(1)}, bf16[176,1024]{1,0:T(8,128)(2,1)S(1)}, u32[]{:S(2)}, u32[]{:S(2)}) collective-permute-start(bf16[176,1024]{1,0:T(8,128)(2,1)S(1)} %get-tuple-element.146), channel_id=1, source_target_pairs={{0,4},{1,5},{2,6},{3,7},{4,0},{5,1},{6,2},{7,3},{8,12},{9,13},{10,... | collective-permute-start | bytes 1081352 | tf_op jit(solution)/shard_map/ppermute | solution.py:63
  89.5 30.2 %collective-permute-start.38 = (bf16[176,1024]{1,0:T(8,128)(2,1)S(1)}, bf16[176,1024]{1,0:T(8,128)(2,1)S(1)}, u32[]{:S(2)}, u32[]{:S(2)}) collective-permute-start(bf16[176,1024]{1,0:T(8,128)(2,1)S(1)} %get-tuple-element.146), channel_id=1, source_target_pairs={{0,2},{1,3},{2,0},{3,1},{4,6},{5,7},{6,4},{7,5},{8,10},{9,11},{10,... | collective-permute-start | bytes 1081352 | tf_op jit(solution)/shard_map/ppermute | solution.py:63
  119.9 35.2 %collective-permute-start.41 = (bf16[4,176,1024]{2,1,0:T(8,128)(2,1)S(1)}, bf16[4,176,1024]{2,1,0:T(8,128)(2,1)S(1)}, u32[]{:S(2)}, u32[]{:S(2)}) collective-permute-start(bf16[4,176,1024]{2,1,0:T(8,128)(2,1)S(1)} %pad_maximum_fusion.refs_11_.refs_2_), channel_id=1, source_target_pairs={{0,1},{1,0},{2,3},{3,2},{4,5},{5,4},{6,7},{7,6},{8,9},{9,8},{10,11... | collective-permute-start | bytes 4325384 | tf_op jit(solution)/shard_map/ppermute | solution.py:63
  120.0 10.5 %collective-permute-start.25 = (f32[8,1024]{1,0:T(8,128)S(1)}, f32[8,1024]{1,0:T(8,128)S(1)}, u32[]{:S(2)}, u32[]{:S(2)}) collective-permute-start(f32[8,1024]{1,0:T(8,128)S(1)} %add.152), channel_id=1, source_target_pairs={{0,4},{1,5},{2,6},{3,7},{4,0},{5,1},{6,2},{7,3},{8,12},{9,13},{10,... | collective-permute-start | bytes 98312 | tf_op jit(solution)/shard_map/ppermute | solution.py:63
  120.2 10.3 %collective-permute-start.26 = (f32[8,1024]{1,0:T(8,128)S(1)}, f32[8,1024]{1,0:T(8,128)S(1)}, u32[]{:S(2)}, u32[]{:S(2)}) collective-permute-start(f32[8,1024]{1,0:T(8,128)S(1)} %add.152), channel_id=1, source_target_pairs={{0,6},{1,7},{2,4},{3,5},{4,2},{5,3},{6,0},{7,1},{8,14},{9,15},{10,... | collective-permute-start | bytes 98312 | tf_op jit(solution)/shard_map/ppermute | solution.py:63
  122.1 8.4 %collective-permute-start.24 = (f32[8,1024]{1,0:T(8,128)S(1)}, f32[8,1024]{1,0:T(8,128)S(1)}, u32[]{:S(2)}, u32[]{:S(2)}) collective-permute-start(f32[8,1024]{1,0:T(8,128)S(1)} %add.152), channel_id=1, source_target_pairs={{0,2},{1,3},{2,0},{3,1},{4,6},{5,7},{6,4},{7,5},{8,10},{9,11},{10,... | collective-permute-start | bytes 98312 | tf_op jit(solution)/shard_map/ppermute | solution.py:63
  135.5 8.3 %collective-permute-start.28 = (f32[16,1024]{1,0:T(8,128)S(1)}, f32[16,1024]{1,0:T(8,128)S(1)}, u32[]{:S(2)}, u32[]{:S(2)}) collective-permute-start(f32[16,1024]{1,0:T(8,128)S(1)} %get-tuple-element.180), channel_id=1, source_target_pairs={{0,2},{1,3},{2,0},{3,1},{4,6},{5,7},{6,4},{7,5},{8,10},{9,11},{10,... | collective-permute-start | bytes 196616 | tf_op jit(solution)/shard_map/ppermute | solution.py:63
  136.2 8.3 %collective-permute-start.29 = (f32[16,1024]{1,0:T(8,128)S(1)}, f32[16,1024]{1,0:T(8,128)S(1)}, u32[]{:S(2)}, u32[]{:S(2)}) collective-permute-start(f32[16,1024]{1,0:T(8,128)S(1)} %get-tuple-element.179), channel_id=1, source_target_pairs={{0,4},{1,5},{2,6},{3,7},{4,0},{5,1},{6,2},{7,3},{8,12},{9,13},{10,... | collective-permute-start | bytes 196616 | tf_op jit(solution)/shard_map/ppermute | solution.py:63
  138.1 6.3 %collective-permute-start.30 = (f32[16,1024]{1,0:T(8,128)S(1)}, f32[16,1024]{1,0:T(8,128)S(1)}, u32[]{:S(2)}, u32[]{:S(2)}) collective-permute-start(f32[16,1024]{1,0:T(8,128)S(1)} %get-tuple-element.178), channel_id=1, source_target_pairs={{0,6},{1,7},{2,4},{3,5},{4,2},{5,3},{6,0},{7,1},{8,14},{9,15},{10,... | collective-permute-start | bytes 196616 | tf_op jit(solution)/shard_map/ppermute | solution.py:63
  144.5 6.6 %collective-permute-start.33 = (f32[16,1024]{1,0:T(8,128)S(1)}, f32[16,1024]{1,0:T(8,128)S(1)}, u32[]{:S(2)}, u32[]{:S(2)}) collective-permute-start(f32[16,1024]{1,0:T(8,128)S(1)} %fusion.5.refs_7_), channel_id=1, source_target_pairs={{0,6},{1,7},{2,4},{3,5},{4,2},{5,3},{6,0},{7,1},{8,14},{9,15},{10,... | collective-permute-start | bytes 196616 | tf_op jit(solution)/shard_map/ppermute | solution.py:63
  146.5 6.0 %collective-permute-start.32 = (f32[16,1024]{1,0:T(8,128)S(1)}, f32[16,1024]{1,0:T(8,128)S(1)}, u32[]{:S(2)}, u32[]{:S(2)}) collective-permute-start(f32[16,1024]{1,0:T(8,128)S(1)} %fusion.5.refs_7_), channel_id=1, source_target_pairs={{0,4},{1,5},{2,6},{3,7},{4,0},{5,1},{6,2},{7,3},{8,12},{9,13},{10,... | collective-permute-start | bytes 196616 | tf_op jit(solution)/shard_map/ppermute | solution.py:63
  148.9 21.6 %collective-permute-start.44 = (f32[664,128]{1,0:T(8,128)S(1)}, f32[664,128]{1,0:T(8,128)S(1)}, u32[]{:S(2)}, u32[]{:S(2)}) collective-permute-start(f32[664,128]{1,0:T(8,128)S(1)} %shard_map.409), channel_id=1, source_target_pairs={{0,16},{8,24},{16,0},{24,8},{1,17},{9,25},{17,1},{25,9},{2,18},{10... | collective-permute-start | bytes 1019912 | tf_op jit(solution)/shard_map/ppermute | solution.py:63
  152.5 8.9 %collective-permute-start.34 = (f32[4,16,1024]{2,1,0:T(8,128)S(1)}, f32[4,16,1024]{2,1,0:T(8,128)S(1)}, u32[]{:S(2)}, u32[]{:S(2)}) collective-permute-start(f32[4,16,1024]{2,1,0:T(8,128)S(1)} %pad_maximum_fusion.2.refs_2_), channel_id=1, source_target_pairs={{0,1},{1,0},{2,3},{3,2},{4,5},{5,4},{6,7},{7,6},{8,9},{9,8},{10,11... | collective-permute-start | bytes 786440 | tf_op jit(solution)/shard_map/ppermute | solution.py:63
  152.6 7.7 %collective-permute-start.36 = (f32[8,128]{1,0:T(8,128)S(1)}, f32[8,128]{1,0:T(8,128)S(1)}, u32[]{:S(2)}, u32[]{:S(2)}) collective-permute-start(f32[8,128]{1,0:T(8,128)S(1)} %slice.77), channel_id=1, source_target_pairs={{0,16},{8,24},{16,0},{24,8},{1,17},{9,25},{17,1},{25,9},{2,18},{10... | collective-permute-start | bytes 12296 | tf_op jit(solution)/shard_map/ppermute | solution.py:63
  153.7 7.6 %collective-permute-start.37 = (f32[8,128]{1,0:T(8,128)S(1)}, f32[8,128]{1,0:T(8,128)S(1)}, u32[]{:S(2)}, u32[]{:S(2)}) collective-permute-start(f32[8,128]{1,0:T(8,128)S(1)} %slice.77), channel_id=1, source_target_pairs={{0,24},{8,16},{16,8},{24,0},{1,25},{9,17},{17,9},{25,1},{2,26},{10... | collective-permute-start | bytes 12296 | tf_op jit(solution)/shard_map/ppermute | solution.py:63
  155.2 6.2 %collective-permute-start.35 = (f32[8,128]{1,0:T(8,128)S(1)}, f32[8,128]{1,0:T(8,128)S(1)}, u32[]{:S(2)}, u32[]{:S(2)}) collective-permute-start(f32[8,128]{1,0:T(8,128)S(1)} %slice.77), channel_id=1, source_target_pairs={{0,8},{8,0},{16,24},{24,16},{1,9},{9,1},{17,25},{25,17},{2,10},{10... | collective-permute-start | bytes 12296 | tf_op jit(solution)/shard_map/ppermute | solution.py:63
  160.3 11.4 %collective-permute-start.46 = (f32[480,128]{1,0:T(8,128)S(1)}, f32[480,128]{1,0:T(8,128)S(1)}, u32[]{:S(2)}, u32[]{:S(2)}) collective-permute-start(f32[480,128]{1,0:T(8,128)S(1)} %shard_map.411), channel_id=1, source_target_pairs={{0,8},{8,0},{16,24},{24,16},{1,9},{9,1},{17,25},{25,17},{2,10},{10... | collective-permute-start | bytes 737288 | tf_op jit(solution)/shard_map/ppermute | solution.py:63
  169.5 7.7 %collective-permute-start.42 = (f32[368,128]{1,0:T(8,128)S(1)}, f32[368,128]{1,0:T(8,128)S(1)}, u32[]{:S(2)}, u32[]{:S(2)}) collective-permute-start(f32[368,128]{1,0:T(8,128)S(1)} %shard_map.410), channel_id=1, source_target_pairs={{0,8},{8,0},{16,24},{24,16},{1,9},{9,1},{17,25},{25,17},{2,10},{10... | collective-permute-start | bytes 565256 | tf_op jit(solution)/shard_map/ppermute | solution.py:63
  170.6 12.2 %collective-permute-start.45 = (f32[664,128]{1,0:T(8,128)S(1)}, f32[664,128]{1,0:T(8,128)S(1)}, u32[]{:S(2)}, u32[]{:S(2)}) collective-permute-start(f32[664,128]{1,0:T(8,128)S(1)} %add.172), channel_id=1, source_target_pairs={{0,8},{8,0},{16,24},{24,16},{1,9},{9,1},{17,25},{25,17},{2,10},{10... | collective-permute-start | bytes 1019912 | tf_op jit(solution)/shard_map/ppermute | solution.py:63
  171.7 11.3 %collective-permute-start.47 = (f32[480,128]{1,0:T(8,128)S(1)}, f32[480,128]{1,0:T(8,128)S(1)}, u32[]{:S(2)}, u32[]{:S(2)}) collective-permute-start(f32[480,128]{1,0:T(8,128)S(1)} %add.174), channel_id=1, source_target_pairs={{0,16},{8,24},{16,0},{24,8},{1,17},{9,25},{17,1},{25,9},{2,18},{10... | collective-permute-start | bytes 737288 | tf_op jit(solution)/shard_map/ppermute | solution.py:63
  177.2 5.8 %collective-permute-start.43 = (f32[368,128]{1,0:T(8,128)S(1)}, f32[368,128]{1,0:T(8,128)S(1)}, u32[]{:S(2)}, u32[]{:S(2)}) collective-permute-start(f32[368,128]{1,0:T(8,128)S(1)} %add.170), channel_id=1, source_target_pairs={{0,16},{8,24},{16,0},{24,8},{1,17},{9,25},{17,1},{25,9},{2,18},{10... | collective-permute-start | bytes 565256 | tf_op jit(solution)/shard_map/ppermute | solution.py:63
  183.8 5.6 %collective-permute-start.50 = (f32[48,128]{1,0:T(8,128)S(1)}, f32[48,128]{1,0:T(8,128)S(1)}, u32[]{:S(2)}, u32[]{:S(2)}) collective-permute-start(f32[48,128]{1,0:T(8,128)S(1)} %get-tuple-element.152), channel_id=1, source_target_pairs={{0,6},{1,7},{2,4},{3,5},{4,2},{5,3},{6,0},{7,1},{8,14},{9,15},{10,... | collective-permute-start | bytes 73736 | tf_op jit(solution)/shard_map/ppermute | solution.py:63
  (49 other events, 326.9 us)

commit v6 on v5

--- a/solution.py
+++ b/solution.py
@@ -263,14 +263,13 @@
     return jnp.concatenate([rows8[:, i * 128 : (i + 1) * 128] for i in range(count)], axis=0)
 
 
-def counts_kernel(rows, span, x_ref, lg_ref, dg_ref, par_ref, batch_ref, lib_ref, logc_ref, mask_ref, side_ref, lib_out, cell_ref, disp_ref, line_ref, held_ref, sum_ref):
+def counts_kernel(rows, span, x_ref, lg_ref, dg_ref, par_ref, batch_ref, lib_ref, logc_ref, mask_ref, side_ref, lib_out, cell_ref, disp_ref, line_ref, held_ref):
     step = pl.program_id(0)
     genes, width = mask_ref.shape
 
     @pl.when(step == 0)
     def _():
         disp_ref[...] = jnp.zeros_like(disp_ref)
-        sum_ref[...] = jnp.zeros_like(sum_ref)
         held_ref[...] = jnp.zeros_like(held_ref)
 
     kinds = held_ref.shape[0]
@@ -284,17 +283,16 @@
     done = []
     for first in range(0, width, span):
         lanes = [slice(first + tile * 128, first + (tile + 1) * 128) for tile in range(tiles)]
-        far_lanes = [pl.ds(pl.multiple_of(step * width + first + tile * 128, 128), 128) for tile in range(tiles)]
 
         def chunk(g, cell):
             at = pl.ds(pl.multiple_of(g * rows, rows), rows)
-            keep = par_ref[4, at, :]
-            xs = [x_ref[at, far_lanes[tile]].astype(F32) for tile in range(tiles)]
+            keep = par_ref[4, at, :].astype(BF)
+            lows = [x_ref[at, lanes[tile]] for tile in range(tiles)]
+            xs = [low.astype(F32) for low in lows]
             logs = [jnp.log(1.0 + x) for x in xs]
             for tile in range(tiles):
                 logc_ref[at, lanes[tile]] = logs[tile].astype(BF)
-                mask_ref[at, lanes[tile]] = (xs[tile] * keep).astype(BF)
-            sum_ref[at, :] += sum(part.astype(BF).astype(F32) for part in logs)
+                mask_ref[at, lanes[tile]] = lows[tile] * keep
             gams = [jnp.zeros_like(xs[0]) for _ in range(tiles)]
             digs = [jnp.zeros_like(xs[0]) for _ in range(tiles)]
             for k in range(COUNT_TOP):
@@ -318,9 +316,7 @@
 
     @pl.when(step == pl.num_programs(0) - 1)
     def _():
-        most = line_ref.shape[0] - 8
-        line_ref[0:most, :] = lines(row_sums(sum_ref[...]), most // 8)
-        line_ref[most:, :] = row_sums(held_ref[...])
+        line_ref[...] = row_sums(held_ref[...])
 
 
 def own_kernel(me_ref, keep_ref, got_ref, one_ref, two_ref, six_ref, batch_ref, enc_b_ref, pre_ref, stat_ref):
@@ -355,8 +351,8 @@
     affine = norm_ref[:, 0:1] * phat + norm_ref[:, 1:2]
     out = nn(head_ref[...], jnp.maximum(affine, 0.0), HI) + bias_ref[:, 0:1]
     lat_mean, lat_logvar = out[:latent], out[16 : 16 + latent]
-    high, mid, low = three(latent_rows(lat_logvar))
-    aff_ref[...] = jnp.concatenate((affine.astype(BF), high, mid, low), axis=0)
+    high, mid, _ = three(latent_rows(lat_logvar))
+    aff_ref[...] = jnp.concatenate((affine.astype(BF), high, mid), axis=0)
     var = jnp.exp(lat_logvar) + 0.0001
     z = latent_rows(lat_mean + jnp.sqrt(var) * noise_ref[...])
     terms = var + lat_mean * lat_mean - 1.0 - jnp.log(var)
@@ -462,20 +458,31 @@
     lse_ref[pl.ds(step, 1), :] = jnp.concatenate(lse, axis=1)
 
 
-def enc_sums_kernel(fast, me_ref, logc_ref, near_ref, far_ref, side_ref, lines_ref, out_ref):
+def enc_sums_kernel(fast, me_ref, logc_ref, near_ref, far_ref, side_ref, line_ref, out_ref, sum_ref):
     step = pl.program_id(0)
     genes = logc_ref.shape[0]
+    hidden = out_ref.shape[1]
     kinds = side_ref.shape[0] - 16
 
     @pl.when(step == 0)
     def _():
         out_ref[...] = jnp.zeros_like(out_ref)
-        out_ref[genes + kinds :, :] = lines_ref[...]
+        sum_ref[...] = jnp.zeros_like(sum_ref)
 
     cells_at = part_of(step, near_ref.shape[2])
-    affine = pick(step, me_ref, fast, near_ref, far_ref)[: out_ref.shape[1]]
-    out_ref[0:genes, :] += nt(logc_ref[:, cells_at], affine)
+    affine = pick(step, me_ref, fast, near_ref, far_ref)[:hidden]
+    part = nt(logc_ref[:, cells_at], jnp.concatenate((affine, side_ref[kinds:, cells_at]), axis=0))
+    out_ref[0:genes, :] += part[:, :hidden]
+    sum_ref[...] += part[:, hidden:]
     out_ref[genes : genes + kinds, :] += nt(side_ref[0:kinds, cells_at], affine)
+
+    @pl.when(step == pl.num_programs(0) - 1)
+    def _():
+        pick_first = jnp.where(lax.broadcasted_iota(jnp.int32, (8, 16), 1) == 0, 1.0, 0.0)
+        base = genes + kinds
+        count = pl.cdiv(genes, 128)
+        out_ref[base : base + 8 * count, :] = lines(nt(pick_first, sum_ref[...], HI), count)
+        out_ref[base + 8 * count :, :] = line_ref[...]
 
 
 def zinb_kernel(rows, span, hid_ref, e_ref, top_ref, w_ref, x_ref, par_ref, lib_ref, lse_ref, gam_ref, g_ref, rt_ref, mass_ref, recon_ref, acc_ref, sc_ref):
@@ -503,7 +510,7 @@
             at = pl.ds(pl.multiple_of(g * rows, rows), rows)
             at_drop = pl.ds(pl.multiple_of(genes + g * rows, rows), rows)
             the, th, log_the, part_th = (par_ref[i, at, :] for i in range(4))
-            sums = [acc_ref[i, at, :] for i in range(3)]
+            sum_t = acc_ref[at, :]
             new = []
             for tile in range(tiles):
                 rec, prod, back = state[tile]
@@ -531,15 +538,14 @@
                 g_ref[at, far_lanes[tile]] = g_mean.astype(BF)
                 g_ref[at_drop, far_lanes[tile]] = g_drop.astype(BF)
                 rt_ref[at, far_lanes[tile]] = mu.astype(BF)
-                sums = [a + b for a, b in zip(sums, (g_mean, g_drop, g_disp))]
+                sum_t = sum_t + g_disp
                 for part in range(rows // 8):
                     sub = slice(part * 8, (part + 1) * 8)
                     rec = rec + term[sub]
                     prod = prod * factor[sub]
                     back = back + g_mean[sub]
                 new.append((rec, prod, back))
-            for i in range(3):
-                acc_ref[i, at, :] = sums[i]
+            acc_ref[at, :] = sum_t
             return tuple(new)
         zero = jnp.zeros((8, 128), F32)
         state = tuple((zero, zero + 1.0, zero) for _ in range(tiles))
@@ -563,7 +569,9 @@
 
     a_ref[:, cells_at] = nn(w_ref[...], g_in_ref[:, cells_at])
     r_ref[:, cells_at] = nn(w_ref[:, :genes], rt_ref[:, cells_at])
-    g_ref[...] += nt(g_in_ref[:, cells_at], relu_low(aff_ref[:, cells_at]))
+    row = lax.broadcasted_iota(jnp.int32, (16, width), 0)
+    ones = jnp.where(row == 0, 1.0, 0.0).astype(BF)
+    g_ref[...] += nt(g_in_ref[:, cells_at], jnp.concatenate((relu_low(aff_ref[:, cells_at]), ones), axis=0))
 
 
 def hidden_grad_kernel(cells, latent, me_ref, a_ref, r_ref, mass_ref, aff_ref, lib_ref, stat_ref, gain_ref, lat_ref, recon_ref, z_ref, side_ref, keep_ref, send_ref, lane_ref, oh_ref):
@@ -641,12 +649,12 @@
     def _():
         scale = -1.0 / cells
         mix = mix_ref[...]
-        dec_ref[:genes, :] = (g_ref[:genes, :] - mix[:, :hidden]) * scale
-        dec_ref[genes : 2 * genes, :] = g_ref[genes:, :] * scale
+        dec_ref[:genes, :] = (g_ref[:genes, :hidden] - mix[:, :hidden]) * scale
+        dec_ref[genes : 2 * genes, :] = g_ref[genes:, :hidden] * scale
         pick = jnp.where(lax.broadcasted_iota(jnp.int32, (8, 16), 1) < 2, 1.0, 0.0)
-        score_row = row_sums(acc_ref[0]) - nt(pick, mix[:, hidden:], HI)
-        drop_row = row_sums(acc_ref[1])
-        disp_row = row_sums((acc_ref[2] + dig_ref[...]) * par_ref[1])
+        score_row = nt(pick, g_ref[:genes, hidden:] - mix[:, hidden:], HI)
+        drop_row = nt(pick, g_ref[genes:, hidden:], HI)
+        disp_row = row_sums((acc_ref[...] + dig_ref[...]) * par_ref[1])
         line = lax.broadcasted_iota(jnp.int32, score_row.shape, 0)
         gene_rows = scale * jnp.where(
             line == 0, score_row, jnp.where(line == 1, drop_row, jnp.where(line == 2, disp_row, 0.0))
@@ -695,8 +703,8 @@
     kept_ref[step] = block[8:]
     grad_z = (block - fixed_ref[:, 0:1] - (both[:16] + both[16:]))[:latent]
     noise = noise_ref[:, cells_at]
-    pieces = take(anear_ref, afar_ref, slice(hidden, hidden + 48), every).astype(F32)
-    lat_logvar = (pieces[:latent] + pieces[16 : 16 + latent]) + pieces[32 : 32 + latent]
+    pieces = take(anear_ref, afar_ref, slice(hidden, hidden + 32), every).astype(F32)
+    lat_logvar = pieces[:latent] + pieces[16 : 16 + latent]
     spread = jnp.exp(lat_logvar)
     var = spread + 0.0001
     inv_std = lax.rsqrt(var)
@@ -912,7 +920,7 @@
             + ([] if near else [pltpu.VMEM((count, genes, share), BF)]),
             scalars=1,
             us=2.0 if near else 3.0,
-            mib=16,
+            mib=6 if near else 8,
         )
 
     slot = pl.BlockSpec((1, hidden, share), lambda i, m: (0, 0, 0))
@@ -968,7 +976,7 @@
         lambda *refs: counts_kernel(16, min(512, width), *refs),
         (blocks,),
         [
-            (x_t, here),
+            (in_hbm(x_t), lane_block(genes)),
             full(lg_tab),
             full(dg_tab),
             full(par),
@@ -982,11 +990,10 @@
             new((blocks, width)),
             new((blocks, width)),
             new((genes, 128)),
-            new((8 * gene_lines + 8, 128)),
+            new((8, 128)),
             new((kinds, 128)),
         ],
-        scratch=[pltpu.VMEM((genes, 128), F32)],
-        mib=16,
+        mib=8,
         us=15.0,
     )
     enc_late = after(enc_pieces, log_lines)
@@ -1016,7 +1023,7 @@
             (batch_own, own_block),
             full(dec_pieces),
         ],
-        [new((16, share)), new((hidden + 48, share), BF), new((1, share))],
+        [new((16, share)), new((hidden + 32, share), BF), new((1, share))],
         scalars=1,
     )
     near, far_pack = gather_genes(pack, fast, blocks, width)
@@ -1054,7 +1061,7 @@
 
     full8 = whole((blocks, width))
     g_both, rt, mass, recon, gene_acc = call(
-        lambda *refs: zinb_kernel(64, min(512, width), *refs),
+        lambda *refs: zinb_kernel(64, min(1024, width), *refs),
         (blocks,),
         [
             (aff_dec, here),
@@ -1068,9 +1075,9 @@
             full(gam_cell),
         ],
         [((2 * genes, rows_all), BF, here), ((genes, rows_all), BF, here)]
-        + [new((blocks, width)), new((blocks, width)), new((3, genes, 128))],
+        + [new((blocks, width)), new((blocks, width)), new((genes, 128))],
         scratch=[pltpu.VMEM((genes, width), F32)],
-        mib=20,
+        mib=16,
         us=28.0,
     )
     mass_low = mass + swap(mass, "genes", 1)
@@ -1087,7 +1094,7 @@
         [
             ((hidden, rows_all), F32, here),
             ((hidden, rows_all), F32, here),
-            new((2 * genes, hidden)),
+            new((2 * genes, hidden + 16)),
         ],
         mib=16,
         us=9.0,
@@ -1107,6 +1114,7 @@
             full(log_lines),
         ],
         [new((fixed_rows, hidden))],
+        scratch=[pltpu.VMEM((genes, 16), F32)],
         scalars=1,
         us=4.0,
     )

time: 195 us -> 193 us (0.990)
  starting transfers between devices: 59.2 us -> 62.7 us
  local copies, waits for them, and re-layouts: 2.66 us -> 0.17 us
  Pallas kernels: 90.3 us -> 87.9 us
    ppermute x52, starting transfers between devices: 59.2 us -> 62.7 us  [swap(): return lax.ppermute(value, axis, [(i, i ^ bit) for i in range(count)])]
    unnamed x58 -> x52, local copies, waits for them, and re-layouts: 2.64 us -> 0.15 us
    pallas_call x15, Pallas kernels: 90.3 us -> 87.9 us  [call(): pl.pallas_call(kernel, out_shape=[pltpu.HBM(out[0], out[1]) if len(out) =...]
where the time goes in v6:
time: 193 us
  Pallas kernels  87.9 us (46%)
  starting transfers between devices  62.7 us (32%)
  waiting for transfers between devices  38.5 us (20%)
  between operations  2.12 us (1%)
    pallas_call x15, Pallas kernels, call(): pl.pallas_call(kernel, out_shape=[pltpu.HBM(out[0], out[1]) if len(out) =...  87.9 us
    ppermute x52, starting transfers between devices, swap(): return lax.ppermute(value, axis, [(i, i ^ bit) for i in range(count)])  62.7 us
    ppermute x52, waiting for transfers between devices, swap(): return lax.ppermute(value, axis, [(i, i ^ bit) for i in range(count)])  38.5 us
  transfers between devices with their start and end apart: 52, of which 25 were waited for; matrix products, arithmetic and copies ran while one was open for 1% of the time, Pallas kernels for 37%

profile of v6, /device:TPU:0, one launch (start us, length us, event | category | flops | bytes accessed | tf_op | source)
XLA Modules:
  0.0 192.9 jit_solution(7693692885966213910)
XLA Ops:
  0.7 3.0 %shard_map.399 = (f32[2,128,1024]{2,1,0:T(8,128)S(1)}, bf16[2,128,1024]{2,1,0:T(8,128)(2,1)S(1)}) custom-call(s32[1]{0:T(128)} %bitcast.refs_0_.me_ref.refs_1_, bf16[320,8192]{1,0:T(8,128)(2,1)} %bitcast.49, f32[320,128]{1,0:T(8,128)} %refs_10_.1), custom_call_target="tpu_custom_call" | custom-call | bytes 11070000 | tf_op jit(solution)/shard_map/pallas_call | solution.py:46
  4.2 2.4 %shard_map.400 = (f32[2,128,1024]{2,1,0:T(8,128)S(1)}, bf16[2,128,1024]{2,1,0:T(8,128)(2,1)S(1)}) custom-call(s32[1]{0:T(128)} %bitcast.refs_0_.me_ref.refs_1_, bf16[320,8192]{1,0:T(8,128)(2,1)S(1)} %bitcast.51, f32[320,128]{1,0:T(8,128)} %refs_10_.1), custom_call_target="tpu_custom_call" | custom-call | bytes 7380000 | tf_op jit(solution)/shard_map/pallas_call | solution.py:46
  7.8 3.8 %collective-permute-start.2 = (bf16[1,128,1024]{2,1,0:T(8,128)(2,1)}, bf16[1,128,1024]{2,1,0:T(8,128)(2,1)S(1)}, u32[]{:S(2)}, u32[]{:S(2)}) collective-permute-start(bf16[1,128,1024]{2,1,0:T(8,128)(2,1)} %get-tuple-element.177), channel_id=1, source_target_pairs={{0,4},{1,5},{2,6},{3,7},{4,0},{5,1},{6,2},{7,3},{8,12},{9,13},{10,... | collective-permute-start | bytes 786440 | tf_op jit(solution)/shard_map/ppermute | solution.py:63
  14.5 16.4 %shard_map.402 = (bf16[320,8192]{1,0:T(8,128)(2,1)}, bf16[320,8192]{1,0:T(8,128)(2,1)}, bf16[144,8192]{1,0:T(8,128)(2,1)S(1)}, f32[8,1024]{1,0:T(8,128)S(1)}, f3...) custom-call(bf16[320,8192]{1,0:T(8,128)(2,1)} %bitcast.50, ...), custom_call_target="tpu_custom_call" | custom-call | bytes 55350000 | tf_op jit(solution)/shard_map/pallas_call | solution.py:46
  33.5 7.0 %collective-permute-start.7 = (f32[8,128]{1,0:T(8,128)S(1)}, f32[8,128]{1,0:T(8,128)S(1)}, u32[]{:S(2)}, u32[]{:S(2)}) collective-permute-start(f32[8,128]{1,0:T(8,128)S(1)} %add.135), channel_id=1, source_target_pairs={{0,4},{1,5},{2,6},{3,7},{4,0},{5,1},{6,2},{7,3},{8,12},{9,13},{10,... | collective-permute-start | bytes 12296 | tf_op jit(solution)/shard_map/ppermute | solution.py:63
  42.1 3.8 %collective-permute-done.8 = f32[8,128]{1,0:T(8,128)S(1)} collective-permute-done((f32[8,128]{1,0:T(8,128)S(1)}, f32[8,128]{1,0:T(8,128)S(1)}, u32[]{:S(2)}, u32[]{:S(2)}) %collective-permute-start.8) | collective-permute-done | bytes 4128 | tf_op jit(solution)/shard_map/ppermute | solution.py:63
  49.6 2.4 %collective-permute-done.11 = f32[8,128]{1,0:T(8,128)S(1)} collective-permute-done((f32[8,128]{1,0:T(8,128)S(1)}, f32[8,128]{1,0:T(8,128)S(1)}, u32[]{:S(2)}, u32[]{:S(2)}) %collective-permute-start.11) | collective-permute-done | bytes 4128 | tf_op jit(solution)/shard_map/ppermute | solution.py:63
  52.6 1.8 shard_map.404
  54.4 2.0 %collective-permute-start.14 = (f32[16,1024]{1,0:T(8,128)S(1)}, f32[16,1024]{1,0:T(8,128)S(1)}, u32[]{:S(2)}, u32[]{:S(2)}) collective-permute-start(f32[16,1024]{1,0:T(8,128)S(1)} %get-tuple-element.117), channel_id=1, source_target_pairs={{0,6},{1,7},{2,4},{3,5},{4,2},{5,3},{6,0},{7,1},{8,14},{9,15},{10,... | collective-permute-start | bytes 196616 | tf_op jit(solution)/shard_map/ppermute | solution.py:63
  56.4 2.4 %collective-permute-start.12 = (f32[16,1024]{1,0:T(8,128)S(1)}, f32[16,1024]{1,0:T(8,128)S(1)}, u32[]{:S(2)}, u32[]{:S(2)}) collective-permute-start(f32[16,1024]{1,0:T(8,128)S(1)} %get-tuple-element.117), channel_id=1, source_target_pairs={{0,2},{1,3},{2,0},{3,1},{4,6},{5,7},{6,4},{7,5},{8,10},{9,11},{10,... | collective-permute-start | bytes 196616 | tf_op jit(solution)/shard_map/ppermute | solution.py:63
  58.8 1.7 collective-permute-done.14
  67.2 2.4 %collective-permute-done.18 = f32[8,128]{1,0:T(8,128)S(1)} collective-permute-done((f32[8,128]{1,0:T(8,128)S(1)}, f32[8,128]{1,0:T(8,128)S(1)}, u32[]{:S(2)}, u32[]{:S(2)}) %collective-permute-start.18) | collective-permute-done | bytes 4128 | tf_op jit(solution)/shard_map/ppermute | solution.py:63
  69.6 7.6 %shard_map.405 = (bf16[128,8192]{1,0:T(8,128)(2,1)S(1)}, f32[8,1024]{1,0:T(8,128)S(1)}, f32[16,8192]{1,0:T(8,128)S(1)}, f32[8,1024]{1,0:T(8,128)S(1)}, f32[320,8192]{1,0:T(8,128)S(1)}) custom-call(s32[1]{0:T(128)} %bitcast.refs_0_.me_ref.refs_1_, f32[4,16,1024]{2,1,0:T(8,128)S(1)} %pad_maximum_fusion.1.refs_1_, ...), custom_call_target="tpu_custom_call" | custom-call | bytes 29520000 | tf_op jit(solution)/shard_map/pallas_call | solution.py:46
  78.5 2.0 %collective-permute-start.22 = (f32[8,1024]{1,0:T(8,128)S(1)}, f32[8,1024]{1,0:T(8,128)S(1)}, u32[]{:S(2)}, u32[]{:S(2)}) collective-permute-start(f32[8,1024]{1,0:T(8,128)S(1)} %log_add_fusion.1), channel_id=1, source_target_pairs={{0,6},{1,7},{2,4},{3,5},{4,2},{5,3},{6,0},{7,1},{8,14},{9,15},{10,... | collective-permute-start | bytes 98312 | tf_op jit(solution)/shard_map/ppermute | solution.py:63
  81.2 1.7 collective-permute-start.20
  85.5 2.0 %collective-permute-start.40 = (bf16[160,1024]{1,0:T(8,128)(2,1)S(1)}, bf16[160,1024]{1,0:T(8,128)(2,1)S(1)}, u32[]{:S(2)}, u32[]{:S(2)}) collective-permute-start(bf16[160,1024]{1,0:T(8,128)(2,1)S(1)} %get-tuple-element.146), channel_id=1, source_target_pairs={{0,6},{1,7},{2,4},{3,5},{4,2},{5,3},{6,0},{7,1},{8,14},{9,15},{10,... | collective-permute-start | bytes 983048 | tf_op jit(solution)/shard_map/ppermute | solution.py:63
  90.0 25.6 %shard_map.406 = (bf16[640,8192]{1,0:T(8,128)(2,1)S(1)}, bf16[320,8192]{1,0:T(8,128)(2,1)S(1)}, f32[8,1024]{1,0:T(8,128)S(1)}, f32[8,1024]{1,0:T(8,128)S(1)}, f32[320,128]{1,0:T(8,128)S(1)}) custom-call(bf16[128,8192]{1,0:T(8,128)(2,1)S(1)} %get-tuple-element.121.refs_0_.refs_2_.refs_4_.refs_1_, f32[320,8192]{1,0:T(8,128)S(1)} %get-tuple-element.122.refs_1_, ...), custom_call_target="tpu_custom_call" | custom-call | bytes 103320000 | tf_op jit(solution)/shard_map/pallas_call | solution.py:46
  118.3 1.9 collective-permute-start.26
  120.8 7.0 %shard_map.407 = (f32[128,8192]{1,0:T(8,128)S(1)}, f32[128,8192]{1,0:T(8,128)S(1)}, f32[640,144]{1,0:T(8,128)S(1)}) custom-call(bf16[640,8192]{1,0:T(8,128)(2,1)S(1)} %get-tuple-element.128.refs_0_, bf16[320,8192]{1,0:T(8,128)(2,1)S(1)} %get-tuple-element.129.refs_1_.refs_0_, bf16[128,8192]{1,0:T(8,128)(2,1)S(1)} %get-tuple-element.121.refs_0_.refs_2_.refs_4_.refs_1_, ...), custom_call_target="tpu_custom_call" | custom-call | bytes 33210000 | tf_op jit(solution)/shard_map/pallas_call | solution.py:46
  127.8 3.4 %shard_map.408 = (f32[4,16,1024]{2,1,0:T(8,128)S(1)}, f32[4,16,1024]{2,1,0:T(8,128)S(1)}) custom-call(s32[1]{0:T(128)} %bitcast.refs_0_.me_ref.refs_1_, f32[128,8192]{1,0:T(8,128)S(1)} %get-tuple-element.131.refs_1_, f32[128,8192]{1,0:T(8,128)S(1)} %get-tuple-element.132.refs_2_, f32[8,1024]{1,0:T(8,128)S(1)} %add_add_fusion.refs_3_.refs_2_, ...), custom_call_target="tpu_custom_call" | custom-call | bytes 18450000 | tf_op jit(solution)/shard_map/pallas_call | solution.py:46
  135.4 1.9 collective-permute-start.30
  137.3 3.6 %shard_map.409 = f32[664,128]{1,0:T(8,128)S(1)} custom-call(bf16[320,8192]{1,0:T(8,128)(2,1)S(1)} %get-tuple-element.129.refs_1_.refs_0_, bf16[128,8192]{1,0:T(8,128)(2,1)S(1)} %get-tuple-element.121.refs_0_.refs_2_.refs_4_.refs_1_, f32[8,1024]{1,0:T(8,128)S(1)} %add_add_fusion.refs_3_.refs_2_, f32[8,1024]{1,0:T(8,128)S(1)} %get-tuple-element.125.refs_6_.refs_5_.refs_3_, ...), custom_call_target="tpu_custom_call" | custom-call | bytes 18450000 | tf_op jit(solution)/shard_map/pallas_call | solution.py:46
  142.4 2.1 %collective-permute-start.33 = (f32[16,1024]{1,0:T(8,128)S(1)}, f32[16,1024]{1,0:T(8,128)S(1)}, u32[]{:S(2)}, u32[]{:S(2)}) collective-permute-start(f32[16,1024]{1,0:T(8,128)S(1)} %fusion.5.refs_7_), channel_id=1, source_target_pairs={{0,6},{1,7},{2,4},{3,5},{4,2},{5,3},{6,0},{7,1},{8,14},{9,15},{10,... | collective-permute-start | bytes 196616 | tf_op jit(solution)/shard_map/ppermute | solution.py:63
  155.1 3.9 %shard_map.411 = f32[480,128]{1,0:T(8,128)S(1)} custom-call(s32[1]{0:T(128)} %bitcast.refs_0_.me_ref.refs_1_, bf16[320,8192]{1,0:T(8,128)(2,1)S(1)} %bitcast.53, bf16[4,160,1024]{2,1,0:T(8,128)(2,1)S(1)} %pad_maximum_fusion.refs_11_.refs_2_, bf16[4,160,1024]{2,1,0:T(8,128)(2,1)S(1)} %collective-permute-done.41.refs_12_.refs_3_, ...), custom_call_target="tpu_custom_call" | custom-call | bytes 14760000 | tf_op jit(solution)/shard_map/pallas_call | solution.py:46
  160.2 8.1 %shard_map.410 = f32[368,128]{1,0:T(8,128)S(1)} custom-call(s32[1]{0:T(128)} %bitcast.refs_0_.me_ref.refs_1_, s32[1]{0:T(128)} %bitcast.refs_0_.me_ref.refs_1_, f32[4,16,1024]{2,1,0:T(8,128)S(1)} %pad_maximum_fusion.2.refs_2_, f32[4,16,1024]{2,1,0:T(8,128)S(1)} %collective-permute-done.34.refs_3_, ...), custom_call_target="tpu_custom_call" | custom-call | bytes 40590000 | tf_op jit(solution)/shard_map/pallas_call | solution.py:46
  170.5 1.6 collective-permute-start.47
  172.0 3.9 %collective-permute-done.42 = f32[368,128]{1,0:T(8,128)S(1)} collective-permute-done((f32[368,128]{1,0:T(8,128)S(1)}, f32[368,128]{1,0:T(8,128)S(1)}, u32[]{:S(2)}, u32[]{:S(2)}) %collective-permute-start.42) | collective-permute-done | bytes 188448 | tf_op jit(solution)/shard_map/ppermute | solution.py:63
  176.0 1.6 collective-permute-start.43
  177.6 4.0 %collective-permute-done.45 = f32[664,128]{1,0:T(8,128)S(1)} collective-permute-done((f32[664,128]{1,0:T(8,128)S(1)}, f32[664,128]{1,0:T(8,128)S(1)}, u32[]{:S(2)}, u32[]{:S(2)}) %collective-permute-start.45) | collective-permute-done | bytes 340000 | tf_op jit(solution)/shard_map/ppermute | solution.py:63
  182.5 1.7 collective-permute-start.50
  184.4 2.5 %collective-permute-start.48 = (f32[48,128]{1,0:T(8,128)S(1)}, f32[48,128]{1,0:T(8,128)S(1)}, u32[]{:S(2)}, u32[]{:S(2)}) collective-permute-start(f32[48,128]{1,0:T(8,128)S(1)} %get-tuple-element.152), channel_id=1, source_target_pairs={{0,2},{1,3},{2,0},{3,1},{4,6},{5,7},{6,4},{7,5},{8,10},{9,11},{10,... | collective-permute-start | bytes 73736 | tf_op jit(solution)/shard_map/ppermute | solution.py:63
  190.5 2.2 %shard_map.413 = (f32[320,128]{1,0:T(8,128)}, f32[320,128]{1,0:T(8,128)}, f32[320,128]{1,0:T(8,128)}, bf16[320,128]{1,0:T(8,128)(2,1)}, f32[2,320,128]{2,1,0:T(8...) custom-call(s32[1]{0:T(128)} %bitcast.refs_0_.me_ref.refs_1_, ...), custom_call_target="tpu_custom_call" | custom-call | bytes 7380000 | tf_op jit(solution)/shard_map/pallas_call | solution.py:46
  (170 shorter events, 53.3 us)
Async XLA Ops:
  6.5 6.4 %collective-permute-start = (bf16[2,128,1024]{2,1,0:T(8,128)(2,1)S(1)}, bf16[2,128,1024]{2,1,0:T(8,128)(2,1)S(1)}, u32[]{:S(2)}, u32[]{:S(2)}) collective-permute-start(bf16[2,128,1024]{2,1,0:T(8,128)(2,1)S(1)} %get-tuple-element.102), channel_id=1, source_target_pairs={{0,1},{1,0},{2,3},{3,2},{4,5},{5,4},{6,7},{7,6},{8,9},{9,8},{10,11... | collective-permute-start | bytes 1572872 | tf_op jit(solution)/shard_map/ppermute | solution.py:63
  7.8 23.1 %collective-permute-start.2 = (bf16[1,128,1024]{2,1,0:T(8,128)(2,1)}, bf16[1,128,1024]{2,1,0:T(8,128)(2,1)S(1)}, u32[]{:S(2)}, u32[]{:S(2)}) collective-permute-start(bf16[1,128,1024]{2,1,0:T(8,128)(2,1)} %get-tuple-element.177), channel_id=1, source_target_pairs={{0,4},{1,5},{2,6},{3,7},{4,0},{5,1},{6,2},{7,3},{8,12},{9,13},{10,... | collective-permute-start | bytes 786440 | tf_op jit(solution)/shard_map/ppermute | solution.py:63
  11.6 19.3 %collective-permute-start.3 = (bf16[1,128,1024]{2,1,0:T(8,128)(2,1)S(1)}, bf16[1,128,1024]{2,1,0:T(8,128)(2,1)S(1)}, u32[]{:S(2)}, u32[]{:S(2)}) collective-permute-start(bf16[1,128,1024]{2,1,0:T(8,128)(2,1)S(1)} %get-tuple-element.176), channel_id=1, source_target_pairs={{0,6},{1,7},{2,4},{3,5},{4,2},{5,3},{6,0},{7,1},{8,14},{9,15},{10,... | collective-permute-start | bytes 786440 | tf_op jit(solution)/shard_map/ppermute | solution.py:63
  13.0 18.1 %collective-permute-start.4 = (bf16[1,128,1024]{2,1,0:T(8,128)(2,1)S(1)}, bf16[1,128,1024]{2,1,0:T(8,128)(2,1)S(1)}, u32[]{:S(2)}, u32[]{:S(2)}) collective-permute-start(bf16[1,128,1024]{2,1,0:T(8,128)(2,1)S(1)} %add_convert_fusion), channel_id=1, source_target_pairs={{0,2},{1,3},{2,0},{3,1},{4,6},{5,7},{6,4},{7,5},{8,10},{9,11},{10,... | collective-permute-start | bytes 786440 | tf_op jit(solution)/shard_map/ppermute | solution.py:63
  33.5 8.6 %collective-permute-start.7 = (f32[8,128]{1,0:T(8,128)S(1)}, f32[8,128]{1,0:T(8,128)S(1)}, u32[]{:S(2)}, u32[]{:S(2)}) collective-permute-start(f32[8,128]{1,0:T(8,128)S(1)} %add.135), channel_id=1, source_target_pairs={{0,4},{1,5},{2,6},{3,7},{4,0},{5,1},{6,2},{7,3},{8,12},{9,13},{10,... | collective-permute-start | bytes 12296 | tf_op jit(solution)/shard_map/ppermute | solution.py:63
  54.4 6.1 %collective-permute-start.14 = (f32[16,1024]{1,0:T(8,128)S(1)}, f32[16,1024]{1,0:T(8,128)S(1)}, u32[]{:S(2)}, u32[]{:S(2)}) collective-permute-start(f32[16,1024]{1,0:T(8,128)S(1)} %get-tuple-element.117), channel_id=1, source_target_pairs={{0,6},{1,7},{2,4},{3,5},{4,2},{5,3},{6,0},{7,1},{8,14},{9,15},{10,... | collective-permute-start | bytes 196616 | tf_op jit(solution)/shard_map/ppermute | solution.py:63
  56.4 5.5 %collective-permute-start.13 = (f32[16,1024]{1,0:T(8,128)S(1)}, f32[16,1024]{1,0:T(8,128)S(1)}, u32[]{:S(2)}, u32[]{:S(2)}) collective-permute-start(f32[16,1024]{1,0:T(8,128)S(1)} %get-tuple-element.117), channel_id=1, source_target_pairs={{0,4},{1,5},{2,6},{3,7},{4,0},{5,1},{6,2},{7,3},{8,12},{9,13},{10,... | collective-permute-start | bytes 196616 | tf_op jit(solution)/shard_map/ppermute | solution.py:63
  56.4 5.5 %collective-permute-start.12 = (f32[16,1024]{1,0:T(8,128)S(1)}, f32[16,1024]{1,0:T(8,128)S(1)}, u32[]{:S(2)}, u32[]{:S(2)}) collective-permute-start(f32[16,1024]{1,0:T(8,128)S(1)} %get-tuple-element.117), channel_id=1, source_target_pairs={{0,2},{1,3},{2,0},{3,1},{4,6},{5,7},{6,4},{7,5},{8,10},{9,11},{10,... | collective-permute-start | bytes 196616 | tf_op jit(solution)/shard_map/ppermute | solution.py:63
  78.5 5.9 %collective-permute-start.22 = (f32[8,1024]{1,0:T(8,128)S(1)}, f32[8,1024]{1,0:T(8,128)S(1)}, u32[]{:S(2)}, u32[]{:S(2)}) collective-permute-start(f32[8,1024]{1,0:T(8,128)S(1)} %log_add_fusion.1), channel_id=1, source_target_pairs={{0,6},{1,7},{2,4},{3,5},{4,2},{5,3},{6,0},{7,1},{8,14},{9,15},{10,... | collective-permute-start | bytes 98312 | tf_op jit(solution)/shard_map/ppermute | solution.py:63
  85.5 31.4 %collective-permute-start.40 = (bf16[160,1024]{1,0:T(8,128)(2,1)S(1)}, bf16[160,1024]{1,0:T(8,128)(2,1)S(1)}, u32[]{:S(2)}, u32[]{:S(2)}) collective-permute-start(bf16[160,1024]{1,0:T(8,128)(2,1)S(1)} %get-tuple-element.146), channel_id=1, source_target_pairs={{0,6},{1,7},{2,4},{3,5},{4,2},{5,3},{6,0},{7,1},{8,14},{9,15},{10,... | collective-permute-start | bytes 983048 | tf_op jit(solution)/shard_map/ppermute | solution.py:63
  87.6 29.3 %collective-permute-start.39 = (bf16[160,1024]{1,0:T(8,128)(2,1)S(1)}, bf16[160,1024]{1,0:T(8,128)(2,1)S(1)}, u32[]{:S(2)}, u32[]{:S(2)}) collective-permute-start(bf16[160,1024]{1,0:T(8,128)(2,1)S(1)} %get-tuple-element.146), channel_id=1, source_target_pairs={{0,4},{1,5},{2,6},{3,7},{4,0},{5,1},{6,2},{7,3},{8,12},{9,13},{10,... | collective-permute-start | bytes 983048 | tf_op jit(solution)/shard_map/ppermute | solution.py:63
  88.5 28.5 %collective-permute-start.38 = (bf16[160,1024]{1,0:T(8,128)(2,1)S(1)}, bf16[160,1024]{1,0:T(8,128)(2,1)S(1)}, u32[]{:S(2)}, u32[]{:S(2)}) collective-permute-start(bf16[160,1024]{1,0:T(8,128)(2,1)S(1)} %get-tuple-element.146), channel_id=1, source_target_pairs={{0,2},{1,3},{2,0},{3,1},{4,6},{5,7},{6,4},{7,5},{8,10},{9,11},{10,... | collective-permute-start | bytes 983048 | tf_op jit(solution)/shard_map/ppermute | solution.py:63
  117.1 36.3 %collective-permute-start.41 = (bf16[4,160,1024]{2,1,0:T(8,128)(2,1)S(1)}, bf16[4,160,1024]{2,1,0:T(8,128)(2,1)S(1)}, u32[]{:S(2)}, u32[]{:S(2)}) collective-permute-start(bf16[4,160,1024]{2,1,0:T(8,128)(2,1)S(1)} %pad_maximum_fusion.refs_11_.refs_2_), channel_id=1, source_target_pairs={{0,1},{1,0},{2,3},{3,2},{4,5},{5,4},{6,7},{7,6},{8,9},{9,8},{10,11... | collective-permute-start | bytes 3932168 | tf_op jit(solution)/shard_map/ppermute | solution.py:63
  117.3 10.5 %collective-permute-start.25 = (f32[8,1024]{1,0:T(8,128)S(1)}, f32[8,1024]{1,0:T(8,128)S(1)}, u32[]{:S(2)}, u32[]{:S(2)}) collective-permute-start(f32[8,1024]{1,0:T(8,128)S(1)} %add.152), channel_id=1, source_target_pairs={{0,4},{1,5},{2,6},{3,7},{4,0},{5,1},{6,2},{7,3},{8,12},{9,13},{10,... | collective-permute-start | bytes 98312 | tf_op jit(solution)/shard_map/ppermute | solution.py:63
  118.3 9.5 %collective-permute-start.26 = (f32[8,1024]{1,0:T(8,128)S(1)}, f32[8,1024]{1,0:T(8,128)S(1)}, u32[]{:S(2)}, u32[]{:S(2)}) collective-permute-start(f32[8,1024]{1,0:T(8,128)S(1)} %add.152), channel_id=1, source_target_pairs={{0,6},{1,7},{2,4},{3,5},{4,2},{5,3},{6,0},{7,1},{8,14},{9,15},{10,... | collective-permute-start | bytes 98312 | tf_op jit(solution)/shard_map/ppermute | solution.py:63
  120.2 7.6 %collective-permute-start.24 = (f32[8,1024]{1,0:T(8,128)S(1)}, f32[8,1024]{1,0:T(8,128)S(1)}, u32[]{:S(2)}, u32[]{:S(2)}) collective-permute-start(f32[8,1024]{1,0:T(8,128)S(1)} %add.152), channel_id=1, source_target_pairs={{0,2},{1,3},{2,0},{3,1},{4,6},{5,7},{6,4},{7,5},{8,10},{9,11},{10,... | collective-permute-start | bytes 98312 | tf_op jit(solution)/shard_map/ppermute | solution.py:63
  132.8 8.1 %collective-permute-start.28 = (f32[16,1024]{1,0:T(8,128)S(1)}, f32[16,1024]{1,0:T(8,128)S(1)}, u32[]{:S(2)}, u32[]{:S(2)}) collective-permute-start(f32[16,1024]{1,0:T(8,128)S(1)} %get-tuple-element.180), channel_id=1, source_target_pairs={{0,2},{1,3},{2,0},{3,1},{4,6},{5,7},{6,4},{7,5},{8,10},{9,11},{10,... | collective-permute-start | bytes 196616 | tf_op jit(solution)/shard_map/ppermute | solution.py:63
  134.3 8.1 %collective-permute-start.29 = (f32[16,1024]{1,0:T(8,128)S(1)}, f32[16,1024]{1,0:T(8,128)S(1)}, u32[]{:S(2)}, u32[]{:S(2)}) collective-permute-start(f32[16,1024]{1,0:T(8,128)S(1)} %get-tuple-element.179), channel_id=1, source_target_pairs={{0,4},{1,5},{2,6},{3,7},{4,0},{5,1},{6,2},{7,3},{8,12},{9,13},{10,... | collective-permute-start | bytes 196616 | tf_op jit(solution)/shard_map/ppermute | solution.py:63
  135.4 7.0 %collective-permute-start.30 = (f32[16,1024]{1,0:T(8,128)S(1)}, f32[16,1024]{1,0:T(8,128)S(1)}, u32[]{:S(2)}, u32[]{:S(2)}) collective-permute-start(f32[16,1024]{1,0:T(8,128)S(1)} %get-tuple-element.178), channel_id=1, source_target_pairs={{0,6},{1,7},{2,4},{3,5},{4,2},{5,3},{6,0},{7,1},{8,14},{9,15},{10,... | collective-permute-start | bytes 196616 | tf_op jit(solution)/shard_map/ppermute | solution.py:63
  142.4 6.9 %collective-permute-start.33 = (f32[16,1024]{1,0:T(8,128)S(1)}, f32[16,1024]{1,0:T(8,128)S(1)}, u32[]{:S(2)}, u32[]{:S(2)}) collective-permute-start(f32[16,1024]{1,0:T(8,128)S(1)} %fusion.5.refs_7_), channel_id=1, source_target_pairs={{0,6},{1,7},{2,4},{3,5},{4,2},{5,3},{6,0},{7,1},{8,14},{9,15},{10,... | collective-permute-start | bytes 196616 | tf_op jit(solution)/shard_map/ppermute | solution.py:63
  144.5 6.3 %collective-permute-start.32 = (f32[16,1024]{1,0:T(8,128)S(1)}, f32[16,1024]{1,0:T(8,128)S(1)}, u32[]{:S(2)}, u32[]{:S(2)}) collective-permute-start(f32[16,1024]{1,0:T(8,128)S(1)} %fusion.5.refs_7_), channel_id=1, source_target_pairs={{0,4},{1,5},{2,6},{3,7},{4,0},{5,1},{6,2},{7,3},{8,12},{9,13},{10,... | collective-permute-start | bytes 196616 | tf_op jit(solution)/shard_map/ppermute | solution.py:63
  146.9 22.4 %collective-permute-start.44 = (f32[664,128]{1,0:T(8,128)S(1)}, f32[664,128]{1,0:T(8,128)S(1)}, u32[]{:S(2)}, u32[]{:S(2)}) collective-permute-start(f32[664,128]{1,0:T(8,128)S(1)} %shard_map.409), channel_id=1, source_target_pairs={{0,16},{8,24},{16,0},{24,8},{1,17},{9,25},{17,1},{25,9},{2,18},{10... | collective-permute-start | bytes 1019912 | tf_op jit(solution)/shard_map/ppermute | solution.py:63
  150.8 9.3 %collective-permute-start.34 = (f32[4,16,1024]{2,1,0:T(8,128)S(1)}, f32[4,16,1024]{2,1,0:T(8,128)S(1)}, u32[]{:S(2)}, u32[]{:S(2)}) collective-permute-start(f32[4,16,1024]{2,1,0:T(8,128)S(1)} %pad_maximum_fusion.2.refs_2_), channel_id=1, source_target_pairs={{0,1},{1,0},{2,3},{3,2},{4,5},{5,4},{6,7},{7,6},{8,9},{9,8},{10,11... | collective-permute-start | bytes 786440 | tf_op jit(solution)/shard_map/ppermute | solution.py:63
  150.9 8.2 %collective-permute-start.36 = (f32[8,128]{1,0:T(8,128)S(1)}, f32[8,128]{1,0:T(8,128)S(1)}, u32[]{:S(2)}, u32[]{:S(2)}) collective-permute-start(f32[8,128]{1,0:T(8,128)S(1)} %slice.77), channel_id=1, source_target_pairs={{0,16},{8,24},{16,0},{24,8},{1,17},{9,25},{17,1},{25,9},{2,18},{10... | collective-permute-start | bytes 12296 | tf_op jit(solution)/shard_map/ppermute | solution.py:63
  152.0 8.1 %collective-permute-start.37 = (f32[8,128]{1,0:T(8,128)S(1)}, f32[8,128]{1,0:T(8,128)S(1)}, u32[]{:S(2)}, u32[]{:S(2)}) collective-permute-start(f32[8,128]{1,0:T(8,128)S(1)} %slice.77), channel_id=1, source_target_pairs={{0,24},{8,16},{16,8},{24,0},{1,25},{9,17},{17,9},{25,1},{2,26},{10... | collective-permute-start | bytes 12296 | tf_op jit(solution)/shard_map/ppermute | solution.py:63
  153.4 6.7 %collective-permute-start.35 = (f32[8,128]{1,0:T(8,128)S(1)}, f32[8,128]{1,0:T(8,128)S(1)}, u32[]{:S(2)}, u32[]{:S(2)}) collective-permute-start(f32[8,128]{1,0:T(8,128)S(1)} %slice.77), channel_id=1, source_target_pairs={{0,8},{8,0},{16,24},{24,16},{1,9},{9,1},{17,25},{25,17},{2,10},{10... | collective-permute-start | bytes 12296 | tf_op jit(solution)/shard_map/ppermute | solution.py:63
  159.1 11.3 %collective-permute-start.46 = (f32[480,128]{1,0:T(8,128)S(1)}, f32[480,128]{1,0:T(8,128)S(1)}, u32[]{:S(2)}, u32[]{:S(2)}) collective-permute-start(f32[480,128]{1,0:T(8,128)S(1)} %shard_map.411), channel_id=1, source_target_pairs={{0,8},{8,0},{16,24},{24,16},{1,9},{9,1},{17,25},{25,17},{2,10},{10... | collective-permute-start | bytes 737288 | tf_op jit(solution)/shard_map/ppermute | solution.py:63
  168.2 7.7 %collective-permute-start.42 = (f32[368,128]{1,0:T(8,128)S(1)}, f32[368,128]{1,0:T(8,128)S(1)}, u32[]{:S(2)}, u32[]{:S(2)}) collective-permute-start(f32[368,128]{1,0:T(8,128)S(1)} %shard_map.410), channel_id=1, source_target_pairs={{0,8},{8,0},{16,24},{24,16},{1,9},{9,1},{17,25},{25,17},{2,10},{10... | collective-permute-start | bytes 565256 | tf_op jit(solution)/shard_map/ppermute | solution.py:63
  169.3 12.2 %collective-permute-start.45 = (f32[664,128]{1,0:T(8,128)S(1)}, f32[664,128]{1,0:T(8,128)S(1)}, u32[]{:S(2)}, u32[]{:S(2)}) collective-permute-start(f32[664,128]{1,0:T(8,128)S(1)} %add.172), channel_id=1, source_target_pairs={{0,8},{8,0},{16,24},{24,16},{1,9},{9,1},{17,25},{25,17},{2,10},{10... | collective-permute-start | bytes 1019912 | tf_op jit(solution)/shard_map/ppermute | solution.py:63
  170.5 11.3 %collective-permute-start.47 = (f32[480,128]{1,0:T(8,128)S(1)}, f32[480,128]{1,0:T(8,128)S(1)}, u32[]{:S(2)}, u32[]{:S(2)}) collective-permute-start(f32[480,128]{1,0:T(8,128)S(1)} %add.174), channel_id=1, source_target_pairs={{0,16},{8,24},{16,0},{24,8},{1,17},{9,25},{17,1},{25,9},{2,18},{10... | collective-permute-start | bytes 737288 | tf_op jit(solution)/shard_map/ppermute | solution.py:63
  176.0 5.8 %collective-permute-start.43 = (f32[368,128]{1,0:T(8,128)S(1)}, f32[368,128]{1,0:T(8,128)S(1)}, u32[]{:S(2)}, u32[]{:S(2)}) collective-permute-start(f32[368,128]{1,0:T(8,128)S(1)} %add.170), channel_id=1, source_target_pairs={{0,16},{8,24},{16,0},{24,8},{1,17},{9,25},{17,1},{25,9},{2,18},{10... | collective-permute-start | bytes 565256 | tf_op jit(solution)/shard_map/ppermute | solution.py:63
  182.5 5.6 %collective-permute-start.50 = (f32[48,128]{1,0:T(8,128)S(1)}, f32[48,128]{1,0:T(8,128)S(1)}, u32[]{:S(2)}, u32[]{:S(2)}) collective-permute-start(f32[48,128]{1,0:T(8,128)S(1)} %get-tuple-element.152), channel_id=1, source_target_pairs={{0,6},{1,7},{2,4},{3,5},{4,2},{5,3},{6,0},{7,1},{8,14},{9,15},{10,... | collective-permute-start | bytes 73736 | tf_op jit(solution)/shard_map/ppermute | solution.py:63
  (46 other events, 305.1 us)

commit v7 on v6

--- a/solution.py
+++ b/solution.py
@@ -385,7 +385,7 @@
     return jnp.where(lax.rem(place, 2) == 0, near_ref[lax.div(place, 2)], far_ref[lax.div(place, 2)])
 
 
-def decode_kernel(cells, latent, fast, me_ref, near_ref, far_ref, side_ref, stat_ref, norm_ref, plain_ref, w_ref, aff_ref, lse_ref, z_ref, top_ref, mass_ref, score_ref, left_ref):
+def decode_kernel(cells, latent, fast, me_ref, near_ref, far_ref, side_ref, stat_ref, norm_ref, plain_ref, w_ref, aff_ref, lse_ref, z_ref, top_ref, mass_ref, low_ref, score_ref, left_ref):
     kinds = plain_ref.shape[1] - 16
     step = pl.program_id(0)
     cells_at = part_of(step, score_ref.shape[1])
@@ -448,7 +448,9 @@
             for index in range(rows // 8):
                 pieces.append(jnp.exp(value[index * 8 : (index + 1) * 8] - wide[tile]))
                 part = part + pieces[-1]
-            mass_ref[at, far_lanes[tile]] = jnp.concatenate(pieces, axis=0)
+            whole_piece = jnp.concatenate(pieces, axis=0)
+            mass_ref[at, far_lanes[tile]] = whole_piece
+            low_ref[at, far_lanes[tile]] = whole_piece.astype(BF)
             new.append(part)
         return tuple(new)
 
@@ -485,7 +487,7 @@
         out_ref[base + 8 * count :, :] = line_ref[...]
 
 
-def zinb_kernel(rows, span, hid_ref, e_ref, top_ref, w_ref, x_ref, par_ref, lib_ref, lse_ref, gam_ref, g_ref, rt_ref, mass_ref, recon_ref, acc_ref, sc_ref):
+def zinb_kernel(rows, span, hid_ref, e_ref, top_ref, w_ref, x_ref, par_ref, lib_ref, lse_ref, gam_ref, g_ref, mass_ref, recon_ref, acc_ref, sc_ref):
     step = pl.program_id(0)
     genes, width = x_ref.shape
 
@@ -537,7 +539,6 @@
                 g_disp = w0 * (gap + part_th) - y
                 g_ref[at, far_lanes[tile]] = g_mean.astype(BF)
                 g_ref[at_drop, far_lanes[tile]] = g_drop.astype(BF)
-                rt_ref[at, far_lanes[tile]] = mu.astype(BF)
                 sum_t = sum_t + g_disp
                 for part in range(rows // 8):
                     sub = slice(part * 8, (part + 1) * 8)
@@ -558,23 +559,18 @@
     recon_ref[one_row, :] = jnp.concatenate(recon_out, axis=1) + gam_row
 
 
-def back_kernel(width, g_in_ref, rt_ref, aff_ref, w_ref, a_ref, r_ref, g_ref):
-    genes = rt_ref.shape[0]
-    step = pl.program_id(0)
-    cells_at = part_of(step, width)
-
-    @pl.when(step == 0)
-    def _():
-        g_ref[...] = jnp.zeros_like(g_ref)
-
+def softmax_kernel(width, mass_ref, w_ref, r_ref):
+    genes = mass_ref.shape[0]
+    cells_at = part_of(pl.program_id(0), width)
+    r_ref[:, cells_at] = nn(w_ref[:, :genes], mass_ref[:, cells_at])
+
+
+def back_kernel(width, g_in_ref, w_ref, a_ref):
+    cells_at = part_of(pl.program_id(0), width)
     a_ref[:, cells_at] = nn(w_ref[...], g_in_ref[:, cells_at])
-    r_ref[:, cells_at] = nn(w_ref[:, :genes], rt_ref[:, cells_at])
-    row = lax.broadcasted_iota(jnp.int32, (16, width), 0)
-    ones = jnp.where(row == 0, 1.0, 0.0).astype(BF)
-    g_ref[...] += nt(g_in_ref[:, cells_at], jnp.concatenate((relu_low(aff_ref[:, cells_at]), ones), axis=0))
-
-
-def hidden_grad_kernel(cells, latent, me_ref, a_ref, r_ref, mass_ref, aff_ref, lib_ref, stat_ref, gain_ref, lat_ref, recon_ref, z_ref, side_ref, keep_ref, send_ref, lane_ref, oh_ref):
+
+
+def hidden_grad_kernel(cells, latent, me_ref, a_ref, r_ref, mass_ref, aff_ref, top_ref, lse_ref, stat_ref, gain_ref, lat_ref, recon_ref, z_ref, side_ref, keep_ref, send_ref, lane_ref, oh_ref):
     step = pl.program_id(0)
     steps = pl.num_programs(0)
     place = step ^ me_ref[0]
@@ -587,7 +583,8 @@
         lane_ref[...] = jnp.zeros_like(lane_ref)
         oh_ref[...] = jnp.zeros_like(oh_ref)
 
-    back = mass_ref[pl.ds(step, 1), :] * jnp.exp(-lib_ref[pl.ds(step, 1), :])
+    line = pl.ds(step, 1)
+    back = mass_ref[line, :] * jnp.exp(top_ref[line, :] - lse_ref[line, :])
     wide = aff_ref[:, cells_at].astype(F32)
     dy = jnp.where(wide > 0, a_ref[:, cells_at] - back * r_ref[:, cells_at], 0.0)
     weighted = dy * wide
@@ -627,7 +624,7 @@
                     ref[index, line : line + 1, lanes] = oh_ref[pl.ds(owner * part + k, 1), :] * scale
 
 
-def dec_grad_kernel(cells, rt_ref, hid_ref, mass_ref, lib_ref, g_ref, acc_ref, dig_ref, par_ref, dec_ref, mix_ref):
+def dec_grad_kernel(cells, rt_ref, hid_ref, mass_ref, top_ref, lse_ref, g_in_ref, acc_ref, dig_ref, par_ref, dec_ref, mix_ref, g_ref):
     step = pl.program_id(0)
     steps = pl.num_programs(0)
     genes = rt_ref.shape[0]
@@ -637,12 +634,17 @@
     @pl.when(step == 0)
     def _():
         mix_ref[...] = jnp.zeros_like(mix_ref)
-
-    back = mass_ref[pl.ds(step, 1), :] * jnp.exp(-lib_ref[pl.ds(step, 1), :])
+        g_ref[...] = jnp.zeros_like(g_ref)
+
+    line = pl.ds(step, 1)
+    back = mass_ref[line, :] * jnp.exp(top_ref[line, :] - lse_ref[line, :])
     back_high, back_mid, back_low = three(back)
     row = lax.broadcasted_iota(jnp.int32, (16, back.shape[1]), 0)
     extra = jnp.where(row == 0, back_high.astype(F32), jnp.where(row == 1, back_mid.astype(F32), 0.0))
-    scaled = (relu_low(hid_ref[:, cells_at]).astype(F32) * back).astype(BF)
+    hidden_low = relu_low(hid_ref[:, cells_at])
+    ones = jnp.where(row == 0, 1.0, 0.0).astype(BF)
+    g_ref[...] += nt(g_in_ref[:, cells_at], jnp.concatenate((hidden_low, ones), axis=0))
+    scaled = (hidden_low.astype(F32) * back).astype(BF)
     mix_ref[...] += nt(rt_ref[:, cells_at], jnp.concatenate((scaled, extra.astype(BF)), axis=0))
 
     @pl.when(step == steps - 1)
@@ -655,9 +657,9 @@
         score_row = nt(pick, g_ref[:genes, hidden:] - mix[:, hidden:], HI)
         drop_row = nt(pick, g_ref[genes:, hidden:], HI)
         disp_row = row_sums((acc_ref[...] + dig_ref[...]) * par_ref[1])
-        line = lax.broadcasted_iota(jnp.int32, score_row.shape, 0)
+        row = lax.broadcasted_iota(jnp.int32, score_row.shape, 0)
         gene_rows = scale * jnp.where(
-            line == 0, score_row, jnp.where(line == 1, drop_row, jnp.where(line == 2, disp_row, 0.0))
+            row == 0, score_row, jnp.where(row == 1, drop_row, jnp.where(row == 2, disp_row, 0.0))
         )
         dec_ref[2 * genes :, :] = lines(gene_rows, pl.cdiv(genes, 128))
 
@@ -1033,7 +1035,7 @@
         stat_dec = lax.psum(pack[8:16, :hidden], "genes")
     stat_dec = total(stat_dec, "cells")
 
-    aff_dec, lse, z_all, top, mass_all = call(
+    aff_dec, lse, z_all, top, mass_all, mass_low_all = call(
         lambda *refs: decode_kernel(cells, latent, fast, *refs),
         (blocks,),
         [
@@ -1052,15 +1054,23 @@
             ((16, rows_all), F32, here),
             new((blocks, width)),
             ((genes, rows_all), F32, here),
+            ((genes, rows_all), BF, here),
         ],
         scratch=[pltpu.VMEM((genes, width), F32), pltpu.VMEM((2 * hidden, kinds + 48), BF)],
         scalars=1,
         us=8.0,
     )
-    lse_all = log_total_of(lse, "genes")
+    (part_r,) = call(
+        lambda *refs: softmax_kernel(width, *refs),
+        (blocks,),
+        [(mass_low_all, here), full(dec_n)],
+        [((hidden, rows_all), F32, here)],
+        us=2.5,
+    )
+    lse_all = after(log_total_of(lse, "genes"), part_r)
 
     full8 = whole((blocks, width))
-    g_both, rt, mass, recon, gene_acc = call(
+    g_both, mass, recon, gene_acc = call(
         lambda *refs: zinb_kernel(64, min(1024, width), *refs),
         (blocks,),
         [
@@ -1074,7 +1084,7 @@
             full(lse_all),
             full(gam_cell),
         ],
-        [((2 * genes, rows_all), BF, here), ((genes, rows_all), BF, here)]
+        [((2 * genes, rows_all), BF, here)]
         + [new((blocks, width)), new((blocks, width)), new((genes, 128))],
         scratch=[pltpu.VMEM((genes, width), F32)],
         mib=16,
@@ -1082,22 +1092,12 @@
     )
     mass_low = mass + swap(mass, "genes", 1)
     mass = total(mass_low, "genes", 1)
-    part_a, part_r, dec_acc = call(
+    (part_a,) = call(
         lambda *refs: back_kernel(width, *refs),
         (blocks,),
-        [
-            (g_both, here),
-            (rt, here),
-            (aff_dec, here),
-            full(dec_n),
-        ],
-        [
-            ((hidden, rows_all), F32, here),
-            ((hidden, rows_all), F32, here),
-            new((2 * genes, hidden + 16)),
-        ],
-        mib=16,
-        us=9.0,
+        [(g_both, here), full(dec_n)],
+        [((hidden, rows_all), F32, here)],
+        us=4.0,
     )
 
     aff_near, aff_far = gather_genes(after(aff_own, lse_all), fast, blocks, width, mass_low)
@@ -1129,7 +1129,8 @@
             (part_r, here),
             (mass, here),
             (aff_dec, here),
-            full(lib8),
+            full(top),
+            full(lse_all),
             full(stat_dec),
             full(norm_par),
             full(lat_row),
@@ -1149,18 +1150,19 @@
         lambda *refs: dec_grad_kernel(cells, *refs),
         (blocks,),
         [
-            (rt, here),
+            (mass_low_all, here),
             (aff_dec, here),
             (mass, here),
-            full(lib8),
-            full(dec_acc),
+            full(top),
+            full(lse_all),
+            (g_both, here),
             full(gene_acc),
             full(dig_acc),
             full(par),
         ],
         [new((2 * genes + 8 * gene_lines, hidden))],
-        scratch=[pltpu.VMEM((genes, hidden + 16), F32)],
-        us=5.0,
+        scratch=[pltpu.VMEM((genes, hidden + 16), F32), pltpu.VMEM((2 * genes, hidden + 16), F32)],
+        us=6.0,
     )
     if fast:
         got_d = swap(send_d, "genes", 1)

time: 193 us -> 191 us (0.990)
  waiting for transfers between devices: 38.5 us -> 34.8 us
    ppermute x52, waiting for transfers between devices: 38.5 us -> 34.8 us  [swap(): return lax.ppermute(value, axis, [(i, i ^ bit) for i in range(count)])]
    pallas_call x15 -> x16, Pallas kernels: 87.9 us -> 89.1 us  [call(): pl.pallas_call(kernel, out_shape=[pltpu.HBM(out[0], out[1]) if len(out) =...]
  transfers between devices with their start and end apart: 52 -> 52, of which waited for: 25 -> 24; matrix products, arithmetic and copies ran while one was open for 1% -> 1% of each run, Pallas kernels for 37% -> 38%
where the time goes in v7:
time: 191 us; the launch traced here: 190 us
  Pallas kernels  89.1 us (47%)
  starting transfers between devices  62.8 us (33%)
  waiting for transfers between devices  34.8 us (18%)
  between operations  2.12 us (1%)
    pallas_call x16, Pallas kernels, call(): pl.pallas_call(kernel, out_shape=[pltpu.HBM(out[0], out[1]) if len(out) =...  89.1 us
    ppermute x52, starting transfers between devices, swap(): return lax.ppermute(value, axis, [(i, i ^ bit) for i in range(count)])  62.8 us
    ppermute x52, waiting for transfers between devices, swap(): return lax.ppermute(value, axis, [(i, i ^ bit) for i in range(count)])  34.8 us
  transfers between devices with their start and end apart: 52, of which 24 were waited for; matrix products, arithmetic and copies ran while one was open for 1% of the time, Pallas kernels for 38%

profile of v7, /device:TPU:0, one launch (start us, length us, event | category | flops | bytes accessed | tf_op | source)
XLA Modules:
  0.0 190.4 jit_solution(16494439674206626835)
XLA Ops:
  0.7 3.0 %shard_map.399 = (f32[2,128,1024]{2,1,0:T(8,128)S(1)}, bf16[2,128,1024]{2,1,0:T(8,128)(2,1)S(1)}) custom-call(s32[1]{0:T(128)} %bitcast.refs_0_.me_ref.refs_1_, bf16[320,8192]{1,0:T(8,128)(2,1)} %bitcast.49, f32[320,128]{1,0:T(8,128)} %refs_10_.1), custom_call_target="tpu_custom_call" | custom-call | bytes 11070000 | tf_op jit(solution)/shard_map/pallas_call | solution.py:46
  4.2 2.4 %shard_map.400 = (f32[2,128,1024]{2,1,0:T(8,128)S(1)}, bf16[2,128,1024]{2,1,0:T(8,128)(2,1)S(1)}) custom-call(s32[1]{0:T(128)} %bitcast.refs_0_.me_ref.refs_1_, bf16[320,8192]{1,0:T(8,128)(2,1)S(1)} %bitcast.51, f32[320,128]{1,0:T(8,128)} %refs_10_.1), custom_call_target="tpu_custom_call" | custom-call | bytes 7380000 | tf_op jit(solution)/shard_map/pallas_call | solution.py:46
  7.9 3.8 %collective-permute-start.2 = (bf16[1,128,1024]{2,1,0:T(8,128)(2,1)}, bf16[1,128,1024]{2,1,0:T(8,128)(2,1)S(1)}, u32[]{:S(2)}, u32[]{:S(2)}) collective-permute-start(bf16[1,128,1024]{2,1,0:T(8,128)(2,1)} %get-tuple-element.173), channel_id=1, source_target_pairs={{0,4},{1,5},{2,6},{3,7},{4,0},{5,1},{6,2},{7,3},{8,12},{9,13},{10,... | collective-permute-start | bytes 786440 | tf_op jit(solution)/shard_map/ppermute | solution.py:63
  14.5 16.5 %shard_map.402 = (bf16[320,8192]{1,0:T(8,128)(2,1)}, bf16[320,8192]{1,0:T(8,128)(2,1)}, bf16[144,8192]{1,0:T(8,128)(2,1)S(1)}, f32[8,1024]{1,0:T(8,128)S(1)}, f3...) custom-call(bf16[320,8192]{1,0:T(8,128)(2,1)} %bitcast.50, ...), custom_call_target="tpu_custom_call" | custom-call | bytes 55350000 | tf_op jit(solution)/shard_map/pallas_call | solution.py:46
  33.5 7.0 %collective-permute-start.7 = (f32[8,128]{1,0:T(8,128)S(1)}, f32[8,128]{1,0:T(8,128)S(1)}, u32[]{:S(2)}, u32[]{:S(2)}) collective-permute-start(f32[8,128]{1,0:T(8,128)S(1)} %add.135), channel_id=1, source_target_pairs={{0,4},{1,5},{2,6},{3,7},{4,0},{5,1},{6,2},{7,3},{8,12},{9,13},{10,... | collective-permute-start | bytes 12296 | tf_op jit(solution)/shard_map/ppermute | solution.py:63
  42.1 3.8 %collective-permute-done.8 = f32[8,128]{1,0:T(8,128)S(1)} collective-permute-done((f32[8,128]{1,0:T(8,128)S(1)}, f32[8,128]{1,0:T(8,128)S(1)}, u32[]{:S(2)}, u32[]{:S(2)}) %collective-permute-start.8) | collective-permute-done | bytes 4128 | tf_op jit(solution)/shard_map/ppermute | solution.py:63
  49.7 2.4 %collective-permute-done.11 = f32[8,128]{1,0:T(8,128)S(1)} collective-permute-done((f32[8,128]{1,0:T(8,128)S(1)}, f32[8,128]{1,0:T(8,128)S(1)}, u32[]{:S(2)}, u32[]{:S(2)}) %collective-permute-start.11) | collective-permute-done | bytes 4128 | tf_op jit(solution)/shard_map/ppermute | solution.py:63
  52.6 1.8 shard_map.404
  54.4 2.0 %collective-permute-start.14 = (f32[16,1024]{1,0:T(8,128)S(1)}, f32[16,1024]{1,0:T(8,128)S(1)}, u32[]{:S(2)}, u32[]{:S(2)}) collective-permute-start(f32[16,1024]{1,0:T(8,128)S(1)} %get-tuple-element.115), channel_id=1, source_target_pairs={{0,6},{1,7},{2,4},{3,5},{4,2},{5,3},{6,0},{7,1},{8,14},{9,15},{10,... | collective-permute-start | bytes 196616 | tf_op jit(solution)/shard_map/ppermute | solution.py:63
  56.4 2.4 %collective-permute-start.12 = (f32[16,1024]{1,0:T(8,128)S(1)}, f32[16,1024]{1,0:T(8,128)S(1)}, u32[]{:S(2)}, u32[]{:S(2)}) collective-permute-start(f32[16,1024]{1,0:T(8,128)S(1)} %get-tuple-element.115), channel_id=1, source_target_pairs={{0,2},{1,3},{2,0},{3,1},{4,6},{5,7},{6,4},{7,5},{8,10},{9,11},{10,... | collective-permute-start | bytes 196616 | tf_op jit(solution)/shard_map/ppermute | solution.py:63
  58.8 1.7 collective-permute-done.14
  67.2 2.4 %collective-permute-done.18 = f32[8,128]{1,0:T(8,128)S(1)} collective-permute-done((f32[8,128]{1,0:T(8,128)S(1)}, f32[8,128]{1,0:T(8,128)S(1)}, u32[]{:S(2)}, u32[]{:S(2)}) %collective-permute-start.18) | collective-permute-done | bytes 4128 | tf_op jit(solution)/shard_map/ppermute | solution.py:63
  69.7 8.3 %shard_map.405 = (bf16[128,8192]{1,0:T(8,128)(2,1)S(1)}, f32[8,1024]{1,0:T(8,128)S(1)}, f32[16,8192]{1,0:T(8,128)S(1)}, f32[8,1024]{1,0:T(8,128)S(1)}, f32[320,8...) custom-call(s32[1]{0:T(128)} %bitcast.refs_0_.me_ref.refs_1_, f32[4,16,1024]{2,1,0:T(8,128)S(1)} %pad_maximum_fusion.1.refs_1_, ...), custom_call_target="tpu_custom_call" | custom-call | bytes 29520000 | tf_op jit(solution)/shard_map/pallas_call | solution.py:46
  79.3 2.0 %collective-permute-start.22 = (f32[8,1024]{1,0:T(8,128)S(1)}, f32[8,1024]{1,0:T(8,128)S(1)}, u32[]{:S(2)}, u32[]{:S(2)}) collective-permute-start(f32[8,1024]{1,0:T(8,128)S(1)} %log_add_fusion.1), channel_id=1, source_target_pairs={{0,6},{1,7},{2,4},{3,5},{4,2},{5,3},{6,0},{7,1},{8,14},{9,15},{10,... | collective-permute-start | bytes 98312 | tf_op jit(solution)/shard_map/ppermute | solution.py:63
  82.0 1.7 collective-permute-start.20
  83.8 2.5 %shard_map.406.refs_2_ = f32[128,8192]{1,0:T(8,128)S(1)} custom-call(bf16[320,8192]{1,0:T(8,128)(2,1)S(1)} %get-tuple-element.125.refs_0_, bf16[128,640]{1,0:T(8,128)(2,1)S(1)} %get-tuple-element.126.refs_1_), custom_call_target="tpu_custom_call" | custom-call | bytes 9225000 | tf_op jit(solution)/shard_map/pallas_call | solution.py:46
  86.3 2.0 %collective-permute-start.40 = (bf16[160,1024]{1,0:T(8,128)(2,1)S(1)}, bf16[160,1024]{1,0:T(8,128)(2,1)S(1)}, u32[]{:S(2)}, u32[]{:S(2)}) collective-permute-start(bf16[160,1024]{1,0:T(8,128)(2,1)S(1)} %get-tuple-element.142), channel_id=1, source_target_pairs={{0,6},{1,7},{2,4},{3,5},{4,2},{5,3},{6,0},{7,1},{8,14},{9,15},{10,... | collective-permute-start | bytes 983048 | tf_op jit(solution)/shard_map/ppermute | solution.py:63
  90.8 24.7 %shard_map.407 = (bf16[640,8192]{1,0:T(8,128)(2,1)S(1)}, f32[8,1024]{1,0:T(8,128)S(1)}, f32[8,1024]{1,0:T(8,128)S(1)}, f32[320,128]{1,0:T(8,128)S(1)}) custom-call(bf16[128,8192]{1,0:T(8,128)(2,1)S(1)} %get-tuple-element.119.refs_0_.refs_4_.refs_1_, f32[320,8192]{1,0:T(8,128)S(1)} %get-tuple-element.120.refs_1_, ...), custom_call_target="tpu_custom_call" | custom-call | bytes 103320000 | tf_op jit(solution)/shard_map/pallas_call | solution.py:46
  118.2 1.9 collective-permute-start.26
  120.7 3.0 %shard_map.408.refs_1_ = f32[128,8192]{1,0:T(8,128)S(1)} custom-call(bf16[640,8192]{1,0:T(8,128)(2,1)S(1)} %get-tuple-element.129.refs_0_.refs_5_, bf16[128,640]{1,0:T(8,128)(2,1)S(1)} %get-tuple-element.126.refs_1_), custom_call_target="tpu_custom_call" | custom-call | bytes 14760000 | tf_op jit(solution)/shard_map/pallas_call | solution.py:46
  124.2 3.5 %shard_map.409 = (f32[4,16,1024]{2,1,0:T(8,128)S(1)}, f32[4,16,1024]{2,1,0:T(8,128)S(1)}) custom-call(s32[1]{0:T(128)} %bitcast.refs_0_.me_ref.refs_1_, f32[128,8192]{1,0:T(8,128)S(1)} %shard_map.408.refs_1_, f32[128,8192]{1,0:T(8,128)S(1)} %shard_map.406.refs_2_, f32[8,1024]{1,0:T(8,128)S(1)} %add_add_fusion.refs_3_.refs_2_, ...), custom_call_target="tpu_custom_call" | custom-call | bytes 18450000 | tf_op jit(solution)/shard_map/pallas_call | solution.py:46
  131.8 2.0 %collective-permute-start.30 = (f32[16,1024]{1,0:T(8,128)S(1)}, f32[16,1024]{1,0:T(8,128)S(1)}, u32[]{:S(2)}, u32[]{:S(2)}) collective-permute-start(f32[16,1024]{1,0:T(8,128)S(1)} %get-tuple-element.174), channel_id=1, source_target_pairs={{0,6},{1,7},{2,4},{3,5},{4,2},{5,3},{6,0},{7,1},{8,14},{9,15},{10,... | collective-permute-start | bytes 196616 | tf_op jit(solution)/shard_map/ppermute | solution.py:63
  133.8 6.3 %shard_map.410 = f32[664,128]{1,0:T(8,128)S(1)} custom-call(bf16[320,8192]{1,0:T(8,128)(2,1)S(1)} %get-tuple-element.125.refs_0_, bf16[128,8192]{1,0:T(8,128)(2,1)S(1)} %get-tuple-element.119.refs_0_.refs_4_.refs_1_, f32[8,1024]{1,0:T(8,128)S(1)} %add_add_fusion.refs_3_.refs_2_, f32[8,1024]{1,0:T(8,128)S(1)} %get-tuple-element.121.refs_2_.refs_5_.refs_3_, ...), custom_call_target="tpu_custom_call" | custom-call | bytes 22140000 | tf_op jit(solution)/shard_map/pallas_call | solution.py:46
  140.2 1.9 %collective-permute-start.33 = (f32[16,1024]{1,0:T(8,128)S(1)}, f32[16,1024]{1,0:T(8,128)S(1)}, u32[]{:S(2)}, u32[]{:S(2)}) collective-permute-start(f32[16,1024]{1,0:T(8,128)S(1)} %fusion.5.refs_7_), channel_id=1, source_target_pairs={{0,6},{1,7},{2,4},{3,5},{4,2},{5,3},{6,0},{7,1},{8,14},{9,15},{10,... | collective-permute-start | bytes 196616 | tf_op jit(solution)/shard_map/ppermute | solution.py:63
  142.1 2.5 %collective-permute-start.31 = (f32[16,1024]{1,0:T(8,128)S(1)}, f32[16,1024]{1,0:T(8,128)S(1)}, u32[]{:S(2)}, u32[]{:S(2)}) collective-permute-start(f32[16,1024]{1,0:T(8,128)S(1)} %fusion.5.refs_7_), channel_id=1, source_target_pairs={{0,2},{1,3},{2,0},{3,1},{4,6},{5,7},{6,4},{7,5},{8,10},{9,11},{10,... | collective-permute-start | bytes 196616 | tf_op jit(solution)/shard_map/ppermute | solution.py:63
  152.5 3.9 %shard_map.412 = f32[480,128]{1,0:T(8,128)S(1)} custom-call(s32[1]{0:T(128)} %bitcast.refs_0_.me_ref.refs_1_, bf16[320,8192]{1,0:T(8,128)(2,1)S(1)} %bitcast.53, bf16[4,160,1024]{2,1,0:T(8,128)(2,1)S(1)} %pad_maximum_fusion.refs_11_.refs_2_, bf16[4,160,1024]{2,1,0:T(8,128)(2,1)S(1)} %collective-permute-done.41.refs_12_.refs_3_, ...), custom_call_target="tpu_custom_call" | custom-call | bytes 14760000 | tf_op jit(solution)/shard_map/pallas_call | solution.py:46
  157.5 8.1 %shard_map.411 = f32[368,128]{1,0:T(8,128)S(1)} custom-call(s32[1]{0:T(128)} %bitcast.refs_0_.me_ref.refs_1_, s32[1]{0:T(128)} %bitcast.refs_0_.me_ref.refs_1_, f32[4,16,1024]{2,1,0:T(8,128)S(1)} %pad_maximum_fusion.2.refs_2_, f32[4,16,1024]{2,1,0:T(8,128)S(1)} %collective-permute-done.34.refs_3_, ...), custom_call_target="tpu_custom_call" | custom-call | bytes 40590000 | tf_op jit(solution)/shard_map/pallas_call | solution.py:46
  169.4 3.9 %collective-permute-done.42 = f32[368,128]{1,0:T(8,128)S(1)} collective-permute-done((f32[368,128]{1,0:T(8,128)S(1)}, f32[368,128]{1,0:T(8,128)S(1)}, u32[]{:S(2)}, u32[]{:S(2)}) %collective-permute-start.42) | collective-permute-done | bytes 188448 | tf_op jit(solution)/shard_map/ppermute | solution.py:63
  174.9 3.9 %collective-permute-done.45 = f32[664,128]{1,0:T(8,128)S(1)} collective-permute-done((f32[664,128]{1,0:T(8,128)S(1)}, f32[664,128]{1,0:T(8,128)S(1)}, u32[]{:S(2)}, u32[]{:S(2)}) %collective-permute-start.45) | collective-permute-done | bytes 340000 | tf_op jit(solution)/shard_map/ppermute | solution.py:63
  179.9 1.9 %collective-permute-start.50 = (f32[48,128]{1,0:T(8,128)S(1)}, f32[48,128]{1,0:T(8,128)S(1)}, u32[]{:S(2)}, u32[]{:S(2)}) collective-permute-start(f32[48,128]{1,0:T(8,128)S(1)} %get-tuple-element.148), channel_id=1, source_target_pairs={{0,6},{1,7},{2,4},{3,5},{4,2},{5,3},{6,0},{7,1},{8,14},{9,15},{10,... | collective-permute-start | bytes 73736 | tf_op jit(solution)/shard_map/ppermute | solution.py:63
  182.1 2.2 %collective-permute-start.48 = (f32[48,128]{1,0:T(8,128)S(1)}, f32[48,128]{1,0:T(8,128)S(1)}, u32[]{:S(2)}, u32[]{:S(2)}) collective-permute-start(f32[48,128]{1,0:T(8,128)S(1)} %get-tuple-element.148), channel_id=1, source_target_pairs={{0,2},{1,3},{2,0},{3,1},{4,6},{5,7},{6,4},{7,5},{8,10},{9,11},{10,... | collective-permute-start | bytes 73736 | tf_op jit(solution)/shard_map/ppermute | solution.py:63
  188.0 2.2 %shard_map.414 = (f32[320,128]{1,0:T(8,128)}, f32[320,128]{1,0:T(8,128)}, f32[320,128]{1,0:T(8,128)}, bf16[320,128]{1,0:T(8,128)(2,1)}, f32[2,320,128]{2,1,0:T(8...) custom-call(s32[1]{0:T(128)} %bitcast.refs_0_.me_ref.refs_1_, ...), custom_call_target="tpu_custom_call" | custom-call | bytes 7380000 | tf_op jit(solution)/shard_map/pallas_call | solution.py:46
  (169 shorter events, 50.6 us)
Async XLA Ops:
  6.5 6.4 %collective-permute-start = (bf16[2,128,1024]{2,1,0:T(8,128)(2,1)S(1)}, bf16[2,128,1024]{2,1,0:T(8,128)(2,1)S(1)}, u32[]{:S(2)}, u32[]{:S(2)}) collective-permute-start(bf16[2,128,1024]{2,1,0:T(8,128)(2,1)S(1)} %get-tuple-element.100), channel_id=1, source_target_pairs={{0,1},{1,0},{2,3},{3,2},{4,5},{5,4},{6,7},{7,6},{8,9},{9,8},{10,11... | collective-permute-start | bytes 1572872 | tf_op jit(solution)/shard_map/ppermute | solution.py:63
  7.9 23.1 %collective-permute-start.2 = (bf16[1,128,1024]{2,1,0:T(8,128)(2,1)}, bf16[1,128,1024]{2,1,0:T(8,128)(2,1)S(1)}, u32[]{:S(2)}, u32[]{:S(2)}) collective-permute-start(bf16[1,128,1024]{2,1,0:T(8,128)(2,1)} %get-tuple-element.173), channel_id=1, source_target_pairs={{0,4},{1,5},{2,6},{3,7},{4,0},{5,1},{6,2},{7,3},{8,12},{9,13},{10,... | collective-permute-start | bytes 786440 | tf_op jit(solution)/shard_map/ppermute | solution.py:63
  11.6 19.3 %collective-permute-start.3 = (bf16[1,128,1024]{2,1,0:T(8,128)(2,1)S(1)}, bf16[1,128,1024]{2,1,0:T(8,128)(2,1)S(1)}, u32[]{:S(2)}, u32[]{:S(2)}) collective-permute-start(bf16[1,128,1024]{2,1,0:T(8,128)(2,1)S(1)} %get-tuple-element.172), channel_id=1, source_target_pairs={{0,6},{1,7},{2,4},{3,5},{4,2},{5,3},{6,0},{7,1},{8,14},{9,15},{10,... | collective-permute-start | bytes 786440 | tf_op jit(solution)/shard_map/ppermute | solution.py:63
  13.0 18.1 %collective-permute-start.4 = (bf16[1,128,1024]{2,1,0:T(8,128)(2,1)S(1)}, bf16[1,128,1024]{2,1,0:T(8,128)(2,1)S(1)}, u32[]{:S(2)}, u32[]{:S(2)}) collective-permute-start(bf16[1,128,1024]{2,1,0:T(8,128)(2,1)S(1)} %add_convert_fusion), channel_id=1, source_target_pairs={{0,2},{1,3},{2,0},{3,1},{4,6},{5,7},{6,4},{7,5},{8,10},{9,11},{10,... | collective-permute-start | bytes 786440 | tf_op jit(solution)/shard_map/ppermute | solution.py:63
  33.5 8.6 %collective-permute-start.7 = (f32[8,128]{1,0:T(8,128)S(1)}, f32[8,128]{1,0:T(8,128)S(1)}, u32[]{:S(2)}, u32[]{:S(2)}) collective-permute-start(f32[8,128]{1,0:T(8,128)S(1)} %add.135), channel_id=1, source_target_pairs={{0,4},{1,5},{2,6},{3,7},{4,0},{5,1},{6,2},{7,3},{8,12},{9,13},{10,... | collective-permute-start | bytes 12296 | tf_op jit(solution)/shard_map/ppermute | solution.py:63
  54.4 6.1 %collective-permute-start.14 = (f32[16,1024]{1,0:T(8,128)S(1)}, f32[16,1024]{1,0:T(8,128)S(1)}, u32[]{:S(2)}, u32[]{:S(2)}) collective-permute-start(f32[16,1024]{1,0:T(8,128)S(1)} %get-tuple-element.115), channel_id=1, source_target_pairs={{0,6},{1,7},{2,4},{3,5},{4,2},{5,3},{6,0},{7,1},{8,14},{9,15},{10,... | collective-permute-start | bytes 196616 | tf_op jit(solution)/shard_map/ppermute | solution.py:63
  56.4 5.5 %collective-permute-start.13 = (f32[16,1024]{1,0:T(8,128)S(1)}, f32[16,1024]{1,0:T(8,128)S(1)}, u32[]{:S(2)}, u32[]{:S(2)}) collective-permute-start(f32[16,1024]{1,0:T(8,128)S(1)} %get-tuple-element.115), channel_id=1, source_target_pairs={{0,4},{1,5},{2,6},{3,7},{4,0},{5,1},{6,2},{7,3},{8,12},{9,13},{10,... | collective-permute-start | bytes 196616 | tf_op jit(solution)/shard_map/ppermute | solution.py:63
  56.4 5.5 %collective-permute-start.12 = (f32[16,1024]{1,0:T(8,128)S(1)}, f32[16,1024]{1,0:T(8,128)S(1)}, u32[]{:S(2)}, u32[]{:S(2)}) collective-permute-start(f32[16,1024]{1,0:T(8,128)S(1)} %get-tuple-element.115), channel_id=1, source_target_pairs={{0,2},{1,3},{2,0},{3,1},{4,6},{5,7},{6,4},{7,5},{8,10},{9,11},{10,... | collective-permute-start | bytes 196616 | tf_op jit(solution)/shard_map/ppermute | solution.py:63
  79.3 6.9 %collective-permute-start.22 = (f32[8,1024]{1,0:T(8,128)S(1)}, f32[8,1024]{1,0:T(8,128)S(1)}, u32[]{:S(2)}, u32[]{:S(2)}) collective-permute-start(f32[8,1024]{1,0:T(8,128)S(1)} %log_add_fusion.1), channel_id=1, source_target_pairs={{0,6},{1,7},{2,4},{3,5},{4,2},{5,3},{6,0},{7,1},{8,14},{9,15},{10,... | collective-permute-start | bytes 98312 | tf_op jit(solution)/shard_map/ppermute | solution.py:63
  86.3 30.4 %collective-permute-start.40 = (bf16[160,1024]{1,0:T(8,128)(2,1)S(1)}, bf16[160,1024]{1,0:T(8,128)(2,1)S(1)}, u32[]{:S(2)}, u32[]{:S(2)}) collective-permute-start(bf16[160,1024]{1,0:T(8,128)(2,1)S(1)} %get-tuple-element.142), channel_id=1, source_target_pairs={{0,6},{1,7},{2,4},{3,5},{4,2},{5,3},{6,0},{7,1},{8,14},{9,15},{10,... | collective-permute-start | bytes 983048 | tf_op jit(solution)/shard_map/ppermute | solution.py:63
  88.4 28.4 %collective-permute-start.39 = (bf16[160,1024]{1,0:T(8,128)(2,1)S(1)}, bf16[160,1024]{1,0:T(8,128)(2,1)S(1)}, u32[]{:S(2)}, u32[]{:S(2)}) collective-permute-start(bf16[160,1024]{1,0:T(8,128)(2,1)S(1)} %get-tuple-element.142), channel_id=1, source_target_pairs={{0,4},{1,5},{2,6},{3,7},{4,0},{5,1},{6,2},{7,3},{8,12},{9,13},{10,... | collective-permute-start | bytes 983048 | tf_op jit(solution)/shard_map/ppermute | solution.py:63
  89.2 27.5 %collective-permute-start.38 = (bf16[160,1024]{1,0:T(8,128)(2,1)S(1)}, bf16[160,1024]{1,0:T(8,128)(2,1)S(1)}, u32[]{:S(2)}, u32[]{:S(2)}) collective-permute-start(bf16[160,1024]{1,0:T(8,128)(2,1)S(1)} %get-tuple-element.142), channel_id=1, source_target_pairs={{0,2},{1,3},{2,0},{3,1},{4,6},{5,7},{6,4},{7,5},{8,10},{9,11},{10,... | collective-permute-start | bytes 983048 | tf_op jit(solution)/shard_map/ppermute | solution.py:63
  116.9 33.9 %collective-permute-start.41 = (bf16[4,160,1024]{2,1,0:T(8,128)(2,1)S(1)}, bf16[4,160,1024]{2,1,0:T(8,128)(2,1)S(1)}, u32[]{:S(2)}, u32[]{:S(2)}) collective-permute-start(bf16[4,160,1024]{2,1,0:T(8,128)(2,1)S(1)} %pad_maximum_fusion.refs_11_.refs_2_), channel_id=1, source_target_pairs={{0,1},{1,0},{2,3},{3,2},{4,5},{5,4},{6,7},{7,6},{8,9},{9,8},{10,11... | collective-permute-start | bytes 3932168 | tf_op jit(solution)/shard_map/ppermute | solution.py:63
  117.2 6.5 %collective-permute-start.25 = (f32[8,1024]{1,0:T(8,128)S(1)}, f32[8,1024]{1,0:T(8,128)S(1)}, u32[]{:S(2)}, u32[]{:S(2)}) collective-permute-start(f32[8,1024]{1,0:T(8,128)S(1)} %add.152), channel_id=1, source_target_pairs={{0,4},{1,5},{2,6},{3,7},{4,0},{5,1},{6,2},{7,3},{8,12},{9,13},{10,... | collective-permute-start | bytes 98312 | tf_op jit(solution)/shard_map/ppermute | solution.py:63
  118.2 5.7 %collective-permute-start.26 = (f32[8,1024]{1,0:T(8,128)S(1)}, f32[8,1024]{1,0:T(8,128)S(1)}, u32[]{:S(2)}, u32[]{:S(2)}) collective-permute-start(f32[8,1024]{1,0:T(8,128)S(1)} %add.152), channel_id=1, source_target_pairs={{0,6},{1,7},{2,4},{3,5},{4,2},{5,3},{6,0},{7,1},{8,14},{9,15},{10,... | collective-permute-start | bytes 98312 | tf_op jit(solution)/shard_map/ppermute | solution.py:63
  129.3 10.8 %collective-permute-start.28 = (f32[16,1024]{1,0:T(8,128)S(1)}, f32[16,1024]{1,0:T(8,128)S(1)}, u32[]{:S(2)}, u32[]{:S(2)}) collective-permute-start(f32[16,1024]{1,0:T(8,128)S(1)} %get-tuple-element.176), channel_id=1, source_target_pairs={{0,2},{1,3},{2,0},{3,1},{4,6},{5,7},{6,4},{7,5},{8,10},{9,11},{10,... | collective-permute-start | bytes 196616 | tf_op jit(solution)/shard_map/ppermute | solution.py:63
  130.3 9.9 %collective-permute-start.29 = (f32[16,1024]{1,0:T(8,128)S(1)}, f32[16,1024]{1,0:T(8,128)S(1)}, u32[]{:S(2)}, u32[]{:S(2)}) collective-permute-start(f32[16,1024]{1,0:T(8,128)S(1)} %get-tuple-element.175), channel_id=1, source_target_pairs={{0,4},{1,5},{2,6},{3,7},{4,0},{5,1},{6,2},{7,3},{8,12},{9,13},{10,... | collective-permute-start | bytes 196616 | tf_op jit(solution)/shard_map/ppermute | solution.py:63
  131.8 8.3 %collective-permute-start.30 = (f32[16,1024]{1,0:T(8,128)S(1)}, f32[16,1024]{1,0:T(8,128)S(1)}, u32[]{:S(2)}, u32[]{:S(2)}) collective-permute-start(f32[16,1024]{1,0:T(8,128)S(1)} %get-tuple-element.174), channel_id=1, source_target_pairs={{0,6},{1,7},{2,4},{3,5},{4,2},{5,3},{6,0},{7,1},{8,14},{9,15},{10,... | collective-permute-start | bytes 196616 | tf_op jit(solution)/shard_map/ppermute | solution.py:63
  140.2 6.7 %collective-permute-start.33 = (f32[16,1024]{1,0:T(8,128)S(1)}, f32[16,1024]{1,0:T(8,128)S(1)}, u32[]{:S(2)}, u32[]{:S(2)}) collective-permute-start(f32[16,1024]{1,0:T(8,128)S(1)} %fusion.5.refs_7_), channel_id=1, source_target_pairs={{0,6},{1,7},{2,4},{3,5},{4,2},{5,3},{6,0},{7,1},{8,14},{9,15},{10,... | collective-permute-start | bytes 196616 | tf_op jit(solution)/shard_map/ppermute | solution.py:63
  142.1 6.0 %collective-permute-start.32 = (f32[16,1024]{1,0:T(8,128)S(1)}, f32[16,1024]{1,0:T(8,128)S(1)}, u32[]{:S(2)}, u32[]{:S(2)}) collective-permute-start(f32[16,1024]{1,0:T(8,128)S(1)} %fusion.5.refs_7_), channel_id=1, source_target_pairs={{0,4},{1,5},{2,6},{3,7},{4,0},{5,1},{6,2},{7,3},{8,12},{9,13},{10,... | collective-permute-start | bytes 196616 | tf_op jit(solution)/shard_map/ppermute | solution.py:63
  142.1 6.0 %collective-permute-start.31 = (f32[16,1024]{1,0:T(8,128)S(1)}, f32[16,1024]{1,0:T(8,128)S(1)}, u32[]{:S(2)}, u32[]{:S(2)}) collective-permute-start(f32[16,1024]{1,0:T(8,128)S(1)} %fusion.5.refs_7_), channel_id=1, source_target_pairs={{0,2},{1,3},{2,0},{3,1},{4,6},{5,7},{6,4},{7,5},{8,10},{9,11},{10,... | collective-permute-start | bytes 196616 | tf_op jit(solution)/shard_map/ppermute | solution.py:63
  144.6 22.0 %collective-permute-start.44 = (f32[664,128]{1,0:T(8,128)S(1)}, f32[664,128]{1,0:T(8,128)S(1)}, u32[]{:S(2)}, u32[]{:S(2)}) collective-permute-start(f32[664,128]{1,0:T(8,128)S(1)} %shard_map.410), channel_id=1, source_target_pairs={{0,16},{8,24},{16,0},{24,8},{1,17},{9,25},{17,1},{25,9},{2,18},{10... | collective-permute-start | bytes 1019912 | tf_op jit(solution)/shard_map/ppermute | solution.py:63
  148.2 9.3 %collective-permute-start.34 = (f32[4,16,1024]{2,1,0:T(8,128)S(1)}, f32[4,16,1024]{2,1,0:T(8,128)S(1)}, u32[]{:S(2)}, u32[]{:S(2)}) collective-permute-start(f32[4,16,1024]{2,1,0:T(8,128)S(1)} %pad_maximum_fusion.2.refs_2_), channel_id=1, source_target_pairs={{0,1},{1,0},{2,3},{3,2},{4,5},{5,4},{6,7},{7,6},{8,9},{9,8},{10,11... | collective-permute-start | bytes 786440 | tf_op jit(solution)/shard_map/ppermute | solution.py:63
  148.3 8.2 %collective-permute-start.36 = (f32[8,128]{1,0:T(8,128)S(1)}, f32[8,128]{1,0:T(8,128)S(1)}, u32[]{:S(2)}, u32[]{:S(2)}) collective-permute-start(f32[8,128]{1,0:T(8,128)S(1)} %slice.77), channel_id=1, source_target_pairs={{0,16},{8,24},{16,0},{24,8},{1,17},{9,25},{17,1},{25,9},{2,18},{10... | collective-permute-start | bytes 12296 | tf_op jit(solution)/shard_map/ppermute | solution.py:63
  149.4 8.1 %collective-permute-start.37 = (f32[8,128]{1,0:T(8,128)S(1)}, f32[8,128]{1,0:T(8,128)S(1)}, u32[]{:S(2)}, u32[]{:S(2)}) collective-permute-start(f32[8,128]{1,0:T(8,128)S(1)} %slice.77), channel_id=1, source_target_pairs={{0,24},{8,16},{16,8},{24,0},{1,25},{9,17},{17,9},{25,1},{2,26},{10... | collective-permute-start | bytes 12296 | tf_op jit(solution)/shard_map/ppermute | solution.py:63
  150.8 6.7 %collective-permute-start.35 = (f32[8,128]{1,0:T(8,128)S(1)}, f32[8,128]{1,0:T(8,128)S(1)}, u32[]{:S(2)}, u32[]{:S(2)}) collective-permute-start(f32[8,128]{1,0:T(8,128)S(1)} %slice.77), channel_id=1, source_target_pairs={{0,8},{8,0},{16,24},{24,16},{1,9},{9,1},{17,25},{25,17},{2,10},{10... | collective-permute-start | bytes 12296 | tf_op jit(solution)/shard_map/ppermute | solution.py:63
  156.4 11.3 %collective-permute-start.46 = (f32[480,128]{1,0:T(8,128)S(1)}, f32[480,128]{1,0:T(8,128)S(1)}, u32[]{:S(2)}, u32[]{:S(2)}) collective-permute-start(f32[480,128]{1,0:T(8,128)S(1)} %shard_map.412), channel_id=1, source_target_pairs={{0,8},{8,0},{16,24},{24,16},{1,9},{9,1},{17,25},{25,17},{2,10},{10... | collective-permute-start | bytes 737288 | tf_op jit(solution)/shard_map/ppermute | solution.py:63
  165.6 7.7 %collective-permute-start.42 = (f32[368,128]{1,0:T(8,128)S(1)}, f32[368,128]{1,0:T(8,128)S(1)}, u32[]{:S(2)}, u32[]{:S(2)}) collective-permute-start(f32[368,128]{1,0:T(8,128)S(1)} %shard_map.411), channel_id=1, source_target_pairs={{0,8},{8,0},{16,24},{24,16},{1,9},{9,1},{17,25},{25,17},{2,10},{10... | collective-permute-start | bytes 565256 | tf_op jit(solution)/shard_map/ppermute | solution.py:63
  166.7 12.2 %collective-permute-start.45 = (f32[664,128]{1,0:T(8,128)S(1)}, f32[664,128]{1,0:T(8,128)S(1)}, u32[]{:S(2)}, u32[]{:S(2)}) collective-permute-start(f32[664,128]{1,0:T(8,128)S(1)} %add.172), channel_id=1, source_target_pairs={{0,8},{8,0},{16,24},{24,16},{1,9},{9,1},{17,25},{25,17},{2,10},{10... | collective-permute-start | bytes 1019912 | tf_op jit(solution)/shard_map/ppermute | solution.py:63
  167.8 11.3 %collective-permute-start.47 = (f32[480,128]{1,0:T(8,128)S(1)}, f32[480,128]{1,0:T(8,128)S(1)}, u32[]{:S(2)}, u32[]{:S(2)}) collective-permute-start(f32[480,128]{1,0:T(8,128)S(1)} %add.174), channel_id=1, source_target_pairs={{0,16},{8,24},{16,0},{24,8},{1,17},{9,25},{17,1},{25,9},{2,18},{10... | collective-permute-start | bytes 737288 | tf_op jit(solution)/shard_map/ppermute | solution.py:63
  173.3 5.7 %collective-permute-start.43 = (f32[368,128]{1,0:T(8,128)S(1)}, f32[368,128]{1,0:T(8,128)S(1)}, u32[]{:S(2)}, u32[]{:S(2)}) collective-permute-start(f32[368,128]{1,0:T(8,128)S(1)} %add.170), channel_id=1, source_target_pairs={{0,16},{8,24},{16,0},{24,8},{1,17},{9,25},{17,1},{25,9},{2,18},{10... | collective-permute-start | bytes 565256 | tf_op jit(solution)/shard_map/ppermute | solution.py:63
  179.9 5.6 %collective-permute-start.50 = (f32[48,128]{1,0:T(8,128)S(1)}, f32[48,128]{1,0:T(8,128)S(1)}, u32[]{:S(2)}, u32[]{:S(2)}) collective-permute-start(f32[48,128]{1,0:T(8,128)S(1)} %get-tuple-element.148), channel_id=1, source_target_pairs={{0,6},{1,7},{2,4},{3,5},{4,2},{5,3},{6,0},{7,1},{8,14},{9,15},{10,... | collective-permute-start | bytes 73736 | tf_op jit(solution)/shard_map/ppermute | solution.py:63
  (45 other events, 299.5 us)

commit v8 on v7

--- a/solution.py
+++ b/solution.py
@@ -559,10 +559,18 @@
     recon_ref[one_row, :] = jnp.concatenate(recon_out, axis=1) + gam_row
 
 
-def softmax_kernel(width, mass_ref, w_ref, r_ref):
+def softmax_kernel(width, mass_ref, w_ref, side_ref, z_ref, aff_ref, r_ref, product_ref):
     genes = mass_ref.shape[0]
-    cells_at = part_of(pl.program_id(0), width)
+    step = pl.program_id(0)
+    cells_at = part_of(step, width)
+
+    @pl.when(step == 0)
+    def _():
+        product_ref[...] = jnp.zeros_like(product_ref)
+
     r_ref[:, cells_at] = nn(w_ref[:, :genes], mass_ref[:, cells_at])
+    left = jnp.concatenate((side_ref[:, cells_at], z_ref[:, cells_at].astype(BF)), axis=0)
+    product_ref[...] += nt(left, aff_ref[:, cells_at])
 
 
 def back_kernel(width, g_in_ref, w_ref, a_ref):
@@ -664,7 +672,7 @@
         dec_ref[2 * genes :, :] = lines(gene_rows, pl.cdiv(genes, 128))
 
 
-def enc_back_kernel(cells, latent, fast, span, me_ref, own_ref, dnear_ref, dfar_ref, aff_dec_ref, sums_ref, stat_ref, gain_ref, lat_ref, noise_ref, klw_ref, anear_ref, afar_ref, side_ref, held_ref, logc_ref, cols_ref, z_ref, out_ref, rest_ref, lane_ref, left_ref, fixed_ref, one_ref, kept_ref, sum_ref):
+def enc_back_kernel(cells, latent, fast, span, me_ref, own_ref, dnear_ref, dfar_ref, aff_dec_ref, sums_ref, stat_ref, gain_ref, lat_ref, noise_ref, klw_ref, anear_ref, afar_ref, side_ref, held_ref, product_ref, logc_ref, cols_ref, z_ref, out_ref, rest_ref, lane_ref, left_ref, fixed_ref, one_ref, kept_ref, sum_ref):
     step = pl.program_id(0)
     steps = kept_ref.shape[0]
     genes, width = logc_ref.shape[0], dnear_ref.shape[2]
@@ -736,9 +744,6 @@
     out_ref[genes : genes + 1, :] += mixed[kinds : kinds + 1]
     rest_ref[kinds : kinds + 32, :] += nt(head_high, one_ref[hidden:, :])
     base = kinds + 40
-    product = nt(jnp.concatenate((side, z.astype(BF)), axis=0), affine_dec)
-    rest_ref[base : base + kinds, :] -= product[:kinds] * m_two
-    rest_ref[base + kinds : base + kinds + 16, :] -= product[kinds + 16 :] * m_two
 
     @pl.when(step == steps - 1)
     def _():
@@ -746,6 +751,8 @@
         rest_ref[kinds + 32 : kinds + 40, 0:32] = row_sums(sum_ref[0:32, :])
         held = jnp.concatenate((held_ref[...], sum_ref[32:, :]), axis=0)
         rest_ref[base : base + kinds + 16, :] -= jnp.sum(held, axis=1, keepdims=True) * m_one
+        rest_ref[base : base + kinds, :] -= product_ref[:kinds, :] * m_two
+        rest_ref[base + kinds : base + kinds + 16, :] -= product_ref[kinds + 16 :, :] * m_two
         count = (kinds + 16) // steps
         for owner in range(steps):
             for k in range(count):
@@ -1060,12 +1067,12 @@
         scalars=1,
         us=8.0,
     )
-    (part_r,) = call(
+    part_r, product = call(
         lambda *refs: softmax_kernel(width, *refs),
         (blocks,),
-        [(mass_low_all, here), full(dec_n)],
-        [((hidden, rows_all), F32, here)],
-        us=2.5,
+        [(mass_low_all, here), full(dec_n), (side, here), (z_all, here), (aff_dec, here)],
+        [((hidden, rows_all), F32, here), new((kinds + 32, hidden))],
+        us=3.0,
     )
     lse_all = after(log_total_of(lse, "genes"), part_r)
 
@@ -1199,6 +1206,7 @@
             (aff_far, here),
             (side, here),
             full(held),
+            full(product),
             (logc, here),
             full(head_cols),
             (z_all, here),

time: 191 us -> 190 us (level)
  transfers between devices with their start and end apart: 52 -> 52, of which waited for: 24 -> 23; matrix products, arithmetic and copies ran while one was open for 1% -> 1% of each run, Pallas kernels for 38% -> 38%
where the time goes in v8:
time: 190 us
  Pallas kernels  88.7 us (47%)
  starting transfers between devices  62.7 us (33%)
  waiting for transfers between devices  34.4 us (18%)
  between operations  2.13 us (1%)
    pallas_call x16, Pallas kernels, call(): pl.pallas_call(kernel, out_shape=[pltpu.HBM(out[0], out[1]) if len(out) =...  88.7 us
    ppermute x52, starting transfers between devices, swap(): return lax.ppermute(value, axis, [(i, i ^ bit) for i in range(count)])  62.7 us
    ppermute x52, waiting for transfers between devices, swap(): return lax.ppermute(value, axis, [(i, i ^ bit) for i in range(count)])  34.4 us
  transfers between devices with their start and end apart: 52, of which 23 were waited for; matrix products, arithmetic and copies ran while one was open for 1% of the time, Pallas kernels for 38%

profile of v8, /device:TPU:0, one launch (start us, length us, event | category | flops | bytes accessed | tf_op | source)
XLA Modules:
  0.0 189.6 jit_solution(3932206929578493076)
XLA Ops:
  0.7 3.0 %shard_map.399 = (f32[2,128,1024]{2,1,0:T(8,128)S(1)}, bf16[2,128,1024]{2,1,0:T(8,128)(2,1)S(1)}) custom-call(s32[1]{0:T(128)} %bitcast.refs_0_.me_ref.refs_1_, bf16[320,8192]{1,0:T(8,128)(2,1)} %bitcast.49, f32[320,128]{1,0:T(8,128)} %refs_10_.1), custom_call_target="tpu_custom_call" | custom-call | bytes 11070000 | tf_op jit(solution)/shard_map/pallas_call | solution.py:46
  4.2 2.4 %shard_map.400 = (f32[2,128,1024]{2,1,0:T(8,128)S(1)}, bf16[2,128,1024]{2,1,0:T(8,128)(2,1)S(1)}) custom-call(s32[1]{0:T(128)} %bitcast.refs_0_.me_ref.refs_1_, bf16[320,8192]{1,0:T(8,128)(2,1)S(1)} %bitcast.51, f32[320,128]{1,0:T(8,128)} %refs_10_.1), custom_call_target="tpu_custom_call" | custom-call | bytes 7380000 | tf_op jit(solution)/shard_map/pallas_call | solution.py:46
  7.9 3.8 %collective-permute-start.2 = (bf16[1,128,1024]{2,1,0:T(8,128)(2,1)}, bf16[1,128,1024]{2,1,0:T(8,128)(2,1)S(1)}, u32[]{:S(2)}, u32[]{:S(2)}) collective-permute-start(bf16[1,128,1024]{2,1,0:T(8,128)(2,1)} %get-tuple-element.177), channel_id=1, source_target_pairs={{0,4},{1,5},{2,6},{3,7},{4,0},{5,1},{6,2},{7,3},{8,12},{9,13},{10,... | collective-permute-start | bytes 786440 | tf_op jit(solution)/shard_map/ppermute | solution.py:63
  14.5 16.5 %shard_map.402 = (bf16[320,8192]{1,0:T(8,128)(2,1)}, bf16[320,8192]{1,0:T(8,128)(2,1)}, bf16[144,8192]{1,0:T(8,128)(2,1)S(1)}, f32[8,1024]{1,0:T(8,128)S(1)}, f3...) custom-call(bf16[320,8192]{1,0:T(8,128)(2,1)} %bitcast.50, ...), custom_call_target="tpu_custom_call" | custom-call | bytes 55350000 | tf_op jit(solution)/shard_map/pallas_call | solution.py:46
  33.5 7.0 %collective-permute-start.7 = (f32[8,128]{1,0:T(8,128)S(1)}, f32[8,128]{1,0:T(8,128)S(1)}, u32[]{:S(2)}, u32[]{:S(2)}) collective-permute-start(f32[8,128]{1,0:T(8,128)S(1)} %add.135), channel_id=1, source_target_pairs={{0,4},{1,5},{2,6},{3,7},{4,0},{5,1},{6,2},{7,3},{8,12},{9,13},{10,... | collective-permute-start | bytes 12296 | tf_op jit(solution)/shard_map/ppermute | solution.py:63
  42.1 3.8 %collective-permute-done.8 = f32[8,128]{1,0:T(8,128)S(1)} collective-permute-done((f32[8,128]{1,0:T(8,128)S(1)}, f32[8,128]{1,0:T(8,128)S(1)}, u32[]{:S(2)}, u32[]{:S(2)}) %collective-permute-start.8) | collective-permute-done | bytes 4128 | tf_op jit(solution)/shard_map/ppermute | solution.py:63
  49.7 2.4 %collective-permute-done.11 = f32[8,128]{1,0:T(8,128)S(1)} collective-permute-done((f32[8,128]{1,0:T(8,128)S(1)}, f32[8,128]{1,0:T(8,128)S(1)}, u32[]{:S(2)}, u32[]{:S(2)}) %collective-permute-start.11) | collective-permute-done | bytes 4128 | tf_op jit(solution)/shard_map/ppermute | solution.py:63
  52.6 1.8 shard_map.404
  54.4 2.0 %collective-permute-start.14 = (f32[16,1024]{1,0:T(8,128)S(1)}, f32[16,1024]{1,0:T(8,128)S(1)}, u32[]{:S(2)}, u32[]{:S(2)}) collective-permute-start(f32[16,1024]{1,0:T(8,128)S(1)} %get-tuple-element.117), channel_id=1, source_target_pairs={{0,6},{1,7},{2,4},{3,5},{4,2},{5,3},{6,0},{7,1},{8,14},{9,15},{10,... | collective-permute-start | bytes 196616 | tf_op jit(solution)/shard_map/ppermute | solution.py:63
  56.4 2.4 %collective-permute-start.12 = (f32[16,1024]{1,0:T(8,128)S(1)}, f32[16,1024]{1,0:T(8,128)S(1)}, u32[]{:S(2)}, u32[]{:S(2)}) collective-permute-start(f32[16,1024]{1,0:T(8,128)S(1)} %get-tuple-element.117), channel_id=1, source_target_pairs={{0,2},{1,3},{2,0},{3,1},{4,6},{5,7},{6,4},{7,5},{8,10},{9,11},{10,... | collective-permute-start | bytes 196616 | tf_op jit(solution)/shard_map/ppermute | solution.py:63
  67.2 2.4 %collective-permute-done.18 = f32[8,128]{1,0:T(8,128)S(1)} collective-permute-done((f32[8,128]{1,0:T(8,128)S(1)}, f32[8,128]{1,0:T(8,128)S(1)}, u32[]{:S(2)}, u32[]{:S(2)}) %collective-permute-start.18) | collective-permute-done | bytes 4128 | tf_op jit(solution)/shard_map/ppermute | solution.py:63
  69.7 8.3 %shard_map.405 = (bf16[128,8192]{1,0:T(8,128)(2,1)S(1)}, f32[8,1024]{1,0:T(8,128)S(1)}, f32[16,8192]{1,0:T(8,128)S(1)}, f32[8,1024]{1,0:T(8,128)S(1)}, f32[320,8...) custom-call(s32[1]{0:T(128)} %bitcast.refs_0_.me_ref.refs_1_, f32[4,16,1024]{2,1,0:T(8,128)S(1)} %pad_maximum_fusion.1.refs_1_, ...), custom_call_target="tpu_custom_call" | custom-call | bytes 29520000 | tf_op jit(solution)/shard_map/pallas_call | solution.py:46
  79.3 2.0 %collective-permute-start.22 = (f32[8,1024]{1,0:T(8,128)S(1)}, f32[8,1024]{1,0:T(8,128)S(1)}, u32[]{:S(2)}, u32[]{:S(2)}) collective-permute-start(f32[8,1024]{1,0:T(8,128)S(1)} %log_add_fusion.1), channel_id=1, source_target_pairs={{0,6},{1,7},{2,4},{3,5},{4,2},{5,3},{6,0},{7,1},{8,14},{9,15},{10,... | collective-permute-start | bytes 98312 | tf_op jit(solution)/shard_map/ppermute | solution.py:63
  82.0 1.7 collective-permute-start.20
  83.7 3.2 %shard_map.406 = (f32[128,8192]{1,0:T(8,128)S(1)}, f32[160,128]{1,0:T(8,128)S(1)}) custom-call(bf16[320,8192]{1,0:T(8,128)(2,1)S(1)} %get-tuple-element.127.refs_0_, bf16[128,640]{1,0:T(8,128)(2,1)S(1)} %get-tuple-element.128.refs_1_, bf16[144,8192]{1,0:T(8,128)(2,1)S(1)} %get-tuple-element.118.refs_3_.refs_2_.refs_12_.refs_13_.refs_4_, ...), custom_call_target="tpu_custom_call" | custom-call | bytes 11070000 | tf_op jit(solution)/shard_map/pallas_call | solution.py:46
  87.0 2.1 %collective-permute-start.40 = (bf16[160,1024]{1,0:T(8,128)(2,1)S(1)}, bf16[160,1024]{1,0:T(8,128)(2,1)S(1)}, u32[]{:S(2)}, u32[]{:S(2)}) collective-permute-start(bf16[160,1024]{1,0:T(8,128)(2,1)S(1)} %get-tuple-element.145), channel_id=1, source_target_pairs={{0,6},{1,7},{2,4},{3,5},{4,2},{5,3},{6,0},{7,1},{8,14},{9,15},{10,... | collective-permute-start | bytes 983048 | tf_op jit(solution)/shard_map/ppermute | solution.py:63
  89.2 2.3 %collective-permute-start.38 = (bf16[160,1024]{1,0:T(8,128)(2,1)S(1)}, bf16[160,1024]{1,0:T(8,128)(2,1)S(1)}, u32[]{:S(2)}, u32[]{:S(2)}) collective-permute-start(bf16[160,1024]{1,0:T(8,128)(2,1)S(1)} %get-tuple-element.145), channel_id=1, source_target_pairs={{0,2},{1,3},{2,0},{3,1},{4,6},{5,7},{6,4},{7,5},{8,10},{9,11},{10,... | collective-permute-start | bytes 983048 | tf_op jit(solution)/shard_map/ppermute | solution.py:63
  91.5 24.7 %shard_map.407 = (bf16[640,8192]{1,0:T(8,128)(2,1)S(1)}, f32[8,1024]{1,0:T(8,128)S(1)}, f32[8,1024]{1,0:T(8,128)S(1)}, f32[320,128]{1,0:T(8,128)S(1)}) custom-call(bf16[128,8192]{1,0:T(8,128)(2,1)S(1)} %get-tuple-element.121.refs_4_.refs_0_.refs_1_, f32[320,8192]{1,0:T(8,128)S(1)} %get-tuple-element.122.refs_1_, ...), custom_call_target="tpu_custom_call" | custom-call | bytes 103320000 | tf_op jit(solution)/shard_map/pallas_call | solution.py:46
  118.4 1.8 collective-permute-start.26
  121.4 3.0 %shard_map.408.refs_1_ = f32[128,8192]{1,0:T(8,128)S(1)} custom-call(bf16[640,8192]{1,0:T(8,128)(2,1)S(1)} %get-tuple-element.133.refs_0_.refs_5_, bf16[128,640]{1,0:T(8,128)(2,1)S(1)} %get-tuple-element.128.refs_1_), custom_call_target="tpu_custom_call" | custom-call | bytes 14760000 | tf_op jit(solution)/shard_map/pallas_call | solution.py:46
  124.5 3.4 %shard_map.409 = (f32[4,16,1024]{2,1,0:T(8,128)S(1)}, f32[4,16,1024]{2,1,0:T(8,128)S(1)}) custom-call(s32[1]{0:T(128)} %bitcast.refs_0_.me_ref.refs_1_, f32[128,8192]{1,0:T(8,128)S(1)} %shard_map.408.refs_1_, f32[128,8192]{1,0:T(8,128)S(1)} %get-tuple-element.130.refs_2_, f32[8,1024]{1,0:T(8,128)S(1)} %add_add_fusion.refs_3_.refs_2_, ...), custom_call_target="tpu_custom_call" | custom-call | bytes 18450000 | tf_op jit(solution)/shard_map/pallas_call | solution.py:46
  132.1 1.9 collective-permute-start.30
  133.9 6.3 %shard_map.410 = f32[664,128]{1,0:T(8,128)S(1)} custom-call(bf16[320,8192]{1,0:T(8,128)(2,1)S(1)} %get-tuple-element.127.refs_0_, bf16[128,8192]{1,0:T(8,128)(2,1)S(1)} %get-tuple-element.121.refs_4_.refs_0_.refs_1_, f32[8,1024]{1,0:T(8,128)S(1)} %add_add_fusion.refs_3_.refs_2_, f32[8,1024]{1,0:T(8,128)S(1)} %get-tuple-element.123.refs_2_.refs_5_.refs_3_, ...), custom_call_target="tpu_custom_call" | custom-call | bytes 22140000 | tf_op jit(solution)/shard_map/pallas_call | solution.py:46
  140.3 2.0 %collective-permute-start.33 = (f32[16,1024]{1,0:T(8,128)S(1)}, f32[16,1024]{1,0:T(8,128)S(1)}, u32[]{:S(2)}, u32[]{:S(2)}) collective-permute-start(f32[16,1024]{1,0:T(8,128)S(1)} %fusion.5.refs_7_), channel_id=1, source_target_pairs={{0,6},{1,7},{2,4},{3,5},{4,2},{5,3},{6,0},{7,1},{8,14},{9,15},{10,... | collective-permute-start | bytes 196616 | tf_op jit(solution)/shard_map/ppermute | solution.py:63
  142.4 2.4 %collective-permute-start.31 = (f32[16,1024]{1,0:T(8,128)S(1)}, f32[16,1024]{1,0:T(8,128)S(1)}, u32[]{:S(2)}, u32[]{:S(2)}) collective-permute-start(f32[16,1024]{1,0:T(8,128)S(1)} %fusion.5.refs_7_), channel_id=1, source_target_pairs={{0,2},{1,3},{2,0},{3,1},{4,6},{5,7},{6,4},{7,5},{8,10},{9,11},{10,... | collective-permute-start | bytes 196616 | tf_op jit(solution)/shard_map/ppermute | solution.py:63
  152.6 3.9 %shard_map.412 = f32[480,128]{1,0:T(8,128)S(1)} custom-call(s32[1]{0:T(128)} %bitcast.refs_0_.me_ref.refs_1_, bf16[320,8192]{1,0:T(8,128)(2,1)S(1)} %bitcast.53, bf16[4,160,1024]{2,1,0:T(8,128)(2,1)S(1)} %pad_maximum_fusion.refs_11_.refs_2_, bf16[4,160,1024]{2,1,0:T(8,128)(2,1)S(1)} %collective-permute-done.41.refs_12_.refs_3_, ...), custom_call_target="tpu_custom_call" | custom-call | bytes 14760000 | tf_op jit(solution)/shard_map/pallas_call | solution.py:46
  157.7 7.1 %shard_map.411 = f32[368,128]{1,0:T(8,128)S(1)} custom-call(s32[1]{0:T(128)} %bitcast.refs_0_.me_ref.refs_1_, s32[1]{0:T(128)} %bitcast.refs_0_.me_ref.refs_1_, f32[4,16,1024]{2,1,0:T(8,128)S(1)} %pad_maximum_fusion.2.refs_2_, f32[4,16,1024]{2,1,0:T(8,128)S(1)} %collective-permute-done.34.refs_3_, ...), custom_call_target="tpu_custom_call" | custom-call | bytes 40590000 | tf_op jit(solution)/shard_map/pallas_call | solution.py:46
  168.6 3.9 %collective-permute-done.42 = f32[368,128]{1,0:T(8,128)S(1)} collective-permute-done((f32[368,128]{1,0:T(8,128)S(1)}, f32[368,128]{1,0:T(8,128)S(1)}, u32[]{:S(2)}, u32[]{:S(2)}) %collective-permute-start.42) | collective-permute-done | bytes 188448 | tf_op jit(solution)/shard_map/ppermute | solution.py:63
  174.1 4.0 %collective-permute-done.45 = f32[664,128]{1,0:T(8,128)S(1)} collective-permute-done((f32[664,128]{1,0:T(8,128)S(1)}, f32[664,128]{1,0:T(8,128)S(1)}, u32[]{:S(2)}, u32[]{:S(2)}) %collective-permute-start.45) | collective-permute-done | bytes 340000 | tf_op jit(solution)/shard_map/ppermute | solution.py:63
  179.1 1.9 %collective-permute-start.50 = (f32[48,128]{1,0:T(8,128)S(1)}, f32[48,128]{1,0:T(8,128)S(1)}, u32[]{:S(2)}, u32[]{:S(2)}) collective-permute-start(f32[48,128]{1,0:T(8,128)S(1)} %get-tuple-element.152), channel_id=1, source_target_pairs={{0,6},{1,7},{2,4},{3,5},{4,2},{5,3},{6,0},{7,1},{8,14},{9,15},{10,... | collective-permute-start | bytes 73736 | tf_op jit(solution)/shard_map/ppermute | solution.py:63
  181.3 2.2 %collective-permute-start.48 = (f32[48,128]{1,0:T(8,128)S(1)}, f32[48,128]{1,0:T(8,128)S(1)}, u32[]{:S(2)}, u32[]{:S(2)}) collective-permute-start(f32[48,128]{1,0:T(8,128)S(1)} %get-tuple-element.152), channel_id=1, source_target_pairs={{0,2},{1,3},{2,0},{3,1},{4,6},{5,7},{6,4},{7,5},{8,10},{9,11},{10,... | collective-permute-start | bytes 73736 | tf_op jit(solution)/shard_map/ppermute | solution.py:63
  187.2 2.2 %shard_map.414 = (f32[320,128]{1,0:T(8,128)}, f32[320,128]{1,0:T(8,128)}, f32[320,128]{1,0:T(8,128)}, bf16[320,128]{1,0:T(8,128)(2,1)}, f32[2,320,128]{2,1,0:T(8...) custom-call(s32[1]{0:T(128)} %bitcast.refs_0_.me_ref.refs_1_, ...), custom_call_target="tpu_custom_call" | custom-call | bytes 7380000 | tf_op jit(solution)/shard_map/pallas_call | solution.py:46
  (169 shorter events, 49.6 us)
Async XLA Ops:
  6.5 6.4 %collective-permute-start = (bf16[2,128,1024]{2,1,0:T(8,128)(2,1)S(1)}, bf16[2,128,1024]{2,1,0:T(8,128)(2,1)S(1)}, u32[]{:S(2)}, u32[]{:S(2)}) collective-permute-start(bf16[2,128,1024]{2,1,0:T(8,128)(2,1)S(1)} %get-tuple-element.102), channel_id=1, source_target_pairs={{0,1},{1,0},{2,3},{3,2},{4,5},{5,4},{6,7},{7,6},{8,9},{9,8},{10,11... | collective-permute-start | bytes 1572872 | tf_op jit(solution)/shard_map/ppermute | solution.py:63
  7.9 23.1 %collective-permute-start.2 = (bf16[1,128,1024]{2,1,0:T(8,128)(2,1)}, bf16[1,128,1024]{2,1,0:T(8,128)(2,1)S(1)}, u32[]{:S(2)}, u32[]{:S(2)}) collective-permute-start(bf16[1,128,1024]{2,1,0:T(8,128)(2,1)} %get-tuple-element.177), channel_id=1, source_target_pairs={{0,4},{1,5},{2,6},{3,7},{4,0},{5,1},{6,2},{7,3},{8,12},{9,13},{10,... | collective-permute-start | bytes 786440 | tf_op jit(solution)/shard_map/ppermute | solution.py:63
  11.6 19.3 %collective-permute-start.3 = (bf16[1,128,1024]{2,1,0:T(8,128)(2,1)S(1)}, bf16[1,128,1024]{2,1,0:T(8,128)(2,1)S(1)}, u32[]{:S(2)}, u32[]{:S(2)}) collective-permute-start(bf16[1,128,1024]{2,1,0:T(8,128)(2,1)S(1)} %get-tuple-element.176), channel_id=1, source_target_pairs={{0,6},{1,7},{2,4},{3,5},{4,2},{5,3},{6,0},{7,1},{8,14},{9,15},{10,... | collective-permute-start | bytes 786440 | tf_op jit(solution)/shard_map/ppermute | solution.py:63
  13.0 18.1 %collective-permute-start.4 = (bf16[1,128,1024]{2,1,0:T(8,128)(2,1)S(1)}, bf16[1,128,1024]{2,1,0:T(8,128)(2,1)S(1)}, u32[]{:S(2)}, u32[]{:S(2)}) collective-permute-start(bf16[1,128,1024]{2,1,0:T(8,128)(2,1)S(1)} %add_convert_fusion), channel_id=1, source_target_pairs={{0,2},{1,3},{2,0},{3,1},{4,6},{5,7},{6,4},{7,5},{8,10},{9,11},{10,... | collective-permute-start | bytes 786440 | tf_op jit(solution)/shard_map/ppermute | solution.py:63
  33.5 8.6 %collective-permute-start.7 = (f32[8,128]{1,0:T(8,128)S(1)}, f32[8,128]{1,0:T(8,128)S(1)}, u32[]{:S(2)}, u32[]{:S(2)}) collective-permute-start(f32[8,128]{1,0:T(8,128)S(1)} %add.135), channel_id=1, source_target_pairs={{0,4},{1,5},{2,6},{3,7},{4,0},{5,1},{6,2},{7,3},{8,12},{9,13},{10,... | collective-permute-start | bytes 12296 | tf_op jit(solution)/shard_map/ppermute | solution.py:63
  54.4 6.1 %collective-permute-start.14 = (f32[16,1024]{1,0:T(8,128)S(1)}, f32[16,1024]{1,0:T(8,128)S(1)}, u32[]{:S(2)}, u32[]{:S(2)}) collective-permute-start(f32[16,1024]{1,0:T(8,128)S(1)} %get-tuple-element.117), channel_id=1, source_target_pairs={{0,6},{1,7},{2,4},{3,5},{4,2},{5,3},{6,0},{7,1},{8,14},{9,15},{10,... | collective-permute-start | bytes 196616 | tf_op jit(solution)/shard_map/ppermute | solution.py:63
  56.4 5.5 %collective-permute-start.13 = (f32[16,1024]{1,0:T(8,128)S(1)}, f32[16,1024]{1,0:T(8,128)S(1)}, u32[]{:S(2)}, u32[]{:S(2)}) collective-permute-start(f32[16,1024]{1,0:T(8,128)S(1)} %get-tuple-element.117), channel_id=1, source_target_pairs={{0,4},{1,5},{2,6},{3,7},{4,0},{5,1},{6,2},{7,3},{8,12},{9,13},{10,... | collective-permute-start | bytes 196616 | tf_op jit(solution)/shard_map/ppermute | solution.py:63
  79.3 7.7 %collective-permute-start.22 = (f32[8,1024]{1,0:T(8,128)S(1)}, f32[8,1024]{1,0:T(8,128)S(1)}, u32[]{:S(2)}, u32[]{:S(2)}) collective-permute-start(f32[8,1024]{1,0:T(8,128)S(1)} %log_add_fusion.1), channel_id=1, source_target_pairs={{0,6},{1,7},{2,4},{3,5},{4,2},{5,3},{6,0},{7,1},{8,14},{9,15},{10,... | collective-permute-start | bytes 98312 | tf_op jit(solution)/shard_map/ppermute | solution.py:63
  81.3 5.7 %collective-permute-start.21 = (f32[8,1024]{1,0:T(8,128)S(1)}, f32[8,1024]{1,0:T(8,128)S(1)}, u32[]{:S(2)}, u32[]{:S(2)}) collective-permute-start(f32[8,1024]{1,0:T(8,128)S(1)} %log_add_fusion.1), channel_id=1, source_target_pairs={{0,4},{1,5},{2,6},{3,7},{4,0},{5,1},{6,2},{7,3},{8,12},{9,13},{10,... | collective-permute-start | bytes 98312 | tf_op jit(solution)/shard_map/ppermute | solution.py:63
  87.0 30.4 %collective-permute-start.40 = (bf16[160,1024]{1,0:T(8,128)(2,1)S(1)}, bf16[160,1024]{1,0:T(8,128)(2,1)S(1)}, u32[]{:S(2)}, u32[]{:S(2)}) collective-permute-start(bf16[160,1024]{1,0:T(8,128)(2,1)S(1)} %get-tuple-element.145), channel_id=1, source_target_pairs={{0,6},{1,7},{2,4},{3,5},{4,2},{5,3},{6,0},{7,1},{8,14},{9,15},{10,... | collective-permute-start | bytes 983048 | tf_op jit(solution)/shard_map/ppermute | solution.py:63
  89.1 28.4 %collective-permute-start.39 = (bf16[160,1024]{1,0:T(8,128)(2,1)S(1)}, bf16[160,1024]{1,0:T(8,128)(2,1)S(1)}, u32[]{:S(2)}, u32[]{:S(2)}) collective-permute-start(bf16[160,1024]{1,0:T(8,128)(2,1)S(1)} %get-tuple-element.145), channel_id=1, source_target_pairs={{0,4},{1,5},{2,6},{3,7},{4,0},{5,1},{6,2},{7,3},{8,12},{9,13},{10,... | collective-permute-start | bytes 983048 | tf_op jit(solution)/shard_map/ppermute | solution.py:63
  89.2 28.3 %collective-permute-start.38 = (bf16[160,1024]{1,0:T(8,128)(2,1)S(1)}, bf16[160,1024]{1,0:T(8,128)(2,1)S(1)}, u32[]{:S(2)}, u32[]{:S(2)}) collective-permute-start(bf16[160,1024]{1,0:T(8,128)(2,1)S(1)} %get-tuple-element.145), channel_id=1, source_target_pairs={{0,2},{1,3},{2,0},{3,1},{4,6},{5,7},{6,4},{7,5},{8,10},{9,11},{10,... | collective-permute-start | bytes 983048 | tf_op jit(solution)/shard_map/ppermute | solution.py:63
  117.6 33.3 %collective-permute-start.41 = (bf16[4,160,1024]{2,1,0:T(8,128)(2,1)S(1)}, bf16[4,160,1024]{2,1,0:T(8,128)(2,1)S(1)}, u32[]{:S(2)}, u32[]{:S(2)}) collective-permute-start(bf16[4,160,1024]{2,1,0:T(8,128)(2,1)S(1)} %pad_maximum_fusion.refs_11_.refs_2_), channel_id=1, source_target_pairs={{0,1},{1,0},{2,3},{3,2},{4,5},{5,4},{6,7},{7,6},{8,9},{9,8},{10,11... | collective-permute-start | bytes 3932168 | tf_op jit(solution)/shard_map/ppermute | solution.py:63
  117.9 6.5 %collective-permute-start.25 = (f32[8,1024]{1,0:T(8,128)S(1)}, f32[8,1024]{1,0:T(8,128)S(1)}, u32[]{:S(2)}, u32[]{:S(2)}) collective-permute-start(f32[8,1024]{1,0:T(8,128)S(1)} %add.152), channel_id=1, source_target_pairs={{0,4},{1,5},{2,6},{3,7},{4,0},{5,1},{6,2},{7,3},{8,12},{9,13},{10,... | collective-permute-start | bytes 98312 | tf_op jit(solution)/shard_map/ppermute | solution.py:63
  118.4 6.0 %collective-permute-start.26 = (f32[8,1024]{1,0:T(8,128)S(1)}, f32[8,1024]{1,0:T(8,128)S(1)}, u32[]{:S(2)}, u32[]{:S(2)}) collective-permute-start(f32[8,1024]{1,0:T(8,128)S(1)} %add.152), channel_id=1, source_target_pairs={{0,6},{1,7},{2,4},{3,5},{4,2},{5,3},{6,0},{7,1},{8,14},{9,15},{10,... | collective-permute-start | bytes 98312 | tf_op jit(solution)/shard_map/ppermute | solution.py:63
  129.5 10.8 %collective-permute-start.28 = (f32[16,1024]{1,0:T(8,128)S(1)}, f32[16,1024]{1,0:T(8,128)S(1)}, u32[]{:S(2)}, u32[]{:S(2)}) collective-permute-start(f32[16,1024]{1,0:T(8,128)S(1)} %get-tuple-element.180), channel_id=1, source_target_pairs={{0,2},{1,3},{2,0},{3,1},{4,6},{5,7},{6,4},{7,5},{8,10},{9,11},{10,... | collective-permute-start | bytes 196616 | tf_op jit(solution)/shard_map/ppermute | solution.py:63
  130.4 9.9 %collective-permute-start.29 = (f32[16,1024]{1,0:T(8,128)S(1)}, f32[16,1024]{1,0:T(8,128)S(1)}, u32[]{:S(2)}, u32[]{:S(2)}) collective-permute-start(f32[16,1024]{1,0:T(8,128)S(1)} %get-tuple-element.179), channel_id=1, source_target_pairs={{0,4},{1,5},{2,6},{3,7},{4,0},{5,1},{6,2},{7,3},{8,12},{9,13},{10,... | collective-permute-start | bytes 196616 | tf_op jit(solution)/shard_map/ppermute | solution.py:63
  132.1 8.2 %collective-permute-start.30 = (f32[16,1024]{1,0:T(8,128)S(1)}, f32[16,1024]{1,0:T(8,128)S(1)}, u32[]{:S(2)}, u32[]{:S(2)}) collective-permute-start(f32[16,1024]{1,0:T(8,128)S(1)} %get-tuple-element.178), channel_id=1, source_target_pairs={{0,6},{1,7},{2,4},{3,5},{4,2},{5,3},{6,0},{7,1},{8,14},{9,15},{10,... | collective-permute-start | bytes 196616 | tf_op jit(solution)/shard_map/ppermute | solution.py:63
  140.3 6.6 %collective-permute-start.33 = (f32[16,1024]{1,0:T(8,128)S(1)}, f32[16,1024]{1,0:T(8,128)S(1)}, u32[]{:S(2)}, u32[]{:S(2)}) collective-permute-start(f32[16,1024]{1,0:T(8,128)S(1)} %fusion.5.refs_7_), channel_id=1, source_target_pairs={{0,6},{1,7},{2,4},{3,5},{4,2},{5,3},{6,0},{7,1},{8,14},{9,15},{10,... | collective-permute-start | bytes 196616 | tf_op jit(solution)/shard_map/ppermute | solution.py:63
  142.4 5.9 %collective-permute-start.32 = (f32[16,1024]{1,0:T(8,128)S(1)}, f32[16,1024]{1,0:T(8,128)S(1)}, u32[]{:S(2)}, u32[]{:S(2)}) collective-permute-start(f32[16,1024]{1,0:T(8,128)S(1)} %fusion.5.refs_7_), channel_id=1, source_target_pairs={{0,4},{1,5},{2,6},{3,7},{4,0},{5,1},{6,2},{7,3},{8,12},{9,13},{10,... | collective-permute-start | bytes 196616 | tf_op jit(solution)/shard_map/ppermute | solution.py:63
  142.4 5.9 %collective-permute-start.31 = (f32[16,1024]{1,0:T(8,128)S(1)}, f32[16,1024]{1,0:T(8,128)S(1)}, u32[]{:S(2)}, u32[]{:S(2)}) collective-permute-start(f32[16,1024]{1,0:T(8,128)S(1)} %fusion.5.refs_7_), channel_id=1, source_target_pairs={{0,2},{1,3},{2,0},{3,1},{4,6},{5,7},{6,4},{7,5},{8,10},{9,11},{10,... | collective-permute-start | bytes 196616 | tf_op jit(solution)/shard_map/ppermute | solution.py:63
  144.8 21.0 %collective-permute-start.44 = (f32[664,128]{1,0:T(8,128)S(1)}, f32[664,128]{1,0:T(8,128)S(1)}, u32[]{:S(2)}, u32[]{:S(2)}) collective-permute-start(f32[664,128]{1,0:T(8,128)S(1)} %shard_map.410), channel_id=1, source_target_pairs={{0,16},{8,24},{16,0},{24,8},{1,17},{9,25},{17,1},{25,9},{2,18},{10... | collective-permute-start | bytes 1019912 | tf_op jit(solution)/shard_map/ppermute | solution.py:63
  148.3 9.4 %collective-permute-start.34 = (f32[4,16,1024]{2,1,0:T(8,128)S(1)}, f32[4,16,1024]{2,1,0:T(8,128)S(1)}, u32[]{:S(2)}, u32[]{:S(2)}) collective-permute-start(f32[4,16,1024]{2,1,0:T(8,128)S(1)} %pad_maximum_fusion.2.refs_2_), channel_id=1, source_target_pairs={{0,1},{1,0},{2,3},{3,2},{4,5},{5,4},{6,7},{7,6},{8,9},{9,8},{10,11... | collective-permute-start | bytes 786440 | tf_op jit(solution)/shard_map/ppermute | solution.py:63
  148.4 8.2 %collective-permute-start.36 = (f32[8,128]{1,0:T(8,128)S(1)}, f32[8,128]{1,0:T(8,128)S(1)}, u32[]{:S(2)}, u32[]{:S(2)}) collective-permute-start(f32[8,128]{1,0:T(8,128)S(1)} %slice.77), channel_id=1, source_target_pairs={{0,16},{8,24},{16,0},{24,8},{1,17},{9,25},{17,1},{25,9},{2,18},{10... | collective-permute-start | bytes 12296 | tf_op jit(solution)/shard_map/ppermute | solution.py:63
  149.5 8.1 %collective-permute-start.37 = (f32[8,128]{1,0:T(8,128)S(1)}, f32[8,128]{1,0:T(8,128)S(1)}, u32[]{:S(2)}, u32[]{:S(2)}) collective-permute-start(f32[8,128]{1,0:T(8,128)S(1)} %slice.77), channel_id=1, source_target_pairs={{0,24},{8,16},{16,8},{24,0},{1,25},{9,17},{17,9},{25,1},{2,26},{10... | collective-permute-start | bytes 12296 | tf_op jit(solution)/shard_map/ppermute | solution.py:63
  151.0 6.7 %collective-permute-start.35 = (f32[8,128]{1,0:T(8,128)S(1)}, f32[8,128]{1,0:T(8,128)S(1)}, u32[]{:S(2)}, u32[]{:S(2)}) collective-permute-start(f32[8,128]{1,0:T(8,128)S(1)} %slice.77), channel_id=1, source_target_pairs={{0,8},{8,0},{16,24},{24,16},{1,9},{9,1},{17,25},{25,17},{2,10},{10... | collective-permute-start | bytes 12296 | tf_op jit(solution)/shard_map/ppermute | solution.py:63
  156.6 10.4 %collective-permute-start.46 = (f32[480,128]{1,0:T(8,128)S(1)}, f32[480,128]{1,0:T(8,128)S(1)}, u32[]{:S(2)}, u32[]{:S(2)}) collective-permute-start(f32[480,128]{1,0:T(8,128)S(1)} %shard_map.412), channel_id=1, source_target_pairs={{0,8},{8,0},{16,24},{24,16},{1,9},{9,1},{17,25},{25,17},{2,10},{10... | collective-permute-start | bytes 737288 | tf_op jit(solution)/shard_map/ppermute | solution.py:63
  164.8 7.7 %collective-permute-start.42 = (f32[368,128]{1,0:T(8,128)S(1)}, f32[368,128]{1,0:T(8,128)S(1)}, u32[]{:S(2)}, u32[]{:S(2)}) collective-permute-start(f32[368,128]{1,0:T(8,128)S(1)} %shard_map.411), channel_id=1, source_target_pairs={{0,8},{8,0},{16,24},{24,16},{1,9},{9,1},{17,25},{25,17},{2,10},{10... | collective-permute-start | bytes 565256 | tf_op jit(solution)/shard_map/ppermute | solution.py:63
  165.8 12.2 %collective-permute-start.45 = (f32[664,128]{1,0:T(8,128)S(1)}, f32[664,128]{1,0:T(8,128)S(1)}, u32[]{:S(2)}, u32[]{:S(2)}) collective-permute-start(f32[664,128]{1,0:T(8,128)S(1)} %add.172), channel_id=1, source_target_pairs={{0,8},{8,0},{16,24},{24,16},{1,9},{9,1},{17,25},{25,17},{2,10},{10... | collective-permute-start | bytes 1019912 | tf_op jit(solution)/shard_map/ppermute | solution.py:63
  167.0 11.3 %collective-permute-start.47 = (f32[480,128]{1,0:T(8,128)S(1)}, f32[480,128]{1,0:T(8,128)S(1)}, u32[]{:S(2)}, u32[]{:S(2)}) collective-permute-start(f32[480,128]{1,0:T(8,128)S(1)} %add.174), channel_id=1, source_target_pairs={{0,16},{8,24},{16,0},{24,8},{1,17},{9,25},{17,1},{25,9},{2,18},{10... | collective-permute-start | bytes 737288 | tf_op jit(solution)/shard_map/ppermute | solution.py:63
  172.5 5.7 %collective-permute-start.43 = (f32[368,128]{1,0:T(8,128)S(1)}, f32[368,128]{1,0:T(8,128)S(1)}, u32[]{:S(2)}, u32[]{:S(2)}) collective-permute-start(f32[368,128]{1,0:T(8,128)S(1)} %add.170), channel_id=1, source_target_pairs={{0,16},{8,24},{16,0},{24,8},{1,17},{9,25},{17,1},{25,9},{2,18},{10... | collective-permute-start | bytes 565256 | tf_op jit(solution)/shard_map/ppermute | solution.py:63
  179.1 5.6 %collective-permute-start.50 = (f32[48,128]{1,0:T(8,128)S(1)}, f32[48,128]{1,0:T(8,128)S(1)}, u32[]{:S(2)}, u32[]{:S(2)}) collective-permute-start(f32[48,128]{1,0:T(8,128)S(1)} %get-tuple-element.152), channel_id=1, source_target_pairs={{0,6},{1,7},{2,4},{3,5},{4,2},{5,3},{6,0},{7,1},{8,14},{9,15},{10,... | collective-permute-start | bytes 73736 | tf_op jit(solution)/shard_map/ppermute | solution.py:63
  (45 other events, 300.8 us)

commit v9 on v8

--- a/solution.py
+++ b/solution.py
@@ -432,7 +432,7 @@
             new.append(part)
         return tuple(new)
 
-    best = lax.fori_loop(0, genes // rows, top, tuple(jnp.full((8, 128), -3e38, F32) for _ in range(tiles)), unroll=5)
+    best = lax.fori_loop(0, genes // rows, top, tuple(jnp.full((8, 128), -3e38, F32) for _ in range(tiles)), unroll=10)
     high = [jnp.max(part, axis=0, keepdims=True) for part in best]
     wide = [jnp.broadcast_to(part, (8, 128)) for part in high]
 
@@ -454,7 +454,7 @@
             new.append(part)
         return tuple(new)
 
-    sums = lax.fori_loop(0, genes // rows, mass, tuple(jnp.zeros((8, 128), F32) for _ in range(tiles)), unroll=5)
+    sums = lax.fori_loop(0, genes // rows, mass, tuple(jnp.zeros((8, 128), F32) for _ in range(tiles)), unroll=10)
     top_ref[pl.ds(step, 1), :] = jnp.concatenate(high, axis=1)
     lse = [high[tile] + jnp.log(jnp.sum(sums[tile], axis=0, keepdims=True)) for tile in range(tiles)]
     lse_ref[pl.ds(step, 1), :] = jnp.concatenate(lse, axis=1)

time: 190 us -> 189 us (level)
  transfers between devices with their start and end apart: 52 -> 52, of which waited for: 23 -> 22; matrix products, arithmetic and copies ran while one was open for 1% -> 1% of each run, Pallas kernels for 38% -> 38%
where the time goes in v9:
time: 189 us
  Pallas kernels  88.1 us (47%)
  starting transfers between devices  62.8 us (33%)
  waiting for transfers between devices  34.3 us (18%)
  between operations  2.14 us (1%)
    pallas_call x16, Pallas kernels, call(): pl.pallas_call(kernel, out_shape=[pltpu.HBM(out[0], out[1]) if len(out) =...  88.1 us
    ppermute x52, starting transfers between devices, swap(): return lax.ppermute(value, axis, [(i, i ^ bit) for i in range(count)])  62.8 us
    ppermute x52, waiting for transfers between devices, swap(): return lax.ppermute(value, axis, [(i, i ^ bit) for i in range(count)])  34.3 us
  transfers between devices with their start and end apart: 52, of which 22 were waited for; matrix products, arithmetic and copies ran while one was open for 1% of the time, Pallas kernels for 38%

profile of v9, /device:TPU:0, one launch (start us, length us, event | category | flops | bytes accessed | tf_op | source)
XLA Modules:
  0.0 189.0 jit_solution(11029738621506471212)
XLA Ops:
  0.7 3.0 %shard_map.399 = (f32[2,128,1024]{2,1,0:T(8,128)S(1)}, bf16[2,128,1024]{2,1,0:T(8,128)(2,1)S(1)}) custom-call(s32[1]{0:T(128)} %bitcast.refs_0_.me_ref.refs_1_, bf16[320,8192]{1,0:T(8,128)(2,1)} %bitcast.49, f32[320,128]{1,0:T(8,128)} %refs_10_.1), custom_call_target="tpu_custom_call" | custom-call | bytes 11070000 | tf_op jit(solution)/shard_map/pallas_call | solution.py:46
  4.2 2.4 %shard_map.400 = (f32[2,128,1024]{2,1,0:T(8,128)S(1)}, bf16[2,128,1024]{2,1,0:T(8,128)(2,1)S(1)}) custom-call(s32[1]{0:T(128)} %bitcast.refs_0_.me_ref.refs_1_, bf16[320,8192]{1,0:T(8,128)(2,1)S(1)} %bitcast.51, f32[320,128]{1,0:T(8,128)} %refs_10_.1), custom_call_target="tpu_custom_call" | custom-call | bytes 7380000 | tf_op jit(solution)/shard_map/pallas_call | solution.py:46
  7.9 3.8 %collective-permute-start.2 = (bf16[1,128,1024]{2,1,0:T(8,128)(2,1)}, bf16[1,128,1024]{2,1,0:T(8,128)(2,1)S(1)}, u32[]{:S(2)}, u32[]{:S(2)}) collective-permute-start(bf16[1,128,1024]{2,1,0:T(8,128)(2,1)} %get-tuple-element.177), channel_id=1, source_target_pairs={{0,4},{1,5},{2,6},{3,7},{4,0},{5,1},{6,2},{7,3},{8,12},{9,13},{10,... | collective-permute-start | bytes 786440 | tf_op jit(solution)/shard_map/ppermute | solution.py:63
  14.5 16.5 %shard_map.402 = (bf16[320,8192]{1,0:T(8,128)(2,1)}, bf16[320,8192]{1,0:T(8,128)(2,1)}, bf16[144,8192]{1,0:T(8,128)(2,1)S(1)}, f32[8,1024]{1,0:T(8,128)S(1)}, f3...) custom-call(bf16[320,8192]{1,0:T(8,128)(2,1)} %bitcast.50, ...), custom_call_target="tpu_custom_call" | custom-call | bytes 55350000 | tf_op jit(solution)/shard_map/pallas_call | solution.py:46
  33.5 7.0 %collective-permute-start.7 = (f32[8,128]{1,0:T(8,128)S(1)}, f32[8,128]{1,0:T(8,128)S(1)}, u32[]{:S(2)}, u32[]{:S(2)}) collective-permute-start(f32[8,128]{1,0:T(8,128)S(1)} %add.135), channel_id=1, source_target_pairs={{0,4},{1,5},{2,6},{3,7},{4,0},{5,1},{6,2},{7,3},{8,12},{9,13},{10,... | collective-permute-start | bytes 12296 | tf_op jit(solution)/shard_map/ppermute | solution.py:63
  42.1 3.8 %collective-permute-done.8 = f32[8,128]{1,0:T(8,128)S(1)} collective-permute-done((f32[8,128]{1,0:T(8,128)S(1)}, f32[8,128]{1,0:T(8,128)S(1)}, u32[]{:S(2)}, u32[]{:S(2)}) %collective-permute-start.8) | collective-permute-done | bytes 4128 | tf_op jit(solution)/shard_map/ppermute | solution.py:63
  49.7 2.4 %collective-permute-done.11 = f32[8,128]{1,0:T(8,128)S(1)} collective-permute-done((f32[8,128]{1,0:T(8,128)S(1)}, f32[8,128]{1,0:T(8,128)S(1)}, u32[]{:S(2)}, u32[]{:S(2)}) %collective-permute-start.11) | collective-permute-done | bytes 4128 | tf_op jit(solution)/shard_map/ppermute | solution.py:63
  52.6 1.8 shard_map.404
  54.4 2.0 %collective-permute-start.14 = (f32[16,1024]{1,0:T(8,128)S(1)}, f32[16,1024]{1,0:T(8,128)S(1)}, u32[]{:S(2)}, u32[]{:S(2)}) collective-permute-start(f32[16,1024]{1,0:T(8,128)S(1)} %get-tuple-element.117), channel_id=1, source_target_pairs={{0,6},{1,7},{2,4},{3,5},{4,2},{5,3},{6,0},{7,1},{8,14},{9,15},{10,... | collective-permute-start | bytes 196616 | tf_op jit(solution)/shard_map/ppermute | solution.py:63
  56.4 2.4 %collective-permute-start.12 = (f32[16,1024]{1,0:T(8,128)S(1)}, f32[16,1024]{1,0:T(8,128)S(1)}, u32[]{:S(2)}, u32[]{:S(2)}) collective-permute-start(f32[16,1024]{1,0:T(8,128)S(1)} %get-tuple-element.117), channel_id=1, source_target_pairs={{0,2},{1,3},{2,0},{3,1},{4,6},{5,7},{6,4},{7,5},{8,10},{9,11},{10,... | collective-permute-start | bytes 196616 | tf_op jit(solution)/shard_map/ppermute | solution.py:63
  67.2 2.4 %collective-permute-done.18 = f32[8,128]{1,0:T(8,128)S(1)} collective-permute-done((f32[8,128]{1,0:T(8,128)S(1)}, f32[8,128]{1,0:T(8,128)S(1)}, u32[]{:S(2)}, u32[]{:S(2)}) %collective-permute-start.18) | collective-permute-done | bytes 4128 | tf_op jit(solution)/shard_map/ppermute | solution.py:63
  69.7 7.6 %shard_map.405 = (bf16[128,8192]{1,0:T(8,128)(2,1)S(1)}, f32[8,1024]{1,0:T(8,128)S(1)}, f32[16,8192]{1,0:T(8,128)S(1)}, f32[8,1024]{1,0:T(8,128)S(1)}, f32[320,8...) custom-call(s32[1]{0:T(128)} %bitcast.refs_0_.me_ref.refs_1_, f32[4,16,1024]{2,1,0:T(8,128)S(1)} %pad_maximum_fusion.1.refs_1_, ...), custom_call_target="tpu_custom_call" | custom-call | bytes 29520000 | tf_op jit(solution)/shard_map/pallas_call | solution.py:46
  78.6 2.0 %collective-permute-start.22 = (f32[8,1024]{1,0:T(8,128)S(1)}, f32[8,1024]{1,0:T(8,128)S(1)}, u32[]{:S(2)}, u32[]{:S(2)}) collective-permute-start(f32[8,1024]{1,0:T(8,128)S(1)} %log_add_fusion.1), channel_id=1, source_target_pairs={{0,6},{1,7},{2,4},{3,5},{4,2},{5,3},{6,0},{7,1},{8,14},{9,15},{10,... | collective-permute-start | bytes 98312 | tf_op jit(solution)/shard_map/ppermute | solution.py:63
  81.3 1.7 collective-permute-start.20
  83.1 3.3 %shard_map.406 = (f32[128,8192]{1,0:T(8,128)S(1)}, f32[160,128]{1,0:T(8,128)S(1)}) custom-call(bf16[320,8192]{1,0:T(8,128)(2,1)S(1)} %get-tuple-element.127.refs_0_, bf16[128,640]{1,0:T(8,128)(2,1)S(1)} %get-tuple-element.128.refs_1_, bf16[144,8192]{1,0:T(8,128)(2,1)S(1)} %get-tuple-element.118.refs_3_.refs_2_.refs_12_.refs_13_.refs_4_, ...), custom_call_target="tpu_custom_call" | custom-call | bytes 11070000 | tf_op jit(solution)/shard_map/pallas_call | solution.py:46
  86.4 2.0 %collective-permute-start.40 = (bf16[160,1024]{1,0:T(8,128)(2,1)S(1)}, bf16[160,1024]{1,0:T(8,128)(2,1)S(1)}, u32[]{:S(2)}, u32[]{:S(2)}) collective-permute-start(bf16[160,1024]{1,0:T(8,128)(2,1)S(1)} %get-tuple-element.145), channel_id=1, source_target_pairs={{0,6},{1,7},{2,4},{3,5},{4,2},{5,3},{6,0},{7,1},{8,14},{9,15},{10,... | collective-permute-start | bytes 983048 | tf_op jit(solution)/shard_map/ppermute | solution.py:63
  88.6 2.3 %collective-permute-start.38 = (bf16[160,1024]{1,0:T(8,128)(2,1)S(1)}, bf16[160,1024]{1,0:T(8,128)(2,1)S(1)}, u32[]{:S(2)}, u32[]{:S(2)}) collective-permute-start(bf16[160,1024]{1,0:T(8,128)(2,1)S(1)} %get-tuple-element.145), channel_id=1, source_target_pairs={{0,2},{1,3},{2,0},{3,1},{4,6},{5,7},{6,4},{7,5},{8,10},{9,11},{10,... | collective-permute-start | bytes 983048 | tf_op jit(solution)/shard_map/ppermute | solution.py:63
  90.9 24.7 %shard_map.407 = (bf16[640,8192]{1,0:T(8,128)(2,1)S(1)}, f32[8,1024]{1,0:T(8,128)S(1)}, f32[8,1024]{1,0:T(8,128)S(1)}, f32[320,128]{1,0:T(8,128)S(1)}) custom-call(bf16[128,8192]{1,0:T(8,128)(2,1)S(1)} %get-tuple-element.121.refs_4_.refs_0_.refs_1_, f32[320,8192]{1,0:T(8,128)S(1)} %get-tuple-element.122.refs_1_, ...), custom_call_target="tpu_custom_call" | custom-call | bytes 103320000 | tf_op jit(solution)/shard_map/pallas_call | solution.py:46
  117.8 1.9 collective-permute-start.26
  120.8 3.0 %shard_map.408.refs_1_ = f32[128,8192]{1,0:T(8,128)S(1)} custom-call(bf16[640,8192]{1,0:T(8,128)(2,1)S(1)} %get-tuple-element.133.refs_0_.refs_5_, bf16[128,640]{1,0:T(8,128)(2,1)S(1)} %get-tuple-element.128.refs_1_), custom_call_target="tpu_custom_call" | custom-call | bytes 14760000 | tf_op jit(solution)/shard_map/pallas_call | solution.py:46
  123.9 3.4 %shard_map.409 = (f32[4,16,1024]{2,1,0:T(8,128)S(1)}, f32[4,16,1024]{2,1,0:T(8,128)S(1)}) custom-call(s32[1]{0:T(128)} %bitcast.refs_0_.me_ref.refs_1_, f32[128,8192]{1,0:T(8,128)S(1)} %shard_map.408.refs_1_, f32[128,8192]{1,0:T(8,128)S(1)} %get-tuple-element.130.refs_2_, f32[8,1024]{1,0:T(8,128)S(1)} %add_add_fusion.refs_3_.refs_2_, ...), custom_call_target="tpu_custom_call" | custom-call | bytes 18450000 | tf_op jit(solution)/shard_map/pallas_call | solution.py:46
  131.4 1.9 collective-permute-start.30
  133.3 6.3 %shard_map.410 = f32[664,128]{1,0:T(8,128)S(1)} custom-call(bf16[320,8192]{1,0:T(8,128)(2,1)S(1)} %get-tuple-element.127.refs_0_, bf16[128,8192]{1,0:T(8,128)(2,1)S(1)} %get-tuple-element.121.refs_4_.refs_0_.refs_1_, f32[8,1024]{1,0:T(8,128)S(1)} %add_add_fusion.refs_3_.refs_2_, f32[8,1024]{1,0:T(8,128)S(1)} %get-tuple-element.123.refs_2_.refs_5_.refs_3_, ...), custom_call_target="tpu_custom_call" | custom-call | bytes 22140000 | tf_op jit(solution)/shard_map/pallas_call | solution.py:46
  139.7 2.0 %collective-permute-start.33 = (f32[16,1024]{1,0:T(8,128)S(1)}, f32[16,1024]{1,0:T(8,128)S(1)}, u32[]{:S(2)}, u32[]{:S(2)}) collective-permute-start(f32[16,1024]{1,0:T(8,128)S(1)} %fusion.5.refs_7_), channel_id=1, source_target_pairs={{0,6},{1,7},{2,4},{3,5},{4,2},{5,3},{6,0},{7,1},{8,14},{9,15},{10,... | collective-permute-start | bytes 196616 | tf_op jit(solution)/shard_map/ppermute | solution.py:63
  141.7 2.4 %collective-permute-start.31 = (f32[16,1024]{1,0:T(8,128)S(1)}, f32[16,1024]{1,0:T(8,128)S(1)}, u32[]{:S(2)}, u32[]{:S(2)}) collective-permute-start(f32[16,1024]{1,0:T(8,128)S(1)} %fusion.5.refs_7_), channel_id=1, source_target_pairs={{0,2},{1,3},{2,0},{3,1},{4,6},{5,7},{6,4},{7,5},{8,10},{9,11},{10,... | collective-permute-start | bytes 196616 | tf_op jit(solution)/shard_map/ppermute | solution.py:63
  152.0 3.9 %shard_map.412 = f32[480,128]{1,0:T(8,128)S(1)} custom-call(s32[1]{0:T(128)} %bitcast.refs_0_.me_ref.refs_1_, bf16[320,8192]{1,0:T(8,128)(2,1)S(1)} %bitcast.53, bf16[4,160,1024]{2,1,0:T(8,128)(2,1)S(1)} %pad_maximum_fusion.refs_11_.refs_2_, bf16[4,160,1024]{2,1,0:T(8,128)(2,1)S(1)} %collective-permute-done.41.refs_12_.refs_3_, ...), custom_call_target="tpu_custom_call" | custom-call | bytes 14760000 | tf_op jit(solution)/shard_map/pallas_call | solution.py:46
  157.1 7.1 %shard_map.411 = f32[368,128]{1,0:T(8,128)S(1)} custom-call(s32[1]{0:T(128)} %bitcast.refs_0_.me_ref.refs_1_, s32[1]{0:T(128)} %bitcast.refs_0_.me_ref.refs_1_, f32[4,16,1024]{2,1,0:T(8,128)S(1)} %pad_maximum_fusion.2.refs_2_, f32[4,16,1024]{2,1,0:T(8,128)S(1)} %collective-permute-done.34.refs_3_, ...), custom_call_target="tpu_custom_call" | custom-call | bytes 40590000 | tf_op jit(solution)/shard_map/pallas_call | solution.py:46
  168.0 3.9 %collective-permute-done.42 = f32[368,128]{1,0:T(8,128)S(1)} collective-permute-done((f32[368,128]{1,0:T(8,128)S(1)}, f32[368,128]{1,0:T(8,128)S(1)}, u32[]{:S(2)}, u32[]{:S(2)}) %collective-permute-start.42) | collective-permute-done | bytes 188448 | tf_op jit(solution)/shard_map/ppermute | solution.py:63
  173.5 3.9 %collective-permute-done.45 = f32[664,128]{1,0:T(8,128)S(1)} collective-permute-done((f32[664,128]{1,0:T(8,128)S(1)}, f32[664,128]{1,0:T(8,128)S(1)}, u32[]{:S(2)}, u32[]{:S(2)}) %collective-permute-start.45) | collective-permute-done | bytes 340000 | tf_op jit(solution)/shard_map/ppermute | solution.py:63
  178.4 2.0 %collective-permute-start.50 = (f32[48,128]{1,0:T(8,128)S(1)}, f32[48,128]{1,0:T(8,128)S(1)}, u32[]{:S(2)}, u32[]{:S(2)}) collective-permute-start(f32[48,128]{1,0:T(8,128)S(1)} %get-tuple-element.152), channel_id=1, source_target_pairs={{0,6},{1,7},{2,4},{3,5},{4,2},{5,3},{6,0},{7,1},{8,14},{9,15},{10,... | collective-permute-start | bytes 73736 | tf_op jit(solution)/shard_map/ppermute | solution.py:63
  180.6 2.2 %collective-permute-start.48 = (f32[48,128]{1,0:T(8,128)S(1)}, f32[48,128]{1,0:T(8,128)S(1)}, u32[]{:S(2)}, u32[]{:S(2)}) collective-permute-start(f32[48,128]{1,0:T(8,128)S(1)} %get-tuple-element.152), channel_id=1, source_target_pairs={{0,2},{1,3},{2,0},{3,1},{4,6},{5,7},{6,4},{7,5},{8,10},{9,11},{10,... | collective-permute-start | bytes 73736 | tf_op jit(solution)/shard_map/ppermute | solution.py:63
  186.6 2.2 %shard_map.414 = (f32[320,128]{1,0:T(8,128)}, f32[320,128]{1,0:T(8,128)}, f32[320,128]{1,0:T(8,128)}, bf16[320,128]{1,0:T(8,128)(2,1)}, f32[2,320,128]{2,1,0:T(8...) custom-call(s32[1]{0:T(128)} %bitcast.refs_0_.me_ref.refs_1_, ...), custom_call_target="tpu_custom_call" | custom-call | bytes 7380000 | tf_op jit(solution)/shard_map/pallas_call | solution.py:46
  (169 shorter events, 49.5 us)
Async XLA Ops:
  6.5 6.4 %collective-permute-start = (bf16[2,128,1024]{2,1,0:T(8,128)(2,1)S(1)}, bf16[2,128,1024]{2,1,0:T(8,128)(2,1)S(1)}, u32[]{:S(2)}, u32[]{:S(2)}) collective-permute-start(bf16[2,128,1024]{2,1,0:T(8,128)(2,1)S(1)} %get-tuple-element.102), channel_id=1, source_target_pairs={{0,1},{1,0},{2,3},{3,2},{4,5},{5,4},{6,7},{7,6},{8,9},{9,8},{10,11... | collective-permute-start | bytes 1572872 | tf_op jit(solution)/shard_map/ppermute | solution.py:63
  7.9 23.1 %collective-permute-start.2 = (bf16[1,128,1024]{2,1,0:T(8,128)(2,1)}, bf16[1,128,1024]{2,1,0:T(8,128)(2,1)S(1)}, u32[]{:S(2)}, u32[]{:S(2)}) collective-permute-start(bf16[1,128,1024]{2,1,0:T(8,128)(2,1)} %get-tuple-element.177), channel_id=1, source_target_pairs={{0,4},{1,5},{2,6},{3,7},{4,0},{5,1},{6,2},{7,3},{8,12},{9,13},{10,... | collective-permute-start | bytes 786440 | tf_op jit(solution)/shard_map/ppermute | solution.py:63
  11.6 19.3 %collective-permute-start.3 = (bf16[1,128,1024]{2,1,0:T(8,128)(2,1)S(1)}, bf16[1,128,1024]{2,1,0:T(8,128)(2,1)S(1)}, u32[]{:S(2)}, u32[]{:S(2)}) collective-permute-start(bf16[1,128,1024]{2,1,0:T(8,128)(2,1)S(1)} %get-tuple-element.176), channel_id=1, source_target_pairs={{0,6},{1,7},{2,4},{3,5},{4,2},{5,3},{6,0},{7,1},{8,14},{9,15},{10,... | collective-permute-start | bytes 786440 | tf_op jit(solution)/shard_map/ppermute | solution.py:63
  13.0 18.1 %collective-permute-start.4 = (bf16[1,128,1024]{2,1,0:T(8,128)(2,1)S(1)}, bf16[1,128,1024]{2,1,0:T(8,128)(2,1)S(1)}, u32[]{:S(2)}, u32[]{:S(2)}) collective-permute-start(bf16[1,128,1024]{2,1,0:T(8,128)(2,1)S(1)} %add_convert_fusion), channel_id=1, source_target_pairs={{0,2},{1,3},{2,0},{3,1},{4,6},{5,7},{6,4},{7,5},{8,10},{9,11},{10,... | collective-permute-start | bytes 786440 | tf_op jit(solution)/shard_map/ppermute | solution.py:63
  33.5 8.6 %collective-permute-start.7 = (f32[8,128]{1,0:T(8,128)S(1)}, f32[8,128]{1,0:T(8,128)S(1)}, u32[]{:S(2)}, u32[]{:S(2)}) collective-permute-start(f32[8,128]{1,0:T(8,128)S(1)} %add.135), channel_id=1, source_target_pairs={{0,4},{1,5},{2,6},{3,7},{4,0},{5,1},{6,2},{7,3},{8,12},{9,13},{10,... | collective-permute-start | bytes 12296 | tf_op jit(solution)/shard_map/ppermute | solution.py:63
  54.4 6.1 %collective-permute-start.14 = (f32[16,1024]{1,0:T(8,128)S(1)}, f32[16,1024]{1,0:T(8,128)S(1)}, u32[]{:S(2)}, u32[]{:S(2)}) collective-permute-start(f32[16,1024]{1,0:T(8,128)S(1)} %get-tuple-element.117), channel_id=1, source_target_pairs={{0,6},{1,7},{2,4},{3,5},{4,2},{5,3},{6,0},{7,1},{8,14},{9,15},{10,... | collective-permute-start | bytes 196616 | tf_op jit(solution)/shard_map/ppermute | solution.py:63
  56.4 5.5 %collective-permute-start.13 = (f32[16,1024]{1,0:T(8,128)S(1)}, f32[16,1024]{1,0:T(8,128)S(1)}, u32[]{:S(2)}, u32[]{:S(2)}) collective-permute-start(f32[16,1024]{1,0:T(8,128)S(1)} %get-tuple-element.117), channel_id=1, source_target_pairs={{0,4},{1,5},{2,6},{3,7},{4,0},{5,1},{6,2},{7,3},{8,12},{9,13},{10,... | collective-permute-start | bytes 196616 | tf_op jit(solution)/shard_map/ppermute | solution.py:63
  78.6 7.7 %collective-permute-start.22 = (f32[8,1024]{1,0:T(8,128)S(1)}, f32[8,1024]{1,0:T(8,128)S(1)}, u32[]{:S(2)}, u32[]{:S(2)}) collective-permute-start(f32[8,1024]{1,0:T(8,128)S(1)} %log_add_fusion.1), channel_id=1, source_target_pairs={{0,6},{1,7},{2,4},{3,5},{4,2},{5,3},{6,0},{7,1},{8,14},{9,15},{10,... | collective-permute-start | bytes 98312 | tf_op jit(solution)/shard_map/ppermute | solution.py:63
  80.7 5.7 %collective-permute-start.21 = (f32[8,1024]{1,0:T(8,128)S(1)}, f32[8,1024]{1,0:T(8,128)S(1)}, u32[]{:S(2)}, u32[]{:S(2)}) collective-permute-start(f32[8,1024]{1,0:T(8,128)S(1)} %log_add_fusion.1), channel_id=1, source_target_pairs={{0,4},{1,5},{2,6},{3,7},{4,0},{5,1},{6,2},{7,3},{8,12},{9,13},{10,... | collective-permute-start | bytes 98312 | tf_op jit(solution)/shard_map/ppermute | solution.py:63
  86.4 30.4 %collective-permute-start.40 = (bf16[160,1024]{1,0:T(8,128)(2,1)S(1)}, bf16[160,1024]{1,0:T(8,128)(2,1)S(1)}, u32[]{:S(2)}, u32[]{:S(2)}) collective-permute-start(bf16[160,1024]{1,0:T(8,128)(2,1)S(1)} %get-tuple-element.145), channel_id=1, source_target_pairs={{0,6},{1,7},{2,4},{3,5},{4,2},{5,3},{6,0},{7,1},{8,14},{9,15},{10,... | collective-permute-start | bytes 983048 | tf_op jit(solution)/shard_map/ppermute | solution.py:63
  88.5 28.4 %collective-permute-start.39 = (bf16[160,1024]{1,0:T(8,128)(2,1)S(1)}, bf16[160,1024]{1,0:T(8,128)(2,1)S(1)}, u32[]{:S(2)}, u32[]{:S(2)}) collective-permute-start(bf16[160,1024]{1,0:T(8,128)(2,1)S(1)} %get-tuple-element.145), channel_id=1, source_target_pairs={{0,4},{1,5},{2,6},{3,7},{4,0},{5,1},{6,2},{7,3},{8,12},{9,13},{10,... | collective-permute-start | bytes 983048 | tf_op jit(solution)/shard_map/ppermute | solution.py:63
  88.6 28.3 %collective-permute-start.38 = (bf16[160,1024]{1,0:T(8,128)(2,1)S(1)}, bf16[160,1024]{1,0:T(8,128)(2,1)S(1)}, u32[]{:S(2)}, u32[]{:S(2)}) collective-permute-start(bf16[160,1024]{1,0:T(8,128)(2,1)S(1)} %get-tuple-element.145), channel_id=1, source_target_pairs={{0,2},{1,3},{2,0},{3,1},{4,6},{5,7},{6,4},{7,5},{8,10},{9,11},{10,... | collective-permute-start | bytes 983048 | tf_op jit(solution)/shard_map/ppermute | solution.py:63
  117.1 33.3 %collective-permute-start.41 = (bf16[4,160,1024]{2,1,0:T(8,128)(2,1)S(1)}, bf16[4,160,1024]{2,1,0:T(8,128)(2,1)S(1)}, u32[]{:S(2)}, u32[]{:S(2)}) collective-permute-start(bf16[4,160,1024]{2,1,0:T(8,128)(2,1)S(1)} %pad_maximum_fusion.refs_11_.refs_2_), channel_id=1, source_target_pairs={{0,1},{1,0},{2,3},{3,2},{4,5},{5,4},{6,7},{7,6},{8,9},{9,8},{10,11... | collective-permute-start | bytes 3932168 | tf_op jit(solution)/shard_map/ppermute | solution.py:63
  117.3 6.5 %collective-permute-start.25 = (f32[8,1024]{1,0:T(8,128)S(1)}, f32[8,1024]{1,0:T(8,128)S(1)}, u32[]{:S(2)}, u32[]{:S(2)}) collective-permute-start(f32[8,1024]{1,0:T(8,128)S(1)} %add.152), channel_id=1, source_target_pairs={{0,4},{1,5},{2,6},{3,7},{4,0},{5,1},{6,2},{7,3},{8,12},{9,13},{10,... | collective-permute-start | bytes 98312 | tf_op jit(solution)/shard_map/ppermute | solution.py:63
  117.8 6.1 %collective-permute-start.26 = (f32[8,1024]{1,0:T(8,128)S(1)}, f32[8,1024]{1,0:T(8,128)S(1)}, u32[]{:S(2)}, u32[]{:S(2)}) collective-permute-start(f32[8,1024]{1,0:T(8,128)S(1)} %add.152), channel_id=1, source_target_pairs={{0,6},{1,7},{2,4},{3,5},{4,2},{5,3},{6,0},{7,1},{8,14},{9,15},{10,... | collective-permute-start | bytes 98312 | tf_op jit(solution)/shard_map/ppermute | solution.py:63
  128.9 10.8 %collective-permute-start.28 = (f32[16,1024]{1,0:T(8,128)S(1)}, f32[16,1024]{1,0:T(8,128)S(1)}, u32[]{:S(2)}, u32[]{:S(2)}) collective-permute-start(f32[16,1024]{1,0:T(8,128)S(1)} %get-tuple-element.180), channel_id=1, source_target_pairs={{0,2},{1,3},{2,0},{3,1},{4,6},{5,7},{6,4},{7,5},{8,10},{9,11},{10,... | collective-permute-start | bytes 196616 | tf_op jit(solution)/shard_map/ppermute | solution.py:63
  129.8 9.9 %collective-permute-start.29 = (f32[16,1024]{1,0:T(8,128)S(1)}, f32[16,1024]{1,0:T(8,128)S(1)}, u32[]{:S(2)}, u32[]{:S(2)}) collective-permute-start(f32[16,1024]{1,0:T(8,128)S(1)} %get-tuple-element.179), channel_id=1, source_target_pairs={{0,4},{1,5},{2,6},{3,7},{4,0},{5,1},{6,2},{7,3},{8,12},{9,13},{10,... | collective-permute-start | bytes 196616 | tf_op jit(solution)/shard_map/ppermute | solution.py:63
  131.4 8.2 %collective-permute-start.30 = (f32[16,1024]{1,0:T(8,128)S(1)}, f32[16,1024]{1,0:T(8,128)S(1)}, u32[]{:S(2)}, u32[]{:S(2)}) collective-permute-start(f32[16,1024]{1,0:T(8,128)S(1)} %get-tuple-element.178), channel_id=1, source_target_pairs={{0,6},{1,7},{2,4},{3,5},{4,2},{5,3},{6,0},{7,1},{8,14},{9,15},{10,... | collective-permute-start | bytes 196616 | tf_op jit(solution)/shard_map/ppermute | solution.py:63
  139.7 6.6 %collective-permute-start.33 = (f32[16,1024]{1,0:T(8,128)S(1)}, f32[16,1024]{1,0:T(8,128)S(1)}, u32[]{:S(2)}, u32[]{:S(2)}) collective-permute-start(f32[16,1024]{1,0:T(8,128)S(1)} %fusion.5.refs_7_), channel_id=1, source_target_pairs={{0,6},{1,7},{2,4},{3,5},{4,2},{5,3},{6,0},{7,1},{8,14},{9,15},{10,... | collective-permute-start | bytes 196616 | tf_op jit(solution)/shard_map/ppermute | solution.py:63
  141.7 6.0 %collective-permute-start.32 = (f32[16,1024]{1,0:T(8,128)S(1)}, f32[16,1024]{1,0:T(8,128)S(1)}, u32[]{:S(2)}, u32[]{:S(2)}) collective-permute-start(f32[16,1024]{1,0:T(8,128)S(1)} %fusion.5.refs_7_), channel_id=1, source_target_pairs={{0,4},{1,5},{2,6},{3,7},{4,0},{5,1},{6,2},{7,3},{8,12},{9,13},{10,... | collective-permute-start | bytes 196616 | tf_op jit(solution)/shard_map/ppermute | solution.py:63
  141.7 6.0 %collective-permute-start.31 = (f32[16,1024]{1,0:T(8,128)S(1)}, f32[16,1024]{1,0:T(8,128)S(1)}, u32[]{:S(2)}, u32[]{:S(2)}) collective-permute-start(f32[16,1024]{1,0:T(8,128)S(1)} %fusion.5.refs_7_), channel_id=1, source_target_pairs={{0,2},{1,3},{2,0},{3,1},{4,6},{5,7},{6,4},{7,5},{8,10},{9,11},{10,... | collective-permute-start | bytes 196616 | tf_op jit(solution)/shard_map/ppermute | solution.py:63
  144.2 21.0 %collective-permute-start.44 = (f32[664,128]{1,0:T(8,128)S(1)}, f32[664,128]{1,0:T(8,128)S(1)}, u32[]{:S(2)}, u32[]{:S(2)}) collective-permute-start(f32[664,128]{1,0:T(8,128)S(1)} %shard_map.410), channel_id=1, source_target_pairs={{0,16},{8,24},{16,0},{24,8},{1,17},{9,25},{17,1},{25,9},{2,18},{10... | collective-permute-start | bytes 1019912 | tf_op jit(solution)/shard_map/ppermute | solution.py:63
  147.7 9.3 %collective-permute-start.34 = (f32[4,16,1024]{2,1,0:T(8,128)S(1)}, f32[4,16,1024]{2,1,0:T(8,128)S(1)}, u32[]{:S(2)}, u32[]{:S(2)}) collective-permute-start(f32[4,16,1024]{2,1,0:T(8,128)S(1)} %pad_maximum_fusion.2.refs_2_), channel_id=1, source_target_pairs={{0,1},{1,0},{2,3},{3,2},{4,5},{5,4},{6,7},{7,6},{8,9},{9,8},{10,11... | collective-permute-start | bytes 786440 | tf_op jit(solution)/shard_map/ppermute | solution.py:63
  147.8 8.2 %collective-permute-start.36 = (f32[8,128]{1,0:T(8,128)S(1)}, f32[8,128]{1,0:T(8,128)S(1)}, u32[]{:S(2)}, u32[]{:S(2)}) collective-permute-start(f32[8,128]{1,0:T(8,128)S(1)} %slice.77), channel_id=1, source_target_pairs={{0,16},{8,24},{16,0},{24,8},{1,17},{9,25},{17,1},{25,9},{2,18},{10... | collective-permute-start | bytes 12296 | tf_op jit(solution)/shard_map/ppermute | solution.py:63
  148.9 8.1 %collective-permute-start.37 = (f32[8,128]{1,0:T(8,128)S(1)}, f32[8,128]{1,0:T(8,128)S(1)}, u32[]{:S(2)}, u32[]{:S(2)}) collective-permute-start(f32[8,128]{1,0:T(8,128)S(1)} %slice.77), channel_id=1, source_target_pairs={{0,24},{8,16},{16,8},{24,0},{1,25},{9,17},{17,9},{25,1},{2,26},{10... | collective-permute-start | bytes 12296 | tf_op jit(solution)/shard_map/ppermute | solution.py:63
  150.3 6.7 %collective-permute-start.35 = (f32[8,128]{1,0:T(8,128)S(1)}, f32[8,128]{1,0:T(8,128)S(1)}, u32[]{:S(2)}, u32[]{:S(2)}) collective-permute-start(f32[8,128]{1,0:T(8,128)S(1)} %slice.77), channel_id=1, source_target_pairs={{0,8},{8,0},{16,24},{24,16},{1,9},{9,1},{17,25},{25,17},{2,10},{10... | collective-permute-start | bytes 12296 | tf_op jit(solution)/shard_map/ppermute | solution.py:63
  156.0 10.4 %collective-permute-start.46 = (f32[480,128]{1,0:T(8,128)S(1)}, f32[480,128]{1,0:T(8,128)S(1)}, u32[]{:S(2)}, u32[]{:S(2)}) collective-permute-start(f32[480,128]{1,0:T(8,128)S(1)} %shard_map.412), channel_id=1, source_target_pairs={{0,8},{8,0},{16,24},{24,16},{1,9},{9,1},{17,25},{25,17},{2,10},{10... | collective-permute-start | bytes 737288 | tf_op jit(solution)/shard_map/ppermute | solution.py:63
  164.1 7.7 %collective-permute-start.42 = (f32[368,128]{1,0:T(8,128)S(1)}, f32[368,128]{1,0:T(8,128)S(1)}, u32[]{:S(2)}, u32[]{:S(2)}) collective-permute-start(f32[368,128]{1,0:T(8,128)S(1)} %shard_map.411), channel_id=1, source_target_pairs={{0,8},{8,0},{16,24},{24,16},{1,9},{9,1},{17,25},{25,17},{2,10},{10... | collective-permute-start | bytes 565256 | tf_op jit(solution)/shard_map/ppermute | solution.py:63
  165.2 12.2 %collective-permute-start.45 = (f32[664,128]{1,0:T(8,128)S(1)}, f32[664,128]{1,0:T(8,128)S(1)}, u32[]{:S(2)}, u32[]{:S(2)}) collective-permute-start(f32[664,128]{1,0:T(8,128)S(1)} %add.172), channel_id=1, source_target_pairs={{0,8},{8,0},{16,24},{24,16},{1,9},{9,1},{17,25},{25,17},{2,10},{10... | collective-permute-start | bytes 1019912 | tf_op jit(solution)/shard_map/ppermute | solution.py:63
  166.4 11.3 %collective-permute-start.47 = (f32[480,128]{1,0:T(8,128)S(1)}, f32[480,128]{1,0:T(8,128)S(1)}, u32[]{:S(2)}, u32[]{:S(2)}) collective-permute-start(f32[480,128]{1,0:T(8,128)S(1)} %add.174), channel_id=1, source_target_pairs={{0,16},{8,24},{16,0},{24,8},{1,17},{9,25},{17,1},{25,9},{2,18},{10... | collective-permute-start | bytes 737288 | tf_op jit(solution)/shard_map/ppermute | solution.py:63
  171.9 5.7 %collective-permute-start.43 = (f32[368,128]{1,0:T(8,128)S(1)}, f32[368,128]{1,0:T(8,128)S(1)}, u32[]{:S(2)}, u32[]{:S(2)}) collective-permute-start(f32[368,128]{1,0:T(8,128)S(1)} %add.170), channel_id=1, source_target_pairs={{0,16},{8,24},{16,0},{24,8},{1,17},{9,25},{17,1},{25,9},{2,18},{10... | collective-permute-start | bytes 565256 | tf_op jit(solution)/shard_map/ppermute | solution.py:63
  178.4 5.6 %collective-permute-start.50 = (f32[48,128]{1,0:T(8,128)S(1)}, f32[48,128]{1,0:T(8,128)S(1)}, u32[]{:S(2)}, u32[]{:S(2)}) collective-permute-start(f32[48,128]{1,0:T(8,128)S(1)} %get-tuple-element.152), channel_id=1, source_target_pairs={{0,6},{1,7},{2,4},{3,5},{4,2},{5,3},{6,0},{7,1},{8,14},{9,15},{10,... | collective-permute-start | bytes 73736 | tf_op jit(solution)/shard_map/ppermute | solution.py:63
  (45 other events, 300.9 us)
